TPU v7x, 32 devices: a whole 2x2x4 slice. The times are simulated.
32 devices in a mesh: dp: 4 (over y, x), table: 8 (over z, core).
Axes of the slice: x: 2, y: 2, z: 4, core: 2. Of those that a mesh axis runs over, the one named last changes fastest.
Arguments:
- hidden_in: bfloat16 [512, 4096], P('dp', 'table'), may hold values from -6 to 6
- gate_weight: bfloat16 [4096, 4096], P('dp', 'table'), may hold values from -0.09375 to 0.09375
- values: bfloat16 [1024, 4096], P('table'), may hold values from -6 to 6
- pick_rows: int32 [512, 32], P('dp'), may hold values from 0 to 1023, all different within a row
- pick_scores: float32 [512, 32], P('dp'), may hold values from -300 to 300
- grad_out: bfloat16 [512, 4096], P('dp', 'table'), may hold values from -6 to 6
Outputs:
- branch_out: bfloat16 [512, 4096], P('dp', 'table')
- grad_hidden: bfloat16 [512, 4096], P('dp', 'table')
- grad_gate: float32 [4096, 4096], P('dp', 'table')
- grad_values: float32 [1024, 4096], P('table')
- grad_scores: float32 [512, 32], P('dp')
Inputs may be any that keep to these rules, and one draw needn't show every extreme that they name: `pick_rows`: the 32 rows of a token are distinct.
All inputs are finite; a program needn't handle non-finite values.
Results may differ from a plain program's by a relative error of at most 0.025.
Values may be sent and summed in bfloat16 or wider, within the bound.
No kernel may reach another device: no remote copies, remote signals or barrier semaphores. Data moves between devices by JAX's collectives and lax.ppermute only.
A program may use at most 64 MiB of HBM per device.

v0:
```python
import jax
import jax.numpy as jnp
from jax import lax
from jax.sharding import PartitionSpec as P


def pick_weights(pick_scores):
    row_max = jnp.max(pick_scores, axis=1, keepdims=True)
    exponent = jnp.exp(pick_scores - row_max)
    return exponent / jnp.sum(exponent, axis=1, keepdims=True)


def spread_weights(row_ids, weights_bf, row_total):
    token_ids = lax.broadcasted_iota(jnp.int32, row_ids.shape, 0)
    empty = jnp.zeros((row_ids.shape[0], row_total), jnp.bfloat16)
    return empty.at[token_ids, row_ids].set(weights_bf, mode="drop")


def local(hidden_in, gate_weight, values, pick_rows, pick_scores, grad_out):
    weights = pick_weights(pick_scores)
    weights_bf = weights.astype(jnp.bfloat16)
    token_count = hidden_in.shape[0]
    col_count = hidden_in.shape[1]
    rows_here = values.shape[0]
    whole_in = lax.all_gather(hidden_in, "table", axis=1, tiled=True)
    weight_full = lax.all_gather(gate_weight, "dp", axis=0, tiled=True)
    local_rows = pick_rows - lax.axis_index("table") * rows_here
    owned = (local_rows >= 0) & (local_rows < rows_here)
    parked = jnp.where(owned, local_rows, rows_here)
    spread = spread_weights(parked, weights_bf, rows_here)
    partial_mem = jnp.dot(spread, values, preferred_element_type=jnp.float32)
    arrived = lax.all_to_all(
        partial_mem.astype(jnp.bfloat16), "table", split_axis=1, concat_axis=0, tiled=True
    ).astype(partial_mem.dtype)
    memory_read = jnp.sum(arrived.reshape(-1, token_count, col_count), axis=0)
    gate_input = jnp.dot(whole_in, weight_full, preferred_element_type=jnp.float32)
    sigmoid_v = jax.nn.sigmoid(gate_input)
    gate_value = gate_input * sigmoid_v
    gate_slope = sigmoid_v * (1.0 + gate_input * (1.0 - sigmoid_v))
    branch_out = (memory_read * gate_value).astype(jnp.bfloat16)
    upstream = grad_out.astype(jnp.float32)
    mem_grad = (upstream * gate_value).astype(jnp.bfloat16)
    gate_grad_in = (upstream * memory_read * gate_slope).astype(jnp.bfloat16)
    grad_full = lax.all_gather(mem_grad, "table", axis=1, tiled=True)
    value_term = lax.dot_general(
        spread, grad_full, (((0,), (0,)), ((), ())), preferred_element_type=jnp.float32
    )
    affinity_all = lax.dot_general(
        grad_full, values, (((1,), (1,)), ((), ())), preferred_element_type=jnp.float32
    )
    picked = jnp.take_along_axis(affinity_all, jnp.where(owned, local_rows, 0), axis=1)
    affinity_part = jnp.where(owned, picked, 0.0)
    affinity = lax.psum(affinity_part, "table")
    grad_scores = weights * (affinity - jnp.sum(weights * affinity, axis=1, keepdims=True))
    grad_values = lax.psum(value_term.astype(jnp.bfloat16), "dp").astype(jnp.float32)
    grad_gate = lax.psum_scatter(
        lax.dot_general(
            whole_in, gate_grad_in, (((0,), (0,)), ((), ())), preferred_element_type=jnp.float32
        ).astype(jnp.bfloat16),
        "dp",
        scatter_dimension=0,
        tiled=True,
    ).astype(jnp.float32)
    input_term = lax.dot_general(
        gate_grad_in, weight_full, (((1,), (1,)), ((), ())), preferred_element_type=jnp.float32
    )
    grad_hidden = lax.psum_scatter(
        input_term.astype(jnp.bfloat16), "table", scatter_dimension=1, tiled=True
    )
    return (branch_out, grad_hidden, grad_gate, grad_values, grad_scores)


def solution(mesh):
    placed = (
        P("dp", "table"),
        P("dp", "table"),
        P("table", None),
        P("dp", None),
        P("dp", None),
        P("dp", "table"),
    )
    return jax.shard_map(
        local,
        mesh=mesh,
        in_specs=placed,
        out_specs=(
            P("dp", "table"),
            P("dp", "table"),
            P("dp", "table"),
            P("table", None),
            P("dp", None),
        ),
        check_vma=False,
    )
```

profile of v0, /device:TPU:2, one launch (start us, length us, event | category | flops | bytes accessed | tf_op | source)
XLA Modules:
  0.0 266.7 jit_solution(17681281666222529993)
XLA Ops:
  7.2 0.7 all-gather.4.cloned.1.call-update
  8.0 0.7 all-gather.6.cloned.1.call-update
  8.7 0.8 copy.22
  9.7 0.7 multiply_reduce_fusion.1
  10.4 0.1 copy.24
  10.5 0.1 reshape.49
  10.6 0.8 copy.25
  11.4 0.7 reduce_max.9
  12.1 0.2 fusion.7
  12.3 0.1 fusion.12
  12.5 0.1 reshape.51
  12.5 28.6 %scatter_custom_fusion = bf16[16384]{0:T(1024)(128)(2,1)S(1)} fusion(s32[4096]{0:T(1024)S(1)} %reshape.49, bf16[4096]{0:T(1024)(128)(2,1)S(1)} %reshape.51, bf16[]{:T(256)} %constant.9.clone.1), kind=kCustom, calls=%fused_computation.33 | custom fusion | bytes 32770
  41.2 0.4 convolution_convert_fusion.3
  41.6 0.1 copy.31
  41.7 31.4 %all_to_all.13 = bf16[128,8,512]{2,0,1:T(8,128)(2,1)S(1)} all-to-all(bf16[128,8,512]{2,0,1:T(8,128)(2,1)S(1)} %bitcast.27), channel_id=1, replica_groups=mesh['dp'=4,'table'=8] {'table'}, dimensions={1} | all-to-all | bytes 2097152 | tf_op jit(solution)/shard_map/all_to_all | solution.py:32
  73.1 0.1 convert_reduce_fusion
  73.3 13.9 %all-gather.6.cloned.1.call-done = bf16[4096,512]{1,0:T(8,128)(2,1)} async-done(((bf16[1024,512]{1,0:T(8,128)(2,1)}), bf16[4096,512]{1,0:T(8,128)(2,1)}) %all-gather.6.cloned.1.call-update) | async-done | bytes 4194320 | tf_op jit(solution)/shard_map/all_gather | solution.py:26
  87.2 4.1 %fusion.2 = (bf16[128,512]{1,0:T(8,128)(2,1)S(1)}, bf16[128,512]{1,0:T(8,128)(2,1)}, bf16[128,512]{1,0:T(8,128)(2,1)}) fusion(f32[128,512]{1,0:T(8,128)S(1)} %convert_reduce_fusion, bf16[128,512]{1,0:T(8,128)(2,1)S(1)} %copy-done.3, bf16[128,4096]{1,0:T(8,128)(2,1)} %all-gather.4.cloned.1.call-done, bf16[4096,512]{1,0:T(8,128)(2,1)} %all-gather.6.cloned.1.call-done), kind=kOutput, calls=%fused_computation.12 | convolution fusion | flops 537919488 | bytes 6029312 | tf_op jit(solution)/shard_map/dot_general | solution.py:36
  91.3 22.2 %all-gather.8.cloned.1.call-done = bf16[128,4096]{1,0:T(8,128)(2,1)} async-done(((bf16[128,512]{1,0:T(8,128)(2,1)}), bf16[128,4096]{1,0:T(8,128)(2,1)}) %all-gather.8.cloned.1.call-update) | async-done | bytes 1048592 | tf_op jit(solution)/shard_map/all_gather | solution.py:44
  113.5 2.7 convolution_convert_fusion.1
  116.3 3.2 %fusion = bf16[4096,512]{0,1:T(8,128)(2,1)} fusion(bf16[128,512]{1,0:T(8,128)(2,1)S(1)} %get-tuple-element.25, bf16[128,4096]{1,0:T(8,128)(2,1)S(1)} %copy-done.2), kind=kOutput, calls=%fused_computation.3 | convolution fusion | flops 538968064 | bytes 5373952 | tf_op jit(solution)/shard_map/dot_general | solution.py:57
  119.6 4.7 %convolution_convert_fusion.2 = bf16[128,4096]{1,0:T(8,128)(2,1)} fusion(bf16[128,512]{1,0:T(8,128)(2,1)S(1)} %get-tuple-element.25, bf16[4096,512]{1,0:T(8,128)(2,1)} %all-gather.6.cloned.1.call-done), kind=kOutput, calls=%fused_computation.5 | convolution fusion | flops 537395200 | bytes 5373952 | tf_op jit(solution)/shard_map/dot_general | solution.py:64
  124.5 0.4 fusion.13
  124.9 25.6 %gather_fusion = f32[4096]{0:T(1024)S(1)} fusion(f32[128,128]{1,0:T(8,128)S(1)} %fusion.13, s32[4096]{0:T(1024)S(1)} %reshape.43), kind=kCustom, calls=%fused_computation | custom fusion | bytes 65536 | tf_op jit(solution)/shard_map/jit(take_along_axis)/gather | solution.py:51
  150.6 27.9 %psum.15 = f32[128,32]{1,0:T(8,128)S(1)} all-reduce(f32[128,32]{1,0:T(8,128)S(1)} %select_select_fusion), channel_id=1, replica_groups=mesh['dp'=4,'table'=8] {'table'}, use_global_device_ids=true, to_apply=%region_7.8 | all-reduce | flops 4096 | bytes 32768 | tf_op jit(solution)/shard_map/psum | solution.py:53
  178.6 0.2 multiply_reduce_fusion
  178.7 0.1 subtract_multiply_fusion
  178.9 0.7 copy.28
  179.6 2.8 %convert_element_type.53 = f32[128,4096]{1,0:T(8,128)} convert(bf16[128,4096]{1,0:T(8,128)(2,1)} %all-reduce.2.cloned.1.call-done) | non-fusion elementwise | flops 524288 | bytes 3145728 | tf_op jit(solution)/shard_map/convert_element_type | solution.py:55
  182.3 42.3 %reduce-scatter.5.cloned.1.call-done = bf16[1024,512]{0,1:T(8,128)(2,1)} async-done(((bf16[4096,512]{0,1:T(8,128)(2,1)}), bf16[1024,512]{0,1:T(8,128)(2,1)}) %reduce-scatter.5.cloned.1.call-update) | async-done | bytes 1048592 | tf_op jit(solution)/shard_map/reduce_scatter | solution.py:56
  224.6 2.6 copy.27
  227.2 32.7 %reduce-scatter.3.cloned.1.call-done = bf16[128,512]{1,0:T(8,128)(2,1)} async-done(((bf16[128,4096]{1,0:T(8,128)(2,1)}), bf16[128,512]{1,0:T(8,128)(2,1)}) %reduce-scatter.3.cloned.1.call-update) | async-done | bytes 131088 | tf_op jit(solution)/shard_map/reduce_scatter | solution.py:67
  (29 shorter events, 0.7 us)
Async XLA Ops:
  7.2 34.0 %copy-start = (bf16[128,4096]{1,0:T(8,128)(2,1)S(1)}, bf16[128,4096]{1,0:T(8,128)(2,1)}, u32[]{:S(2)}) copy-start(bf16[128,4096]{1,0:T(8,128)(2,1)} %param.8) | copy-start | bytes 3145732
  7.2 66.1 %all-gather.4.cloned.1.call-start = ((), (), s32[]{:S(2)}) async-start(), calls=%async_computation.3 | async-start | bytes 1179648 | tf_op jit(solution)/shard_map/all_gather | solution.py:25
  7.9 79.3 %all-gather.6.cloned.1.call-start = ((), (), s32[]{:S(2)}) async-start(), calls=%async_computation.4 | async-start | bytes 5242880 | tf_op jit(solution)/shard_map/all_gather | solution.py:26
  8.7 104.9 %all-gather.8.cloned.1.call-start = ((), (), s32[]{:S(2)}) async-start(), calls=%async_computation.7 | async-start | bytes 1179648 | tf_op jit(solution)/shard_map/all_gather | solution.py:44
  41.7 45.5 %copy-start.3 = (bf16[128,512]{1,0:T(8,128)(2,1)S(1)}, bf16[128,512]{1,0:T(8,128)(2,1)}, u32[]{:S(2)}) copy-start(bf16[128,512]{1,0:T(8,128)(2,1)} %param.11) | copy-start | bytes 393220
  91.3 25.0 %copy-start.2 = (bf16[128,4096]{1,0:T(8,128)(2,1)S(1)}, bf16[128,4096]{1,0:T(8,128)(2,1)}, u32[]{:S(2)}) copy-start(bf16[128,4096]{1,0:T(8,128)(2,1)} %all-gather.4.cloned.1.call-done) | copy-start | bytes 3145732
  91.3 88.3 %all-reduce.2.cloned.1.call-start = ((), (), s32[]{:S(2)}) async-start(), calls=%async_computation.8 | async-start | bytes 2097152 | tf_op jit(solution)/shard_map/psum | solution.py:55
  116.2 108.5 %reduce-scatter.5.cloned.1.call-start = ((), (), s32[]{:S(2)}) async-start(), calls=%async_computation.6 | async-start | bytes 5242880 | tf_op jit(solution)/shard_map/reduce_scatter | solution.py:56
  119.5 4.9 %copy-start.1 = (bf16[128,4096]{1,0:T(8,128)(2,1)S(1)}, bf16[128,4096]{1,0:T(8,128)(2,1)}, u32[]{:S(2)}) copy-start(bf16[128,4096]{1,0:T(8,128)(2,1)} %all-gather.8.cloned.1.call-done) | copy-start | bytes 3145732
  119.5 140.4 %reduce-scatter.3.cloned.1.call-start = ((), (), s32[]{:S(2)}) async-start(), calls=%async_computation.5 | async-start | bytes 1179648 | tf_op jit(solution)/shard_map/reduce_scatter | solution.py:67
Sparse Core Ops, SparseCore 0:
  9.6 23.3 all-gather.3
  34.8 52.3 all-gather.5
  91.4 22.0 all-gather.7
  117.0 52.1 all-reduce.1
  172.0 52.5 reduce-scatter.4
  227.5 32.3 reduce-scatter.2
where the time goes:
time: 269 us; the launch traced here: 267 us
  waiting for transfers between devices  113 us (42%)
  local copies, waits for them, and re-layouts  59.7 us (22%)
  blocking collectives  59.3 us (22%)
  matrix products  15.5 us (6%)
  between operations  14.3 us (5%)
  other arithmetic  5.13 us (2%)
    reduce_scatter x1, waiting for transfers between devices, local(): lax.psum_scatter(lax.dot_general(whole_in, gate_grad_in, (((0,), (0,)), (...  42.3 us
    unnamed x15, local copies, waits for them, and re-layouts  33.7 us
    reduce_scatter x1, waiting for transfers between devices, local(): lax.psum_scatter(input_term.astype(jnp.bfloat16), 'table', scatter_dimens...  32.7 us
    all_to_all x1, blocking collectives, local(): lax.all_to_all(partial_mem.astype(jnp.bfloat16), 'table', split_axis=1, c...  31.4 us
    psum x1, blocking collectives, local(): affinity = lax.psum(affinity_part, 'table')  27.9 us
    gather x3, local copies, waits for them, and re-layouts, local(): jnp.take_along_axis(affinity_all, jnp.where(owned, local_rows, 0), axis=1)  25.8 us
    all_gather x1, waiting for transfers between devices, local(): grad_full = lax.all_gather(mem_grad, 'table', axis=1, tiled=True)  22.2 us
    all_gather x1, waiting for transfers between devices, local(): weight_full = lax.all_gather(gate_weight, 'dp', axis=0, tiled=True)  13.9 us
  transfers between devices with their start and end apart: 6, of which 4 were waited for; matrix products, arithmetic and copies ran while one was open for 28% of the time, Pallas kernels for 0%

commit v1 on v0

v1 whole, which is shorter than its diff:
```python
import functools

import jax
import jax.numpy as jnp
from jax import lax
from jax.experimental import pallas as pl
from jax.experimental.pallas import tpu as pltpu
from jax.sharding import PartitionSpec as P

DIRECT = 4


def block(x, index):
    return lax.dynamic_index_in_dim(x, index, 0, keepdims=False)


def placed(pieces, indices):
    out = jnp.zeros((len(pieces),) + pieces[0].shape, pieces[0].dtype)
    for piece, index in zip(pieces, indices):
        out = lax.dynamic_update_index_in_dim(out, piece, index, 0)
    return out


def hop(x, axis, size, mask):
    return lax.ppermute(x, axis, [(i, i ^ mask) for i in range(size)])


def order(axis, size):
    return [lax.axis_index(axis) ^ k for k in range(size)]


def gather(x, axis, size):
    if size <= DIRECT:
        return [x] + [hop(x, axis, size, k) for k in range(1, size)]
    whole = lax.all_gather(x, axis, axis=0)
    return [block(whole, k) for k in order(axis, size)]


def swap(pieces, axis, size, step=1):
    if len(pieces) <= DIRECT:
        return [pieces[0]] + [
            hop(pieces[k], axis, size, k * step) for k in range(1, len(pieces))
        ]
    ids = order(axis, size)
    whole = lax.all_to_all(placed(pieces, ids), axis, split_axis=0, concat_axis=0)
    return [block(whole, k) for k in ids]


def swap_table(pieces, size):
    if size // 2 <= DIRECT:
        rows, cols = pieces.shape[1:]
        pairs = pieces.reshape(size // 2, 2, rows, cols)
        other = hop(pairs[:, 1], "table", size, 1)
        both = jnp.stack([pairs[:, 0], other], axis=1)
        return swap([both[i] for i in range(size // 2)], "table", size, 2)
    got = swap([pieces[k] for k in range(size)], "table", size)
    return [jnp.stack(got[2 * i : 2 * i + 2]) for i in range(size // 2)]


def spread_kernel(rows_ref, weights_ref, out_ref):
    tile = 32
    tokens = rows_ref.shape[1]

    def step(i, carry):
        base = pl.multiple_of(i * tile, tile)
        here = lax.broadcasted_iota(jnp.int32, (tile, tokens), 0) + base
        total = jnp.zeros((tile, tokens), jnp.float32)
        for k in range(rows_ref.shape[0]):
            hit = rows_ref[k : k + 1, :] == here
            total = jnp.where(hit, weights_ref[k : k + 1, :], total)
        out_ref[pl.ds(base, tile), :] = total.astype(out_ref.dtype)
        return carry

    lax.fori_loop(0, out_ref.shape[0] // tile, step, 0)


def spread(rows, weights, row_total):
    picks, tokens = rows.shape
    width = min(tokens, 512)
    return pl.pallas_call(
        spread_kernel,
        grid=(tokens // width,),
        in_specs=[pl.BlockSpec((picks, width), lambda i: (0, i))] * 2,
        out_specs=pl.BlockSpec((row_total, width), lambda i: (0, i)),
        out_shape=jax.ShapeDtypeStruct((row_total, tokens), jnp.bfloat16),
        compiler_params=pltpu.CompilerParams(vmem_limit_bytes=16 << 20),
        cost_estimate=pl.CostEstimate(
            flops=2 * picks * tokens * row_total,
            bytes_accessed=2 * tokens * row_total,
            transcendentals=0,
        ),
    )(rows, weights)


def pick_kernel(table_ref, rows_ref, out_ref):
    lanes = 128
    rows = rows_ref[...]
    inner = rows & (lanes - 1)
    outer = rows >> 7
    total = jnp.zeros(out_ref.shape, jnp.float32)
    for j in range(table_ref.shape[1] // lanes):
        part = table_ref[:, j * lanes : (j + 1) * lanes]
        found = jnp.take_along_axis(part, inner, axis=1)
        total = jnp.where(outer == j, found, total)
    out_ref[...] = total


def pick(table, rows):
    return pl.pallas_call(
        pick_kernel,
        out_shape=jax.ShapeDtypeStruct(rows.shape, jnp.float32),
        cost_estimate=pl.CostEstimate(
            flops=rows.size * 16, bytes_accessed=4 * table.size, transcendentals=0
        ),
    )(table, rows)


def pick_weights(pick_scores):
    row_max = jnp.max(pick_scores, axis=1, keepdims=True)
    exponent = jnp.exp(pick_scores - row_max)
    return exponent / jnp.sum(exponent, axis=1, keepdims=True)


def hidden_rows(hidden_in, dp, table):
    tokens, cols = hidden_in.shape
    me, here = lax.axis_index("dp"), lax.axis_index("table")
    if table == 2 * dp and dp <= DIRECT:
        moved = []
        for k in range(dp):
            perm = [
                ((e * dp + z) * 2 + h, (z * dp + (e ^ k)) * 2 + h)
                for e in range(dp)
                for z in range(dp)
                for h in range(2)
            ]
            moved.append(lax.ppermute(hidden_in, ("dp", "table"), perm))
        mine = placed(moved, [(here // 2) ^ me ^ k for k in range(dp)])
        mine = mine.reshape(dp * tokens, cols)
        return [mine, hop(mine, "table", table, 1)]
    width = cols * table // dp
    wide = lax.all_gather(hidden_in, "table", axis=1, tiled=True)
    got = swap(
        [
            lax.dynamic_slice_in_dim(wide, k * width, width, 1)
            for k in order("dp", dp)
        ],
        "dp",
        dp,
    )
    return [jnp.concatenate(got, axis=0)]


def gate_slices(gate_weight, halves):
    if halves == 1:
        return [gate_weight]
    parts = gate_weight.reshape(2, -1, gate_weight.shape[1])
    core = lax.axis_index("table") % 2
    return [block(parts, core), block(parts, 1 - core)]


def return_hidden(grad_cols, weights, dp, table, tokens, cols):
    me, here = lax.axis_index("dp"), lax.axis_index("table")

    def term(weight):
        return lax.dot_general(
            grad_cols, weight, (((1,), (1,)), ((), ())), preferred_element_type=jnp.float32
        )

    if len(weights) == 2:
        arrived = hop(term(weights[1]).astype(jnp.bfloat16), "table", table, 1)
        pair = (term(weights[0]) + arrived.astype(jnp.float32)).astype(jnp.bfloat16)
        pair = pair.reshape(dp, tokens, cols)
        got = jnp.stack(swap([pair[k] for k in range(dp)], "dp", dp))
        sent = [block(got, (here // 2) ^ me ^ i) for i in range(dp)]
        terms = swap(sent, "table", table, 2)
    else:
        width = weights[0].shape[0]
        parts = term(weights[0]).astype(jnp.bfloat16).reshape(dp, tokens, width)
        got = swap([parts[k] for k in range(dp)], "dp", dp)
        wide = jnp.concatenate(
            list(placed(got, order("dp", dp))), axis=1
        ).reshape(tokens, table, cols)
        terms = swap([wide[:, k] for k in order("table", table)], "table", table)
    return functools.reduce(
        jnp.add, [t.astype(jnp.float32) for t in terms]
    ).astype(jnp.bfloat16)


def local(dp, table, hidden_in, gate_weight, values, pick_rows, pick_scores, grad_out):
    tokens, cols = hidden_in.shape
    rows_here, width = values.shape
    sub = rows_here // dp
    row_total = rows_here * table
    me, here = lax.axis_index("dp"), lax.axis_index("table")
    f32, bf16 = jnp.float32, jnp.bfloat16

    hidden_parts = hidden_rows(hidden_in, dp, table)
    weight_parts = gate_slices(gate_weight, len(hidden_parts))

    quarter = block(values.reshape(dp, sub, table, cols), me)
    sent = jnp.stack([lax.dynamic_index_in_dim(quarter, k, 1, keepdims=False) for k in order("table", table)])
    quarter = jnp.concatenate(
        [p.reshape(2 * sub, cols) for p in swap_table(sent, table)], axis=0
    )
    value_cols = jnp.concatenate(gather(quarter, "dp", dp), axis=0)

    owner, inner = pick_rows // rows_here, pick_rows % rows_here
    weights = pick_weights(pick_scores)
    weights_bf = weights.astype(bf16)

    def moved_row(row):
        owner, inner = row // rows_here, row % rows_here
        return ((inner // sub) ^ me) * (table * sub) + (owner ^ here) * sub + inner % sub

    small = jnp.concatenate(
        [pick_rows.astype(f32).T, weights_bf.astype(f32).T], axis=0
    )
    small_all = jnp.concatenate(gather(small, "dp", dp), axis=1)
    grad_out_all = jnp.concatenate(gather(grad_out, "dp", dp), axis=0)
    picks = pick_rows.shape[1]
    spread_all = spread(
        moved_row(small_all[:picks].astype(jnp.int32)), small_all[picks:], row_total
    )

    partial_gate = functools.reduce(
        jnp.add,
        [jnp.dot(a, b, preferred_element_type=f32) for a, b in zip(hidden_parts, weight_parts)],
    ).astype(bf16).reshape(dp, tokens, cols)
    terms = swap([partial_gate[k] for k in range(dp)], "dp", dp)
    gate_own = functools.reduce(jnp.add, [t.astype(f32) for t in terms]).astype(bf16)
    gate_input = jnp.concatenate(gather(gate_own, "dp", dp), axis=0).astype(f32)

    memory_read = lax.dot_general(
        spread_all, value_cols, (((0,), (0,)), ((), ())), preferred_element_type=f32
    )
    sigmoid_v = jax.nn.sigmoid(gate_input)
    gate_value = gate_input * sigmoid_v
    gate_slope = sigmoid_v * (1.0 + gate_input * (1.0 - sigmoid_v))
    upstream = grad_out_all.astype(f32)
    mem_grad = (upstream * gate_value).astype(bf16)
    gate_grad_in = (upstream * memory_read * gate_slope).astype(bf16)
    branch_out = (memory_read[:tokens] * gate_value[:tokens]).astype(bf16)

    value_term = jnp.dot(spread_all[: table * sub], mem_grad, preferred_element_type=f32)
    back = swap_table(value_term.astype(bf16).reshape(table, sub, cols), table)
    back = jnp.concatenate(back, axis=0)
    back = jnp.stack([block(back, k) for k in order("table", table)], axis=1)
    rows_back = gather(back.reshape(sub, width), "dp", dp)
    grad_values = placed(
        [r.astype(f32) for r in rows_back], order("dp", dp)
    ).reshape(rows_here, width)

    grad_hidden = return_hidden(gate_grad_in, weight_parts, dp, table, tokens, cols)

    if len(hidden_parts) == 2:
        core = here % 2
        hidden_abs = [jnp.where(core == j, *hidden_parts) for j in range(2)]
    else:
        hidden_abs = hidden_parts
    grad_gate = jnp.concatenate(
        [
            lax.dot_general(h, gate_grad_in, (((0,), (0,)), ((), ())), preferred_element_type=f32)
            for h in hidden_abs
        ],
        axis=0,
    )

    affinity_all = lax.dot_general(
        mem_grad[:tokens], value_cols, (((1,), (1,)), ((), ())), preferred_element_type=f32
    )
    own_rows = jnp.pad(moved_row(pick_rows), ((0, 0), (0, 128 - picks)))
    affinity = pick(affinity_all, own_rows)[:, :picks]
    if table // 2 <= DIRECT:
        affinity = affinity + hop(affinity, "table", table, 1)
        affinity = functools.reduce(
            jnp.add, [affinity] + [hop(affinity, "table", table, 2 * k) for k in range(1, table // 2)]
        )
    else:
        affinity = lax.psum(affinity, "table")
    grad_scores = weights * (affinity - jnp.sum(weights * affinity, axis=1, keepdims=True))
    return (branch_out, grad_hidden, grad_gate, grad_values, grad_scores)


def solution(mesh):
    split = P("dp", "table")
    return jax.shard_map(
        functools.partial(local, mesh.shape["dp"], mesh.shape["table"]),
        mesh=mesh,
        in_specs=(split, split, P("table", None), P("dp", None), P("dp", None), split),
        out_specs=(split, split, split, P("table", None), P("dp", None)),
        check_vma=False,
    )
```

time: 269 us -> 149 us (0.55)
  the two profiles are of different devices: /device:TPU:2 before, /device:TPU:0 now
where the time goes in v1:
time: 149 us; the launch traced here: 148 us
  waiting for transfers between devices  58.1 us (39%)
  starting transfers between devices  55.7 us (37%)
  other arithmetic  11.3 us (8%)
  Pallas kernels  7.45 us (5%)
  local copies, waits for them, and re-layouts  7.37 us (5%)
  matrix products  7.07 us (5%)
    ppermute x38, waiting for transfers between devices, hop(): return lax.ppermute(x, axis, [(i, i ^ mask) for i in range(size)])  58.1 us
    ppermute x38, starting transfers between devices, hop(): return lax.ppermute(x, axis, [(i, i ^ mask) for i in range(size)])  45.1 us
    ppermute x4, starting transfers between devices, hidden_rows(): moved.append(lax.ppermute(hidden_in, ('dp', 'table'), perm))  10.6 us
    pallas_call x1, Pallas kernels, spread(): pl.pallas_call(spread_kernel, grid=(tokens // width,), in_specs=[pl.Block...  5.36 us
    unnamed x40, local copies, waits for them, and re-layouts  4.29 us
  transfers between devices with their start and end apart: 42, of which 20 were waited for; matrix products, arithmetic and copies ran while one was open for 12% of the time, Pallas kernels for 4%

profile of v1, /device:TPU:0, one launch (start us, length us, event | category | flops | bytes accessed | tf_op | source)
XLA Modules:
  0.0 148.2 jit_solution(2166906844170217224)
XLA Ops:
  3.5 4.0 %collective-permute-start.2 = (f32[64,128]{0,1:T(8,128)S(1)}, f32[64,128]{0,1:T(8,128)S(1)}, u32[]{:S(2)}, u32[]{:S(2)}) collective-permute-start(f32[64,128]{0,1:T(8,128)S(1)} %pad_maximum_fusion.9), channel_id=1, source_target_pairs={{0,24},{8,16},{16,8},{24,0},{1,25},{9,17},{17,9},{25,1},{2,26},{10... | collective-permute-start | bytes 98312 | tf_op jit(solution)/shard_map/ppermute | solution.py:25
  8.1 2.0 %collective-permute-start.11 = (bf16[128,512]{1,0:T(8,128)(2,1)}, bf16[128,512]{1,0:T(8,128)(2,1)S(1)}, u32[]{:S(2)}, u32[]{:S(2)}) collective-permute-start(bf16[128,512]{1,0:T(8,128)(2,1)} %param.6), channel_id=1, source_target_pairs={{0,2},{1,3},{2,10},{3,11},{4,18},{5,19},{6,26},{7,27},{8,0},{9,1},... | collective-permute-start | bytes 393224 | tf_op jit(solution)/shard_map/ppermute | solution.py:136
  12.5 1.7 %copy.81 = bf16[16,8,8,512]{3,2,1,0:T(8,128)(2,1)S(1)} copy(bf16[16,8,8,512]{3,1,2,0:T(8,128)(2,1)} %bitcast.138) | data formatting | bytes 2097152
  15.8 7.0 %collective-permute-start.13 = (bf16[128,512]{1,0:T(8,128)(2,1)S(1)}, bf16[128,512]{1,0:T(8,128)(2,1)S(1)}, u32[]{:S(2)}, u32[]{:S(2)}) collective-permute-start(bf16[128,512]{1,0:T(8,128)(2,1)S(1)} %copy-done.6), channel_id=1, source_target_pairs={{0,6},{1,7},{2,14},{3,15},{4,22},{5,23},{6,30},{7,31},{8,4},{9,5},... | collective-permute-start | bytes 393224 | tf_op jit(solution)/shard_map/ppermute | solution.py:136
  23.8 5.4 %shard_map.101 = bf16[1024,512]{1,0:T(8,128)(2,1)S(1)} custom-call(s32[32,512]{1,0:T(8,128)S(1)} %copy.52.rows_ref, f32[32,512]{1,0:T(8,128)S(1)} %copy.53.weights_ref), custom_call_target="tpu_custom_call" | custom-call | flops 33554432 | bytes 1048576 | tf_op jit(solution)/shard_map/pallas_call | solution.py:80
  30.0 2.0 %collective-permute-start.6 = (bf16[2,32,512]{2,1,0:T(8,128)(2,1)S(1)}, bf16[2,32,512]{2,1,0:T(8,128)(2,1)S(1)}, u32[]{:S(2)}, u32[]{:S(2)}) collective-permute-start(bf16[2,32,512]{2,1,0:T(8,128)(2,1)S(1)} %get-tuple-element.53), channel_id=1, source_target_pairs={{0,6},{1,7},{2,4},{3,5},{4,2},{5,3},{6,0},{7,1},{8,14},{9,15},{10,... | collective-permute-start | bytes 196616 | tf_op jit(solution)/shard_map/ppermute | solution.py:25
  32.6 1.8 %collective-permute-start.5 = (bf16[2,32,512]{2,1,0:T(8,128)(2,1)S(1)}, bf16[2,32,512]{2,1,0:T(8,128)(2,1)S(1)}, u32[]{:S(2)}, u32[]{:S(2)}) collective-permute-start(bf16[2,32,512]{2,1,0:T(8,128)(2,1)S(1)} %get-tuple-element.56), channel_id=1, source_target_pairs={{0,4},{1,5},{2,6},{3,7},{4,0},{5,1},{6,2},{7,3},{8,12},{9,13},{10,... | collective-permute-start | bytes 196616 | tf_op jit(solution)/shard_map/ppermute | solution.py:25
  34.4 1.8 %collective-permute-done.6 = bf16[2,32,512]{2,1,0:T(8,128)(2,1)S(1)} collective-permute-done((bf16[2,32,512]{2,1,0:T(8,128)(2,1)S(1)}, bf16[2,32,512]{2,1,0:T(8,128)(2,1)S(1)}, u32[]{:S(2)}, u32[]{:S(2)}) %collective-permute-start.6) | collective-permute-done | bytes 65568 | tf_op jit(solution)/shard_map/ppermute | solution.py:25
  37.3 2.8 %collective-permute-done.5 = bf16[2,32,512]{2,1,0:T(8,128)(2,1)S(1)} collective-permute-done((bf16[2,32,512]{2,1,0:T(8,128)(2,1)S(1)}, bf16[2,32,512]{2,1,0:T(8,128)(2,1)S(1)}, u32[]{:S(2)}, u32[]{:S(2)}) %collective-permute-start.5) | collective-permute-done | bytes 65568 | tf_op jit(solution)/shard_map/ppermute | solution.py:25
  41.2 3.4 %collective-permute-start.7 = (bf16[256,512]{1,0:T(8,128)(2,1)S(1)}, bf16[256,512]{1,0:T(8,128)(2,1)S(1)}, u32[]{:S(2)}, u32[]{:S(2)}) collective-permute-start(bf16[256,512]{1,0:T(8,128)(2,1)S(1)} %pad_maximum_fusion.5), channel_id=1, source_target_pairs={{0,8},{8,0},{16,24},{24,16},{1,9},{9,1},{17,25},{25,17},{2,10},{10... | collective-permute-start | bytes 786440 | tf_op jit(solution)/shard_map/ppermute | solution.py:25
  46.9 2.3 %collective-permute-start.16 = (bf16[128,512]{1,0:T(8,128)(2,1)S(1)}, bf16[128,512]{1,0:T(8,128)(2,1)S(1)}, u32[]{:S(2)}, u32[]{:S(2)}) collective-permute-start(bf16[128,512]{1,0:T(8,128)(2,1)S(1)} %get-tuple-element.46), channel_id=1, source_target_pairs={{0,16},{8,24},{16,0},{24,8},{1,17},{9,25},{17,1},{25,9},{2,18},{10... | collective-permute-start | bytes 393224 | tf_op jit(solution)/shard_map/ppermute | solution.py:25
  49.2 8.3 %collective-permute-done.7 = bf16[256,512]{1,0:T(8,128)(2,1)S(1)} collective-permute-done((bf16[256,512]{1,0:T(8,128)(2,1)S(1)}, bf16[256,512]{1,0:T(8,128)(2,1)S(1)}, u32[]{:S(2)}, u32[]{:S(2)}) %collective-permute-start.7) | collective-permute-done | bytes 262176 | tf_op jit(solution)/shard_map/ppermute | solution.py:25
  57.5 2.8 %collective-permute-done.15 = bf16[128,512]{1,0:T(8,128)(2,1)S(1)} collective-permute-done((bf16[128,512]{1,0:T(8,128)(2,1)S(1)}, bf16[128,512]{1,0:T(8,128)(2,1)S(1)}, u32[]{:S(2)}, u32[]{:S(2)}) %collective-permute-start.15) | collective-permute-done | bytes 131104 | tf_op jit(solution)/shard_map/ppermute | solution.py:25
  60.5 1.7 %collective-permute-start.21 = (bf16[128,512]{1,0:T(8,128)(2,1)S(1)}, bf16[128,512]{1,0:T(8,128)(2,1)S(1)}, u32[]{:S(2)}, u32[]{:S(2)}) collective-permute-start(bf16[128,512]{1,0:T(8,128)(2,1)S(1)} %copy-done.7), channel_id=1, source_target_pairs={{0,8},{8,0},{16,24},{24,16},{1,9},{9,1},{17,25},{25,17},{2,10},{10... | collective-permute-start | bytes 393224 | tf_op jit(solution)/shard_map/ppermute | solution.py:25
  62.1 2.6 %collective-permute-start.23 = (bf16[128,512]{1,0:T(8,128)(2,1)S(1)}, bf16[128,512]{1,0:T(8,128)(2,1)S(1)}, u32[]{:S(2)}, u32[]{:S(2)}) collective-permute-start(bf16[128,512]{1,0:T(8,128)(2,1)S(1)} %copy-done.7), channel_id=1, source_target_pairs={{0,24},{8,16},{16,8},{24,0},{1,25},{9,17},{17,9},{25,1},{2,26},{10... | collective-permute-start | bytes 393224 | tf_op jit(solution)/shard_map/ppermute | solution.py:25
  64.9 6.2 %collective-permute-done.22 = bf16[128,512]{1,0:T(8,128)(2,1)S(1)} collective-permute-done((bf16[128,512]{1,0:T(8,128)(2,1)S(1)}, bf16[128,512]{1,0:T(8,128)(2,1)S(1)}, u32[]{:S(2)}, u32[]{:S(2)}) %collective-permute-start.22) | collective-permute-done | bytes 131104 | tf_op jit(solution)/shard_map/ppermute | solution.py:25
  71.5 2.4 %collective-permute-start.19 = (bf16[128,512]{1,0:T(8,128)(2,1)S(1)}, bf16[128,512]{1,0:T(8,128)(2,1)S(1)}, u32[]{:S(2)}, u32[]{:S(2)}) collective-permute-start(bf16[128,512]{1,0:T(8,128)(2,1)S(1)} %add_convert_fusion.1), channel_id=1, source_target_pairs={{0,16},{8,24},{16,0},{24,8},{1,17},{9,25},{17,1},{25,9},{2,18},{10... | collective-permute-start | bytes 393224 | tf_op jit(solution)/shard_map/ppermute | solution.py:25
  75.0 2.8 %collective-permute-done.20 = bf16[128,512]{1,0:T(8,128)(2,1)S(1)} collective-permute-done((bf16[128,512]{1,0:T(8,128)(2,1)S(1)}, bf16[128,512]{1,0:T(8,128)(2,1)S(1)}, u32[]{:S(2)}, u32[]{:S(2)}) %collective-permute-start.20) | collective-permute-done | bytes 131104 | tf_op jit(solution)/shard_map/ppermute | solution.py:25
  79.2 1.9 %fusion.3 = (bf16[512,512]{1,0:T(8,128)(2,1)S(1)}, bf16[512,512]{1,0:T(8,128)(2,1)S(1)}, f32[512,512]{1,0:T(8,128)}) fusion(bf16[128,512]{1,0:T(8,128)(2,1)S(1)} %collective-permute-done.23, bf16[128,512]{1,0:T(8,128)(2,1)S(1)} %collective-permute-done.22, bf16[128,512]{1,0:T(8,128)(2,1)S(1)} %collective-permute-done.21, ...), kind=kOutput, calls=%fused_computation.12 | convolution fusion | flops 544473088 | bytes 5242880 | tf_op jit(solution)/shard_map/dot_general | solution.py:233
  83.4 2.1 %shard_map.102 = f32[128,128]{1,0:T(8,128)} custom-call(f32[128,1024]{1,0:T(8,128)} %fusion.44.table_ref, s32[128,128]{1,0:T(8,128)} %pad.4.rows_ref), custom_call_target="tpu_custom_call" | custom-call | flops 262144 | bytes 524288 | tf_op jit(solution)/shard_map/pallas_call | solution.py:109
  92.9 2.0 %collective-permute-start.40 = (f32[128,32]{1,0:T(8,128)S(1)}, f32[128,32]{1,0:T(8,128)S(1)}, u32[]{:S(2)}, u32[]{:S(2)}) collective-permute-start(f32[128,32]{1,0:T(8,128)S(1)} %slice_add_fusion), channel_id=1, source_target_pairs={{0,4},{1,5},{2,6},{3,7},{4,0},{5,1},{6,2},{7,3},{8,12},{9,13},{10,... | collective-permute-start | bytes 49160 | tf_op jit(solution)/shard_map/ppermute | solution.py:25
  97.7 4.0 %collective-permute-done.40 = f32[128,32]{1,0:T(8,128)S(1)} collective-permute-done((f32[128,32]{1,0:T(8,128)S(1)}, f32[128,32]{1,0:T(8,128)S(1)}, u32[]{:S(2)}, u32[]{:S(2)}) %collective-permute-start.40) | collective-permute-done | bytes 16416 | tf_op jit(solution)/shard_map/ppermute | solution.py:25
  102.1 1.7 %collective-permute-start.34 = (bf16[2,32,512]{2,1,0:T(8,128)(2,1)S(1)}, bf16[2,32,512]{2,1,0:T(8,128)(2,1)S(1)}, u32[]{:S(2)}, u32[]{:S(2)}) collective-permute-start(bf16[2,32,512]{2,1,0:T(8,128)(2,1)S(1)} %get-tuple-element.49), channel_id=1, source_target_pairs={{0,6},{1,7},{2,4},{3,5},{4,2},{5,3},{6,0},{7,1},{8,14},{9,15},{10,... | collective-permute-start | bytes 196616 | tf_op jit(solution)/shard_map/ppermute | solution.py:25
  103.8 1.8 %collective-permute-start.33 = (bf16[2,32,512]{2,1,0:T(8,128)(2,1)S(1)}, bf16[2,32,512]{2,1,0:T(8,128)(2,1)S(1)}, u32[]{:S(2)}, u32[]{:S(2)}) collective-permute-start(bf16[2,32,512]{2,1,0:T(8,128)(2,1)S(1)} %get-tuple-element.50), channel_id=1, source_target_pairs={{0,4},{1,5},{2,6},{3,7},{4,0},{5,1},{6,2},{7,3},{8,12},{9,13},{10,... | collective-permute-start | bytes 196616 | tf_op jit(solution)/shard_map/ppermute | solution.py:25
  106.4 2.3 %collective-permute-done.34 = bf16[2,32,512]{2,1,0:T(8,128)(2,1)S(1)} collective-permute-done((bf16[2,32,512]{2,1,0:T(8,128)(2,1)S(1)}, bf16[2,32,512]{2,1,0:T(8,128)(2,1)S(1)}, u32[]{:S(2)}, u32[]{:S(2)}) %collective-permute-start.34) | collective-permute-done | bytes 65568 | tf_op jit(solution)/shard_map/ppermute | solution.py:25
  108.7 2.7 %collective-permute-done.33 = bf16[2,32,512]{2,1,0:T(8,128)(2,1)S(1)} collective-permute-done((bf16[2,32,512]{2,1,0:T(8,128)(2,1)S(1)}, bf16[2,32,512]{2,1,0:T(8,128)(2,1)S(1)}, u32[]{:S(2)}, u32[]{:S(2)}) %collective-permute-start.33) | collective-permute-done | bytes 65568 | tf_op jit(solution)/shard_map/ppermute | solution.py:25
  113.4 1.8 %collective-permute-start.35 = (bf16[32,4096]{1,0:T(8,128)(2,1)S(1)}, bf16[32,4096]{1,0:T(8,128)(2,1)}, u32[]{:S(2)}, u32[]{:S(2)}) collective-permute-start(bf16[32,4096]{1,0:T(8,128)(2,1)S(1)} %bitcast.148), channel_id=1, source_target_pairs={{0,8},{8,0},{16,24},{24,16},{1,9},{9,1},{17,25},{25,17},{2,10},{10... | collective-permute-start | bytes 786440 | tf_op jit(solution)/shard_map/ppermute | solution.py:25
  115.7 9.2 %collective-permute-done.35 = bf16[32,4096]{1,0:T(8,128)(2,1)} collective-permute-done((bf16[32,4096]{1,0:T(8,128)(2,1)S(1)}, bf16[32,4096]{1,0:T(8,128)(2,1)}, u32[]{:S(2)}, u32[]{:S(2)}) %collective-permute-start.35) | collective-permute-done | bytes 262176 | tf_op jit(solution)/shard_map/ppermute | solution.py:25
  131.0 2.1 %collective-permute-done.27 = bf16[128,512]{1,0:T(8,128)(2,1)S(1)} collective-permute-done((bf16[128,512]{1,0:T(8,128)(2,1)S(1)}, bf16[128,512]{1,0:T(8,128)(2,1)S(1)}, u32[]{:S(2)}, u32[]{:S(2)}) %collective-permute-start.27) | collective-permute-done | bytes 131104 | tf_op jit(solution)/shard_map/ppermute | solution.py:25
  134.5 2.3 %collective-permute-start.30 = (bf16[128,512]{1,0:T(8,128)(2,1)S(1)}, bf16[128,512]{1,0:T(8,128)(2,1)S(1)}, u32[]{:S(2)}, u32[]{:S(2)}) collective-permute-start(bf16[128,512]{1,0:T(8,128)(2,1)S(1)} %get-tuple-element.38), channel_id=1, source_target_pairs={{0,6},{1,7},{2,4},{3,5},{4,2},{5,3},{6,0},{7,1},{8,14},{9,15},{10,... | collective-permute-start | bytes 393224 | tf_op jit(solution)/shard_map/ppermute | solution.py:25
  139.9 2.7 %collective-permute-done.30 = bf16[128,512]{1,0:T(8,128)(2,1)S(1)} collective-permute-done((bf16[128,512]{1,0:T(8,128)(2,1)S(1)}, bf16[128,512]{1,0:T(8,128)(2,1)S(1)}, u32[]{:S(2)}, u32[]{:S(2)}) %collective-permute-start.30) | collective-permute-done | bytes 131104 | tf_op jit(solution)/shard_map/ppermute | solution.py:25
  142.6 4.9 %collective-permute-done.29 = bf16[128,512]{1,0:T(8,128)(2,1)S(1)} collective-permute-done((bf16[128,512]{1,0:T(8,128)(2,1)S(1)}, bf16[128,512]{1,0:T(8,128)(2,1)S(1)}, u32[]{:S(2)}, u32[]{:S(2)}) %collective-permute-start.29) | collective-permute-done | bytes 131104 | tf_op jit(solution)/shard_map/ppermute | solution.py:25
  (151 shorter events, 44.5 us)
Async XLA Ops:
  3.5 12.3 %collective-permute-start.2 = (f32[64,128]{0,1:T(8,128)S(1)}, f32[64,128]{0,1:T(8,128)S(1)}, u32[]{:S(2)}, u32[]{:S(2)}) collective-permute-start(f32[64,128]{0,1:T(8,128)S(1)} %pad_maximum_fusion.9), channel_id=1, source_target_pairs={{0,24},{8,16},{16,8},{24,0},{1,25},{9,17},{17,9},{25,1},{2,26},{10... | collective-permute-start | bytes 98312 | tf_op jit(solution)/shard_map/ppermute | solution.py:25
  7.5 15.3 %collective-permute-start.1 = (f32[64,128]{0,1:T(8,128)S(1)}, f32[64,128]{0,1:T(8,128)S(1)}, u32[]{:S(2)}, u32[]{:S(2)}) collective-permute-start(f32[64,128]{0,1:T(8,128)S(1)} %pad_maximum_fusion.9), channel_id=1, source_target_pairs={{0,16},{8,24},{16,0},{24,8},{1,17},{9,25},{17,1},{25,9},{2,18},{10... | collective-permute-start | bytes 98312 | tf_op jit(solution)/shard_map/ppermute | solution.py:25
  8.0 14.8 %collective-permute-start = (f32[64,128]{0,1:T(8,128)S(1)}, f32[64,128]{0,1:T(8,128)S(1)}, u32[]{:S(2)}, u32[]{:S(2)}) collective-permute-start(f32[64,128]{0,1:T(8,128)S(1)} %pad_maximum_fusion.9), channel_id=1, source_target_pairs={{0,8},{8,0},{16,24},{24,16},{1,9},{9,1},{17,25},{25,17},{2,10},{10... | collective-permute-start | bytes 98312 | tf_op jit(solution)/shard_map/ppermute | solution.py:25
  8.1 21.2 %collective-permute-start.11 = (bf16[128,512]{1,0:T(8,128)(2,1)}, bf16[128,512]{1,0:T(8,128)(2,1)S(1)}, u32[]{:S(2)}, u32[]{:S(2)}) collective-permute-start(bf16[128,512]{1,0:T(8,128)(2,1)} %param.6), channel_id=1, source_target_pairs={{0,2},{1,3},{2,10},{3,11},{4,18},{5,19},{6,26},{7,27},{8,0},{9,1},... | collective-permute-start | bytes 393224 | tf_op jit(solution)/shard_map/ppermute | solution.py:136
  10.1 19.1 %collective-permute-start.10 = (bf16[128,512]{1,0:T(8,128)(2,1)}, bf16[128,512]{1,0:T(8,128)(2,1)S(1)}, u32[]{:S(2)}, u32[]{:S(2)}) collective-permute-start(bf16[128,512]{1,0:T(8,128)(2,1)} %param.6), channel_id=1, source_target_pairs={{0,0},{1,1},{2,8},{3,9},{4,16},{5,17},{6,24},{7,25},{8,2},{9,3},{1... | collective-permute-start | bytes 393224 | tf_op jit(solution)/shard_map/ppermute | solution.py:136
  15.8 13.6 %collective-permute-start.13 = (bf16[128,512]{1,0:T(8,128)(2,1)S(1)}, bf16[128,512]{1,0:T(8,128)(2,1)S(1)}, u32[]{:S(2)}, u32[]{:S(2)}) collective-permute-start(bf16[128,512]{1,0:T(8,128)(2,1)S(1)} %copy-done.6), channel_id=1, source_target_pairs={{0,6},{1,7},{2,14},{3,15},{4,22},{5,23},{6,30},{7,31},{8,4},{9,5},... | collective-permute-start | bytes 393224 | tf_op jit(solution)/shard_map/ppermute | solution.py:136
  22.8 7.2 %collective-permute-start.3 = (bf16[4,32,512]{2,1,0:T(8,128)(2,1)S(1)}, bf16[4,32,512]{2,1,0:T(8,128)(2,1)S(1)}, u32[]{:S(2)}, u32[]{:S(2)}) collective-permute-start(bf16[4,32,512]{2,1,0:T(8,128)(2,1)S(1)} %get-tuple-element.57), channel_id=1, source_target_pairs={{0,1},{1,0},{2,3},{3,2},{4,5},{5,4},{6,7},{7,6},{8,9},{9,8},{10,11... | collective-permute-start | bytes 393224 | tf_op jit(solution)/shard_map/ppermute | solution.py:25
  29.4 15.3 %collective-permute-start.14 = (bf16[512,512]{1,0:T(8,128)(2,1)S(1)}, bf16[512,512]{1,0:T(8,128)(2,1)S(1)}, u32[]{:S(2)}, u32[]{:S(2)}) collective-permute-start(bf16[512,512]{1,0:T(8,128)(2,1)S(1)} %bitcast.131), channel_id=1, source_target_pairs={{0,1},{1,0},{2,3},{3,2},{4,5},{5,4},{6,7},{7,6},{8,9},{9,8},{10,11... | collective-permute-start | bytes 1572872 | tf_op jit(solution)/shard_map/ppermute | solution.py:25
  32.6 7.5 %collective-permute-start.5 = (bf16[2,32,512]{2,1,0:T(8,128)(2,1)S(1)}, bf16[2,32,512]{2,1,0:T(8,128)(2,1)S(1)}, u32[]{:S(2)}, u32[]{:S(2)}) collective-permute-start(bf16[2,32,512]{2,1,0:T(8,128)(2,1)S(1)} %get-tuple-element.56), channel_id=1, source_target_pairs={{0,4},{1,5},{2,6},{3,7},{4,0},{5,1},{6,2},{7,3},{8,12},{9,13},{10,... | collective-permute-start | bytes 196616 | tf_op jit(solution)/shard_map/ppermute | solution.py:25
  40.1 31.4 %collective-permute-start.9 = (bf16[256,512]{1,0:T(8,128)(2,1)S(1)}, bf16[256,512]{1,0:T(8,128)(2,1)S(1)}, u32[]{:S(2)}, u32[]{:S(2)}) collective-permute-start(bf16[256,512]{1,0:T(8,128)(2,1)S(1)} %pad_maximum_fusion.5), channel_id=1, source_target_pairs={{0,24},{8,16},{16,8},{24,0},{1,25},{9,17},{17,9},{25,1},{2,26},{10... | collective-permute-start | bytes 786440 | tf_op jit(solution)/shard_map/ppermute | solution.py:25
  41.2 16.2 %collective-permute-start.7 = (bf16[256,512]{1,0:T(8,128)(2,1)S(1)}, bf16[256,512]{1,0:T(8,128)(2,1)S(1)}, u32[]{:S(2)}, u32[]{:S(2)}) collective-permute-start(bf16[256,512]{1,0:T(8,128)(2,1)S(1)} %pad_maximum_fusion.5), channel_id=1, source_target_pairs={{0,8},{8,0},{16,24},{24,16},{1,9},{9,1},{17,25},{25,17},{2,10},{10... | collective-permute-start | bytes 786440 | tf_op jit(solution)/shard_map/ppermute | solution.py:25
  45.6 14.6 %collective-permute-start.15 = (bf16[128,512]{1,0:T(8,128)(2,1)S(1)}, bf16[128,512]{1,0:T(8,128)(2,1)S(1)}, u32[]{:S(2)}, u32[]{:S(2)}) collective-permute-start(bf16[128,512]{1,0:T(8,128)(2,1)S(1)} %get-tuple-element.44), channel_id=1, source_target_pairs={{0,8},{8,0},{16,24},{24,16},{1,9},{9,1},{17,25},{25,17},{2,10},{10... | collective-permute-start | bytes 393224 | tf_op jit(solution)/shard_map/ppermute | solution.py:25
  45.7 14.8 %collective-permute-start.17 = (bf16[128,512]{1,0:T(8,128)(2,1)S(1)}, bf16[128,512]{1,0:T(8,128)(2,1)S(1)}, u32[]{:S(2)}, u32[]{:S(2)}) collective-permute-start(bf16[128,512]{1,0:T(8,128)(2,1)S(1)} %get-tuple-element.45), channel_id=1, source_target_pairs={{0,24},{8,16},{16,8},{24,0},{1,25},{9,17},{17,9},{25,1},{2,26},{10... | collective-permute-start | bytes 393224 | tf_op jit(solution)/shard_map/ppermute | solution.py:25
  46.9 15.2 %collective-permute-start.16 = (bf16[128,512]{1,0:T(8,128)(2,1)S(1)}, bf16[128,512]{1,0:T(8,128)(2,1)S(1)}, u32[]{:S(2)}, u32[]{:S(2)}) collective-permute-start(bf16[128,512]{1,0:T(8,128)(2,1)S(1)} %get-tuple-element.46), channel_id=1, source_target_pairs={{0,16},{8,24},{16,0},{24,8},{1,17},{9,25},{17,1},{25,9},{2,18},{10... | collective-permute-start | bytes 393224 | tf_op jit(solution)/shard_map/ppermute | solution.py:25
  57.4 16.6 %collective-permute-start.8 = (bf16[256,512]{1,0:T(8,128)(2,1)S(1)}, bf16[256,512]{1,0:T(8,128)(2,1)S(1)}, u32[]{:S(2)}, u32[]{:S(2)}) collective-permute-start(bf16[256,512]{1,0:T(8,128)(2,1)S(1)} %pad_maximum_fusion.5), channel_id=1, source_target_pairs={{0,16},{8,24},{16,0},{24,8},{1,17},{9,25},{17,1},{25,9},{2,18},{10... | collective-permute-start | bytes 786440 | tf_op jit(solution)/shard_map/ppermute | solution.py:25
  60.2 10.8 %collective-permute-start.22 = (bf16[128,512]{1,0:T(8,128)(2,1)S(1)}, bf16[128,512]{1,0:T(8,128)(2,1)S(1)}, u32[]{:S(2)}, u32[]{:S(2)}) collective-permute-start(bf16[128,512]{1,0:T(8,128)(2,1)S(1)} %copy-done.7), channel_id=1, source_target_pairs={{0,16},{8,24},{16,0},{24,8},{1,17},{9,25},{17,1},{25,9},{2,18},{10... | collective-permute-start | bytes 393224 | tf_op jit(solution)/shard_map/ppermute | solution.py:25
  60.5 14.5 %collective-permute-start.21 = (bf16[128,512]{1,0:T(8,128)(2,1)S(1)}, bf16[128,512]{1,0:T(8,128)(2,1)S(1)}, u32[]{:S(2)}, u32[]{:S(2)}) collective-permute-start(bf16[128,512]{1,0:T(8,128)(2,1)S(1)} %copy-done.7), channel_id=1, source_target_pairs={{0,8},{8,0},{16,24},{24,16},{1,9},{9,1},{17,25},{25,17},{2,10},{10... | collective-permute-start | bytes 393224 | tf_op jit(solution)/shard_map/ppermute | solution.py:25
  62.1 12.8 %collective-permute-start.23 = (bf16[128,512]{1,0:T(8,128)(2,1)S(1)}, bf16[128,512]{1,0:T(8,128)(2,1)S(1)}, u32[]{:S(2)}, u32[]{:S(2)}) collective-permute-start(bf16[128,512]{1,0:T(8,128)(2,1)S(1)} %copy-done.7), channel_id=1, source_target_pairs={{0,24},{8,16},{16,8},{24,0},{1,25},{9,17},{17,9},{25,1},{2,26},{10... | collective-permute-start | bytes 393224 | tf_op jit(solution)/shard_map/ppermute | solution.py:25
  71.0 6.7 %collective-permute-start.20 = (bf16[128,512]{1,0:T(8,128)(2,1)S(1)}, bf16[128,512]{1,0:T(8,128)(2,1)S(1)}, u32[]{:S(2)}, u32[]{:S(2)}) collective-permute-start(bf16[128,512]{1,0:T(8,128)(2,1)S(1)} %add_convert_fusion.1), channel_id=1, source_target_pairs={{0,24},{8,16},{16,8},{24,0},{1,25},{9,17},{17,9},{25,1},{2,26},{10... | collective-permute-start | bytes 393224 | tf_op jit(solution)/shard_map/ppermute | solution.py:25
  71.5 6.8 %collective-permute-start.19 = (bf16[128,512]{1,0:T(8,128)(2,1)S(1)}, bf16[128,512]{1,0:T(8,128)(2,1)S(1)}, u32[]{:S(2)}, u32[]{:S(2)}) collective-permute-start(bf16[128,512]{1,0:T(8,128)(2,1)S(1)} %add_convert_fusion.1), channel_id=1, source_target_pairs={{0,16},{8,24},{16,0},{24,8},{1,17},{9,25},{17,1},{25,9},{2,18},{10... | collective-permute-start | bytes 393224 | tf_op jit(solution)/shard_map/ppermute | solution.py:25
  85.5 16.4 %collective-permute-start.31 = (bf16[4,32,512]{2,1,0:T(8,128)(2,1)}, bf16[4,32,512]{2,1,0:T(8,128)(2,1)S(1)}, u32[]{:S(2)}, u32[]{:S(2)}) collective-permute-start(bf16[4,32,512]{2,1,0:T(8,128)(2,1)} %get-tuple-element.52), channel_id=1, source_target_pairs={{0,1},{1,0},{2,3},{3,2},{4,5},{5,4},{6,7},{7,6},{8,9},{9,8},{10,11... | collective-permute-start | bytes 393224 | tf_op jit(solution)/shard_map/ppermute | solution.py:25
  87.3 38.6 %collective-permute-start.24 = (bf16[512,512]{1,0:T(8,128)(2,1)}, bf16[512,512]{1,0:T(8,128)(2,1)S(1)}, u32[]{:S(2)}, u32[]{:S(2)}) collective-permute-start(bf16[512,512]{1,0:T(8,128)(2,1)} %convolution_convert_fusion), channel_id=1, source_target_pairs={{0,1},{1,0},{2,3},{3,2},{4,5},{5,4},{6,7},{7,6},{8,9},{9,8},{10,11... | collective-permute-start | bytes 1572872 | tf_op jit(solution)/shard_map/ppermute | solution.py:25
  92.9 8.9 %collective-permute-start.40 = (f32[128,32]{1,0:T(8,128)S(1)}, f32[128,32]{1,0:T(8,128)S(1)}, u32[]{:S(2)}, u32[]{:S(2)}) collective-permute-start(f32[128,32]{1,0:T(8,128)S(1)} %slice_add_fusion), channel_id=1, source_target_pairs={{0,4},{1,5},{2,6},{3,7},{4,0},{5,1},{6,2},{7,3},{8,12},{9,13},{10,... | collective-permute-start | bytes 49160 | tf_op jit(solution)/shard_map/ppermute | solution.py:25
  94.9 6.9 %collective-permute-start.39 = (f32[128,32]{1,0:T(8,128)S(1)}, f32[128,32]{1,0:T(8,128)S(1)}, u32[]{:S(2)}, u32[]{:S(2)}) collective-permute-start(f32[128,32]{1,0:T(8,128)S(1)} %slice_add_fusion), channel_id=1, source_target_pairs={{0,2},{1,3},{2,0},{3,1},{4,6},{5,7},{6,4},{7,5},{8,10},{9,11},{10,... | collective-permute-start | bytes 49160 | tf_op jit(solution)/shard_map/ppermute | solution.py:25
  102.1 6.6 %collective-permute-start.34 = (bf16[2,32,512]{2,1,0:T(8,128)(2,1)S(1)}, bf16[2,32,512]{2,1,0:T(8,128)(2,1)S(1)}, u32[]{:S(2)}, u32[]{:S(2)}) collective-permute-start(bf16[2,32,512]{2,1,0:T(8,128)(2,1)S(1)} %get-tuple-element.49), channel_id=1, source_target_pairs={{0,6},{1,7},{2,4},{3,5},{4,2},{5,3},{6,0},{7,1},{8,14},{9,15},{10,... | collective-permute-start | bytes 196616 | tf_op jit(solution)/shard_map/ppermute | solution.py:25
  103.8 7.6 %collective-permute-start.33 = (bf16[2,32,512]{2,1,0:T(8,128)(2,1)S(1)}, bf16[2,32,512]{2,1,0:T(8,128)(2,1)S(1)}, u32[]{:S(2)}, u32[]{:S(2)}) collective-permute-start(bf16[2,32,512]{2,1,0:T(8,128)(2,1)S(1)} %get-tuple-element.50), channel_id=1, source_target_pairs={{0,4},{1,5},{2,6},{3,7},{4,0},{5,1},{6,2},{7,3},{8,12},{9,13},{10,... | collective-permute-start | bytes 196616 | tf_op jit(solution)/shard_map/ppermute | solution.py:25
  111.6 26.3 %collective-permute-start.37 = (bf16[32,4096]{1,0:T(8,128)(2,1)S(1)}, bf16[32,4096]{1,0:T(8,128)(2,1)}, u32[]{:S(2)}, u32[]{:S(2)}) collective-permute-start(bf16[32,4096]{1,0:T(8,128)(2,1)S(1)} %bitcast.146), channel_id=1, source_target_pairs={{0,24},{8,16},{16,8},{24,0},{1,25},{9,17},{17,9},{25,1},{2,26},{10... | collective-permute-start | bytes 786440 | tf_op jit(solution)/shard_map/ppermute | solution.py:25
  112.4 17.6 %collective-permute-start.36 = (bf16[32,4096]{1,0:T(8,128)(2,1)S(1)}, bf16[32,4096]{1,0:T(8,128)(2,1)}, u32[]{:S(2)}, u32[]{:S(2)}) collective-permute-start(bf16[32,4096]{1,0:T(8,128)(2,1)S(1)} %bitcast.147), channel_id=1, source_target_pairs={{0,16},{8,24},{16,0},{24,8},{1,17},{9,25},{17,1},{25,9},{2,18},{10... | collective-permute-start | bytes 786440 | tf_op jit(solution)/shard_map/ppermute | solution.py:25
  113.4 11.6 %collective-permute-start.35 = (bf16[32,4096]{1,0:T(8,128)(2,1)S(1)}, bf16[32,4096]{1,0:T(8,128)(2,1)}, u32[]{:S(2)}, u32[]{:S(2)}) collective-permute-start(bf16[32,4096]{1,0:T(8,128)(2,1)S(1)} %bitcast.148), channel_id=1, source_target_pairs={{0,8},{8,0},{16,24},{24,16},{1,9},{9,1},{17,25},{25,17},{2,10},{10... | collective-permute-start | bytes 786440 | tf_op jit(solution)/shard_map/ppermute | solution.py:25
  126.5 6.6 %collective-permute-start.27 = (bf16[128,512]{1,0:T(8,128)(2,1)S(1)}, bf16[128,512]{1,0:T(8,128)(2,1)S(1)}, u32[]{:S(2)}, u32[]{:S(2)}) collective-permute-start(bf16[128,512]{1,0:T(8,128)(2,1)S(1)} %get-tuple-element.41), channel_id=1, source_target_pairs={{0,24},{8,16},{16,8},{24,0},{1,25},{9,17},{17,9},{25,1},{2,26},{10... | collective-permute-start | bytes 393224 | tf_op jit(solution)/shard_map/ppermute | solution.py:25
  134.5 8.2 %collective-permute-start.30 = (bf16[128,512]{1,0:T(8,128)(2,1)S(1)}, bf16[128,512]{1,0:T(8,128)(2,1)S(1)}, u32[]{:S(2)}, u32[]{:S(2)}) collective-permute-start(bf16[128,512]{1,0:T(8,128)(2,1)S(1)} %get-tuple-element.38), channel_id=1, source_target_pairs={{0,6},{1,7},{2,4},{3,5},{4,2},{5,3},{6,0},{7,1},{8,14},{9,15},{10,... | collective-permute-start | bytes 393224 | tf_op jit(solution)/shard_map/ppermute | solution.py:25
  136.8 10.7 %collective-permute-start.29 = (bf16[128,512]{1,0:T(8,128)(2,1)S(1)}, bf16[128,512]{1,0:T(8,128)(2,1)S(1)}, u32[]{:S(2)}, u32[]{:S(2)}) collective-permute-start(bf16[128,512]{1,0:T(8,128)(2,1)S(1)} %get-tuple-element.39), channel_id=1, source_target_pairs={{0,4},{1,5},{2,6},{3,7},{4,0},{5,1},{6,2},{7,3},{8,12},{9,13},{10,... | collective-permute-start | bytes 393224 | tf_op jit(solution)/shard_map/ppermute | solution.py:25
  (18 other events, 139.4 us)

commit v2 on v1

v2 whole, which is shorter than its diff:
```python
import functools

import jax
import jax.numpy as jnp
from jax import lax
from jax.experimental import pallas as pl
from jax.experimental.pallas import tpu as pltpu
from jax.sharding import Mesh
from jax.sharding import PartitionSpec as P

DIRECT = 4
TABLE = ("pair", "core")


def block(x, index):
    return lax.dynamic_index_in_dim(x, index, 0, keepdims=False)


def placed(pieces, indices):
    out = jnp.zeros((len(pieces),) + pieces[0].shape, pieces[0].dtype)
    for piece, index in zip(pieces, indices):
        out = lax.dynamic_update_index_in_dim(out, piece, index, 0)
    return out


def hop(x, axis, size, mask):
    return lax.ppermute(x, axis, [(i, i ^ mask) for i in range(size)])


def order(axis, size):
    return [lax.axis_index(axis) ^ k for k in range(size)]


def gather(x, axis, size):
    if size <= DIRECT:
        return [x] + [hop(x, axis, size, k) for k in range(1, size)]
    whole = lax.all_gather(x, axis, axis=0)
    return [block(whole, k) for k in order(axis, size)]


def swap(pieces, axis, size):
    if size <= DIRECT:
        return [pieces[0]] + [hop(pieces[k], axis, size, k) for k in range(1, size)]
    ids = order(axis, size)
    whole = lax.all_to_all(placed(pieces, ids), axis, split_axis=0, concat_axis=0)
    return [block(whole, k) for k in ids]


def exchange(x, axis):
    return lax.all_to_all(x, axis, split_axis=0, concat_axis=0, tiled=True)


def total(terms):
    return functools.reduce(jnp.add, [t.astype(jnp.float32) for t in terms])


def spread_kernel(rows_ref, weights_ref, out_ref):
    tile = 32
    tokens = rows_ref.shape[1]

    def step(i, carry):
        base = pl.multiple_of(i * tile, tile)
        here = lax.broadcasted_iota(jnp.int32, (tile, tokens), 0) + base
        total = jnp.zeros((tile, tokens), jnp.float32)
        for k in range(rows_ref.shape[0]):
            hit = rows_ref[k : k + 1, :] == here
            total = jnp.where(hit, weights_ref[k : k + 1, :], total)
        out_ref[pl.ds(base, tile), :] = total.astype(out_ref.dtype)
        return carry

    lax.fori_loop(0, out_ref.shape[0] // tile, step, 0)


def spread(rows, weights, row_total):
    picks, tokens = rows.shape
    width = min(tokens, 512)
    return pl.pallas_call(
        spread_kernel,
        grid=(tokens // width,),
        in_specs=[pl.BlockSpec((picks, width), lambda i: (0, i))] * 2,
        out_specs=pl.BlockSpec((row_total, width), lambda i: (0, i)),
        out_shape=jax.ShapeDtypeStruct((row_total, tokens), jnp.bfloat16),
        compiler_params=pltpu.CompilerParams(vmem_limit_bytes=16 << 20),
        cost_estimate=pl.CostEstimate(
            flops=2 * picks * tokens * row_total,
            bytes_accessed=2 * tokens * row_total,
            transcendentals=0,
        ),
    )(rows, weights)


def pick_kernel(table_ref, rows_ref, out_ref):
    lanes = 128
    rows = rows_ref[...]
    inner = rows & (lanes - 1)
    outer = rows >> 7
    total = jnp.zeros(out_ref.shape, jnp.float32)
    for j in range(table_ref.shape[1] // lanes):
        part = table_ref[:, j * lanes : (j + 1) * lanes]
        found = jnp.take_along_axis(part, inner, axis=1)
        total = jnp.where(outer == j, found, total)
    out_ref[...] = total


def pick(table, rows):
    return pl.pallas_call(
        pick_kernel,
        out_shape=jax.ShapeDtypeStruct(rows.shape, jnp.float32),
        cost_estimate=pl.CostEstimate(
            flops=rows.size * 16, bytes_accessed=4 * table.size, transcendentals=0
        ),
    )(table, rows)


def pick_weights(pick_scores):
    row_max = jnp.max(pick_scores, axis=1, keepdims=True)
    exponent = jnp.exp(pick_scores - row_max)
    return exponent / jnp.sum(exponent, axis=1, keepdims=True)


def contract(a, b, dim_a, dim_b):
    return lax.dot_general(
        a, b, (((dim_a,), (dim_b,)), ((), ())), preferred_element_type=jnp.float32
    )


def local_general(dp, pairs, hidden_in, gate_weight, values, pick_rows, pick_scores, grad_out):
    tokens, cols = hidden_in.shape
    rows_here, width = values.shape
    picks = pick_rows.shape[1]
    table = 2 * pairs
    sub = rows_here // dp
    me, pair, core = (lax.axis_index(a) for a in ("dp",) + TABLE)
    here = 2 * pair + core
    f32, bf16 = jnp.float32, jnp.bfloat16

    wide = lax.all_gather(hidden_in, TABLE, axis=1, tiled=True)
    wide = wide.reshape(tokens, dp, table * cols // dp).transpose(1, 0, 2)
    hidden_all = exchange(wide, "dp").reshape(dp * tokens, -1)

    weights = pick_weights(pick_scores)
    weights_bf = weights.astype(bf16)
    small = jnp.concatenate([weights_bf, (pick_rows >> 5).astype(bf16), (pick_rows & 31).astype(bf16)], axis=1)
    small = small.T.reshape(-1, cols)
    sent = lax.all_gather(jnp.concatenate([grad_out, small], axis=0), "dp", axis=0)
    grad_out_all = sent[:, :tokens].reshape(dp * tokens, cols)
    small = sent[:, tokens:].reshape(dp, 3, picks, tokens).transpose(1, 2, 0, 3)
    small = small.reshape(3, picks, dp * tokens).astype(f32)
    rows_all = small[1].astype(jnp.int32) * 32 + small[2].astype(jnp.int32)

    def moved_row(row):
        return ((row // rows_here) ^ here) * rows_here + row % rows_here

    spread_all = spread(moved_row(rows_all), small[0], rows_here * table)

    by_core = values.reshape(rows_here, pairs, 2, cols).transpose(2, 1, 0, 3)
    mine = block(by_core, core)
    other = hop(block(by_core, 1 - core), "core", 2, 1)
    value_sent = [
        jnp.concatenate([block(mine, z), block(other, z)], axis=0) for z in order("pair", pairs)
    ]
    value_cols = jnp.concatenate(swap(value_sent, "pair", pairs), axis=0)

    partial_gate = contract(hidden_all, gate_weight, 1, 0).astype(bf16)
    terms = exchange(partial_gate.reshape(dp, tokens, cols), "dp")
    gate_own = total([terms[k] for k in range(dp)]).astype(bf16)
    gate_input = lax.all_gather(gate_own, "dp", axis=0, tiled=True).astype(f32)

    memory_read = contract(spread_all, value_cols, 0, 0)
    sigmoid_v = jax.nn.sigmoid(gate_input)
    gate_value = gate_input * sigmoid_v
    gate_slope = sigmoid_v * (1.0 + gate_input * (1.0 - sigmoid_v))
    upstream = grad_out_all.astype(f32)
    mem_grad = (upstream * gate_value).astype(bf16)
    gate_grad_in = (upstream * memory_read * gate_slope).astype(bf16)

    def own(x):
        return block(x.reshape(dp, tokens, cols), me)

    branch_out = (own(memory_read) * own(gate_value)).astype(bf16)

    input_term = contract(gate_grad_in, gate_weight, 1, 1).astype(bf16)
    input_got = exchange(input_term.reshape(dp, tokens, -1), "dp")

    spread_parts = spread_all.reshape(pairs, 2, dp, sub, dp * tokens)
    part = jnp.concatenate(
        [
            lax.dynamic_slice(
                spread_parts, (z ^ pair, 0, me, 0, 0), (1, 2, 1, sub, dp * tokens)
            ).reshape(2 * sub, dp * tokens)
            for z in range(pairs)
        ],
        axis=0,
    )
    value_term = contract(part, mem_grad, 1, 0).astype(bf16).reshape(pairs, 2, sub, cols)
    value_other = hop(value_term[:, 1], "core", 2, 1)

    affinity_all = contract(own(mem_grad), value_cols, 1, 1)
    own_rows = jnp.pad(moved_row(pick_rows), ((0, 0), (0, 128 - picks)))
    affinity = pick(affinity_all, own_rows)[:, :picks]
    affinity = affinity + hop(affinity, "core", 2, 1)
    high = affinity.astype(bf16)
    low = (affinity - high.astype(f32)).astype(bf16)
    parts = jnp.concatenate([high, low], axis=1).reshape(-1, cols)

    back = exchange(
        jnp.concatenate(
            [value_term[:, 0], value_other, jnp.broadcast_to(parts, (pairs,) + parts.shape)], axis=1
        ),
        "pair",
    )
    affinity = back[:, 2 * sub :].reshape(pairs, tokens, 2 * picks).astype(f32)
    affinity = jnp.sum(affinity[:, :, :picks] + affinity[:, :, picks:], axis=0)
    grad_scores = weights * (affinity - jnp.sum(weights * affinity, axis=1, keepdims=True))

    first, second = back[:, :sub], back[:, sub : 2 * sub]
    back = jnp.stack(
        [jnp.where(core == 0, first, second), jnp.where(core == 0, second, first)], axis=1
    )
    back = back.transpose(2, 0, 1, 3).reshape(sub, width)
    grad_values = placed(
        [r.astype(f32) for r in gather(back, "dp", dp)], order("dp", dp)
    ).reshape(rows_here, width)

    wide = input_got.transpose(1, 0, 2).reshape(tokens, table, cols)
    input_terms = exchange(wide.transpose(1, 0, 2), TABLE)
    grad_hidden = total([input_terms[k] for k in range(table)]).astype(bf16)
    grad_gate = contract(hidden_all, gate_grad_in, 0, 0)
    return (branch_out, grad_hidden, grad_gate, grad_values, grad_scores)


def kernel_call(body, outs, *args, scratch=(), flops=0, after=()):
    count = len(args)
    size = sum(a.size * a.dtype.itemsize for a in args)
    size += sum(o.size * o.dtype.itemsize for o in outs)

    def whole_body(*refs):
        body(*refs[:count], *refs[count + len(after) :])

    vmem = pl.BlockSpec(memory_space=pltpu.VMEM)
    return pl.pallas_call(
        whole_body,
        in_specs=[pl.BlockSpec(memory_space=pltpu.SMEM)] + [vmem] * (count + len(after) - 1),
        out_specs=[vmem] * len(outs),
        out_shape=list(outs),
        scratch_shapes=list(scratch),
        compiler_params=pltpu.CompilerParams(vmem_limit_bytes=12 << 20),
        cost_estimate=pl.CostEstimate(flops=0, bytes_accessed=0, transcendentals=0),
    )(*args, *after)


def shape(dims, dtype=jnp.bfloat16):
    return jax.ShapeDtypeStruct(dims, dtype)


TOKEN = shape((8, 128), jnp.float32)


def sign(token):
    token[...] = jnp.zeros(token.shape, token.dtype)


def aligned(index, size):
    return pl.ds(pl.multiple_of(index * size, size), size)


def pack_rows(out_ref, first, x):
    count, lanes = x.shape
    per = out_ref.shape[1] // lanes
    for j in range(count):
        row, lane = (first + j) // per, (first + j) % per * lanes
        out_ref[row : row + 1, lane : lane + lanes] = x[j : j + 1, :]


def row_of(packed, j, lanes):
    per = packed.shape[1] // lanes
    return packed[j // per : j // per + 1, j % per * lanes : (j % per + 1) * lanes]


def prepare_body(ids, scores, rows, sent, weights, packed):
    x = scores[...]
    exponent = jnp.exp(x - jnp.max(x, axis=0, keepdims=True))
    w = exponent / jnp.sum(exponent, axis=0, keepdims=True)
    weights[...] = w
    packed[...] = jnp.zeros(packed.shape, packed.dtype)
    count = w.shape[0]
    pack_rows(packed, 0, w)
    pack_rows(packed, count, (rows[...] >> 5).astype(jnp.float32))
    pack_rows(packed, 2 * count, (rows[...] & 31).astype(jnp.float32))
    sent[...] = packed[...].astype(sent.dtype)


def moved(row, rows_here, pairs, pair, core):
    owner, inner = lax.div(row, rows_here), lax.rem(row, rows_here)
    return ((owner & 1) ^ core) * (pairs * rows_here) + ((owner >> 1) ^ pair) * rows_here + inner


def spread_body(picks, rows_here, ids, sent, out, part, token, rows, weights):
    sign(token)
    me, pair, core = ids[0], ids[1], ids[2]
    dp = sent.shape[0]
    tokens = rows.shape[1] // dp
    pairs = part.shape[0] // (2 * (rows_here // dp))
    for e in range(dp):
        packed = sent[e].astype(jnp.float32)
        span = slice(e * tokens, (e + 1) * tokens)
        for k in range(picks):
            weights[k : k + 1, span] = row_of(packed, k, tokens)
            high, low = row_of(packed, picks + k, tokens), row_of(packed, 2 * picks + k, tokens)
            rows[k : k + 1, span] = (high * 32.0 + low).astype(jnp.int32)
    rows[...] = moved(rows[...], rows_here, pairs, pair, core)
    tile = 32

    def step(i, carry):
        base = pl.multiple_of(i * tile, tile)
        here = lax.broadcasted_iota(jnp.int32, (tile, rows.shape[1]), 0) + base
        acc = jnp.zeros((tile, rows.shape[1]), jnp.float32)
        for k in range(picks):
            acc = jnp.where(rows[k : k + 1, :] == here, weights[k : k + 1, :], acc)
        out[pl.ds(base, tile), :] = acc.astype(out.dtype)
        return carry

    lax.fori_loop(0, out.shape[0] // tile, step, 0)
    sub = rows_here // dp
    for g in range(2):
        for z in range(pairs):
            at = (g * pairs + z) * rows_here + me * sub
            spot = (g * pairs + z) * sub
            part[spot : spot + sub, :] = out[pl.ds(pl.multiple_of(at, sub), sub), :]


def columns_body(ids, values, *outs):
    width = outs[0].shape[1]
    for k, out in enumerate(outs):
        out[...] = values[:, aligned(ids[1] ^ k, width)]


def halves_body(ids, *refs):
    pieces, (own, other) = refs[:-2], refs[-2:]
    rows, cols = pieces[0].shape[0], own.shape[1]
    for k, piece in enumerate(pieces):
        span = slice(k * rows, (k + 1) * rows)
        own[span, :] = piece[:, aligned(ids[2], cols)]
        other[span, :] = piece[:, aligned(1 - ids[2], cols)]


def dot(a, b, dim_a=1, dim_b=0):
    return lax.dot_general(
        a, b, (((dim_a,), (dim_b,)), ((), ())), preferred_element_type=jnp.float32
    )


def gate_body(ids, *refs):
    weight, first, second, stage = refs[-4:]
    dp = (len(refs) - 4) // 2
    cols = weight.shape[1]
    own, other = weight[aligned(ids[2], cols), :], weight[aligned(1 - ids[2], cols), :]
    for k in range(dp):
        term = dot(refs[k][...], own) + dot(refs[dp + k][...], other)
        stage[ids[1] ^ k] = term.astype(stage.dtype)
    half = dp // 2
    rows = stage.shape[1]
    for e in range(half):
        first[e * rows : (e + 1) * rows, :] = stage[e]
        second[e * rows : (e + 1) * rows, :] = stage[half + e]


def add_body(ids, a, a_got, b, b_got, a_keep, b_keep, a_send, b_send):
    f32 = jnp.float32
    for x, got, keep, send in ((a, a_got, a_keep, a_send), (b, b_got, b_keep, b_send)):
        keep[...] = (x[...].astype(f32) + got[...].astype(f32)).astype(keep.dtype)
        send[...] = keep[...]


def gate_value_of(stage, a0, a1, b0, b1):
    half = a0.shape[0]
    stage[:half, :] = a0[...].astype(jnp.float32) + a1[...].astype(jnp.float32)
    stage[half:, :] = b0[...].astype(jnp.float32) + b1[...].astype(jnp.float32)


def values_body(ids, a0, a1, b0, b1, grad_out, part, mem_grad, factor, value_own, keep, send, token, stage):
    tokens = value_own.shape[0]
    gate_value_of(stage, a0, a1, b0, b1)
    for k in range(grad_out.shape[0]):
        span = aligned(ids[0] ^ k, tokens)
        gate = stage[span, :]
        s = jax.nn.sigmoid(gate)
        upstream = grad_out[ids[0] ^ k].astype(jnp.float32)
        mem_grad[span, :] = (upstream * (gate * s)).astype(mem_grad.dtype)
        factor[span, :] = upstream * (s * (1.0 + gate * (1.0 - s)))
        if k == 0:
            value_own[...] = gate * s
    half = keep.shape[0]
    term = dot(part[...], mem_grad[...])
    keep[...] = term[:half].astype(keep.dtype)
    send[...] = term[half:].astype(send.dtype)
    sign(token)


def messages_body(ids, keep, got, *refs):
    messages, token = refs[:-1], refs[-1]
    sign(token)
    sub = messages[0].shape[0] // 2
    for z, message in enumerate(messages):
        message[:sub, :] = keep[z * sub : (z + 1) * sub, :]
        message[sub:, :] = got[z * sub : (z + 1) * sub, :]


def grads_body(ids, factor, value_own, spread_ref, own, other, weight, gate_grad, branch, term):
    tokens = branch.shape[0]
    half = own.shape[0]
    for k in range(factor.shape[0] // tokens):
        span = aligned(ids[0] ^ k, tokens)
        memory = dot(spread_ref[:half, span], own[...], 0, 0)
        memory = memory + dot(spread_ref[half:, span], other[...], 0, 0)
        gate_grad[span, :] = (factor[span, :] * memory).astype(gate_grad.dtype)
        if k == 0:
            branch[...] = (memory * value_own[...]).astype(branch.dtype)
    across = weight[aligned(1 - ids[2], weight.shape[1]), :]
    term[...] = dot(gate_grad[...], across, 1, 1).astype(term.dtype)


def affinity_body(rows_here, ids, mem_grad, own, other, rows, out, packed):
    f32 = jnp.float32
    half, tokens = own.shape[0], rows.shape[1]
    count = rows.shape[0]
    pairs = half // rows_here
    at = moved(rows[...], rows_here, pairs, ids[1], ids[2])
    at = jnp.concatenate([at] * (tokens // count), axis=0).T
    inner, outer = at & 127, at >> 7
    grads = mem_grad[aligned(ids[0], tokens), :]
    found = jnp.zeros(at.shape, f32)
    blocks = half // 128
    for j, table in enumerate((own, other)):
        all_rows = dot(grads, table[...], 1, 1)
        for i in range(blocks):
            hit = jnp.take_along_axis(all_rows[:, i * 128 : (i + 1) * 128], inner, axis=1)
            found = jnp.where(outer == j * blocks + i, hit, found)
    affinity = found.T[:count]
    high = affinity.astype(jnp.bfloat16).astype(f32)
    pack_rows(packed, 0, high)
    pack_rows(packed, count, affinity - high)
    out[...] = packed[...].astype(out.dtype)


def inputs_body(ids, gate_grad, weight, arrived, *refs):
    inputs = refs[:-1]
    sign(refs[-1])
    tokens, cols = inputs[0].shape
    own = weight[aligned(ids[2], cols), :]
    for k, out in enumerate(inputs):
        span = aligned(ids[0] ^ k, tokens)
        term = dot(gate_grad[span, :], own, 1, 1) + arrived[span, :].astype(jnp.float32)
        out[...] = term.astype(out.dtype)


def owners_body(ids, *refs):
    f32 = jnp.float32
    count = (len(refs) - 4) // 2
    pieces, outs, token, stage = refs[:count], refs[count + 2 : -2], refs[-2], refs[-1]
    sign(token)
    whole = refs[count][...].astype(f32) + refs[count + 1][...].astype(f32)
    half = whole.shape[0] // 2
    whole = whole[:half] + whole[half:]
    high = whole.astype(jnp.bfloat16).astype(f32)
    whole = jnp.concatenate([high, whole - high], axis=0).astype(jnp.bfloat16)
    rows = pieces[0].shape[0]
    for k, piece in enumerate(pieces):
        stage[ids[0] ^ k] = piece[...]
    for i, out in enumerate(outs):
        out[:rows, :] = stage[ids[1] ^ i]
        out[rows:, :] = whole


def finish_body(ids, *refs):
    weights, out, grads = refs[-3:]
    f32 = jnp.float32
    whole = refs[0][...].astype(f32)
    for piece in refs[1:-3]:
        whole = whole + piece[...].astype(f32)
    tokens = out.shape[0]
    out[...] = whole[:tokens].astype(out.dtype)
    whole = whole[tokens:]
    half = whole.shape[0] // 2
    whole = whole[:half] + whole[half:]
    w = weights[...]
    count, lanes = w.shape
    affinity = jnp.concatenate([row_of(whole, k, lanes) for k in range(count)], axis=0)
    grads[...] = w * (affinity - jnp.sum(w * affinity, axis=0, keepdims=True))


def rows_body(ids, *refs):
    back, out = refs[:-1], refs[-1]
    height, cols = back[0].shape
    sub = height // 2
    for e in range(out.shape[0]):
        for z, piece in enumerate(back):
            at = 2 * (ids[1] ^ z)
            out[e, :, aligned(at + ids[2], cols)] = piece[:sub, :]
            out[e, :, aligned(at + 1 - ids[2], cols)] = piece[sub:, :]


def widen_body(x, out):
    out[...] = x[0].astype(out.dtype)


def widen(x):
    count, rows, cols = x.shape
    return pl.pallas_call(
        widen_body,
        grid=(count,),
        in_specs=[pl.BlockSpec((1, rows, cols), lambda i: (i, 0, 0))],
        out_specs=pl.BlockSpec((rows, cols), lambda i: (i, 0)),
        out_shape=shape((count * rows, cols), jnp.float32),
        compiler_params=pltpu.CompilerParams(vmem_limit_bytes=16 << 20),
        cost_estimate=pl.CostEstimate(flops=0, bytes_accessed=6 * x.size, transcendentals=0),
    )(x)


def gate_grads_body(ids, *refs):
    gate_grad, out = refs[-2:]
    dp = (len(refs) - 2) // 2
    tokens, cols = refs[0].shape
    for j in range(2):
        acc = jnp.zeros((cols, out.shape[1]), jnp.float32)
        for k in range(dp):
            grads = gate_grad[aligned(ids[1] ^ k, tokens), :]
            acc = acc + dot(refs[j * dp + k][...], grads, 0, 0)
        out[aligned(ids[2] ^ j, cols), :] = acc


def local_square(dp, pairs, hidden_in, gate_weight, values, pick_rows, pick_scores, grad_out):
    tokens, cols = hidden_in.shape
    rows_here, width = values.shape
    picks = pick_rows.shape[1]
    sub = rows_here // dp
    f32 = jnp.float32
    me, pair, core = (lax.axis_index(a) for a in ("dp",) + TABLE)
    ids = jnp.stack([me, pair, core]).astype(jnp.int32)
    every = dp * tokens

    mine = []
    for k in range(dp):
        perm = [
            ((e * pairs + z) * 2 + h, (z * pairs + (e ^ k)) * 2 + h)
            for e in range(dp)
            for z in range(pairs)
            for h in range(2)
        ]
        mine.append(lax.ppermute(hidden_in, ("dp",) + TABLE, perm))
    other = [hop(x, "core", 2, 1) for x in mine]
    pieces = mine + other

    rows_t = pick_rows.T
    small = -(-3 * picks * tokens // cols // 16) * 16
    sent, weights_t = kernel_call(
        prepare_body,
        [shape((small, cols)), shape((picks, tokens), f32)],
        ids, pick_scores.T, rows_t,
        scratch=[pltpu.VMEM((small, cols), f32)],
    )
    sent = lax.all_gather(sent, "dp", axis=0)
    upstream = lax.all_gather(grad_out, "dp", axis=0)
    first, second = kernel_call(
        gate_body,
        [shape((every // 2, cols))] * 2,
        ids, *pieces, gate_weight,
        scratch=[pltpu.VMEM((dp, tokens, cols), jnp.bfloat16)],
        flops=1 << 29,
        after=[sent],
    )
    spread_all, spread_part, token = kernel_call(
        functools.partial(spread_body, picks, rows_here),
        [shape((2 * pairs * rows_here, every)), shape((2 * pairs * sub, every)), TOKEN],
        ids, sent,
        scratch=[pltpu.VMEM((picks, every), jnp.int32), pltpu.VMEM((picks, every), f32)],
        flops=1 << 27,
    )
    value_sent = kernel_call(
        columns_body, [shape((rows_here, 2 * cols))] * pairs, ids, values, after=mine + [sent]
    )
    value_got = swap(value_sent, "pair", pairs)
    first, second, *added = kernel_call(
        add_body,
        [shape((every // 2, cols))] * 4,
        ids, first, hop(first, "dp", dp, 1), second, hop(second, "dp", dp, 2),
        after=[token, value_got[1]],
    )
    gates = [first, hop(added[0], "dp", dp, 2), second, hop(added[1], "dp", dp, 1)]

    mem_grad, factor, value_part, keep, send, token = kernel_call(
        values_body,
        [shape((every, cols)), shape((every, cols), f32), shape((tokens, cols), f32)]
        + [shape((pairs * sub, cols))] * 2
        + [TOKEN],
        ids, *gates, upstream, spread_part,
        scratch=[pltpu.VMEM((every, cols), f32)], flops=1 << 28,
    )
    *messages, sent_on = kernel_call(
        messages_body, [shape((2 * sub, cols))] * pairs + [TOKEN], ids, keep, hop(send, "core", 2, 1)
    )

    value_own, value_send = kernel_call(
        halves_body, [shape((pairs * rows_here, cols))] * 2, ids, *value_got, after=[token]
    )
    value_other = hop(value_send, "core", 2, 1)

    extra = 2 * picks * tokens // cols
    gate_grad, branch_out, term = kernel_call(
        grads_body,
        [shape((every, cols)), shape((tokens, cols)), shape((every, cols))],
        ids, factor, value_part, spread_all, value_own, value_other, gate_weight,
        flops=1 << 30, after=[sent_on],
    )
    *sends, token = kernel_call(
        inputs_body,
        [shape((tokens, cols))] * dp + [TOKEN],
        ids, gate_grad, gate_weight, hop(term, "core", 2, 1),
        flops=1 << 28,
    )
    grad_gate = kernel_call(
        gate_grads_body, [shape((2 * cols, cols), f32)], ids, *pieces, gate_grad,
        flops=1 << 29, after=[token],
    )[0]
    affinity = kernel_call(
        functools.partial(affinity_body, rows_here),
        [shape((extra, cols))],
        ids, mem_grad, value_own, value_other, rows_t,
        scratch=[pltpu.VMEM((extra, cols), f32)], flops=1 << 27, after=[token],
    )[0]
    inputs = swap(sends, "dp", dp)
    affinity_got = hop(affinity, "core", 2, 1)
    *inputs, token = kernel_call(
        owners_body,
        [shape((tokens + extra, cols))] * pairs + [TOKEN],
        ids, *inputs, affinity, affinity_got,
        scratch=[pltpu.VMEM((dp, tokens, cols), jnp.bfloat16)],
    )
    grad_hidden, grad_scores = kernel_call(
        finish_body,
        [shape((tokens, cols)), shape((picks, tokens), f32)],
        ids, *swap(inputs, "pair", pairs), weights_t,
    )

    back = swap(messages, "pair", pairs)
    rows = kernel_call(rows_body, [shape((dp, sub, width))], ids, *back, after=[token])[0]
    grad_values = widen(exchange(rows, "dp"))
    return (branch_out, grad_hidden, grad_gate, grad_values, grad_scores.T)


def local(dp, pairs, *args):
    tokens, cols = args[0].shape
    square = dp == pairs == DIRECT and tokens == 128 and cols == 4 * tokens
    return (local_square if square else local_general)(dp, pairs, *args)


def solution(mesh):
    dp, table = mesh.shape["dp"], mesh.shape["table"]
    pairs = Mesh(mesh.devices.reshape(dp, table // 2, 2), ("dp",) + TABLE)
    split, rows, tokens = P("dp", TABLE), P(TABLE, None), P("dp", None)
    return jax.shard_map(
        functools.partial(local, dp, table // 2),
        mesh=pairs,
        in_specs=(split, split, rows, tokens, tokens, split),
        out_specs=(split, split, split, rows, tokens),
        check_vma=False,
    )
```

time: 149 us -> 118 us (0.79)
  the two profiles are of different devices: /device:TPU:0 before, /device:TPU:2 now
where the time goes in v2:
time: 118 us; the launch traced here: 116 us
  starting transfers between devices  42.6 us (36%)
  waiting for transfers between devices  27.5 us (23%)
  Pallas kernels  24.9 us (21%)
  blocking collectives  17.8 us (15%)
  local copies, waits for them, and re-layouts  2.68 us (2%)
    ppermute x24, starting transfers between devices, hop(): return lax.ppermute(x, axis, [(i, i ^ mask) for i in range(size)])  27.2 us
    pallas_call x15, Pallas kernels, kernel_call(): pl.pallas_call(whole_body, in_specs=[pl.BlockSpec(memory_space=pltpu.SMEM...  23.1 us
    ppermute x24, waiting for transfers between devices, hop(): return lax.ppermute(x, axis, [(i, i ^ mask) for i in range(size)])  18.7 us
    ppermute x4, starting transfers between devices, local_square(): mine.append(lax.ppermute(hidden_in, ('dp',) + TABLE, perm))  10.2 us
    all_gather x1, blocking collectives, local_square(): upstream = lax.all_gather(grad_out, 'dp', axis=0)  10.2 us
    ppermute x4, waiting for transfers between devices, local_square(): mine.append(lax.ppermute(hidden_in, ('dp',) + TABLE, perm))  8.85 us
    all_gather x1, blocking collectives, local_square(): sent = lax.all_gather(sent, 'dp', axis=0)  7.56 us
    all_to_all x1, starting transfers between devices, exchange(): return lax.all_to_all(x, axis, split_axis=0, concat_axis=0, tiled=True)  5.14 us
  transfers between devices with their start and end apart: 29, of which 8 were waited for; matrix products, arithmetic and copies ran while one was open for 0% of the time, Pallas kernels for 14%

profile of v2, /device:TPU:2, one launch (start us, length us, event | category | flops | bytes accessed | tf_op | source)
XLA Modules:
  0.0 116.4 jit_solution(17558339128526135303)
XLA Ops:
  0.7 4.9 %collective-permute-start = (bf16[128,512]{1,0:T(8,128)(2,1)}, bf16[128,512]{1,0:T(8,128)(2,1)S(1)}, u32[]{:S(2)}, u32[]{:S(2)}) collective-permute-start(bf16[128,512]{1,0:T(8,128)(2,1)} %param.6), channel_id=1, source_target_pairs={{0,0},{1,1},{2,8},{3,9},{4,16},{5,17},{6,24},{7,25},{8,2},{9,3},{1... | collective-permute-start | bytes 393224 | tf_op jit(solution)/shard_map/ppermute | solution.py:550
  5.6 4.4 %collective-permute-start.3 = (bf16[128,512]{1,0:T(8,128)(2,1)}, bf16[128,512]{1,0:T(8,128)(2,1)S(1)}, u32[]{:S(2)}, u32[]{:S(2)}) collective-permute-start(bf16[128,512]{1,0:T(8,128)(2,1)} %param.6), channel_id=1, source_target_pairs={{0,6},{1,7},{2,14},{3,15},{4,22},{5,23},{6,30},{7,31},{8,4},{9,5},... | collective-permute-start | bytes 393224 | tf_op jit(solution)/shard_map/ppermute | solution.py:550
  11.4 4.5 %collective-permute-done.3.refs_4_.refs_5_ = bf16[128,512]{1,0:T(8,128)(2,1)S(1)} collective-permute-done((bf16[128,512]{1,0:T(8,128)(2,1)}, bf16[128,512]{1,0:T(8,128)(2,1)S(1)}, u32[]{:S(2)}, u32[]{:S(2)}) %collective-permute-start.3) | collective-permute-done | bytes 131104 | tf_op jit(solution)/shard_map/ppermute | solution.py:550
  15.9 4.4 %collective-permute-done.2.refs_3_.refs_4_ = bf16[128,512]{1,0:T(8,128)(2,1)S(1)} collective-permute-done((bf16[128,512]{1,0:T(8,128)(2,1)}, bf16[128,512]{1,0:T(8,128)(2,1)S(1)}, u32[]{:S(2)}, u32[]{:S(2)}) %collective-permute-start.2) | collective-permute-done | bytes 131104 | tf_op jit(solution)/shard_map/ppermute | solution.py:550
  22.4 7.6 %all-gather = bf16[128,512]{1,0:T(8,128)(2,1)S(1)} all-gather(bf16[32,512]{1,0:T(8,128)(2,1)S(1)} %get-tuple-element.48), channel_id=2, replica_groups=mesh['dp'=4,'pair'=4,'core'=2] {'dp'}, dimensions={0}, use_global_device_ids=true | all-gather | bytes 163840 | tf_op jit(solution)/shard_map/all_gather | solution.py:562
  31.8 1.5 %collective-permute-start.10 = (bf16[128,1024]{1,0:T(8,128)(2,1)S(1)}, bf16[128,1024]{1,0:T(8,128)(2,1)S(1)}, u32[]{:S(2)}, u32[]{:S(2)}) collective-permute-start(bf16[128,1024]{1,0:T(8,128)(2,1)S(1)} %get-tuple-element.52), channel_id=1, source_target_pairs={{0,2},{2,0},{4,6},{6,4},{1,3},{3,1},{5,7},{7,5},{8,10},{10,8},{12,... | collective-permute-start | bytes 786440 | tf_op jit(solution)/shard_map/ppermute | solution.py:27
  33.4 1.3 %shard_map.102 = (bf16[256,512]{1,0:T(8,128)(2,1)S(1)}, bf16[256,512]{1,0:T(8,128)(2,1)S(1)}) custom-call(s32[3]{0:T(128)S(1)} %pad_add_fusion.refs_0_, bf16[128,512]{1,0:T(8,128)(2,1)S(1)} %collective-permute-done.refs_1_.refs_2_, bf16[128,512]{1,0:T(8,128)(2,1)S(1)} %collective-permute-done.1.refs_2_.refs_3_, ...), custom_call_target="tpu_custom_call" | custom-call | tf_op jit(solution)/shard_map/pallas_call | solution.py:241
  34.7 2.1 %collective-permute-start.8 = (bf16[256,512]{1,0:T(8,128)(2,1)S(1)}, bf16[256,512]{1,0:T(8,128)(2,1)S(1)}, u32[]{:S(2)}, u32[]{:S(2)}) collective-permute-start(bf16[256,512]{1,0:T(8,128)(2,1)S(1)} %get-tuple-element.49.refs_1_), channel_id=1, source_target_pairs={{0,8},{8,0},{16,24},{24,16},{1,9},{9,1},{17,25},{25,17},{2,10},{10... | collective-permute-start | bytes 786440 | tf_op jit(solution)/shard_map/ppermute | solution.py:27
  36.8 6.0 %shard_map.103 = (bf16[1024,512]{1,0:T(8,128)(2,1)S(1)}, bf16[256,512]{1,0:T(8,128)(2,1)S(1)}, f32[8,128]{1,0:T(8,128)S(1)}) custom-call(s32[3]{0:T(128)S(1)} %pad_add_fusion.refs_0_, bf16[4,32,512]{2,1,0:T(8,128)(2,1)S(1)} %bitcast.10), custom_call_target="tpu_custom_call" | custom-call | tf_op jit(solution)/shard_map/pallas_call | solution.py:241
  43.9 1.7 %collective-permute-start.11 = (bf16[256,512]{1,0:T(8,128)(2,1)S(1)}, bf16[256,512]{1,0:T(8,128)(2,1)S(1)}, u32[]{:S(2)}, u32[]{:S(2)}) collective-permute-start(bf16[256,512]{1,0:T(8,128)(2,1)S(1)} %get-tuple-element.54), channel_id=1, source_target_pairs={{0,16},{8,24},{16,0},{24,8},{1,17},{9,25},{17,1},{25,9},{2,18},{10... | collective-permute-start | bytes 786440 | tf_op jit(solution)/shard_map/ppermute | solution.py:27
  46.0 2.5 %collective-permute-start.13 = (bf16[128,1024]{1,0:T(8,128)(2,1)S(1)}, bf16[128,1024]{1,0:T(8,128)(2,1)S(1)}, u32[]{:S(2)}, u32[]{:S(2)}) collective-permute-start(bf16[128,1024]{1,0:T(8,128)(2,1)S(1)} %get-tuple-element.62), channel_id=1, source_target_pairs={{0,4},{2,6},{4,0},{6,2},{1,5},{3,7},{5,1},{7,3},{8,12},{10,14},{12... | collective-permute-start | bytes 786440 | tf_op jit(solution)/shard_map/ppermute | solution.py:27
  49.0 10.2 %all-gather.1 = bf16[512,512]{1,0:T(8,128)(2,1)S(1)} all-gather(bf16[128,512]{1,0:T(8,128)(2,1)S(1)} %copy-done.5), channel_id=3, replica_groups=mesh['dp'=4,'pair'=4,'core'=2] {'dp'}, dimensions={0}, use_global_device_ids=true | all-gather | bytes 655360 | tf_op jit(solution)/shard_map/all_gather | solution.py:563
  59.2 1.6 %shard_map.106 = (bf16[512,512]{1,0:T(8,128)(2,1)S(1)}, f32[512,512]{1,0:T(8,128)S(1)}, f32[128,512]{1,0:T(8,128)S(1)}, bf16[128,512]{1,0:T(8,128)(2,1)S(1)}, bf...) custom-call(s32[3]{0:T(128)S(1)} %pad_add_fusion.refs_0_, bf16[256,512]{1,0:T(8,128)(2,1)S(1)} %get-tuple-element.53.refs_1_, ...), custom_call_target="tpu_custom_call" | custom-call | tf_op jit(solution)/shard_map/pallas_call | solution.py:241
  60.7 3.1 %collective-permute-done.13.refs_3_ = bf16[128,1024]{1,0:T(8,128)(2,1)S(1)} collective-permute-done((bf16[128,1024]{1,0:T(8,128)(2,1)S(1)}, bf16[128,1024]{1,0:T(8,128)(2,1)S(1)}, u32[]{:S(2)}, u32[]{:S(2)}) %collective-permute-start.13) | collective-permute-done | bytes 262176 | tf_op jit(solution)/shard_map/ppermute | solution.py:27
  65.1 1.6 %collective-permute-done.16.refs_2_ = bf16[128,512]{1,0:T(8,128)(2,1)S(1)} collective-permute-done((bf16[128,512]{1,0:T(8,128)(2,1)S(1)}, bf16[128,512]{1,0:T(8,128)(2,1)S(1)}, u32[]{:S(2)}, u32[]{:S(2)}) %collective-permute-start.16) | collective-permute-done | bytes 131104 | tf_op jit(solution)/shard_map/ppermute | solution.py:27
  67.2 1.9 %shard_map.109 = (bf16[512,512]{1,0:T(8,128)(2,1)S(1)}, bf16[128,512]{1,0:T(8,128)(2,1)}, bf16[512,512]{1,0:T(8,128)(2,1)S(1)}) custom-call(s32[3]{0:T(128)S(1)} %pad_add_fusion.refs_0_, f32[512,512]{1,0:T(8,128)S(1)} %get-tuple-element.58.refs_1_, f32[128,512]{1,0:T(8,128)S(1)} %get-tuple-element.59.refs_2_, ...), custom_call_target="tpu_custom_call" | custom-call | tf_op jit(solution)/shard_map/pallas_call | solution.py:241
  69.2 1.8 %collective-permute-done.17.refs_3_ = bf16[512,512]{1,0:T(8,128)(2,1)S(1)} collective-permute-done((bf16[512,512]{1,0:T(8,128)(2,1)S(1)}, bf16[512,512]{1,0:T(8,128)(2,1)S(1)}, u32[]{:S(2)}, u32[]{:S(2)}) %collective-permute-start.17) | collective-permute-done | bytes 524320 | tf_op jit(solution)/shard_map/ppermute | solution.py:27
  71.0 1.4 %shard_map.110 = (bf16[128,512]{1,0:T(8,128)(2,1)S(1)}, bf16[128,512]{1,0:T(8,128)(2,1)S(1)}, bf16[128,512]{1,0:T(8,128)(2,1)S(1)}, bf16[128,512]{1,0:T(8,128)(2,1)S(1)}, f32[8,128]{1,0:T(8,128)S(1)}) custom-call(s32[3]{0:T(128)S(1)} %pad_add_fusion.refs_0_, bf16[512,512]{1,0:T(8,128)(2,1)S(1)} %get-tuple-element.71.refs_1_.refs_9_, ...), custom_call_target="tpu_custom_call" | custom-call | tf_op jit(solution)/shard_map/pallas_call | solution.py:241
  72.4 1.7 %collective-permute-start.18 = (bf16[128,512]{1,0:T(8,128)(2,1)S(1)}, bf16[128,512]{1,0:T(8,128)(2,1)S(1)}, u32[]{:S(2)}, u32[]{:S(2)}) collective-permute-start(bf16[128,512]{1,0:T(8,128)(2,1)S(1)} %get-tuple-element.74), channel_id=1, source_target_pairs={{0,8},{8,0},{16,24},{24,16},{1,9},{9,1},{17,25},{25,17},{2,10},{10... | collective-permute-start | bytes 393224 | tf_op jit(solution)/shard_map/ppermute | solution.py:27
  74.5 1.5 %collective-permute-start.20 = (bf16[128,512]{1,0:T(8,128)(2,1)S(1)}, bf16[128,512]{1,0:T(8,128)(2,1)S(1)}, u32[]{:S(2)}, u32[]{:S(2)}) collective-permute-start(bf16[128,512]{1,0:T(8,128)(2,1)S(1)} %get-tuple-element.76), channel_id=1, source_target_pairs={{0,24},{8,16},{16,8},{24,0},{1,25},{9,17},{17,9},{25,1},{2,26},{10... | collective-permute-start | bytes 393224 | tf_op jit(solution)/shard_map/ppermute | solution.py:27
  77.3 5.8 %collective-permute-start.25 = (bf16[64,512]{1,0:T(8,128)(2,1)S(1)}, bf16[64,512]{1,0:T(8,128)(2,1)S(1)}, u32[]{:S(2)}, u32[]{:S(2)}) collective-permute-start(bf16[64,512]{1,0:T(8,128)(2,1)S(1)} %get-tuple-element.86), channel_id=1, source_target_pairs={{0,2},{2,0},{4,6},{6,4},{1,3},{3,1},{5,7},{7,5},{8,10},{10,8},{12,... | collective-permute-start | bytes 196616 | tf_op jit(solution)/shard_map/ppermute | solution.py:27
  83.0 2.1 %collective-permute-start.26 = (bf16[64,512]{1,0:T(8,128)(2,1)S(1)}, bf16[64,512]{1,0:T(8,128)(2,1)S(1)}, u32[]{:S(2)}, u32[]{:S(2)}) collective-permute-start(bf16[64,512]{1,0:T(8,128)(2,1)S(1)} %get-tuple-element.87), channel_id=1, source_target_pairs={{0,4},{2,6},{4,0},{6,2},{1,5},{3,7},{5,1},{7,3},{8,12},{10,14},{12... | collective-permute-start | bytes 196616 | tf_op jit(solution)/shard_map/ppermute | solution.py:27
  85.2 1.3 %collective-permute-start.27 = (bf16[64,512]{1,0:T(8,128)(2,1)S(1)}, bf16[64,512]{1,0:T(8,128)(2,1)S(1)}, u32[]{:S(2)}, u32[]{:S(2)}) collective-permute-start(bf16[64,512]{1,0:T(8,128)(2,1)S(1)} %get-tuple-element.88), channel_id=1, source_target_pairs={{0,6},{2,4},{4,2},{6,0},{1,7},{3,5},{5,3},{7,1},{8,14},{10,12},{12... | collective-permute-start | bytes 196616 | tf_op jit(solution)/shard_map/ppermute | solution.py:27
  87.2 4.3 %collective-permute-done.26.refs_3_ = bf16[64,512]{1,0:T(8,128)(2,1)S(1)} collective-permute-done((bf16[64,512]{1,0:T(8,128)(2,1)S(1)}, bf16[64,512]{1,0:T(8,128)(2,1)S(1)}, u32[]{:S(2)}, u32[]{:S(2)}) %collective-permute-start.26) | collective-permute-done | bytes 65568 | tf_op jit(solution)/shard_map/ppermute | solution.py:27
  91.5 1.6 %shard_map.115 = bf16[4,32,4096]{2,1,0:T(8,128)(2,1)} custom-call(s32[3]{0:T(128)S(1)} %pad_add_fusion.refs_0_, bf16[64,512]{1,0:T(8,128)(2,1)S(1)} %get-tuple-element.85.refs_1_, bf16[64,512]{1,0:T(8,128)(2,1)S(1)} %collective-permute-done.25.refs_2_, bf16[64,512]{1,0:T(8,128)(2,1)S(1)} %collective-permute-done.26.refs_3_, ...), custom_call_target="tpu_custom_call" | custom-call | tf_op jit(solution)/shard_map/pallas_call | solution.py:241
  93.1 5.1 %all-to-all-start = ((bf16[4,32,4096]{2,1,0:T(8,128)(2,1)}), bf16[4,32,4096]{2,1,0:T(8,128)(2,1)S(1)}, u32[]{:S(2)}, u32[]{:S(2)}) async-start(bf16[4,32,4096]{2,1,0:T(8,128)(2,1)} %shard_map.115), calls=%async_computation | async-start | bytes 2097152 | tf_op jit(solution)/shard_map/all_to_all | solution.py:50
  98.2 1.5 %collective-permute-start.22 = (bf16[144,512]{1,0:T(8,128)(2,1)S(1)}, bf16[144,512]{1,0:T(8,128)(2,1)S(1)}, u32[]{:S(2)}, u32[]{:S(2)}) collective-permute-start(bf16[144,512]{1,0:T(8,128)(2,1)S(1)} %get-tuple-element.80), channel_id=1, source_target_pairs={{0,2},{2,0},{4,6},{6,4},{1,3},{3,1},{5,7},{7,5},{8,10},{10,8},{12,... | collective-permute-start | bytes 442376 | tf_op jit(solution)/shard_map/ppermute | solution.py:27
  99.7 1.6 %collective-permute-start.23 = (bf16[144,512]{1,0:T(8,128)(2,1)S(1)}, bf16[144,512]{1,0:T(8,128)(2,1)S(1)}, u32[]{:S(2)}, u32[]{:S(2)}) collective-permute-start(bf16[144,512]{1,0:T(8,128)(2,1)S(1)} %get-tuple-element.81), channel_id=1, source_target_pairs={{0,4},{2,6},{4,0},{6,2},{1,5},{3,7},{5,1},{7,3},{8,12},{10,14},{12... | collective-permute-start | bytes 442376 | tf_op jit(solution)/shard_map/ppermute | solution.py:27
  102.6 3.1 %shard_map.114 = f32[1024,512]{1,0:T(8,128)} custom-call(s32[3]{0:T(128)S(1)} %pad_add_fusion.refs_0_, bf16[128,512]{1,0:T(8,128)(2,1)S(1)} %collective-permute-done.refs_1_.refs_2_, bf16[128,512]{1,0:T(8,128)(2,1)S(1)} %collective-permute-done.1.refs_2_.refs_3_, bf16[128,512]{1,0:T(8,128)(2,1)S(1)} %collective-permute-done.2.refs_3_.refs_4_, ...), custom_call_target="tpu_custom_call" | custom-call | tf_op jit(solution)/shard_map/pallas_call | solution.py:241
  105.7 7.6 %collective-permute-done.23.refs_3_ = bf16[144,512]{1,0:T(8,128)(2,1)S(1)} collective-permute-done((bf16[144,512]{1,0:T(8,128)(2,1)S(1)}, bf16[144,512]{1,0:T(8,128)(2,1)S(1)}, u32[]{:S(2)}, u32[]{:S(2)}) %collective-permute-start.23) | collective-permute-done | bytes 147488 | tf_op jit(solution)/shard_map/ppermute | solution.py:27
  113.3 1.3 %shard_map.113 = (bf16[128,512]{1,0:T(8,128)(2,1)}, f32[32,128]{1,0:T(8,128)}) custom-call(s32[3]{0:T(128)S(1)} %pad_add_fusion.refs_0_, bf16[144,512]{1,0:T(8,128)(2,1)S(1)} %get-tuple-element.79.refs_1_, bf16[144,512]{1,0:T(8,128)(2,1)S(1)} %collective-permute-done.22.refs_2_, bf16[144,512]{1,0:T(8,128)(2,1)S(1)} %collective-permute-done.23.refs_3_, ...), custom_call_target="tpu_custom_call" | custom-call | tf_op jit(solution)/shard_map/pallas_call | solution.py:241
  114.5 1.8 %shard_map.116 = f32[128,4096]{1,0:T(8,128)} custom-call(bf16[4,32,4096]{2,1,0:T(8,128)(2,1)S(1)} %all-to-all-done.x), custom_call_target="tpu_custom_call" | custom-call | bytes 3145728 | tf_op jit(solution)/shard_map/pallas_call | solution.py:509
  (57 shorter events, 12.8 us)
Async XLA Ops:
  0.6 32.7 %copy-start = (bf16[1024,512]{1,0:T(8,128)(2,1)S(1)}, bf16[1024,512]{1,0:T(8,128)(2,1)}, u32[]{:S(2)}) copy-start(bf16[1024,512]{1,0:T(8,128)(2,1)} %refs_2_.1) | copy-start | bytes 3145732
  0.6 10.3 %collective-permute-start.1 = (bf16[128,512]{1,0:T(8,128)(2,1)}, bf16[128,512]{1,0:T(8,128)(2,1)S(1)}, u32[]{:S(2)}, u32[]{:S(2)}) collective-permute-start(bf16[128,512]{1,0:T(8,128)(2,1)} %param.6), channel_id=1, source_target_pairs={{0,2},{1,3},{2,10},{3,11},{4,18},{5,19},{6,26},{7,27},{8,0},{9,1},... | collective-permute-start | bytes 393224 | tf_op jit(solution)/shard_map/ppermute | solution.py:550
  0.7 10.2 %collective-permute-start = (bf16[128,512]{1,0:T(8,128)(2,1)}, bf16[128,512]{1,0:T(8,128)(2,1)S(1)}, u32[]{:S(2)}, u32[]{:S(2)}) collective-permute-start(bf16[128,512]{1,0:T(8,128)(2,1)} %param.6), channel_id=1, source_target_pairs={{0,0},{1,1},{2,8},{3,9},{4,16},{5,17},{6,24},{7,25},{8,2},{9,3},{1... | collective-permute-start | bytes 393224 | tf_op jit(solution)/shard_map/ppermute | solution.py:550
  5.6 10.2 %collective-permute-start.3 = (bf16[128,512]{1,0:T(8,128)(2,1)}, bf16[128,512]{1,0:T(8,128)(2,1)S(1)}, u32[]{:S(2)}, u32[]{:S(2)}) collective-permute-start(bf16[128,512]{1,0:T(8,128)(2,1)} %param.6), channel_id=1, source_target_pairs={{0,6},{1,7},{2,14},{3,15},{4,22},{5,23},{6,30},{7,31},{8,4},{9,5},... | collective-permute-start | bytes 393224 | tf_op jit(solution)/shard_map/ppermute | solution.py:550
  10.0 10.2 %collective-permute-start.2 = (bf16[128,512]{1,0:T(8,128)(2,1)}, bf16[128,512]{1,0:T(8,128)(2,1)S(1)}, u32[]{:S(2)}, u32[]{:S(2)}) collective-permute-start(bf16[128,512]{1,0:T(8,128)(2,1)} %param.6), channel_id=1, source_target_pairs={{0,4},{1,5},{2,12},{3,13},{4,20},{5,21},{6,28},{7,29},{8,6},{9,7},... | collective-permute-start | bytes 393224 | tf_op jit(solution)/shard_map/ppermute | solution.py:550
  10.9 22.4 %collective-permute-start.5 = (bf16[128,512]{1,0:T(8,128)(2,1)S(1)}, bf16[128,512]{1,0:T(8,128)(2,1)S(1)}, u32[]{:S(2)}, u32[]{:S(2)}) collective-permute-start(bf16[128,512]{1,0:T(8,128)(2,1)S(1)} %collective-permute-done.1.refs_2_.refs_3_), channel_id=1, source_target_pairs={{0,1},{1,0},{2,3},{3,2},{4,5},{5,4},{6,7},{7,6},{8,9},{9,8},{10,11... | collective-permute-start | bytes 393224 | tf_op jit(solution)/shard_map/ppermute | solution.py:27
  10.9 22.4 %collective-permute-start.4 = (bf16[128,512]{1,0:T(8,128)(2,1)S(1)}, bf16[128,512]{1,0:T(8,128)(2,1)S(1)}, u32[]{:S(2)}, u32[]{:S(2)}) collective-permute-start(bf16[128,512]{1,0:T(8,128)(2,1)S(1)} %collective-permute-done.refs_1_.refs_2_), channel_id=1, source_target_pairs={{0,1},{1,0},{2,3},{3,2},{4,5},{5,4},{6,7},{7,6},{8,9},{9,8},{10,11... | collective-permute-start | bytes 393224 | tf_op jit(solution)/shard_map/ppermute | solution.py:27
  15.9 17.5 %collective-permute-start.7 = (bf16[128,512]{1,0:T(8,128)(2,1)S(1)}, bf16[128,512]{1,0:T(8,128)(2,1)S(1)}, u32[]{:S(2)}, u32[]{:S(2)}) collective-permute-start(bf16[128,512]{1,0:T(8,128)(2,1)S(1)} %collective-permute-done.3.refs_4_.refs_5_), channel_id=1, source_target_pairs={{0,1},{1,0},{2,3},{3,2},{4,5},{5,4},{6,7},{7,6},{8,9},{9,8},{10,11... | collective-permute-start | bytes 393224 | tf_op jit(solution)/shard_map/ppermute | solution.py:27
  20.3 13.1 %collective-permute-start.6 = (bf16[128,512]{1,0:T(8,128)(2,1)S(1)}, bf16[128,512]{1,0:T(8,128)(2,1)S(1)}, u32[]{:S(2)}, u32[]{:S(2)}) collective-permute-start(bf16[128,512]{1,0:T(8,128)(2,1)S(1)} %collective-permute-done.2.refs_3_.refs_4_), channel_id=1, source_target_pairs={{0,1},{1,0},{2,3},{3,2},{4,5},{5,4},{6,7},{7,6},{8,9},{9,8},{10,11... | collective-permute-start | bytes 393224 | tf_op jit(solution)/shard_map/ppermute | solution.py:27
  31.8 17.2 %copy-start.5 = (bf16[128,512]{1,0:T(8,128)(2,1)S(1)}, bf16[128,512]{1,0:T(8,128)(2,1)}, u32[]{:S(2)}) copy-start(bf16[128,512]{1,0:T(8,128)(2,1)} %param.11) | copy-start | bytes 393220
  31.8 11.0 %collective-permute-start.10 = (bf16[128,1024]{1,0:T(8,128)(2,1)S(1)}, bf16[128,1024]{1,0:T(8,128)(2,1)S(1)}, u32[]{:S(2)}, u32[]{:S(2)}) collective-permute-start(bf16[128,1024]{1,0:T(8,128)(2,1)S(1)} %get-tuple-element.52), channel_id=1, source_target_pairs={{0,2},{2,0},{4,6},{6,4},{1,3},{3,1},{5,7},{7,5},{8,10},{10,8},{12,... | collective-permute-start | bytes 786440 | tf_op jit(solution)/shard_map/ppermute | solution.py:27
  34.7 8.2 %collective-permute-start.8 = (bf16[256,512]{1,0:T(8,128)(2,1)S(1)}, bf16[256,512]{1,0:T(8,128)(2,1)S(1)}, u32[]{:S(2)}, u32[]{:S(2)}) collective-permute-start(bf16[256,512]{1,0:T(8,128)(2,1)S(1)} %get-tuple-element.49.refs_1_), channel_id=1, source_target_pairs={{0,8},{8,0},{16,24},{24,16},{1,9},{9,1},{17,25},{25,17},{2,10},{10... | collective-permute-start | bytes 786440 | tf_op jit(solution)/shard_map/ppermute | solution.py:27
  36.8 6.4 %collective-permute-start.9 = (bf16[256,512]{1,0:T(8,128)(2,1)S(1)}, bf16[256,512]{1,0:T(8,128)(2,1)S(1)}, u32[]{:S(2)}, u32[]{:S(2)}) collective-permute-start(bf16[256,512]{1,0:T(8,128)(2,1)S(1)} %get-tuple-element.50.refs_3_), channel_id=1, source_target_pairs={{0,16},{8,24},{16,0},{24,8},{1,17},{9,25},{17,1},{25,9},{2,18},{10... | collective-permute-start | bytes 786440 | tf_op jit(solution)/shard_map/ppermute | solution.py:27
  43.9 15.2 %collective-permute-start.11 = (bf16[256,512]{1,0:T(8,128)(2,1)S(1)}, bf16[256,512]{1,0:T(8,128)(2,1)S(1)}, u32[]{:S(2)}, u32[]{:S(2)}) collective-permute-start(bf16[256,512]{1,0:T(8,128)(2,1)S(1)} %get-tuple-element.54), channel_id=1, source_target_pairs={{0,16},{8,24},{16,0},{24,8},{1,17},{9,25},{17,1},{25,9},{2,18},{10... | collective-permute-start | bytes 786440 | tf_op jit(solution)/shard_map/ppermute | solution.py:27
  45.7 13.5 %collective-permute-start.12 = (bf16[256,512]{1,0:T(8,128)(2,1)S(1)}, bf16[256,512]{1,0:T(8,128)(2,1)S(1)}, u32[]{:S(2)}, u32[]{:S(2)}) collective-permute-start(bf16[256,512]{1,0:T(8,128)(2,1)S(1)} %get-tuple-element.56), channel_id=1, source_target_pairs={{0,8},{8,0},{16,24},{24,16},{1,9},{9,1},{17,25},{25,17},{2,10},{10... | collective-permute-start | bytes 786440 | tf_op jit(solution)/shard_map/ppermute | solution.py:27
  46.0 17.8 %collective-permute-start.13 = (bf16[128,1024]{1,0:T(8,128)(2,1)S(1)}, bf16[128,1024]{1,0:T(8,128)(2,1)S(1)}, u32[]{:S(2)}, u32[]{:S(2)}) collective-permute-start(bf16[128,1024]{1,0:T(8,128)(2,1)S(1)} %get-tuple-element.62), channel_id=1, source_target_pairs={{0,4},{2,6},{4,0},{6,2},{1,5},{3,7},{5,1},{7,3},{8,12},{10,14},{12... | collective-permute-start | bytes 786440 | tf_op jit(solution)/shard_map/ppermute | solution.py:27
  48.5 15.3 %collective-permute-start.14 = (bf16[128,1024]{1,0:T(8,128)(2,1)S(1)}, bf16[128,1024]{1,0:T(8,128)(2,1)S(1)}, u32[]{:S(2)}, u32[]{:S(2)}) collective-permute-start(bf16[128,1024]{1,0:T(8,128)(2,1)S(1)} %get-tuple-element.63), channel_id=1, source_target_pairs={{0,6},{2,4},{4,2},{6,0},{1,7},{3,5},{5,3},{7,1},{8,14},{10,12},{12... | collective-permute-start | bytes 786440 | tf_op jit(solution)/shard_map/ppermute | solution.py:27
  64.5 2.7 %collective-permute-start.15 = (bf16[512,512]{1,0:T(8,128)(2,1)S(1)}, bf16[512,512]{1,0:T(8,128)(2,1)S(1)}, u32[]{:S(2)}, u32[]{:S(2)}) collective-permute-start(bf16[512,512]{1,0:T(8,128)(2,1)S(1)} %get-tuple-element.66), channel_id=1, source_target_pairs={{0,1},{1,0},{2,3},{3,2},{4,5},{5,4},{6,7},{7,6},{8,9},{9,8},{10,11... | collective-permute-start | bytes 1572872 | tf_op jit(solution)/shard_map/ppermute | solution.py:27
  64.6 2.1 %collective-permute-start.16 = (bf16[128,512]{1,0:T(8,128)(2,1)S(1)}, bf16[128,512]{1,0:T(8,128)(2,1)S(1)}, u32[]{:S(2)}, u32[]{:S(2)}) collective-permute-start(bf16[128,512]{1,0:T(8,128)(2,1)S(1)} %get-tuple-element.68), channel_id=1, source_target_pairs={{0,1},{1,0},{2,3},{3,2},{4,5},{5,4},{6,7},{7,6},{8,9},{9,8},{10,11... | collective-permute-start | bytes 393224 | tf_op jit(solution)/shard_map/ppermute | solution.py:27
  69.1 6.8 %copy-start.3 = (s32[128,32]{0,1:T(8,128)S(1)}, s32[128,32]{0,1:T(8,128)}, u32[]{:S(2)}) copy-start(s32[128,32]{0,1:T(8,128)} %param.9) | copy-start | bytes 49156
  69.1 1.9 %collective-permute-start.17 = (bf16[512,512]{1,0:T(8,128)(2,1)S(1)}, bf16[512,512]{1,0:T(8,128)(2,1)S(1)}, u32[]{:S(2)}, u32[]{:S(2)}) collective-permute-start(bf16[512,512]{1,0:T(8,128)(2,1)S(1)} %get-tuple-element.72), channel_id=1, source_target_pairs={{0,1},{1,0},{2,3},{3,2},{4,5},{5,4},{6,7},{7,6},{8,9},{9,8},{10,11... | collective-permute-start | bytes 1572872 | tf_op jit(solution)/shard_map/ppermute | solution.py:27
  72.4 12.8 %collective-permute-start.18 = (bf16[128,512]{1,0:T(8,128)(2,1)S(1)}, bf16[128,512]{1,0:T(8,128)(2,1)S(1)}, u32[]{:S(2)}, u32[]{:S(2)}) collective-permute-start(bf16[128,512]{1,0:T(8,128)(2,1)S(1)} %get-tuple-element.74), channel_id=1, source_target_pairs={{0,8},{8,0},{16,24},{24,16},{1,9},{9,1},{17,25},{25,17},{2,10},{10... | collective-permute-start | bytes 393224 | tf_op jit(solution)/shard_map/ppermute | solution.py:27
  74.1 12.4 %collective-permute-start.19 = (bf16[128,512]{1,0:T(8,128)(2,1)S(1)}, bf16[128,512]{1,0:T(8,128)(2,1)S(1)}, u32[]{:S(2)}, u32[]{:S(2)}) collective-permute-start(bf16[128,512]{1,0:T(8,128)(2,1)S(1)} %get-tuple-element.75), channel_id=1, source_target_pairs={{0,16},{8,24},{16,0},{24,8},{1,17},{9,25},{17,1},{25,9},{2,18},{10... | collective-permute-start | bytes 393224 | tf_op jit(solution)/shard_map/ppermute | solution.py:27
  74.5 12.1 %collective-permute-start.20 = (bf16[128,512]{1,0:T(8,128)(2,1)S(1)}, bf16[128,512]{1,0:T(8,128)(2,1)S(1)}, u32[]{:S(2)}, u32[]{:S(2)}) collective-permute-start(bf16[128,512]{1,0:T(8,128)(2,1)S(1)} %get-tuple-element.76), channel_id=1, source_target_pairs={{0,24},{8,16},{16,8},{24,0},{1,25},{9,17},{17,9},{25,1},{2,26},{10... | collective-permute-start | bytes 393224 | tf_op jit(solution)/shard_map/ppermute | solution.py:27
  77.2 5.9 %collective-permute-start.21 = (bf16[16,512]{1,0:T(8,128)(2,1)S(1)}, bf16[16,512]{1,0:T(8,128)(2,1)S(1)}, u32[]{:S(2)}, u32[]{:S(2)}) collective-permute-start(bf16[16,512]{1,0:T(8,128)(2,1)S(1)} %shard_map.111.refs_5_), channel_id=1, source_target_pairs={{0,1},{1,0},{2,3},{3,2},{4,5},{5,4},{6,7},{7,6},{8,9},{9,8},{10,11... | collective-permute-start | bytes 49160 | tf_op jit(solution)/shard_map/ppermute | solution.py:27
  77.3 9.9 %collective-permute-start.25 = (bf16[64,512]{1,0:T(8,128)(2,1)S(1)}, bf16[64,512]{1,0:T(8,128)(2,1)S(1)}, u32[]{:S(2)}, u32[]{:S(2)}) collective-permute-start(bf16[64,512]{1,0:T(8,128)(2,1)S(1)} %get-tuple-element.86), channel_id=1, source_target_pairs={{0,2},{2,0},{4,6},{6,4},{1,3},{3,1},{5,7},{7,5},{8,10},{10,8},{12,... | collective-permute-start | bytes 196616 | tf_op jit(solution)/shard_map/ppermute | solution.py:27
  83.0 8.4 %collective-permute-start.26 = (bf16[64,512]{1,0:T(8,128)(2,1)S(1)}, bf16[64,512]{1,0:T(8,128)(2,1)S(1)}, u32[]{:S(2)}, u32[]{:S(2)}) collective-permute-start(bf16[64,512]{1,0:T(8,128)(2,1)S(1)} %get-tuple-element.87), channel_id=1, source_target_pairs={{0,4},{2,6},{4,0},{6,2},{1,5},{3,7},{5,1},{7,3},{8,12},{10,14},{12... | collective-permute-start | bytes 196616 | tf_op jit(solution)/shard_map/ppermute | solution.py:27
  85.2 6.3 %collective-permute-start.27 = (bf16[64,512]{1,0:T(8,128)(2,1)S(1)}, bf16[64,512]{1,0:T(8,128)(2,1)S(1)}, u32[]{:S(2)}, u32[]{:S(2)}) collective-permute-start(bf16[64,512]{1,0:T(8,128)(2,1)S(1)} %get-tuple-element.88), channel_id=1, source_target_pairs={{0,6},{2,4},{4,2},{6,0},{1,7},{3,5},{5,3},{7,1},{8,14},{10,12},{12... | collective-permute-start | bytes 196616 | tf_op jit(solution)/shard_map/ppermute | solution.py:27
  93.1 21.5 %all-to-all-start = ((bf16[4,32,4096]{2,1,0:T(8,128)(2,1)}), bf16[4,32,4096]{2,1,0:T(8,128)(2,1)S(1)}, u32[]{:S(2)}, u32[]{:S(2)}) async-start(bf16[4,32,4096]{2,1,0:T(8,128)(2,1)} %shard_map.115), calls=%async_computation | async-start | bytes 2097152 | tf_op jit(solution)/shard_map/all_to_all | solution.py:50
  98.2 7.5 %collective-permute-start.22 = (bf16[144,512]{1,0:T(8,128)(2,1)S(1)}, bf16[144,512]{1,0:T(8,128)(2,1)S(1)}, u32[]{:S(2)}, u32[]{:S(2)}) collective-permute-start(bf16[144,512]{1,0:T(8,128)(2,1)S(1)} %get-tuple-element.80), channel_id=1, source_target_pairs={{0,2},{2,0},{4,6},{6,4},{1,3},{3,1},{5,7},{7,5},{8,10},{10,8},{12,... | collective-permute-start | bytes 442376 | tf_op jit(solution)/shard_map/ppermute | solution.py:27
  99.7 13.5 %collective-permute-start.23 = (bf16[144,512]{1,0:T(8,128)(2,1)S(1)}, bf16[144,512]{1,0:T(8,128)(2,1)S(1)}, u32[]{:S(2)}, u32[]{:S(2)}) collective-permute-start(bf16[144,512]{1,0:T(8,128)(2,1)S(1)} %get-tuple-element.81), channel_id=1, source_target_pairs={{0,4},{2,6},{4,0},{6,2},{1,5},{3,7},{5,1},{7,3},{8,12},{10,14},{12... | collective-permute-start | bytes 442376 | tf_op jit(solution)/shard_map/ppermute | solution.py:27
  101.3 11.9 %collective-permute-start.24 = (bf16[144,512]{1,0:T(8,128)(2,1)S(1)}, bf16[144,512]{1,0:T(8,128)(2,1)S(1)}, u32[]{:S(2)}, u32[]{:S(2)}) collective-permute-start(bf16[144,512]{1,0:T(8,128)(2,1)S(1)} %get-tuple-element.82), channel_id=1, source_target_pairs={{0,6},{2,4},{4,2},{6,0},{1,7},{3,5},{5,3},{7,1},{8,14},{10,12},{12... | collective-permute-start | bytes 442376 | tf_op jit(solution)/shard_map/ppermute | solution.py:27
  (3 other events, 2.7 us)

commit v3 on v2

--- a/solution.py
+++ b/solution.py
@@ -277,7 +277,8 @@
     return packed[j // per : j // per + 1, j % per * lanes : (j % per + 1) * lanes]
 
 
-def prepare_body(ids, scores, rows, sent, weights, packed):
+def prepare_body(ids, scores, rows, grad_out, sent, weights, packed):
+    tokens = grad_out.shape[0]
     x = scores[...]
     exponent = jnp.exp(x - jnp.max(x, axis=0, keepdims=True))
     w = exponent / jnp.sum(exponent, axis=0, keepdims=True)
@@ -287,28 +288,28 @@
     pack_rows(packed, 0, w)
     pack_rows(packed, count, (rows[...] >> 5).astype(jnp.float32))
     pack_rows(packed, 2 * count, (rows[...] & 31).astype(jnp.float32))
-    sent[...] = packed[...].astype(sent.dtype)
-
-
-def moved(row, rows_here, pairs, pair, core):
+    sent[:tokens, :] = grad_out[...]
+    sent[tokens:, :] = packed[...].astype(sent.dtype)
+
+
+def moved(row, rows_here, pair, core):
     owner, inner = lax.div(row, rows_here), lax.rem(row, rows_here)
-    return ((owner & 1) ^ core) * (pairs * rows_here) + ((owner >> 1) ^ pair) * rows_here + inner
-
-
-def spread_body(picks, rows_here, ids, sent, out, part, token, rows, weights):
-    sign(token)
+    return (owner ^ (2 * pair + core)) * rows_here + inner
+
+
+def spread_body(picks, rows_here, ids, sent, out, part, rows, weights):
     me, pair, core = ids[0], ids[1], ids[2]
     dp = sent.shape[0]
     tokens = rows.shape[1] // dp
     pairs = part.shape[0] // (2 * (rows_here // dp))
     for e in range(dp):
-        packed = sent[e].astype(jnp.float32)
+        packed = sent[e, tokens:, :].astype(jnp.float32)
         span = slice(e * tokens, (e + 1) * tokens)
         for k in range(picks):
             weights[k : k + 1, span] = row_of(packed, k, tokens)
             high, low = row_of(packed, picks + k, tokens), row_of(packed, 2 * picks + k, tokens)
             rows[k : k + 1, span] = (high * 32.0 + low).astype(jnp.int32)
-    rows[...] = moved(rows[...], rows_here, pairs, pair, core)
+    rows[...] = moved(rows[...], rows_here, pair, core)
     tile = 32
 
     def step(i, carry):
@@ -324,24 +325,25 @@
     sub = rows_here // dp
     for g in range(2):
         for z in range(pairs):
-            at = (g * pairs + z) * rows_here + me * sub
+            at = (2 * z + g) * rows_here + me * sub
             spot = (g * pairs + z) * sub
             part[spot : spot + sub, :] = out[pl.ds(pl.multiple_of(at, sub), sub), :]
 
 
-def columns_body(ids, values, *outs):
-    width = outs[0].shape[1]
+def columns_body(ids, values, own, other):
+    rows, cols = values.shape[0], own.shape[1]
+    for k in range(own.shape[0] // rows):
+        span, at = slice(k * rows, (k + 1) * rows), 2 * (ids[1] ^ k)
+        own[span, :] = values[:, aligned(at + ids[2], cols)]
+        other[span, :] = values[:, aligned(at + 1 - ids[2], cols)]
+
+
+def halves_body(ids, own, got, *outs):
+    rows = outs[0].shape[0] // 2
     for k, out in enumerate(outs):
-        out[...] = values[:, aligned(ids[1] ^ k, width)]
-
-
-def halves_body(ids, *refs):
-    pieces, (own, other) = refs[:-2], refs[-2:]
-    rows, cols = pieces[0].shape[0], own.shape[1]
-    for k, piece in enumerate(pieces):
         span = slice(k * rows, (k + 1) * rows)
-        own[span, :] = piece[:, aligned(ids[2], cols)]
-        other[span, :] = piece[:, aligned(1 - ids[2], cols)]
+        out[:rows, :] = own[span, :]
+        out[rows:, :] = got[span, :]
 
 
 def dot(a, b, dim_a=1, dim_b=0):
@@ -350,22 +352,29 @@
     )
 
 
+def join_body(ids, *refs):
+    pieces, out = refs[:-1], refs[-1]
+    rows = pieces[0].shape[0]
+    for k, piece in enumerate(pieces):
+        out[k * rows : (k + 1) * rows, :] = piece[...]
+
+
 def gate_body(ids, *refs):
-    weight, first, second, stage = refs[-4:]
-    dp = (len(refs) - 4) // 2
+    pieces, (others, weight, first, second, stage) = refs[:-5], refs[-5:]
+    dp, rows = len(pieces), stage.shape[1]
     cols = weight.shape[1]
     own, other = weight[aligned(ids[2], cols), :], weight[aligned(1 - ids[2], cols), :]
-    for k in range(dp):
-        term = dot(refs[k][...], own) + dot(refs[dp + k][...], other)
+    for k, piece in enumerate(pieces):
+        term = dot(piece[...], own) + dot(others[k * rows : (k + 1) * rows, :], other)
         stage[ids[1] ^ k] = term.astype(stage.dtype)
     half = dp // 2
-    rows = stage.shape[1]
     for e in range(half):
         first[e * rows : (e + 1) * rows, :] = stage[e]
         second[e * rows : (e + 1) * rows, :] = stage[half + e]
 
 
-def add_body(ids, a, a_got, b, b_got, a_keep, b_keep, a_send, b_send):
+def add_body(ids, a, a_got, b, b_got, a_keep, b_keep, a_send, b_send, token):
+    sign(token)
     f32 = jnp.float32
     for x, got, keep, send in ((a, a_got, a_keep, a_send), (b, b_got, b_keep, b_send)):
         keep[...] = (x[...].astype(f32) + got[...].astype(f32)).astype(keep.dtype)
@@ -378,14 +387,14 @@
     stage[half:, :] = b0[...].astype(jnp.float32) + b1[...].astype(jnp.float32)
 
 
-def values_body(ids, a0, a1, b0, b1, grad_out, part, mem_grad, factor, value_own, keep, send, token, stage):
+def values_body(ids, a0, a1, b0, b1, sent, part, mem_grad, factor, value_own, keep, send, token, stage):
     tokens = value_own.shape[0]
     gate_value_of(stage, a0, a1, b0, b1)
-    for k in range(grad_out.shape[0]):
+    for k in range(sent.shape[0]):
         span = aligned(ids[0] ^ k, tokens)
         gate = stage[span, :]
         s = jax.nn.sigmoid(gate)
-        upstream = grad_out[ids[0] ^ k].astype(jnp.float32)
+        upstream = sent[ids[0] ^ k, :tokens, :].astype(jnp.float32)
         mem_grad[span, :] = (upstream * (gate * s)).astype(mem_grad.dtype)
         factor[span, :] = upstream * (s * (1.0 + gate * (1.0 - s)))
         if k == 0:
@@ -406,13 +415,14 @@
         message[sub:, :] = got[z * sub : (z + 1) * sub, :]
 
 
-def grads_body(ids, factor, value_own, spread_ref, own, other, weight, gate_grad, branch, term):
-    tokens = branch.shape[0]
-    half = own.shape[0]
+def grads_body(ids, factor, value_own, spread_ref, *refs):
+    values, (weight, gate_grad, branch, term) = refs[:-4], refs[-4:]
+    tokens, rows = branch.shape[0], values[0].shape[0]
     for k in range(factor.shape[0] // tokens):
         span = aligned(ids[0] ^ k, tokens)
-        memory = dot(spread_ref[:half, span], own[...], 0, 0)
-        memory = memory + dot(spread_ref[half:, span], other[...], 0, 0)
+        memory = 0.0
+        for i, piece in enumerate(values):
+            memory = memory + dot(spread_ref[i * rows : (i + 1) * rows, span], piece[...], 0, 0)
         gate_grad[span, :] = (factor[span, :] * memory).astype(gate_grad.dtype)
         if k == 0:
             branch[...] = (memory * value_own[...]).astype(branch.dtype)
@@ -420,18 +430,18 @@
     term[...] = dot(gate_grad[...], across, 1, 1).astype(term.dtype)
 
 
-def affinity_body(rows_here, ids, mem_grad, own, other, rows, out, packed):
+def affinity_body(rows_here, ids, mem_grad, *refs):
     f32 = jnp.float32
-    half, tokens = own.shape[0], rows.shape[1]
+    values, (rows, out, packed) = refs[:-3], refs[-3:]
+    tokens = rows.shape[1]
     count = rows.shape[0]
-    pairs = half // rows_here
-    at = moved(rows[...], rows_here, pairs, ids[1], ids[2])
+    at = moved(rows[...], rows_here, ids[1], ids[2])
     at = jnp.concatenate([at] * (tokens // count), axis=0).T
     inner, outer = at & 127, at >> 7
     grads = mem_grad[aligned(ids[0], tokens), :]
     found = jnp.zeros(at.shape, f32)
-    blocks = half // 128
-    for j, table in enumerate((own, other)):
+    blocks = values[0].shape[0] // 128
+    for j, table in enumerate(values):
         all_rows = dot(grads, table[...], 1, 1)
         for i in range(blocks):
             hit = jnp.take_along_axis(all_rows[:, i * 128 : (i + 1) * 128], inner, axis=1)
@@ -443,46 +453,36 @@
     out[...] = packed[...].astype(out.dtype)
 
 
-def inputs_body(ids, gate_grad, weight, arrived, *refs):
-    inputs = refs[:-1]
-    sign(refs[-1])
-    tokens, cols = inputs[0].shape
+def inputs_body(ids, gate_grad, weight, arrived, affinity, *refs):
+    outs, token = refs[:-1], refs[-1]
+    sign(token)
+    tokens, cols = outs[0].shape[0] - affinity.shape[0], outs[0].shape[1]
     own = weight[aligned(ids[2], cols), :]
-    for k, out in enumerate(inputs):
-        span = aligned(ids[0] ^ k, tokens)
+    for i, out in enumerate(outs):
+        span = aligned(ids[1] ^ i, tokens)
         term = dot(gate_grad[span, :], own, 1, 1) + arrived[span, :].astype(jnp.float32)
-        out[...] = term.astype(out.dtype)
-
-
-def owners_body(ids, *refs):
-    f32 = jnp.float32
-    count = (len(refs) - 4) // 2
-    pieces, outs, token, stage = refs[:count], refs[count + 2 : -2], refs[-2], refs[-1]
-    sign(token)
-    whole = refs[count][...].astype(f32) + refs[count + 1][...].astype(f32)
-    half = whole.shape[0] // 2
-    whole = whole[:half] + whole[half:]
-    high = whole.astype(jnp.bfloat16).astype(f32)
-    whole = jnp.concatenate([high, whole - high], axis=0).astype(jnp.bfloat16)
-    rows = pieces[0].shape[0]
-    for k, piece in enumerate(pieces):
-        stage[ids[0] ^ k] = piece[...]
-    for i, out in enumerate(outs):
-        out[:rows, :] = stage[ids[1] ^ i]
-        out[rows:, :] = whole
-
-
-def finish_body(ids, *refs):
-    weights, out, grads = refs[-3:]
-    f32 = jnp.float32
-    whole = refs[0][...].astype(f32)
-    for piece in refs[1:-3]:
-        whole = whole + piece[...].astype(f32)
+        out[:tokens, :] = term.astype(out.dtype)
+        out[tokens:, :] = affinity[...]
+
+
+def sums_body(ids, *refs):
+    pieces, out, affinity = refs[:-2], refs[-2], refs[-1]
+    whole = 0.0
+    for piece in pieces:
+        whole = whole + piece[...].astype(jnp.float32)
     tokens = out.shape[0]
     out[...] = whole[:tokens].astype(out.dtype)
-    whole = whole[tokens:]
-    half = whole.shape[0] // 2
-    whole = whole[:half] + whole[half:]
+    half = (whole.shape[0] - tokens) // 2
+    affinity[...] = whole[tokens : tokens + half] + whole[tokens + half :]
+
+
+def copy_body(ids, x, out):
+    out[...] = x[...]
+
+
+def scores_body(ids, own, got, weights, grads, token):
+    sign(token)
+    whole = own[...] + got[...]
     w = weights[...]
     count, lanes = w.shape
     affinity = jnp.concatenate([row_of(whole, k, lanes) for k in range(count)], axis=0)
@@ -490,43 +490,67 @@
 
 
 def rows_body(ids, *refs):
-    back, out = refs[:-1], refs[-1]
-    height, cols = back[0].shape
-    sub = height // 2
-    for e in range(out.shape[0]):
-        for z, piece in enumerate(back):
+    back, halves = refs[:-2], refs[-2:]
+    cols = back[0].shape[1]
+    sub, half = back[0].shape[0] // 2, halves[0].shape[0]
+    for z, piece in enumerate(back):
+        for j, out in enumerate(halves):
             at = 2 * (ids[1] ^ z)
-            out[e, :, aligned(at + ids[2], cols)] = piece[:sub, :]
-            out[e, :, aligned(at + 1 - ids[2], cols)] = piece[sub:, :]
-
-
-def widen_body(x, out):
-    out[...] = x[0].astype(out.dtype)
-
-
-def widen(x):
-    count, rows, cols = x.shape
+            span = slice(j * half, (j + 1) * half)
+            out[:, aligned(at + ids[2], cols)] = piece[span, :]
+            out[:, aligned(at + 1 - ids[2], cols)] = piece[sub + j * half : sub + (j + 1) * half, :]
+
+
+def pairs_body(ids, a, a_got, b, b_got, first, second):
+    half = a.shape[0]
+    for x, got, out in ((a, a_got, first), (b, b_got, second)):
+        out[:half, :] = x[...]
+        out[half:, :] = got[...]
+
+
+def widen_body(ids, a, a_got, b, b_got, out, token):
+    sign(token)
+    half = a.shape[0] // 2
+    for k in range(4):
+        at = (ids[0] ^ k) * 2 * half
+        first, second = (a_got if k & 2 else a), (b_got if k & 1 else b)
+        i, j = k & 1, k >> 1
+        spot = pl.ds(pl.multiple_of(at, half), half)
+        out[spot, :] = first[i * half : (i + 1) * half, :].astype(out.dtype)
+        spot = pl.ds(pl.multiple_of(at + half, half), half)
+        out[spot, :] = second[j * half : (j + 1) * half, :].astype(out.dtype)
+
+
+def widen(ids, pieces):
+    rows, width = pieces[0].shape
+    cols = width // 4
     return pl.pallas_call(
         widen_body,
-        grid=(count,),
-        in_specs=[pl.BlockSpec((1, rows, cols), lambda i: (i, 0, 0))],
-        out_specs=pl.BlockSpec((rows, cols), lambda i: (i, 0)),
-        out_shape=shape((count * rows, cols), jnp.float32),
-        compiler_params=pltpu.CompilerParams(vmem_limit_bytes=16 << 20),
-        cost_estimate=pl.CostEstimate(flops=0, bytes_accessed=6 * x.size, transcendentals=0),
-    )(x)
+        grid=(width // cols,),
+        in_specs=[pl.BlockSpec(memory_space=pltpu.SMEM)]
+        + [pl.BlockSpec((rows, cols), lambda i: (0, i))] * len(pieces),
+        out_specs=[
+            pl.BlockSpec((len(pieces) * rows, cols), lambda i: (0, i)),
+            pl.BlockSpec(TOKEN.shape, lambda i: (0, 0)),
+        ],
+        out_shape=[shape((len(pieces) * rows, width), jnp.float32), TOKEN],
+        compiler_params=pltpu.CompilerParams(vmem_limit_bytes=12 << 20),
+        cost_estimate=pl.CostEstimate(flops=0, bytes_accessed=0, transcendentals=0),
+    )(ids, *pieces)
 
 
 def gate_grads_body(ids, *refs):
-    gate_grad, out = refs[-2:]
-    dp = (len(refs) - 2) // 2
-    tokens, cols = refs[0].shape
-    for j in range(2):
-        acc = jnp.zeros((cols, out.shape[1]), jnp.float32)
-        for k in range(dp):
-            grads = gate_grad[aligned(ids[1] ^ k, tokens), :]
-            acc = acc + dot(refs[j * dp + k][...], grads, 0, 0)
-        out[aligned(ids[2] ^ j, cols), :] = acc
+    pieces, (others, gate_grad, out, token) = refs[:-4], refs[-4:]
+    sign(token)
+    tokens, cols = pieces[0].shape
+    own = jnp.zeros((cols, out.shape[1]), jnp.float32)
+    other = own
+    for k, piece in enumerate(pieces):
+        grads = gate_grad[aligned(ids[1] ^ k, tokens), :]
+        own = own + dot(piece[...], grads, 0, 0)
+        other = other + dot(others[k * tokens : (k + 1) * tokens, :], grads, 0, 0)
+    out[aligned(ids[2], cols), :] = own
+    out[aligned(1 - ids[2], cols), :] = other
 
 
 def local_square(dp, pairs, hidden_in, gate_weight, values, pick_rows, pick_scores, grad_out):
@@ -548,43 +572,45 @@
             for h in range(2)
         ]
         mine.append(lax.ppermute(hidden_in, ("dp",) + TABLE, perm))
-    other = [hop(x, "core", 2, 1) for x in mine]
-    pieces = mine + other
-
     rows_t = pick_rows.T
     small = -(-3 * picks * tokens // cols // 16) * 16
     sent, weights_t = kernel_call(
         prepare_body,
-        [shape((small, cols)), shape((picks, tokens), f32)],
-        ids, pick_scores.T, rows_t,
+        [shape((tokens + small, cols)), shape((picks, tokens), f32)],
+        ids, pick_scores.T, rows_t, grad_out,
         scratch=[pltpu.VMEM((small, cols), f32)],
     )
-    sent = lax.all_gather(sent, "dp", axis=0)
-    upstream = lax.all_gather(grad_out, "dp", axis=0)
+    sent_own = sent
+    sent = lax.all_gather(sent_own, "dp", axis=0)
+    joined = kernel_call(join_body, [shape((every, cols))], ids, *mine, after=[sent_own])[0]
+    others = hop(joined, "core", 2, 1)
     first, second = kernel_call(
         gate_body,
         [shape((every // 2, cols))] * 2,
-        ids, *pieces, gate_weight,
+        ids, *mine, others, gate_weight,
         scratch=[pltpu.VMEM((dp, tokens, cols), jnp.bfloat16)],
         flops=1 << 29,
-        after=[sent],
-    )
-    spread_all, spread_part, token = kernel_call(
+    )
+    value_own, value_send = kernel_call(
+        columns_body, [shape((pairs * rows_here, cols))] * 2, ids, values
+    )
+    value_sent = kernel_call(
+        halves_body, [shape((2 * rows_here, cols))] * pairs,
+        ids, value_own, hop(value_send, "core", 2, 1),
+    )
+    value_got = swap(value_sent, "pair", pairs)
+    first, second, *added, token = kernel_call(
+        add_body,
+        [shape((every // 2, cols))] * 4 + [TOKEN],
+        ids, first, hop(first, "dp", dp, 1), second, hop(second, "dp", dp, 2),
+        after=[sent] + value_got[1:3],
+    )
+    spread_all, spread_part = kernel_call(
         functools.partial(spread_body, picks, rows_here),
-        [shape((2 * pairs * rows_here, every)), shape((2 * pairs * sub, every)), TOKEN],
+        [shape((2 * pairs * rows_here, every)), shape((2 * pairs * sub, every))],
         ids, sent,
         scratch=[pltpu.VMEM((picks, every), jnp.int32), pltpu.VMEM((picks, every), f32)],
-        flops=1 << 27,
-    )
-    value_sent = kernel_call(
-        columns_body, [shape((rows_here, 2 * cols))] * pairs, ids, values, after=mine + [sent]
-    )
-    value_got = swap(value_sent, "pair", pairs)
-    first, second, *added = kernel_call(
-        add_body,
-        [shape((every // 2, cols))] * 4,
-        ids, first, hop(first, "dp", dp, 1), second, hop(second, "dp", dp, 2),
-        after=[token, value_got[1]],
+        flops=1 << 27, after=[token],
     )
     gates = [first, hop(added[0], "dp", dp, 2), second, hop(added[1], "dp", dp, 1)]
 
@@ -593,58 +619,69 @@
         [shape((every, cols)), shape((every, cols), f32), shape((tokens, cols), f32)]
         + [shape((pairs * sub, cols))] * 2
         + [TOKEN],
-        ids, *gates, upstream, spread_part,
+        ids, *gates, sent, spread_part,
         scratch=[pltpu.VMEM((every, cols), f32)], flops=1 << 28,
     )
     *messages, sent_on = kernel_call(
         messages_body, [shape((2 * sub, cols))] * pairs + [TOKEN], ids, keep, hop(send, "core", 2, 1)
     )
 
-    value_own, value_send = kernel_call(
-        halves_body, [shape((pairs * rows_here, cols))] * 2, ids, *value_got, after=[token]
-    )
-    value_other = hop(value_send, "core", 2, 1)
-
+    back = swap(messages, "pair", pairs)
     extra = 2 * picks * tokens // cols
     gate_grad, branch_out, term = kernel_call(
         grads_body,
         [shape((every, cols)), shape((tokens, cols)), shape((every, cols))],
-        ids, factor, value_part, spread_all, value_own, value_other, gate_weight,
-        flops=1 << 30, after=[sent_on],
-    )
-    *sends, token = kernel_call(
-        inputs_body,
-        [shape((tokens, cols))] * dp + [TOKEN],
-        ids, gate_grad, gate_weight, hop(term, "core", 2, 1),
-        flops=1 << 28,
-    )
-    grad_gate = kernel_call(
-        gate_grads_body, [shape((2 * cols, cols), f32)], ids, *pieces, gate_grad,
-        flops=1 << 29, after=[token],
-    )[0]
+        ids, factor, value_part, spread_all, *value_got, gate_weight,
+        after=[sent_on],
+        flops=1 << 30,
+    )
     affinity = kernel_call(
         functools.partial(affinity_body, rows_here),
         [shape((extra, cols))],
-        ids, mem_grad, value_own, value_other, rows_t,
-        scratch=[pltpu.VMEM((extra, cols), f32)], flops=1 << 27, after=[token],
+        ids, mem_grad, *value_got, rows_t,
+        scratch=[pltpu.VMEM((extra, cols), f32)],
     )[0]
-    inputs = swap(sends, "dp", dp)
-    affinity_got = hop(affinity, "core", 2, 1)
-    *inputs, token = kernel_call(
-        owners_body,
+    *inputs, sent_inputs = kernel_call(
+        inputs_body,
         [shape((tokens + extra, cols))] * pairs + [TOKEN],
-        ids, *inputs, affinity, affinity_got,
-        scratch=[pltpu.VMEM((dp, tokens, cols), jnp.bfloat16)],
-    )
-    grad_hidden, grad_scores = kernel_call(
-        finish_body,
-        [shape((tokens, cols)), shape((picks, tokens), f32)],
-        ids, *swap(inputs, "pair", pairs), weights_t,
-    )
-
-    back = swap(messages, "pair", pairs)
-    rows = kernel_call(rows_body, [shape((dp, sub, width))], ids, *back, after=[token])[0]
-    grad_values = widen(exchange(rows, "dp"))
+        ids, gate_grad, gate_weight, hop(term, "core", 2, 1), affinity,
+        after=back[1:2],
+    )
+    grad_gate, done = kernel_call(
+        gate_grads_body,
+        [shape((2 * cols, cols), f32), TOKEN],
+        ids, *mine, others, gate_grad, after=[sent_inputs],
+    )
+    grad_hidden, affinity = kernel_call(
+        sums_body,
+        [shape((tokens, cols)), shape((extra // 2, cols), f32)],
+        ids, *swap(inputs, "pair", pairs), after=[done],
+    )
+    perm = [
+        ((d * pairs + z) * 2 + h, (z * pairs + d) * 2 + h)
+        for d in range(dp)
+        for z in range(pairs)
+        for h in range(2)
+    ]
+    grad_hidden = lax.ppermute(grad_hidden, ("dp",) + TABLE, perm)
+    first, second = kernel_call(
+        rows_body, [shape((sub // 2, width))] * 2, ids, *back, after=[sent_inputs]
+    )
+    first, second = kernel_call(
+        pairs_body, [shape((sub, width))] * 2,
+        ids, first, hop(first, "dp", dp, 1), second, hop(second, "dp", dp, 2),
+    )
+    grad_values, token = widen(
+        ids, [first, hop(first, "dp", dp, 2), second, hop(second, "dp", dp, 1)]
+    )
+    grad_scores, scored = kernel_call(
+        scores_body,
+        [shape((picks, tokens), f32), TOKEN],
+        ids, affinity, hop(affinity, "core", 2, 1), weights_t, after=[token],
+    )
+    grad_hidden = kernel_call(
+        copy_body, [shape((tokens, cols))], ids, grad_hidden, after=[token, scored]
+    )[0]
     return (branch_out, grad_hidden, grad_gate, grad_values, grad_scores.T)
 
 

time: 118 us -> 98.5 us (0.83); the launches traced: 116 us -> 98.1 us
  waiting for transfers between devices: 27.5 us -> 15.7 us
  starting transfers between devices: 42.6 us -> 35.9 us
  blocking collectives: 17.8 us -> 14.8 us
  Pallas kernels: 24.9 us -> 27.1 us
    ppermute x24 -> x22, waiting for transfers between devices: 18.7 us -> 8.22 us  [hop(): return lax.ppermute(x, axis, [(i, i ^ mask) for i in range(size)])]
    ppermute x24 -> x22, starting transfers between devices: 27.2 us -> 21.1 us  [hop(): return lax.ppermute(x, axis, [(i, i ^ mask) for i in range(size)])]
    all_to_all x1 -> x0, starting transfers between devices: 5.14 us -> none  [exchange(): return lax.all_to_all(x, axis, split_axis=0, concat_axis=0, tiled=True)]
    ppermute x0 -> x1, starting transfers between devices: none -> 4.52 us  [local_square(): grad_hidden = lax.ppermute(grad_hidden, ('dp',) + TABLE, perm)]
    ppermute x4, waiting for transfers between devices: 8.85 us -> 4.41 us  [local_square(): mine.append(lax.ppermute(hidden_in, ('dp',) + TABLE, perm))]
    ppermute x0 -> x1, waiting for transfers between devices: none -> 3.08 us  [local_square(): grad_hidden = lax.ppermute(grad_hidden, ('dp',) + TABLE, perm)]
    all_gather x2 -> x1, blocking collectives: 17.8 us -> 14.8 us  [local_square(): sent = lax.all_gather(sent_own, 'dp', axis=0)]
    pallas_call x15 -> x18, Pallas kernels: 23.1 us -> 24.6 us  [kernel_call(): pl.pallas_call(whole_body, in_specs=[pl.BlockSpec(memory_space=pltpu.SMEM...]
  transfers between devices with their start and end apart: 29 -> 27, of which waited for: 8 -> 6; matrix products, arithmetic and copies ran while one was open for 0% -> 0% of each run, Pallas kernels for 14% -> 23%
where the time goes in v3:
time: 98.5 us; the launch traced here: 98.1 us
  starting transfers between devices  35.9 us (36%)
  Pallas kernels  27.1 us (28%)
  waiting for transfers between devices  15.7 us (16%)
  blocking collectives  14.8 us (15%)
  local copies, waits for them, and re-layouts  3.57 us (4%)
    pallas_call x18, Pallas kernels, kernel_call(): pl.pallas_call(whole_body, in_specs=[pl.BlockSpec(memory_space=pltpu.SMEM...  24.6 us
    ppermute x22, starting transfers between devices, hop(): return lax.ppermute(x, axis, [(i, i ^ mask) for i in range(size)])  21.1 us
    all_gather x1, blocking collectives, local_square(): sent = lax.all_gather(sent_own, 'dp', axis=0)  14.8 us
    ppermute x4, starting transfers between devices, local_square(): mine.append(lax.ppermute(hidden_in, ('dp',) + TABLE, perm))  10.2 us
    ppermute x22, waiting for transfers between devices, hop(): return lax.ppermute(x, axis, [(i, i ^ mask) for i in range(size)])  8.22 us
    ppermute x1, starting transfers between devices, local_square(): grad_hidden = lax.ppermute(grad_hidden, ('dp',) + TABLE, perm)  4.52 us
    ppermute x4, waiting for transfers between devices, local_square(): mine.append(lax.ppermute(hidden_in, ('dp',) + TABLE, perm))  4.41 us
    unnamed x12, local copies, waits for them, and re-layouts  3.57 us
  transfers between devices with their start and end apart: 27, of which 6 were waited for; matrix products, arithmetic and copies ran while one was open for 0% of the time, Pallas kernels for 23%

profile of v3, /device:TPU:2, one launch (start us, length us, event | category | flops | bytes accessed | tf_op | source)
XLA Modules:
  0.0 98.1 jit_solution(6314274506080229765)
XLA Ops:
  0.7 4.9 %collective-permute-start = (bf16[128,512]{1,0:T(8,128)(2,1)}, bf16[128,512]{1,0:T(8,128)(2,1)S(1)}, u32[]{:S(2)}, u32[]{:S(2)}) collective-permute-start(bf16[128,512]{1,0:T(8,128)(2,1)} %param.6), channel_id=1, source_target_pairs={{0,0},{1,1},{2,8},{3,9},{4,16},{5,17},{6,24},{7,25},{8,2},{9,3},{1... | collective-permute-start | bytes 393224 | tf_op jit(solution)/shard_map/ppermute | solution.py:574
  5.6 4.4 %collective-permute-start.3 = (bf16[128,512]{1,0:T(8,128)(2,1)}, bf16[128,512]{1,0:T(8,128)(2,1)S(1)}, u32[]{:S(2)}, u32[]{:S(2)}) collective-permute-start(bf16[128,512]{1,0:T(8,128)(2,1)} %param.6), channel_id=1, source_target_pairs={{0,6},{1,7},{2,14},{3,15},{4,22},{5,23},{6,30},{7,31},{8,4},{9,5},... | collective-permute-start | bytes 393224 | tf_op jit(solution)/shard_map/ppermute | solution.py:574
  11.0 1.2 %copy-done.1 = bf16[128,4096]{1,0:T(8,128)(2,1)S(1)} copy-done((bf16[128,4096]{1,0:T(8,128)(2,1)S(1)}, bf16[128,4096]{1,0:T(8,128)(2,1)}, u32[]{:S(2)}) %copy-start.1) | copy-done | bytes 1048600
  12.9 0.9 copy-done.2
  15.9 4.4 %collective-permute-done.2.refs_3_ = bf16[128,512]{1,0:T(8,128)(2,1)S(1)} collective-permute-done((bf16[128,512]{1,0:T(8,128)(2,1)}, bf16[128,512]{1,0:T(8,128)(2,1)S(1)}, u32[]{:S(2)}, u32[]{:S(2)}) %collective-permute-start.2) | collective-permute-done | bytes 131104 | tf_op jit(solution)/shard_map/ppermute | solution.py:574
  21.6 1.4 %collective-permute-start.8 = (bf16[256,512]{1,0:T(8,128)(2,1)S(1)}, bf16[256,512]{1,0:T(8,128)(2,1)S(1)}, u32[]{:S(2)}, u32[]{:S(2)}) collective-permute-start(bf16[256,512]{1,0:T(8,128)(2,1)S(1)} %get-tuple-element.57), channel_id=1, source_target_pairs={{0,2},{2,0},{4,6},{6,4},{1,3},{3,1},{5,7},{7,5},{8,10},{10,8},{12,... | collective-permute-start | bytes 786440 | tf_op jit(solution)/shard_map/ppermute | solution.py:27
  22.9 3.3 %collective-permute-start.9 = (bf16[256,512]{1,0:T(8,128)(2,1)S(1)}, bf16[256,512]{1,0:T(8,128)(2,1)S(1)}, u32[]{:S(2)}, u32[]{:S(2)}) collective-permute-start(bf16[256,512]{1,0:T(8,128)(2,1)S(1)} %get-tuple-element.58), channel_id=1, source_target_pairs={{0,4},{2,6},{4,0},{6,2},{1,5},{3,7},{5,1},{7,3},{8,12},{10,14},{12... | collective-permute-start | bytes 786440 | tf_op jit(solution)/shard_map/ppermute | solution.py:27
  26.2 1.3 %shard_map.103 = (bf16[256,512]{1,0:T(8,128)(2,1)S(1)}, bf16[256,512]{1,0:T(8,128)(2,1)S(1)}) custom-call(s32[3]{0:T(128)S(1)} %pad_add_fusion.refs_0_.ids, bf16[128,512]{1,0:T(8,128)(2,1)S(1)} %collective-permute-done.refs_1_, bf16[128,512]{1,0:T(8,128)(2,1)S(1)} %collective-permute-done.1.refs_2_, bf16[128,512]{1,0:T(8,128)(2,1)S(1)} %collective-permute-done.2.refs_3_, ...), custom_call_target="tpu_custom_call" | custom-call | tf_op jit(solution)/shard_map/pallas_call | solution.py:241
  27.7 14.8 %all-gather = bf16[640,512]{1,0:T(8,128)(2,1)S(1)} all-gather(bf16[160,512]{1,0:T(8,128)(2,1)S(1)} %get-tuple-element.52.refs_5_), channel_id=2, replica_groups=mesh['dp'=4,'pair'=4,'core'=2] {'dp'}, dimensions={0}, use_global_device_ids=true | all-gather | bytes 819200 | tf_op jit(solution)/shard_map/all_gather | solution.py:584
  43.9 1.5 %collective-permute-start.11 = (bf16[256,512]{1,0:T(8,128)(2,1)S(1)}, bf16[256,512]{1,0:T(8,128)(2,1)S(1)}, u32[]{:S(2)}, u32[]{:S(2)}) collective-permute-start(bf16[256,512]{1,0:T(8,128)(2,1)S(1)} %get-tuple-element.62), channel_id=1, source_target_pairs={{0,8},{8,0},{16,24},{24,16},{1,9},{9,1},{17,25},{25,17},{2,10},{10... | collective-permute-start | bytes 786440 | tf_op jit(solution)/shard_map/ppermute | solution.py:27
  45.5 0.9 collective-permute-start.12
  46.3 5.9 %shard_map.107 = (bf16[1024,512]{1,0:T(8,128)(2,1)S(1)}, bf16[256,512]{1,0:T(8,128)(2,1)S(1)}) custom-call(s32[3]{0:T(128)S(1)} %pad_add_fusion.refs_0_.ids, bf16[4,160,512]{2,1,0:T(8,128)(2,1)S(1)} %bitcast.8, f32[8,128]{1,0:T(8,128)S(1)} %get-tuple-element.63.refs_2_), custom_call_target="tpu_custom_call" | custom-call | tf_op jit(solution)/shard_map/pallas_call | solution.py:241
  52.3 1.9 %shard_map.108 = (bf16[512,512]{1,0:T(8,128)(2,1)S(1)}, f32[512,512]{1,0:T(8,128)S(1)}, f32[128,512]{1,0:T(8,128)S(1)}, bf16[128,512]{1,0:T(8,128)(2,1)S(1)}, bf...) custom-call(s32[3]{0:T(128)S(1)} %pad_add_fusion.refs_0_.ids, bf16[256,512]{1,0:T(8,128)(2,1)S(1)} %get-tuple-element.59.refs_1_, ...), custom_call_target="tpu_custom_call" | custom-call | tf_op jit(solution)/shard_map/pallas_call | solution.py:241
  54.2 1.3 %collective-permute-done.13.refs_2_ = bf16[128,512]{1,0:T(8,128)(2,1)S(1)} collective-permute-done((bf16[128,512]{1,0:T(8,128)(2,1)S(1)}, bf16[128,512]{1,0:T(8,128)(2,1)S(1)}, u32[]{:S(2)}, u32[]{:S(2)}) %collective-permute-start.13) | collective-permute-done | bytes 131104 | tf_op jit(solution)/shard_map/ppermute | solution.py:27
  56.2 1.9 %shard_map.110 = (bf16[512,512]{1,0:T(8,128)(2,1)S(1)}, bf16[128,512]{1,0:T(8,128)(2,1)}, bf16[512,512]{1,0:T(8,128)(2,1)S(1)}) custom-call(s32[3]{0:T(128)S(1)} %pad_add_fusion.refs_0_.ids, f32[512,512]{1,0:T(8,128)S(1)} %get-tuple-element.65.refs_1_, f32[128,512]{1,0:T(8,128)S(1)} %get-tuple-element.66.refs_2_, ...), custom_call_target="tpu_custom_call" | custom-call | tf_op jit(solution)/shard_map/pallas_call | solution.py:241
  58.2 1.1 %collective-permute-start.15 = (bf16[64,512]{1,0:T(8,128)(2,1)S(1)}, bf16[64,512]{1,0:T(8,128)(2,1)S(1)}, u32[]{:S(2)}, u32[]{:S(2)}) collective-permute-start(bf16[64,512]{1,0:T(8,128)(2,1)S(1)} %get-tuple-element.77), channel_id=1, source_target_pairs={{0,2},{2,0},{4,6},{6,4},{1,3},{3,1},{5,7},{7,5},{8,10},{10,8},{12,... | collective-permute-start | bytes 196616 | tf_op jit(solution)/shard_map/ppermute | solution.py:27
  59.3 2.4 %collective-permute-start.20 = (bf16[64,512]{1,0:T(8,128)(2,1)S(1)}, bf16[64,512]{1,0:T(8,128)(2,1)S(1)}, u32[]{:S(2)}, u32[]{:S(2)}) collective-permute-start(bf16[64,512]{1,0:T(8,128)(2,1)S(1)} %get-tuple-element.86), channel_id=1, source_target_pairs={{0,4},{2,6},{4,0},{6,2},{1,5},{3,7},{5,1},{7,3},{8,12},{10,14},{12... | collective-permute-start | bytes 196616 | tf_op jit(solution)/shard_map/ppermute | solution.py:27
  62.6 1.2 %shard_map.111.refs_4_ = bf16[16,512]{1,0:T(8,128)(2,1)S(1)} custom-call(s32[3]{0:T(128)S(1)} %pad_add_fusion.refs_0_.ids, bf16[512,512]{1,0:T(8,128)(2,1)S(1)} %get-tuple-element.76.refs_1_, bf16[256,512]{1,0:T(8,128)(2,1)S(1)} %get-tuple-element.68.refs_4_.refs_2_, bf16[256,512]{1,0:T(8,128)(2,1)S(1)} %collective-permute-done.8.refs_6_.refs_5_.refs_3_, ...), custom_call_target="tpu_custom_call" | custom-call | tf_op jit(solution)/shard_map/pallas_call | solution.py:241
  63.9 1.4 %shard_map.112 = (bf16[144,512]{1,0:T(8,128)(2,1)S(1)}, bf16[144,512]{1,0:T(8,128)(2,1)S(1)}, bf16[144,512]{1,0:T(8,128)(2,1)S(1)}, bf16[144,512]{1,0:T(8,128)(2,1)S(1)}, f32[8,128]{1,0:T(8,128)S(1)}) custom-call(s32[3]{0:T(128)S(1)} %pad_add_fusion.refs_0_.ids, bf16[512,512]{1,0:T(8,128)(2,1)S(1)} %get-tuple-element.74.refs_1_.refs_6_, ...), custom_call_target="tpu_custom_call" | custom-call | tf_op jit(solution)/shard_map/pallas_call | solution.py:241
  65.2 1.8 %collective-permute-done.20.refs_3_ = bf16[64,512]{1,0:T(8,128)(2,1)S(1)} collective-permute-done((bf16[64,512]{1,0:T(8,128)(2,1)S(1)}, bf16[64,512]{1,0:T(8,128)(2,1)S(1)}, u32[]{:S(2)}, u32[]{:S(2)}) %collective-permute-start.20) | collective-permute-done | bytes 65568 | tf_op jit(solution)/shard_map/ppermute | solution.py:27
  69.0 1.5 %collective-permute-start.23 = (bf16[16,4096]{1,0:T(8,128)(2,1)S(1)}, bf16[16,4096]{1,0:T(8,128)(2,1)S(1)}, u32[]{:S(2)}, u32[]{:S(2)}) collective-permute-start(bf16[16,4096]{1,0:T(8,128)(2,1)S(1)} %get-tuple-element.89.refs_3_), channel_id=1, source_target_pairs={{0,16},{8,24},{16,0},{24,8},{1,17},{9,25},{17,1},{25,9},{2,18},{10... | collective-permute-start | bytes 393224 | tf_op jit(solution)/shard_map/ppermute | solution.py:27
  70.5 1.3 %collective-permute-start.16 = (bf16[144,512]{1,0:T(8,128)(2,1)S(1)}, bf16[144,512]{1,0:T(8,128)(2,1)S(1)}, u32[]{:S(2)}, u32[]{:S(2)}) collective-permute-start(bf16[144,512]{1,0:T(8,128)(2,1)S(1)} %get-tuple-element.79), channel_id=1, source_target_pairs={{0,2},{2,0},{4,6},{6,4},{1,3},{3,1},{5,7},{7,5},{8,10},{10,8},{12,... | collective-permute-start | bytes 442376 | tf_op jit(solution)/shard_map/ppermute | solution.py:27
  71.8 1.2 %collective-permute-start.17 = (bf16[144,512]{1,0:T(8,128)(2,1)S(1)}, bf16[144,512]{1,0:T(8,128)(2,1)S(1)}, u32[]{:S(2)}, u32[]{:S(2)}) collective-permute-start(bf16[144,512]{1,0:T(8,128)(2,1)S(1)} %get-tuple-element.80), channel_id=1, source_target_pairs={{0,4},{2,6},{4,0},{6,2},{1,5},{3,7},{5,1},{7,3},{8,12},{10,14},{12... | collective-permute-start | bytes 442376 | tf_op jit(solution)/shard_map/ppermute | solution.py:27
  73.0 1.9 %collective-permute-start.18 = (bf16[144,512]{1,0:T(8,128)(2,1)S(1)}, bf16[144,512]{1,0:T(8,128)(2,1)S(1)}, u32[]{:S(2)}, u32[]{:S(2)}) collective-permute-start(bf16[144,512]{1,0:T(8,128)(2,1)S(1)} %get-tuple-element.81), channel_id=1, source_target_pairs={{0,6},{2,4},{4,2},{6,0},{1,7},{3,5},{5,3},{7,1},{8,14},{10,12},{12... | collective-permute-start | bytes 442376 | tf_op jit(solution)/shard_map/ppermute | solution.py:27
  76.1 1.5 %collective-permute-start.25 = (bf16[32,4096]{1,0:T(8,128)(2,1)S(1)}, bf16[32,4096]{1,0:T(8,128)(2,1)S(1)}, u32[]{:S(2)}, u32[]{:S(2)}) collective-permute-start(bf16[32,4096]{1,0:T(8,128)(2,1)S(1)} %get-tuple-element.91.b), channel_id=1, source_target_pairs={{0,8},{8,0},{16,24},{24,16},{1,9},{9,1},{17,25},{25,17},{2,10},{10... | collective-permute-start | bytes 786440 | tf_op jit(solution)/shard_map/ppermute | solution.py:27
  77.6 3.1 %shard_map.113 = (f32[1024,512]{1,0:T(8,128)}, f32[8,128]{1,0:T(8,128)S(1)}) custom-call(s32[3]{0:T(128)S(1)} %pad_add_fusion.refs_0_.ids, bf16[128,512]{1,0:T(8,128)(2,1)S(1)} %collective-permute-done.refs_1_, bf16[128,512]{1,0:T(8,128)(2,1)S(1)} %collective-permute-done.1.refs_2_, bf16[128,512]{1,0:T(8,128)(2,1)S(1)} %collective-permute-done.2.refs_3_, ...), custom_call_target="tpu_custom_call" | custom-call | tf_op jit(solution)/shard_map/pallas_call | solution.py:241
  80.7 4.2 %collective-permute-done.17.refs_3_ = bf16[144,512]{1,0:T(8,128)(2,1)S(1)} collective-permute-done((bf16[144,512]{1,0:T(8,128)(2,1)S(1)}, bf16[144,512]{1,0:T(8,128)(2,1)S(1)}, u32[]{:S(2)}, u32[]{:S(2)}) %collective-permute-start.17) | collective-permute-done | bytes 147488 | tf_op jit(solution)/shard_map/ppermute | solution.py:27
  85.6 4.5 %collective-permute-start.19 = (bf16[128,512]{1,0:T(8,128)(2,1)S(1)}, bf16[128,512]{1,0:T(8,128)(2,1)S(1)}, u32[]{:S(2)}, u32[]{:S(2)}) collective-permute-start(bf16[128,512]{1,0:T(8,128)(2,1)S(1)} %get-tuple-element.84), channel_id=1, source_target_pairs={{0,0},{1,1},{2,8},{3,9},{4,16},{5,17},{6,24},{7,25},{8,2},{9,3},{1... | collective-permute-start | bytes 393224 | tf_op jit(solution)/shard_map/ppermute | solution.py:666
  90.2 2.5 %shard_map.117 = (f32[128,4096]{1,0:T(8,128)}, f32[8,128]{1,0:T(8,128)S(1)}) custom-call(s32[3]{0:T(128)S(1)} %pad_add_fusion.refs_0_.ids, bf16[32,4096]{1,0:T(8,128)(2,1)S(1)} %get-tuple-element.90.a, bf16[32,4096]{1,0:T(8,128)(2,1)S(1)} %collective-permute-done.24.a_got, bf16[32,4096]{1,0:T(8,128)(2,1)S(1)} %get-tuple-element.91.b, ...), custom_call_target="tpu_custom_call" | custom-call | tf_op jit(solution)/shard_map/pallas_call | solution.py:527
  92.7 1.2 %shard_map.118 = (f32[32,128]{1,0:T(8,128)}, f32[8,128]{1,0:T(8,128)S(1)}) custom-call(s32[3]{0:T(128)S(1)} %pad_add_fusion.refs_0_.ids, f32[8,512]{1,0:T(8,128)S(1)} %get-tuple-element.93.refs_1_, f32[8,512]{1,0:T(8,128)S(1)} %collective-permute-done.26.refs_2_, f32[32,128]{1,0:T(8,128)S(1)} %get-tuple-element.94.refs_3_, ...), custom_call_target="tpu_custom_call" | custom-call | tf_op jit(solution)/shard_map/pallas_call | solution.py:241
  93.8 3.1 %collective-permute-done.19.refs_1_ = bf16[128,512]{1,0:T(8,128)(2,1)S(1)} collective-permute-done((bf16[128,512]{1,0:T(8,128)(2,1)S(1)}, bf16[128,512]{1,0:T(8,128)(2,1)S(1)}, u32[]{:S(2)}, u32[]{:S(2)}) %collective-permute-start.19) | collective-permute-done | bytes 131104 | tf_op jit(solution)/shard_map/ppermute | solution.py:666
  96.9 1.2 %shard_map.119 = bf16[128,512]{1,0:T(8,128)(2,1)} custom-call(s32[3]{0:T(128)S(1)} %pad_add_fusion.refs_0_.ids, bf16[128,512]{1,0:T(8,128)(2,1)S(1)} %collective-permute-done.19.refs_1_, f32[8,128]{1,0:T(8,128)S(1)} %get-tuple-element.92.refs_4_.refs_2_, f32[8,128]{1,0:T(8,128)S(1)} %get-tuple-element.95.refs_3_), custom_call_target="tpu_custom_call" | custom-call | tf_op jit(solution)/shard_map/pallas_call | solution.py:241
  (55 shorter events, 11.9 us)
Async XLA Ops:
  0.6 25.6 %copy-start = (bf16[1024,512]{1,0:T(8,128)(2,1)S(1)}, bf16[1024,512]{1,0:T(8,128)(2,1)}, u32[]{:S(2)}) copy-start(bf16[1024,512]{1,0:T(8,128)(2,1)} %refs_2_.1) | copy-start | bytes 3145732
  0.6 15.2 %collective-permute-start.1 = (bf16[128,512]{1,0:T(8,128)(2,1)}, bf16[128,512]{1,0:T(8,128)(2,1)S(1)}, u32[]{:S(2)}, u32[]{:S(2)}) collective-permute-start(bf16[128,512]{1,0:T(8,128)(2,1)} %param.6), channel_id=1, source_target_pairs={{0,2},{1,3},{2,10},{3,11},{4,18},{5,19},{6,26},{7,27},{8,0},{9,1},... | collective-permute-start | bytes 393224 | tf_op jit(solution)/shard_map/ppermute | solution.py:574
  0.7 15.2 %collective-permute-start = (bf16[128,512]{1,0:T(8,128)(2,1)}, bf16[128,512]{1,0:T(8,128)(2,1)S(1)}, u32[]{:S(2)}, u32[]{:S(2)}) collective-permute-start(bf16[128,512]{1,0:T(8,128)(2,1)} %param.6), channel_id=1, source_target_pairs={{0,0},{1,1},{2,8},{3,9},{4,16},{5,17},{6,24},{7,25},{8,2},{9,3},{1... | collective-permute-start | bytes 393224 | tf_op jit(solution)/shard_map/ppermute | solution.py:574
  5.6 10.2 %collective-permute-start.3 = (bf16[128,512]{1,0:T(8,128)(2,1)}, bf16[128,512]{1,0:T(8,128)(2,1)S(1)}, u32[]{:S(2)}, u32[]{:S(2)}) collective-permute-start(bf16[128,512]{1,0:T(8,128)(2,1)} %param.6), channel_id=1, source_target_pairs={{0,6},{1,7},{2,14},{3,15},{4,22},{5,23},{6,30},{7,31},{8,4},{9,5},... | collective-permute-start | bytes 393224 | tf_op jit(solution)/shard_map/ppermute | solution.py:574
  10.0 10.2 %collective-permute-start.2 = (bf16[128,512]{1,0:T(8,128)(2,1)}, bf16[128,512]{1,0:T(8,128)(2,1)S(1)}, u32[]{:S(2)}, u32[]{:S(2)}) collective-permute-start(bf16[128,512]{1,0:T(8,128)(2,1)} %param.6), channel_id=1, source_target_pairs={{0,4},{1,5},{2,12},{3,13},{4,20},{5,21},{6,28},{7,29},{8,6},{9,7},... | collective-permute-start | bytes 393224 | tf_op jit(solution)/shard_map/ppermute | solution.py:574
  11.0 1.2 %copy-start.1 = (bf16[128,4096]{1,0:T(8,128)(2,1)S(1)}, bf16[128,4096]{1,0:T(8,128)(2,1)}, u32[]{:S(2)}) copy-start(bf16[128,4096]{1,0:T(8,128)(2,1)} %refs_1_.1) | copy-start | bytes 3145732
  12.8 8.1 %collective-permute-start.7 = (bf16[512,512]{1,0:T(8,128)(2,1)S(1)}, bf16[512,512]{1,0:T(8,128)(2,1)S(1)}, u32[]{:S(2)}, u32[]{:S(2)}) collective-permute-start(bf16[512,512]{1,0:T(8,128)(2,1)S(1)} %get-tuple-element.56), channel_id=1, source_target_pairs={{0,1},{1,0},{2,3},{3,2},{4,5},{5,4},{6,7},{7,6},{8,9},{9,8},{10,11... | collective-permute-start | bytes 1572872 | tf_op jit(solution)/shard_map/ppermute | solution.py:27
  12.9 0.9 copy-start.2
  13.8 0.7 copy-start.3
  20.8 5.4 %collective-permute-start.4 = (bf16[512,512]{1,0:T(8,128)(2,1)S(1)}, bf16[512,512]{1,0:T(8,128)(2,1)S(1)}, u32[]{:S(2)}, u32[]{:S(2)}) collective-permute-start(bf16[512,512]{1,0:T(8,128)(2,1)S(1)} %shard_map.102), channel_id=1, source_target_pairs={{0,1},{1,0},{2,3},{3,2},{4,5},{5,4},{6,7},{7,6},{8,9},{9,8},{10,11... | collective-permute-start | bytes 1572872 | tf_op jit(solution)/shard_map/ppermute | solution.py:27
  21.6 21.0 %collective-permute-start.8 = (bf16[256,512]{1,0:T(8,128)(2,1)S(1)}, bf16[256,512]{1,0:T(8,128)(2,1)S(1)}, u32[]{:S(2)}, u32[]{:S(2)}) collective-permute-start(bf16[256,512]{1,0:T(8,128)(2,1)S(1)} %get-tuple-element.57), channel_id=1, source_target_pairs={{0,2},{2,0},{4,6},{6,4},{1,3},{3,1},{5,7},{7,5},{8,10},{10,8},{12,... | collective-permute-start | bytes 786440 | tf_op jit(solution)/shard_map/ppermute | solution.py:27
  22.9 19.6 %collective-permute-start.9 = (bf16[256,512]{1,0:T(8,128)(2,1)S(1)}, bf16[256,512]{1,0:T(8,128)(2,1)S(1)}, u32[]{:S(2)}, u32[]{:S(2)}) collective-permute-start(bf16[256,512]{1,0:T(8,128)(2,1)S(1)} %get-tuple-element.58), channel_id=1, source_target_pairs={{0,4},{2,6},{4,0},{6,2},{1,5},{3,7},{5,1},{7,3},{8,12},{10,14},{12... | collective-permute-start | bytes 786440 | tf_op jit(solution)/shard_map/ppermute | solution.py:27
  27.5 15.0 %collective-permute-start.5 = (bf16[256,512]{1,0:T(8,128)(2,1)S(1)}, bf16[256,512]{1,0:T(8,128)(2,1)S(1)}, u32[]{:S(2)}, u32[]{:S(2)}) collective-permute-start(bf16[256,512]{1,0:T(8,128)(2,1)S(1)} %get-tuple-element.53.refs_1_), channel_id=1, source_target_pairs={{0,8},{8,0},{16,24},{24,16},{1,9},{9,1},{17,25},{25,17},{2,10},{10... | collective-permute-start | bytes 786440 | tf_op jit(solution)/shard_map/ppermute | solution.py:27
  27.6 14.9 %collective-permute-start.6 = (bf16[256,512]{1,0:T(8,128)(2,1)S(1)}, bf16[256,512]{1,0:T(8,128)(2,1)S(1)}, u32[]{:S(2)}, u32[]{:S(2)}) collective-permute-start(bf16[256,512]{1,0:T(8,128)(2,1)S(1)} %get-tuple-element.54.refs_3_), channel_id=1, source_target_pairs={{0,16},{8,24},{16,0},{24,8},{1,17},{9,25},{17,1},{25,9},{2,18},{10... | collective-permute-start | bytes 786440 | tf_op jit(solution)/shard_map/ppermute | solution.py:27
  43.4 8.9 %collective-permute-start.10 = (bf16[256,512]{1,0:T(8,128)(2,1)S(1)}, bf16[256,512]{1,0:T(8,128)(2,1)S(1)}, u32[]{:S(2)}, u32[]{:S(2)}) collective-permute-start(bf16[256,512]{1,0:T(8,128)(2,1)S(1)} %get-tuple-element.60), channel_id=1, source_target_pairs={{0,16},{8,24},{16,0},{24,8},{1,17},{9,25},{17,1},{25,9},{2,18},{10... | collective-permute-start | bytes 786440 | tf_op jit(solution)/shard_map/ppermute | solution.py:27
  43.9 8.4 %collective-permute-start.11 = (bf16[256,512]{1,0:T(8,128)(2,1)S(1)}, bf16[256,512]{1,0:T(8,128)(2,1)S(1)}, u32[]{:S(2)}, u32[]{:S(2)}) collective-permute-start(bf16[256,512]{1,0:T(8,128)(2,1)S(1)} %get-tuple-element.62), channel_id=1, source_target_pairs={{0,8},{8,0},{16,24},{24,16},{1,9},{9,1},{17,25},{25,17},{2,10},{10... | collective-permute-start | bytes 786440 | tf_op jit(solution)/shard_map/ppermute | solution.py:27
  45.5 10.7 %collective-permute-start.12 = (bf16[256,512]{1,0:T(8,128)(2,1)S(1)}, bf16[256,512]{1,0:T(8,128)(2,1)S(1)}, u32[]{:S(2)}, u32[]{:S(2)}) collective-permute-start(bf16[256,512]{1,0:T(8,128)(2,1)S(1)} %get-tuple-element.69), channel_id=1, source_target_pairs={{0,6},{2,4},{4,2},{6,0},{1,7},{3,5},{5,3},{7,1},{8,14},{10,12},{12... | collective-permute-start | bytes 786440 | tf_op jit(solution)/shard_map/ppermute | solution.py:27
  54.2 1.3 %collective-permute-start.13 = (bf16[128,512]{1,0:T(8,128)(2,1)S(1)}, bf16[128,512]{1,0:T(8,128)(2,1)S(1)}, u32[]{:S(2)}, u32[]{:S(2)}) collective-permute-start(bf16[128,512]{1,0:T(8,128)(2,1)S(1)} %get-tuple-element.71), channel_id=1, source_target_pairs={{0,1},{1,0},{2,3},{3,2},{4,5},{5,4},{6,7},{7,6},{8,9},{9,8},{10,11... | collective-permute-start | bytes 393224 | tf_op jit(solution)/shard_map/ppermute | solution.py:27
  56.2 6.4 %copy-start.4 = (s32[128,32]{0,1:T(8,128)S(1)}, s32[128,32]{0,1:T(8,128)}, u32[]{:S(2)}) copy-start(s32[128,32]{0,1:T(8,128)} %param.9) | copy-start | bytes 49156
  58.0 5.8 %collective-permute-start.14 = (bf16[512,512]{1,0:T(8,128)(2,1)S(1)}, bf16[512,512]{1,0:T(8,128)(2,1)S(1)}, u32[]{:S(2)}, u32[]{:S(2)}) collective-permute-start(bf16[512,512]{1,0:T(8,128)(2,1)S(1)} %get-tuple-element.75), channel_id=1, source_target_pairs={{0,1},{1,0},{2,3},{3,2},{4,5},{5,4},{6,7},{7,6},{8,9},{9,8},{10,11... | collective-permute-start | bytes 1572872 | tf_op jit(solution)/shard_map/ppermute | solution.py:27
  58.2 5.7 %collective-permute-start.15 = (bf16[64,512]{1,0:T(8,128)(2,1)S(1)}, bf16[64,512]{1,0:T(8,128)(2,1)S(1)}, u32[]{:S(2)}, u32[]{:S(2)}) collective-permute-start(bf16[64,512]{1,0:T(8,128)(2,1)S(1)} %get-tuple-element.77), channel_id=1, source_target_pairs={{0,2},{2,0},{4,6},{6,4},{1,3},{3,1},{5,7},{7,5},{8,10},{10,8},{12,... | collective-permute-start | bytes 196616 | tf_op jit(solution)/shard_map/ppermute | solution.py:27
  59.3 7.8 %collective-permute-start.20 = (bf16[64,512]{1,0:T(8,128)(2,1)S(1)}, bf16[64,512]{1,0:T(8,128)(2,1)S(1)}, u32[]{:S(2)}, u32[]{:S(2)}) collective-permute-start(bf16[64,512]{1,0:T(8,128)(2,1)S(1)} %get-tuple-element.86), channel_id=1, source_target_pairs={{0,4},{2,6},{4,0},{6,2},{1,5},{3,7},{5,1},{7,3},{8,12},{10,14},{12... | collective-permute-start | bytes 196616 | tf_op jit(solution)/shard_map/ppermute | solution.py:27
  61.7 6.1 %collective-permute-start.21 = (bf16[64,512]{1,0:T(8,128)(2,1)S(1)}, bf16[64,512]{1,0:T(8,128)(2,1)S(1)}, u32[]{:S(2)}, u32[]{:S(2)}) collective-permute-start(bf16[64,512]{1,0:T(8,128)(2,1)S(1)} %get-tuple-element.87), channel_id=1, source_target_pairs={{0,6},{2,4},{4,2},{6,0},{1,7},{3,5},{5,3},{7,1},{8,14},{10,12},{12... | collective-permute-start | bytes 196616 | tf_op jit(solution)/shard_map/ppermute | solution.py:27
  68.4 6.5 %collective-permute-start.22 = (bf16[16,4096]{1,0:T(8,128)(2,1)S(1)}, bf16[16,4096]{1,0:T(8,128)(2,1)S(1)}, u32[]{:S(2)}, u32[]{:S(2)}) collective-permute-start(bf16[16,4096]{1,0:T(8,128)(2,1)S(1)} %get-tuple-element.88.refs_1_), channel_id=1, source_target_pairs={{0,8},{8,0},{16,24},{24,16},{1,9},{9,1},{17,25},{25,17},{2,10},{10... | collective-permute-start | bytes 393224 | tf_op jit(solution)/shard_map/ppermute | solution.py:27
  69.0 5.9 %collective-permute-start.23 = (bf16[16,4096]{1,0:T(8,128)(2,1)S(1)}, bf16[16,4096]{1,0:T(8,128)(2,1)S(1)}, u32[]{:S(2)}, u32[]{:S(2)}) collective-permute-start(bf16[16,4096]{1,0:T(8,128)(2,1)S(1)} %get-tuple-element.89.refs_3_), channel_id=1, source_target_pairs={{0,16},{8,24},{16,0},{24,8},{1,17},{9,25},{17,1},{25,9},{2,18},{10... | collective-permute-start | bytes 393224 | tf_op jit(solution)/shard_map/ppermute | solution.py:27
  70.5 10.2 %collective-permute-start.16 = (bf16[144,512]{1,0:T(8,128)(2,1)S(1)}, bf16[144,512]{1,0:T(8,128)(2,1)S(1)}, u32[]{:S(2)}, u32[]{:S(2)}) collective-permute-start(bf16[144,512]{1,0:T(8,128)(2,1)S(1)} %get-tuple-element.79), channel_id=1, source_target_pairs={{0,2},{2,0},{4,6},{6,4},{1,3},{3,1},{5,7},{7,5},{8,10},{10,8},{12,... | collective-permute-start | bytes 442376 | tf_op jit(solution)/shard_map/ppermute | solution.py:27
  71.8 13.1 %collective-permute-start.17 = (bf16[144,512]{1,0:T(8,128)(2,1)S(1)}, bf16[144,512]{1,0:T(8,128)(2,1)S(1)}, u32[]{:S(2)}, u32[]{:S(2)}) collective-permute-start(bf16[144,512]{1,0:T(8,128)(2,1)S(1)} %get-tuple-element.80), channel_id=1, source_target_pairs={{0,4},{2,6},{4,0},{6,2},{1,5},{3,7},{5,1},{7,3},{8,12},{10,14},{12... | collective-permute-start | bytes 442376 | tf_op jit(solution)/shard_map/ppermute | solution.py:27
  73.0 11.9 %collective-permute-start.18 = (bf16[144,512]{1,0:T(8,128)(2,1)S(1)}, bf16[144,512]{1,0:T(8,128)(2,1)S(1)}, u32[]{:S(2)}, u32[]{:S(2)}) collective-permute-start(bf16[144,512]{1,0:T(8,128)(2,1)S(1)} %get-tuple-element.81), channel_id=1, source_target_pairs={{0,6},{2,4},{4,2},{6,0},{1,7},{3,5},{5,3},{7,1},{8,14},{10,12},{12... | collective-permute-start | bytes 442376 | tf_op jit(solution)/shard_map/ppermute | solution.py:27
  75.5 14.7 %collective-permute-start.24 = (bf16[32,4096]{1,0:T(8,128)(2,1)S(1)}, bf16[32,4096]{1,0:T(8,128)(2,1)S(1)}, u32[]{:S(2)}, u32[]{:S(2)}) collective-permute-start(bf16[32,4096]{1,0:T(8,128)(2,1)S(1)} %get-tuple-element.90.a), channel_id=1, source_target_pairs={{0,16},{8,24},{16,0},{24,8},{1,17},{9,25},{17,1},{25,9},{2,18},{10... | collective-permute-start | bytes 786440 | tf_op jit(solution)/shard_map/ppermute | solution.py:27
  76.1 14.1 %collective-permute-start.25 = (bf16[32,4096]{1,0:T(8,128)(2,1)S(1)}, bf16[32,4096]{1,0:T(8,128)(2,1)S(1)}, u32[]{:S(2)}, u32[]{:S(2)}) collective-permute-start(bf16[32,4096]{1,0:T(8,128)(2,1)S(1)} %get-tuple-element.91.b), channel_id=1, source_target_pairs={{0,8},{8,0},{16,24},{24,16},{1,9},{9,1},{17,25},{25,17},{2,10},{10... | collective-permute-start | bytes 786440 | tf_op jit(solution)/shard_map/ppermute | solution.py:27
  85.6 11.3 %collective-permute-start.19 = (bf16[128,512]{1,0:T(8,128)(2,1)S(1)}, bf16[128,512]{1,0:T(8,128)(2,1)S(1)}, u32[]{:S(2)}, u32[]{:S(2)}) collective-permute-start(bf16[128,512]{1,0:T(8,128)(2,1)S(1)} %get-tuple-element.84), channel_id=1, source_target_pairs={{0,0},{1,1},{2,8},{3,9},{4,16},{5,17},{6,24},{7,25},{8,2},{9,3},{1... | collective-permute-start | bytes 393224 | tf_op jit(solution)/shard_map/ppermute | solution.py:666
  90.1 2.6 %collective-permute-start.26 = (f32[8,512]{1,0:T(8,128)S(1)}, f32[8,512]{1,0:T(8,128)S(1)}, u32[]{:S(2)}, u32[]{:S(2)}) collective-permute-start(f32[8,512]{1,0:T(8,128)S(1)} %get-tuple-element.93.refs_1_), channel_id=1, source_target_pairs={{0,1},{1,0},{2,3},{3,2},{4,5},{5,4},{6,7},{7,6},{8,9},{9,8},{10,11... | collective-permute-start | bytes 49160 | tf_op jit(solution)/shard_map/ppermute | solution.py:27
  (1 other events, 0.7 us)

commit v4 on v3

--- a/solution.py
+++ b/solution.py
@@ -430,9 +430,8 @@
     term[...] = dot(gate_grad[...], across, 1, 1).astype(term.dtype)
 
 
-def affinity_body(rows_here, ids, mem_grad, *refs):
+def affinity_part(rows_here, ids, mem_grad, values, rows, packed):
     f32 = jnp.float32
-    values, (rows, out, packed) = refs[:-3], refs[-3:]
     tokens = rows.shape[1]
     count = rows.shape[0]
     at = moved(rows[...], rows_here, ids[1], ids[2])
@@ -450,19 +449,22 @@
     high = affinity.astype(jnp.bfloat16).astype(f32)
     pack_rows(packed, 0, high)
     pack_rows(packed, count, affinity - high)
-    out[...] = packed[...].astype(out.dtype)
-
-
-def inputs_body(ids, gate_grad, weight, arrived, affinity, *refs):
-    outs, token = refs[:-1], refs[-1]
+    return packed[...].astype(jnp.bfloat16)
+
+
+def inputs_body(rows_here, ids, gate_grad, weight, arrived, mem_grad, rows, *refs):
+    pairs = (len(refs) - 2) // 2
+    values, outs, token, packed = refs[:pairs], refs[pairs:-2], refs[-2], refs[-1]
     sign(token)
-    tokens, cols = outs[0].shape[0] - affinity.shape[0], outs[0].shape[1]
+    extra, cols = packed.shape
+    tokens = outs[0].shape[0] - extra
+    affinity = affinity_part(rows_here, ids, mem_grad, values, rows, packed)
     own = weight[aligned(ids[2], cols), :]
     for i, out in enumerate(outs):
         span = aligned(ids[1] ^ i, tokens)
         term = dot(gate_grad[span, :], own, 1, 1) + arrived[span, :].astype(jnp.float32)
         out[:tokens, :] = term.astype(out.dtype)
-        out[tokens:, :] = affinity[...]
+        out[tokens:, :] = affinity
 
 
 def sums_body(ids, *refs):
@@ -474,10 +476,6 @@
     out[...] = whole[:tokens].astype(out.dtype)
     half = (whole.shape[0] - tokens) // 2
     affinity[...] = whole[tokens : tokens + half] + whole[tokens + half :]
-
-
-def copy_body(ids, x, out):
-    out[...] = x[...]
 
 
 def scores_body(ids, own, got, weights, grads, token):
@@ -501,24 +499,13 @@
             out[:, aligned(at + 1 - ids[2], cols)] = piece[sub + j * half : sub + (j + 1) * half, :]
 
 
-def pairs_body(ids, a, a_got, b, b_got, first, second):
-    half = a.shape[0]
-    for x, got, out in ((a, a_got, first), (b, b_got, second)):
-        out[:half, :] = x[...]
-        out[half:, :] = got[...]
-
-
-def widen_body(ids, a, a_got, b, b_got, out, token):
+def widen_body(ids, *refs):
+    pieces, (out, token) = refs[:-2], refs[-2:]
     sign(token)
-    half = a.shape[0] // 2
-    for k in range(4):
-        at = (ids[0] ^ k) * 2 * half
-        first, second = (a_got if k & 2 else a), (b_got if k & 1 else b)
-        i, j = k & 1, k >> 1
-        spot = pl.ds(pl.multiple_of(at, half), half)
-        out[spot, :] = first[i * half : (i + 1) * half, :].astype(out.dtype)
-        spot = pl.ds(pl.multiple_of(at + half, half), half)
-        out[spot, :] = second[j * half : (j + 1) * half, :].astype(out.dtype)
+    half, count = pieces[0].shape[0], len(pieces) // 2
+    for k, piece in enumerate(pieces):
+        at = (ids[0] ^ (k % count)) * 2 * half + k // count * half
+        out[pl.ds(pl.multiple_of(at, half), half), :] = piece[...].astype(out.dtype)
 
 
 def widen(ids, pieces):
@@ -635,16 +622,11 @@
         after=[sent_on],
         flops=1 << 30,
     )
-    affinity = kernel_call(
-        functools.partial(affinity_body, rows_here),
-        [shape((extra, cols))],
-        ids, mem_grad, *value_got, rows_t,
+    *inputs, sent_inputs = kernel_call(
+        functools.partial(inputs_body, rows_here),
+        [shape((tokens + extra, cols))] * pairs + [TOKEN],
+        ids, gate_grad, gate_weight, hop(term, "core", 2, 1), mem_grad, rows_t, *value_got,
         scratch=[pltpu.VMEM((extra, cols), f32)],
-    )[0]
-    *inputs, sent_inputs = kernel_call(
-        inputs_body,
-        [shape((tokens + extra, cols))] * pairs + [TOKEN],
-        ids, gate_grad, gate_weight, hop(term, "core", 2, 1), affinity,
         after=back[1:2],
     )
     grad_gate, done = kernel_call(
@@ -667,21 +649,16 @@
     first, second = kernel_call(
         rows_body, [shape((sub // 2, width))] * 2, ids, *back, after=[sent_inputs]
     )
-    first, second = kernel_call(
-        pairs_body, [shape((sub, width))] * 2,
-        ids, first, hop(first, "dp", dp, 1), second, hop(second, "dp", dp, 2),
-    )
-    grad_values, token = widen(
-        ids, [first, hop(first, "dp", dp, 2), second, hop(second, "dp", dp, 1)]
-    )
+    along_x, along_y = hop(first, "dp", dp, 1), hop(second, "dp", dp, 2)
+    first = [first, along_x, hop(first, "dp", dp, 2), hop(along_x, "dp", dp, 2)]
+    second = [second, hop(second, "dp", dp, 1), along_y, hop(along_y, "dp", dp, 1)]
+    grad_values, token = widen(ids, first + second)
     grad_scores, scored = kernel_call(
         scores_body,
         [shape((picks, tokens), f32), TOKEN],
         ids, affinity, hop(affinity, "core", 2, 1), weights_t, after=[token],
     )
-    grad_hidden = kernel_call(
-        copy_body, [shape((tokens, cols))], ids, grad_hidden, after=[token, scored]
-    )[0]
+    grad_hidden = grad_hidden + (token[0, 0] + scored[0, 0]).astype(grad_hidden.dtype)
     return (branch_out, grad_hidden, grad_gate, grad_values, grad_scores.T)
 
 

time: 98.5 us -> 96.2 us (0.977)
  waiting for transfers between devices: 15.7 us -> 11.9 us
  Pallas kernels: 27.1 us -> 24.5 us
  between operations: 0.93 us -> 2.21 us
  local copies, waits for them, and re-layouts: 3.57 us -> 4.61 us
    pallas_call x18 -> x15, Pallas kernels: 24.6 us -> 22 us  [kernel_call(): pl.pallas_call(whole_body, in_specs=[pl.BlockSpec(memory_space=pltpu.SMEM...]
    ppermute x22 -> x24, waiting for transfers between devices: 8.22 us -> 5.73 us  [hop(): return lax.ppermute(x, axis, [(i, i ^ mask) for i in range(size)])]
    ppermute x22 -> x24, starting transfers between devices: 21.1 us -> 23.2 us  [hop(): return lax.ppermute(x, axis, [(i, i ^ mask) for i in range(size)])]
    ppermute x1, starting transfers between devices: 4.52 us -> 2.63 us  [local_square(): grad_hidden = lax.ppermute(grad_hidden, ('dp',) + TABLE, perm)]
    ppermute x1, waiting for transfers between devices: 3.08 us -> 1.8 us  [local_square(): grad_hidden = lax.ppermute(grad_hidden, ('dp',) + TABLE, perm)]
    slice x0 -> x2, local copies, waits for them, and re-layouts: none -> 1.05 us  [the longest x1 0.53 us: local_square(): scored[0, 0]]
  transfers between devices with their start and end apart: 27 -> 29, of which waited for: 6 -> 5; matrix products, arithmetic and copies ran while one was open for 0% -> 1% of each run, Pallas kernels for 23% -> 23%
where the time goes in v4:
time: 96.2 us; the launch traced here: 94.8 us
  starting transfers between devices  36 us (37%)
  Pallas kernels  24.5 us (25%)
  blocking collectives  14.8 us (15%)
  waiting for transfers between devices  11.9 us (12%)
  local copies, waits for them, and re-layouts  4.61 us (5%)
  between operations  2.21 us (2%)
    ppermute x24, starting transfers between devices, hop(): return lax.ppermute(x, axis, [(i, i ^ mask) for i in range(size)])  23.2 us
    pallas_call x15, Pallas kernels, kernel_call(): pl.pallas_call(whole_body, in_specs=[pl.BlockSpec(memory_space=pltpu.SMEM...  22 us
    all_gather x1, blocking collectives, local_square(): sent = lax.all_gather(sent_own, 'dp', axis=0)  14.8 us
    ppermute x4, starting transfers between devices, local_square(): mine.append(lax.ppermute(hidden_in, ('dp',) + TABLE, perm))  10.2 us
    ppermute x24, waiting for transfers between devices, hop(): return lax.ppermute(x, axis, [(i, i ^ mask) for i in range(size)])  5.73 us
    ppermute x4, waiting for transfers between devices, local_square(): mine.append(lax.ppermute(hidden_in, ('dp',) + TABLE, perm))  4.41 us
    unnamed x12, local copies, waits for them, and re-layouts  3.57 us
    ppermute x1, starting transfers between devices, local_square(): grad_hidden = lax.ppermute(grad_hidden, ('dp',) + TABLE, perm)  2.63 us
  transfers between devices with their start and end apart: 29, of which 5 were waited for; matrix products, arithmetic and copies ran while one was open for 1% of the time, Pallas kernels for 23%

profile of v4, /device:TPU:2, one launch (start us, length us, event | category | flops | bytes accessed | tf_op | source)
XLA Modules:
  0.0 94.8 jit_solution(4047535505908329071)
XLA Ops:
  0.7 4.9 %collective-permute-start = (bf16[128,512]{1,0:T(8,128)(2,1)}, bf16[128,512]{1,0:T(8,128)(2,1)S(1)}, u32[]{:S(2)}, u32[]{:S(2)}) collective-permute-start(bf16[128,512]{1,0:T(8,128)(2,1)} %param.6), channel_id=1, source_target_pairs={{0,0},{1,1},{2,8},{3,9},{4,16},{5,17},{6,24},{7,25},{8,2},{9,3},{1... | collective-permute-start | bytes 393224 | tf_op jit(solution)/shard_map/ppermute | solution.py:561
  5.6 4.4 %collective-permute-start.3 = (bf16[128,512]{1,0:T(8,128)(2,1)}, bf16[128,512]{1,0:T(8,128)(2,1)S(1)}, u32[]{:S(2)}, u32[]{:S(2)}) collective-permute-start(bf16[128,512]{1,0:T(8,128)(2,1)} %param.6), channel_id=1, source_target_pairs={{0,6},{1,7},{2,14},{3,15},{4,22},{5,23},{6,30},{7,31},{8,4},{9,5},... | collective-permute-start | bytes 393224 | tf_op jit(solution)/shard_map/ppermute | solution.py:561
  10.0 0.9 collective-permute-start.2
  11.0 1.2 %copy-done.1 = bf16[128,4096]{1,0:T(8,128)(2,1)S(1)} copy-done((bf16[128,4096]{1,0:T(8,128)(2,1)S(1)}, bf16[128,4096]{1,0:T(8,128)(2,1)}, u32[]{:S(2)}) %copy-start.1) | copy-done | bytes 1048600
  12.9 0.9 copy-done.2
  15.9 4.4 %collective-permute-done.2.refs_3_ = bf16[128,512]{1,0:T(8,128)(2,1)S(1)} collective-permute-done((bf16[128,512]{1,0:T(8,128)(2,1)}, bf16[128,512]{1,0:T(8,128)(2,1)S(1)}, u32[]{:S(2)}, u32[]{:S(2)}) %collective-permute-start.2) | collective-permute-done | bytes 131104 | tf_op jit(solution)/shard_map/ppermute | solution.py:561
  21.6 1.4 %collective-permute-start.8 = (bf16[256,512]{1,0:T(8,128)(2,1)S(1)}, bf16[256,512]{1,0:T(8,128)(2,1)S(1)}, u32[]{:S(2)}, u32[]{:S(2)}) collective-permute-start(bf16[256,512]{1,0:T(8,128)(2,1)S(1)} %get-tuple-element.55), channel_id=1, source_target_pairs={{0,2},{2,0},{4,6},{6,4},{1,3},{3,1},{5,7},{7,5},{8,10},{10,8},{12,... | collective-permute-start | bytes 786440 | tf_op jit(solution)/shard_map/ppermute | solution.py:27
  22.9 3.3 %collective-permute-start.9 = (bf16[256,512]{1,0:T(8,128)(2,1)S(1)}, bf16[256,512]{1,0:T(8,128)(2,1)S(1)}, u32[]{:S(2)}, u32[]{:S(2)}) collective-permute-start(bf16[256,512]{1,0:T(8,128)(2,1)S(1)} %get-tuple-element.56), channel_id=1, source_target_pairs={{0,4},{2,6},{4,0},{6,2},{1,5},{3,7},{5,1},{7,3},{8,12},{10,14},{12... | collective-permute-start | bytes 786440 | tf_op jit(solution)/shard_map/ppermute | solution.py:27
  26.2 1.3 %shard_map.103 = (bf16[256,512]{1,0:T(8,128)(2,1)S(1)}, bf16[256,512]{1,0:T(8,128)(2,1)S(1)}) custom-call(s32[3]{0:T(128)S(1)} %pad_add_fusion.refs_0_.ids, bf16[128,512]{1,0:T(8,128)(2,1)S(1)} %collective-permute-done.refs_1_, bf16[128,512]{1,0:T(8,128)(2,1)S(1)} %collective-permute-done.1.refs_2_, bf16[128,512]{1,0:T(8,128)(2,1)S(1)} %collective-permute-done.2.refs_3_, ...), custom_call_target="tpu_custom_call" | custom-call | tf_op jit(solution)/shard_map/pallas_call | solution.py:241
  27.7 14.8 %all-gather = bf16[640,512]{1,0:T(8,128)(2,1)S(1)} all-gather(bf16[160,512]{1,0:T(8,128)(2,1)S(1)} %get-tuple-element.50.refs_5_), channel_id=2, replica_groups=mesh['dp'=4,'pair'=4,'core'=2] {'dp'}, dimensions={0}, use_global_device_ids=true | all-gather | bytes 819200 | tf_op jit(solution)/shard_map/all_gather | solution.py:571
  43.9 1.5 %collective-permute-start.11 = (bf16[256,512]{1,0:T(8,128)(2,1)S(1)}, bf16[256,512]{1,0:T(8,128)(2,1)S(1)}, u32[]{:S(2)}, u32[]{:S(2)}) collective-permute-start(bf16[256,512]{1,0:T(8,128)(2,1)S(1)} %get-tuple-element.60), channel_id=1, source_target_pairs={{0,8},{8,0},{16,24},{24,16},{1,9},{9,1},{17,25},{25,17},{2,10},{10... | collective-permute-start | bytes 786440 | tf_op jit(solution)/shard_map/ppermute | solution.py:27
  45.5 0.9 collective-permute-start.12
  46.3 5.9 %shard_map.107 = (bf16[1024,512]{1,0:T(8,128)(2,1)S(1)}, bf16[256,512]{1,0:T(8,128)(2,1)S(1)}) custom-call(s32[3]{0:T(128)S(1)} %pad_add_fusion.refs_0_.ids, bf16[4,160,512]{2,1,0:T(8,128)(2,1)S(1)} %bitcast.9, f32[8,128]{1,0:T(8,128)S(1)} %get-tuple-element.61.refs_2_), custom_call_target="tpu_custom_call" | custom-call | tf_op jit(solution)/shard_map/pallas_call | solution.py:241
  52.3 1.9 %shard_map.108 = (bf16[512,512]{1,0:T(8,128)(2,1)S(1)}, f32[512,512]{1,0:T(8,128)S(1)}, f32[128,512]{1,0:T(8,128)S(1)}, bf16[128,512]{1,0:T(8,128)(2,1)S(1)}, bf...) custom-call(s32[3]{0:T(128)S(1)} %pad_add_fusion.refs_0_.ids, bf16[256,512]{1,0:T(8,128)(2,1)S(1)} %get-tuple-element.57.refs_1_, ...), custom_call_target="tpu_custom_call" | custom-call | tf_op jit(solution)/shard_map/pallas_call | solution.py:241
  54.2 1.3 %collective-permute-done.13.refs_2_ = bf16[128,512]{1,0:T(8,128)(2,1)S(1)} collective-permute-done((bf16[128,512]{1,0:T(8,128)(2,1)S(1)}, bf16[128,512]{1,0:T(8,128)(2,1)S(1)}, u32[]{:S(2)}, u32[]{:S(2)}) %collective-permute-start.13) | collective-permute-done | bytes 131104 | tf_op jit(solution)/shard_map/ppermute | solution.py:27
  56.2 1.9 %shard_map.110 = (bf16[512,512]{1,0:T(8,128)(2,1)S(1)}, bf16[128,512]{1,0:T(8,128)(2,1)}, bf16[512,512]{1,0:T(8,128)(2,1)S(1)}) custom-call(s32[3]{0:T(128)S(1)} %pad_add_fusion.refs_0_.ids, f32[512,512]{1,0:T(8,128)S(1)} %get-tuple-element.63.refs_1_, f32[128,512]{1,0:T(8,128)S(1)} %get-tuple-element.64.refs_2_, ...), custom_call_target="tpu_custom_call" | custom-call | tf_op jit(solution)/shard_map/pallas_call | solution.py:241
  58.2 1.1 %collective-permute-start.15 = (bf16[64,512]{1,0:T(8,128)(2,1)S(1)}, bf16[64,512]{1,0:T(8,128)(2,1)S(1)}, u32[]{:S(2)}, u32[]{:S(2)}) collective-permute-start(bf16[64,512]{1,0:T(8,128)(2,1)S(1)} %get-tuple-element.75), channel_id=1, source_target_pairs={{0,2},{2,0},{4,6},{6,4},{1,3},{3,1},{5,7},{7,5},{8,10},{10,8},{12,... | collective-permute-start | bytes 196616 | tf_op jit(solution)/shard_map/ppermute | solution.py:27
  59.3 2.4 %collective-permute-start.20 = (bf16[64,512]{1,0:T(8,128)(2,1)S(1)}, bf16[64,512]{1,0:T(8,128)(2,1)S(1)}, u32[]{:S(2)}, u32[]{:S(2)}) collective-permute-start(bf16[64,512]{1,0:T(8,128)(2,1)S(1)} %get-tuple-element.84), channel_id=1, source_target_pairs={{0,4},{2,6},{4,0},{6,2},{1,5},{3,7},{5,1},{7,3},{8,12},{10,14},{12... | collective-permute-start | bytes 196616 | tf_op jit(solution)/shard_map/ppermute | solution.py:27
  61.7 0.9 collective-permute-start.21
  62.6 1.7 %shard_map.111 = (bf16[144,512]{1,0:T(8,128)(2,1)S(1)}, bf16[144,512]{1,0:T(8,128)(2,1)S(1)}, bf16[144,512]{1,0:T(8,128)(2,1)S(1)}, bf16[144,512]{1,0:T(8,128)(2,1)S(1)}, f32[8,128]{1,0:T(8,128)S(1)}) custom-call(s32[3]{0:T(128)S(1)} %pad_add_fusion.refs_0_.ids, bf16[512,512]{1,0:T(8,128)(2,1)S(1)} %get-tuple-element.72.refs_1_.refs_6_, ...), custom_call_target="tpu_custom_call" | custom-call | tf_op jit(solution)/shard_map/pallas_call | solution.py:241
  64.3 1.2 %collective-permute-start.16 = (bf16[144,512]{1,0:T(8,128)(2,1)S(1)}, bf16[144,512]{1,0:T(8,128)(2,1)S(1)}, u32[]{:S(2)}, u32[]{:S(2)}) collective-permute-start(bf16[144,512]{1,0:T(8,128)(2,1)S(1)} %get-tuple-element.77), channel_id=1, source_target_pairs={{0,2},{2,0},{4,6},{6,4},{1,3},{3,1},{5,7},{7,5},{8,10},{10,8},{12,... | collective-permute-start | bytes 442376 | tf_op jit(solution)/shard_map/ppermute | solution.py:27
  65.6 3.3 %collective-permute-start.17 = (bf16[144,512]{1,0:T(8,128)(2,1)S(1)}, bf16[144,512]{1,0:T(8,128)(2,1)S(1)}, u32[]{:S(2)}, u32[]{:S(2)}) collective-permute-start(bf16[144,512]{1,0:T(8,128)(2,1)S(1)} %get-tuple-element.78), channel_id=1, source_target_pairs={{0,4},{2,6},{4,0},{6,2},{1,5},{3,7},{5,1},{7,3},{8,12},{10,14},{12... | collective-permute-start | bytes 442376 | tf_op jit(solution)/shard_map/ppermute | solution.py:27
  70.0 0.8 collective-permute-start.18
  70.9 1.6 %collective-permute-start.26 = (bf16[16,4096]{1,0:T(8,128)(2,1)S(1)}, bf16[16,4096]{1,0:T(8,128)(2,1)S(1)}, u32[]{:S(2)}, u32[]{:S(2)}) collective-permute-start(bf16[16,4096]{1,0:T(8,128)(2,1)S(1)} %get-tuple-element.87.refs_4_), channel_id=1, source_target_pairs={{0,16},{8,24},{16,0},{24,8},{1,17},{9,25},{17,1},{25,9},{2,18},{10... | collective-permute-start | bytes 393224 | tf_op jit(solution)/shard_map/ppermute | solution.py:27
  72.4 2.1 %collective-permute-done.22.refs_1_ = bf16[16,4096]{1,0:T(8,128)(2,1)S(1)} collective-permute-done((bf16[16,4096]{1,0:T(8,128)(2,1)S(1)}, bf16[16,4096]{1,0:T(8,128)(2,1)S(1)}, u32[]{:S(2)}, u32[]{:S(2)}) %collective-permute-start.22) | collective-permute-done | bytes 131104 | tf_op jit(solution)/shard_map/ppermute | solution.py:27
  75.0 2.2 %collective-permute-done.26.refs_6_ = bf16[16,4096]{1,0:T(8,128)(2,1)S(1)} collective-permute-done((bf16[16,4096]{1,0:T(8,128)(2,1)S(1)}, bf16[16,4096]{1,0:T(8,128)(2,1)S(1)}, u32[]{:S(2)}, u32[]{:S(2)}) %collective-permute-start.26) | collective-permute-done | bytes 131104 | tf_op jit(solution)/shard_map/ppermute | solution.py:27
  77.8 1.4 %collective-permute-start.24 = (bf16[16,4096]{1,0:T(8,128)(2,1)S(1)}, bf16[16,4096]{1,0:T(8,128)(2,1)S(1)}, u32[]{:S(2)}, u32[]{:S(2)}) collective-permute-start(bf16[16,4096]{1,0:T(8,128)(2,1)S(1)} %collective-permute-done.22.refs_1_), channel_id=1, source_target_pairs={{0,16},{8,24},{16,0},{24,8},{1,17},{9,25},{17,1},{25,9},{2,18},{10... | collective-permute-start | bytes 393224 | tf_op jit(solution)/shard_map/ppermute | solution.py:27
  79.8 3.1 %shard_map.112 = (f32[1024,512]{1,0:T(8,128)}, f32[8,128]{1,0:T(8,128)S(1)}) custom-call(s32[3]{0:T(128)S(1)} %pad_add_fusion.refs_0_.ids, bf16[128,512]{1,0:T(8,128)(2,1)S(1)} %collective-permute-done.refs_1_, bf16[128,512]{1,0:T(8,128)(2,1)S(1)} %collective-permute-done.1.refs_2_, bf16[128,512]{1,0:T(8,128)(2,1)S(1)} %collective-permute-done.2.refs_3_, ...), custom_call_target="tpu_custom_call" | custom-call | tf_op jit(solution)/shard_map/pallas_call | solution.py:241
  83.6 2.6 %collective-permute-start.19 = (bf16[128,512]{1,0:T(8,128)(2,1)S(1)}, bf16[128,512]{1,0:T(8,128)(2,1)S(1)}, u32[]{:S(2)}, u32[]{:S(2)}) collective-permute-start(bf16[128,512]{1,0:T(8,128)(2,1)S(1)} %get-tuple-element.82), channel_id=1, source_target_pairs={{0,0},{1,1},{2,8},{3,9},{4,16},{5,17},{6,24},{7,25},{8,2},{9,3},{1... | collective-permute-start | bytes 393224 | tf_op jit(solution)/shard_map/ppermute | solution.py:648
  86.4 2.5 %shard_map.115 = (f32[128,4096]{1,0:T(8,128)}, f32[8,128]{1,0:T(8,128)S(1)}) custom-call(s32[3]{0:T(128)S(1)} %pad_add_fusion.refs_0_.ids, bf16[16,4096]{1,0:T(8,128)(2,1)S(1)} %get-tuple-element.86.refs_0_, bf16[16,4096]{1,0:T(8,128)(2,1)S(1)} %collective-permute-done.22.refs_1_, bf16[16,4096]{1,0:T(8,128)(2,1)S(1)} %collective-permute-done.23.refs_2_, ...), custom_call_target="tpu_custom_call" | custom-call | tf_op jit(solution)/shard_map/pallas_call | solution.py:514
  89.4 1.2 %shard_map.116 = (f32[32,128]{1,0:T(8,128)}, f32[8,128]{1,0:T(8,128)S(1)}) custom-call(s32[3]{0:T(128)S(1)} %pad_add_fusion.refs_0_.ids, f32[8,512]{1,0:T(8,128)S(1)} %get-tuple-element.89.refs_1_, f32[8,512]{1,0:T(8,128)S(1)} %collective-permute-done.28.refs_2_, f32[32,128]{1,0:T(8,128)S(1)} %get-tuple-element.90.refs_3_, ...), custom_call_target="tpu_custom_call" | custom-call | tf_op jit(solution)/shard_map/pallas_call | solution.py:241
  92.4 1.8 %collective-permute-done.19 = bf16[128,512]{1,0:T(8,128)(2,1)S(1)} collective-permute-done((bf16[128,512]{1,0:T(8,128)(2,1)S(1)}, bf16[128,512]{1,0:T(8,128)(2,1)S(1)}, u32[]{:S(2)}, u32[]{:S(2)}) %collective-permute-start.19) | collective-permute-done | bytes 131104 | tf_op jit(solution)/shard_map/ppermute | solution.py:648
  (59 shorter events, 11.6 us)
Async XLA Ops:
  0.6 25.6 %copy-start = (bf16[1024,512]{1,0:T(8,128)(2,1)S(1)}, bf16[1024,512]{1,0:T(8,128)(2,1)}, u32[]{:S(2)}) copy-start(bf16[1024,512]{1,0:T(8,128)(2,1)} %refs_2_.1) | copy-start | bytes 3145732
  0.6 15.2 %collective-permute-start.1 = (bf16[128,512]{1,0:T(8,128)(2,1)}, bf16[128,512]{1,0:T(8,128)(2,1)S(1)}, u32[]{:S(2)}, u32[]{:S(2)}) collective-permute-start(bf16[128,512]{1,0:T(8,128)(2,1)} %param.6), channel_id=1, source_target_pairs={{0,2},{1,3},{2,10},{3,11},{4,18},{5,19},{6,26},{7,27},{8,0},{9,1},... | collective-permute-start | bytes 393224 | tf_op jit(solution)/shard_map/ppermute | solution.py:561
  0.7 15.2 %collective-permute-start = (bf16[128,512]{1,0:T(8,128)(2,1)}, bf16[128,512]{1,0:T(8,128)(2,1)S(1)}, u32[]{:S(2)}, u32[]{:S(2)}) collective-permute-start(bf16[128,512]{1,0:T(8,128)(2,1)} %param.6), channel_id=1, source_target_pairs={{0,0},{1,1},{2,8},{3,9},{4,16},{5,17},{6,24},{7,25},{8,2},{9,3},{1... | collective-permute-start | bytes 393224 | tf_op jit(solution)/shard_map/ppermute | solution.py:561
  5.6 10.2 %collective-permute-start.3 = (bf16[128,512]{1,0:T(8,128)(2,1)}, bf16[128,512]{1,0:T(8,128)(2,1)S(1)}, u32[]{:S(2)}, u32[]{:S(2)}) collective-permute-start(bf16[128,512]{1,0:T(8,128)(2,1)} %param.6), channel_id=1, source_target_pairs={{0,6},{1,7},{2,14},{3,15},{4,22},{5,23},{6,30},{7,31},{8,4},{9,5},... | collective-permute-start | bytes 393224 | tf_op jit(solution)/shard_map/ppermute | solution.py:561
  10.0 10.2 %collective-permute-start.2 = (bf16[128,512]{1,0:T(8,128)(2,1)}, bf16[128,512]{1,0:T(8,128)(2,1)S(1)}, u32[]{:S(2)}, u32[]{:S(2)}) collective-permute-start(bf16[128,512]{1,0:T(8,128)(2,1)} %param.6), channel_id=1, source_target_pairs={{0,4},{1,5},{2,12},{3,13},{4,20},{5,21},{6,28},{7,29},{8,6},{9,7},... | collective-permute-start | bytes 393224 | tf_op jit(solution)/shard_map/ppermute | solution.py:561
  11.0 1.2 %copy-start.1 = (bf16[128,4096]{1,0:T(8,128)(2,1)S(1)}, bf16[128,4096]{1,0:T(8,128)(2,1)}, u32[]{:S(2)}) copy-start(bf16[128,4096]{1,0:T(8,128)(2,1)} %refs_1_.1) | copy-start | bytes 3145732
  12.8 8.1 %collective-permute-start.7 = (bf16[512,512]{1,0:T(8,128)(2,1)S(1)}, bf16[512,512]{1,0:T(8,128)(2,1)S(1)}, u32[]{:S(2)}, u32[]{:S(2)}) collective-permute-start(bf16[512,512]{1,0:T(8,128)(2,1)S(1)} %get-tuple-element.54), channel_id=1, source_target_pairs={{0,1},{1,0},{2,3},{3,2},{4,5},{5,4},{6,7},{7,6},{8,9},{9,8},{10,11... | collective-permute-start | bytes 1572872 | tf_op jit(solution)/shard_map/ppermute | solution.py:27
  20.8 5.4 %collective-permute-start.4 = (bf16[512,512]{1,0:T(8,128)(2,1)S(1)}, bf16[512,512]{1,0:T(8,128)(2,1)S(1)}, u32[]{:S(2)}, u32[]{:S(2)}) collective-permute-start(bf16[512,512]{1,0:T(8,128)(2,1)S(1)} %shard_map.102), channel_id=1, source_target_pairs={{0,1},{1,0},{2,3},{3,2},{4,5},{5,4},{6,7},{7,6},{8,9},{9,8},{10,11... | collective-permute-start | bytes 1572872 | tf_op jit(solution)/shard_map/ppermute | solution.py:27
  21.6 21.0 %collective-permute-start.8 = (bf16[256,512]{1,0:T(8,128)(2,1)S(1)}, bf16[256,512]{1,0:T(8,128)(2,1)S(1)}, u32[]{:S(2)}, u32[]{:S(2)}) collective-permute-start(bf16[256,512]{1,0:T(8,128)(2,1)S(1)} %get-tuple-element.55), channel_id=1, source_target_pairs={{0,2},{2,0},{4,6},{6,4},{1,3},{3,1},{5,7},{7,5},{8,10},{10,8},{12,... | collective-permute-start | bytes 786440 | tf_op jit(solution)/shard_map/ppermute | solution.py:27
  22.9 19.6 %collective-permute-start.9 = (bf16[256,512]{1,0:T(8,128)(2,1)S(1)}, bf16[256,512]{1,0:T(8,128)(2,1)S(1)}, u32[]{:S(2)}, u32[]{:S(2)}) collective-permute-start(bf16[256,512]{1,0:T(8,128)(2,1)S(1)} %get-tuple-element.56), channel_id=1, source_target_pairs={{0,4},{2,6},{4,0},{6,2},{1,5},{3,7},{5,1},{7,3},{8,12},{10,14},{12... | collective-permute-start | bytes 786440 | tf_op jit(solution)/shard_map/ppermute | solution.py:27
  27.5 15.0 %collective-permute-start.5 = (bf16[256,512]{1,0:T(8,128)(2,1)S(1)}, bf16[256,512]{1,0:T(8,128)(2,1)S(1)}, u32[]{:S(2)}, u32[]{:S(2)}) collective-permute-start(bf16[256,512]{1,0:T(8,128)(2,1)S(1)} %get-tuple-element.51.refs_1_), channel_id=1, source_target_pairs={{0,8},{8,0},{16,24},{24,16},{1,9},{9,1},{17,25},{25,17},{2,10},{10... | collective-permute-start | bytes 786440 | tf_op jit(solution)/shard_map/ppermute | solution.py:27
  27.6 14.9 %collective-permute-start.6 = (bf16[256,512]{1,0:T(8,128)(2,1)S(1)}, bf16[256,512]{1,0:T(8,128)(2,1)S(1)}, u32[]{:S(2)}, u32[]{:S(2)}) collective-permute-start(bf16[256,512]{1,0:T(8,128)(2,1)S(1)} %get-tuple-element.52.refs_3_), channel_id=1, source_target_pairs={{0,16},{8,24},{16,0},{24,8},{1,17},{9,25},{17,1},{25,9},{2,18},{10... | collective-permute-start | bytes 786440 | tf_op jit(solution)/shard_map/ppermute | solution.py:27
  43.4 8.9 %collective-permute-start.10 = (bf16[256,512]{1,0:T(8,128)(2,1)S(1)}, bf16[256,512]{1,0:T(8,128)(2,1)S(1)}, u32[]{:S(2)}, u32[]{:S(2)}) collective-permute-start(bf16[256,512]{1,0:T(8,128)(2,1)S(1)} %get-tuple-element.58), channel_id=1, source_target_pairs={{0,16},{8,24},{16,0},{24,8},{1,17},{9,25},{17,1},{25,9},{2,18},{10... | collective-permute-start | bytes 786440 | tf_op jit(solution)/shard_map/ppermute | solution.py:27
  43.9 8.4 %collective-permute-start.11 = (bf16[256,512]{1,0:T(8,128)(2,1)S(1)}, bf16[256,512]{1,0:T(8,128)(2,1)S(1)}, u32[]{:S(2)}, u32[]{:S(2)}) collective-permute-start(bf16[256,512]{1,0:T(8,128)(2,1)S(1)} %get-tuple-element.60), channel_id=1, source_target_pairs={{0,8},{8,0},{16,24},{24,16},{1,9},{9,1},{17,25},{25,17},{2,10},{10... | collective-permute-start | bytes 786440 | tf_op jit(solution)/shard_map/ppermute | solution.py:27
  45.5 10.7 %collective-permute-start.12 = (bf16[256,512]{1,0:T(8,128)(2,1)S(1)}, bf16[256,512]{1,0:T(8,128)(2,1)S(1)}, u32[]{:S(2)}, u32[]{:S(2)}) collective-permute-start(bf16[256,512]{1,0:T(8,128)(2,1)S(1)} %get-tuple-element.67), channel_id=1, source_target_pairs={{0,6},{2,4},{4,2},{6,0},{1,7},{3,5},{5,3},{7,1},{8,14},{10,12},{12... | collective-permute-start | bytes 786440 | tf_op jit(solution)/shard_map/ppermute | solution.py:27
  54.2 1.3 %collective-permute-start.13 = (bf16[128,512]{1,0:T(8,128)(2,1)S(1)}, bf16[128,512]{1,0:T(8,128)(2,1)S(1)}, u32[]{:S(2)}, u32[]{:S(2)}) collective-permute-start(bf16[128,512]{1,0:T(8,128)(2,1)S(1)} %get-tuple-element.69), channel_id=1, source_target_pairs={{0,1},{1,0},{2,3},{3,2},{4,5},{5,4},{6,7},{7,6},{8,9},{9,8},{10,11... | collective-permute-start | bytes 393224 | tf_op jit(solution)/shard_map/ppermute | solution.py:27
  56.2 6.5 %copy-start.4 = (s32[128,32]{0,1:T(8,128)S(1)}, s32[128,32]{0,1:T(8,128)}, u32[]{:S(2)}) copy-start(s32[128,32]{0,1:T(8,128)} %param.9) | copy-start | bytes 49156
  58.0 4.6 %collective-permute-start.14 = (bf16[512,512]{1,0:T(8,128)(2,1)S(1)}, bf16[512,512]{1,0:T(8,128)(2,1)S(1)}, u32[]{:S(2)}, u32[]{:S(2)}) collective-permute-start(bf16[512,512]{1,0:T(8,128)(2,1)S(1)} %get-tuple-element.73), channel_id=1, source_target_pairs={{0,1},{1,0},{2,3},{3,2},{4,5},{5,4},{6,7},{7,6},{8,9},{9,8},{10,11... | collective-permute-start | bytes 1572872 | tf_op jit(solution)/shard_map/ppermute | solution.py:27
  58.2 4.4 %collective-permute-start.15 = (bf16[64,512]{1,0:T(8,128)(2,1)S(1)}, bf16[64,512]{1,0:T(8,128)(2,1)S(1)}, u32[]{:S(2)}, u32[]{:S(2)}) collective-permute-start(bf16[64,512]{1,0:T(8,128)(2,1)S(1)} %get-tuple-element.75), channel_id=1, source_target_pairs={{0,2},{2,0},{4,6},{6,4},{1,3},{3,1},{5,7},{7,5},{8,10},{10,8},{12,... | collective-permute-start | bytes 196616 | tf_op jit(solution)/shard_map/ppermute | solution.py:27
  59.3 9.6 %collective-permute-start.20 = (bf16[64,512]{1,0:T(8,128)(2,1)S(1)}, bf16[64,512]{1,0:T(8,128)(2,1)S(1)}, u32[]{:S(2)}, u32[]{:S(2)}) collective-permute-start(bf16[64,512]{1,0:T(8,128)(2,1)S(1)} %get-tuple-element.84), channel_id=1, source_target_pairs={{0,4},{2,6},{4,0},{6,2},{1,5},{3,7},{5,1},{7,3},{8,12},{10,14},{12... | collective-permute-start | bytes 196616 | tf_op jit(solution)/shard_map/ppermute | solution.py:27
  61.7 7.2 %collective-permute-start.21 = (bf16[64,512]{1,0:T(8,128)(2,1)S(1)}, bf16[64,512]{1,0:T(8,128)(2,1)S(1)}, u32[]{:S(2)}, u32[]{:S(2)}) collective-permute-start(bf16[64,512]{1,0:T(8,128)(2,1)S(1)} %get-tuple-element.85), channel_id=1, source_target_pairs={{0,6},{2,4},{4,2},{6,0},{1,7},{3,5},{5,3},{7,1},{8,14},{10,12},{12... | collective-permute-start | bytes 196616 | tf_op jit(solution)/shard_map/ppermute | solution.py:27
  64.3 13.5 %collective-permute-start.16 = (bf16[144,512]{1,0:T(8,128)(2,1)S(1)}, bf16[144,512]{1,0:T(8,128)(2,1)S(1)}, u32[]{:S(2)}, u32[]{:S(2)}) collective-permute-start(bf16[144,512]{1,0:T(8,128)(2,1)S(1)} %get-tuple-element.77), channel_id=1, source_target_pairs={{0,2},{2,0},{4,6},{6,4},{1,3},{3,1},{5,7},{7,5},{8,10},{10,8},{12,... | collective-permute-start | bytes 442376 | tf_op jit(solution)/shard_map/ppermute | solution.py:27
  65.6 13.7 %collective-permute-start.17 = (bf16[144,512]{1,0:T(8,128)(2,1)S(1)}, bf16[144,512]{1,0:T(8,128)(2,1)S(1)}, u32[]{:S(2)}, u32[]{:S(2)}) collective-permute-start(bf16[144,512]{1,0:T(8,128)(2,1)S(1)} %get-tuple-element.78), channel_id=1, source_target_pairs={{0,4},{2,6},{4,0},{6,2},{1,5},{3,7},{5,1},{7,3},{8,12},{10,14},{12... | collective-permute-start | bytes 442376 | tf_op jit(solution)/shard_map/ppermute | solution.py:27
  69.5 5.0 %collective-permute-start.22 = (bf16[16,4096]{1,0:T(8,128)(2,1)S(1)}, bf16[16,4096]{1,0:T(8,128)(2,1)S(1)}, u32[]{:S(2)}, u32[]{:S(2)}) collective-permute-start(bf16[16,4096]{1,0:T(8,128)(2,1)S(1)} %get-tuple-element.86.refs_0_), channel_id=1, source_target_pairs={{0,8},{8,0},{16,24},{24,16},{1,9},{9,1},{17,25},{25,17},{2,10},{10... | collective-permute-start | bytes 393224 | tf_op jit(solution)/shard_map/ppermute | solution.py:27
  70.0 12.9 %collective-permute-start.18 = (bf16[144,512]{1,0:T(8,128)(2,1)S(1)}, bf16[144,512]{1,0:T(8,128)(2,1)S(1)}, u32[]{:S(2)}, u32[]{:S(2)}) collective-permute-start(bf16[144,512]{1,0:T(8,128)(2,1)S(1)} %get-tuple-element.79), channel_id=1, source_target_pairs={{0,6},{2,4},{4,2},{6,0},{1,7},{3,5},{5,3},{7,1},{8,14},{10,12},{12... | collective-permute-start | bytes 442376 | tf_op jit(solution)/shard_map/ppermute | solution.py:27
  70.9 6.4 %collective-permute-start.26 = (bf16[16,4096]{1,0:T(8,128)(2,1)S(1)}, bf16[16,4096]{1,0:T(8,128)(2,1)S(1)}, u32[]{:S(2)}, u32[]{:S(2)}) collective-permute-start(bf16[16,4096]{1,0:T(8,128)(2,1)S(1)} %get-tuple-element.87.refs_4_), channel_id=1, source_target_pairs={{0,16},{8,24},{16,0},{24,8},{1,17},{9,25},{17,1},{25,9},{2,18},{10... | collective-permute-start | bytes 393224 | tf_op jit(solution)/shard_map/ppermute | solution.py:27
  74.5 11.7 %collective-permute-start.23 = (bf16[16,4096]{1,0:T(8,128)(2,1)S(1)}, bf16[16,4096]{1,0:T(8,128)(2,1)S(1)}, u32[]{:S(2)}, u32[]{:S(2)}) collective-permute-start(bf16[16,4096]{1,0:T(8,128)(2,1)S(1)} %get-tuple-element.86.refs_0_), channel_id=1, source_target_pairs={{0,16},{8,24},{16,0},{24,8},{1,17},{9,25},{17,1},{25,9},{2,18},{10... | collective-permute-start | bytes 393224 | tf_op jit(solution)/shard_map/ppermute | solution.py:27
  77.2 9.1 %collective-permute-start.25 = (bf16[16,4096]{1,0:T(8,128)(2,1)S(1)}, bf16[16,4096]{1,0:T(8,128)(2,1)S(1)}, u32[]{:S(2)}, u32[]{:S(2)}) collective-permute-start(bf16[16,4096]{1,0:T(8,128)(2,1)S(1)} %get-tuple-element.87.refs_4_), channel_id=1, source_target_pairs={{0,8},{8,0},{16,24},{24,16},{1,9},{9,1},{17,25},{25,17},{2,10},{10... | collective-permute-start | bytes 393224 | tf_op jit(solution)/shard_map/ppermute | solution.py:27
  77.8 8.5 %collective-permute-start.24 = (bf16[16,4096]{1,0:T(8,128)(2,1)S(1)}, bf16[16,4096]{1,0:T(8,128)(2,1)S(1)}, u32[]{:S(2)}, u32[]{:S(2)}) collective-permute-start(bf16[16,4096]{1,0:T(8,128)(2,1)S(1)} %collective-permute-done.22.refs_1_), channel_id=1, source_target_pairs={{0,16},{8,24},{16,0},{24,8},{1,17},{9,25},{17,1},{25,9},{2,18},{10... | collective-permute-start | bytes 393224 | tf_op jit(solution)/shard_map/ppermute | solution.py:27
  79.3 7.1 %collective-permute-start.27 = (bf16[16,4096]{1,0:T(8,128)(2,1)S(1)}, bf16[16,4096]{1,0:T(8,128)(2,1)S(1)}, u32[]{:S(2)}, u32[]{:S(2)}) collective-permute-start(bf16[16,4096]{1,0:T(8,128)(2,1)S(1)} %collective-permute-done.26.refs_6_), channel_id=1, source_target_pairs={{0,8},{8,0},{16,24},{24,16},{1,9},{9,1},{17,25},{25,17},{2,10},{10... | collective-permute-start | bytes 393224 | tf_op jit(solution)/shard_map/ppermute | solution.py:27
  83.6 10.6 %collective-permute-start.19 = (bf16[128,512]{1,0:T(8,128)(2,1)S(1)}, bf16[128,512]{1,0:T(8,128)(2,1)S(1)}, u32[]{:S(2)}, u32[]{:S(2)}) collective-permute-start(bf16[128,512]{1,0:T(8,128)(2,1)S(1)} %get-tuple-element.82), channel_id=1, source_target_pairs={{0,0},{1,1},{2,8},{3,9},{4,16},{5,17},{6,24},{7,25},{8,2},{9,3},{1... | collective-permute-start | bytes 393224 | tf_op jit(solution)/shard_map/ppermute | solution.py:648
  86.3 3.1 %collective-permute-start.28 = (f32[8,512]{1,0:T(8,128)S(1)}, f32[8,512]{1,0:T(8,128)S(1)}, u32[]{:S(2)}, u32[]{:S(2)}) collective-permute-start(f32[8,512]{1,0:T(8,128)S(1)} %get-tuple-element.89.refs_1_), channel_id=1, source_target_pairs={{0,1},{1,0},{2,3},{3,2},{4,5},{5,4},{6,7},{7,6},{8,9},{9,8},{10,11... | collective-permute-start | bytes 49160 | tf_op jit(solution)/shard_map/ppermute | solution.py:27
  (3 other events, 2.3 us)

commit v5 on v4

--- a/solution.py
+++ b/solution.py
@@ -229,10 +229,8 @@
     return (branch_out, grad_hidden, grad_gate, grad_values, grad_scores)
 
 
-def kernel_call(body, outs, *args, scratch=(), flops=0, after=()):
+def kernel_call(body, outs, *args, scratch=(), after=()):
     count = len(args)
-    size = sum(a.size * a.dtype.itemsize for a in args)
-    size += sum(o.size * o.dtype.itemsize for o in outs)
 
     def whole_body(*refs):
         body(*refs[:count], *refs[count + len(after) :])
@@ -415,8 +413,9 @@
         message[sub:, :] = got[z * sub : (z + 1) * sub, :]
 
 
-def grads_body(ids, factor, value_own, spread_ref, *refs):
-    values, (weight, gate_grad, branch, term) = refs[:-4], refs[-4:]
+def grads_body(rows_here, ids, factor, value_own, spread_ref, mem_grad, rows_ref, *refs):
+    values, (weight, gate_grad, branch, term, packed) = refs[:-5], refs[-5:]
+    every = gate_grad.shape[0]
     tokens, rows = branch.shape[0], values[0].shape[0]
     for k in range(factor.shape[0] // tokens):
         span = aligned(ids[0] ^ k, tokens)
@@ -427,7 +426,8 @@
         if k == 0:
             branch[...] = (memory * value_own[...]).astype(branch.dtype)
     across = weight[aligned(1 - ids[2], weight.shape[1]), :]
-    term[...] = dot(gate_grad[...], across, 1, 1).astype(term.dtype)
+    term[:every, :] = dot(gate_grad[...], across, 1, 1).astype(term.dtype)
+    term[every:, :] = affinity_part(rows_here, ids, mem_grad, values, rows_ref, packed)
 
 
 def affinity_part(rows_here, ids, mem_grad, values, rows, packed):
@@ -452,35 +452,34 @@
     return packed[...].astype(jnp.bfloat16)
 
 
-def inputs_body(rows_here, ids, gate_grad, weight, arrived, mem_grad, rows, *refs):
-    pairs = (len(refs) - 2) // 2
-    values, outs, token, packed = refs[:pairs], refs[pairs:-2], refs[-2], refs[-1]
+def inputs_body(ids, gate_grad, weight, term, arrived, *refs):
+    f32 = jnp.float32
+    outs, token = refs[:-1], refs[-1]
     sign(token)
-    extra, cols = packed.shape
+    every = gate_grad.shape[0]
+    whole = term[every:, :].astype(f32) + arrived[every:, :].astype(f32)
+    extra = whole.shape[0]
+    whole = whole[: extra // 2] + whole[extra // 2 :]
+    high = whole.astype(jnp.bfloat16).astype(f32)
+    affinity = jnp.concatenate([high, whole - high], axis=0).astype(jnp.bfloat16)
     tokens = outs[0].shape[0] - extra
-    affinity = affinity_part(rows_here, ids, mem_grad, values, rows, packed)
-    own = weight[aligned(ids[2], cols), :]
+    own = weight[aligned(ids[2], weight.shape[1]), :]
     for i, out in enumerate(outs):
         span = aligned(ids[1] ^ i, tokens)
-        term = dot(gate_grad[span, :], own, 1, 1) + arrived[span, :].astype(jnp.float32)
-        out[:tokens, :] = term.astype(out.dtype)
+        total_term = dot(gate_grad[span, :], own, 1, 1) + arrived[span, :].astype(f32)
+        out[:tokens, :] = total_term.astype(out.dtype)
         out[tokens:, :] = affinity
 
 
 def sums_body(ids, *refs):
-    pieces, out, affinity = refs[:-2], refs[-2], refs[-1]
+    pieces, (weights, out, grads) = refs[:-3], refs[-3:]
     whole = 0.0
     for piece in pieces:
         whole = whole + piece[...].astype(jnp.float32)
     tokens = out.shape[0]
     out[...] = whole[:tokens].astype(out.dtype)
     half = (whole.shape[0] - tokens) // 2
-    affinity[...] = whole[tokens : tokens + half] + whole[tokens + half :]
-
-
-def scores_body(ids, own, got, weights, grads, token):
-    sign(token)
-    whole = own[...] + got[...]
+    whole = whole[tokens : tokens + half] + whole[tokens + half :]
     w = weights[...]
     count, lanes = w.shape
     affinity = jnp.concatenate([row_of(whole, k, lanes) for k in range(count)], axis=0)
@@ -529,15 +528,42 @@
 def gate_grads_body(ids, *refs):
     pieces, (others, gate_grad, out, token) = refs[:-4], refs[-4:]
     sign(token)
-    tokens, cols = pieces[0].shape
-    own = jnp.zeros((cols, out.shape[1]), jnp.float32)
-    other = own
-    for k, piece in enumerate(pieces):
-        grads = gate_grad[aligned(ids[1] ^ k, tokens), :]
-        own = own + dot(piece[...], grads, 0, 0)
-        other = other + dot(others[k * tokens : (k + 1) * tokens, :], grads, 0, 0)
-    out[aligned(ids[2], cols), :] = own
-    out[aligned(1 - ids[2], cols), :] = other
+    tokens = pieces[0].shape[0]
+    for j in range(2):
+
+        @pl.when(pl.program_id(0) == j)
+        def _():
+            acc = 0.0
+            for k, piece in enumerate(pieces):
+                grads = gate_grad[aligned(ids[1] ^ k, tokens), :]
+                part = others[k * tokens : (k + 1) * tokens, :] if j else piece[...]
+                acc = acc + dot(part, grads, 0, 0)
+            out[...] = acc
+
+
+def gate_grads(ids, pieces, others, gate_grad, after):
+    cols = gate_grad.shape[1]
+    vmem = pl.BlockSpec(memory_space=pltpu.VMEM)
+    count = len(pieces) + 2
+
+    def whole_body(ids, *refs):
+        gate_grads_body(ids, *refs[:count], *refs[count + 1 :])
+
+    return pl.pallas_call(
+        whole_body,
+        grid_spec=pltpu.PrefetchScalarGridSpec(
+            num_scalar_prefetch=1,
+            grid=(2,),
+            in_specs=[vmem] * (count + 1),
+            out_specs=[
+                pl.BlockSpec((cols, cols), lambda j, ids: (ids[2] ^ j, 0)),
+                pl.BlockSpec(TOKEN.shape, lambda j, ids: (0, 0)),
+            ],
+        ),
+        out_shape=[shape((2 * cols, cols), jnp.float32), TOKEN],
+        compiler_params=pltpu.CompilerParams(vmem_limit_bytes=12 << 20),
+        cost_estimate=pl.CostEstimate(flops=0, bytes_accessed=0, transcendentals=0),
+    )(ids, *pieces, others, gate_grad, after)
 
 
 def local_square(dp, pairs, hidden_in, gate_weight, values, pick_rows, pick_scores, grad_out):
@@ -569,14 +595,13 @@
     )
     sent_own = sent
     sent = lax.all_gather(sent_own, "dp", axis=0)
-    joined = kernel_call(join_body, [shape((every, cols))], ids, *mine, after=[sent_own])[0]
+    joined = kernel_call(join_body, [shape((every, cols))], ids, *mine)[0]
     others = hop(joined, "core", 2, 1)
     first, second = kernel_call(
         gate_body,
         [shape((every // 2, cols))] * 2,
         ids, *mine, others, gate_weight,
         scratch=[pltpu.VMEM((dp, tokens, cols), jnp.bfloat16)],
-        flops=1 << 29,
     )
     value_own, value_send = kernel_call(
         columns_body, [shape((pairs * rows_here, cols))] * 2, ids, values
@@ -597,7 +622,7 @@
         [shape((2 * pairs * rows_here, every)), shape((2 * pairs * sub, every))],
         ids, sent,
         scratch=[pltpu.VMEM((picks, every), jnp.int32), pltpu.VMEM((picks, every), f32)],
-        flops=1 << 27, after=[token],
+        after=[token],
     )
     gates = [first, hop(added[0], "dp", dp, 2), second, hop(added[1], "dp", dp, 1)]
 
@@ -607,7 +632,7 @@
         + [shape((pairs * sub, cols))] * 2
         + [TOKEN],
         ids, *gates, sent, spread_part,
-        scratch=[pltpu.VMEM((every, cols), f32)], flops=1 << 28,
+        scratch=[pltpu.VMEM((every, cols), f32)],
     )
     *messages, sent_on = kernel_call(
         messages_body, [shape((2 * sub, cols))] * pairs + [TOKEN], ids, keep, hop(send, "core", 2, 1)
@@ -616,28 +641,23 @@
     back = swap(messages, "pair", pairs)
     extra = 2 * picks * tokens // cols
     gate_grad, branch_out, term = kernel_call(
-        grads_body,
-        [shape((every, cols)), shape((tokens, cols)), shape((every, cols))],
-        ids, factor, value_part, spread_all, *value_got, gate_weight,
+        functools.partial(grads_body, rows_here),
+        [shape((every, cols)), shape((tokens, cols)), shape((every + extra, cols))],
+        ids, factor, value_part, spread_all, mem_grad, rows_t, *value_got, gate_weight,
+        scratch=[pltpu.VMEM((extra, cols), f32)],
         after=[sent_on],
-        flops=1 << 30,
     )
     *inputs, sent_inputs = kernel_call(
-        functools.partial(inputs_body, rows_here),
+        inputs_body,
         [shape((tokens + extra, cols))] * pairs + [TOKEN],
-        ids, gate_grad, gate_weight, hop(term, "core", 2, 1), mem_grad, rows_t, *value_got,
-        scratch=[pltpu.VMEM((extra, cols), f32)],
+        ids, gate_grad, gate_weight, term, hop(term, "core", 2, 1),
         after=back[1:2],
     )
-    grad_gate, done = kernel_call(
-        gate_grads_body,
-        [shape((2 * cols, cols), f32), TOKEN],
-        ids, *mine, others, gate_grad, after=[sent_inputs],
-    )
-    grad_hidden, affinity = kernel_call(
+    grad_gate, done = gate_grads(ids, mine, others, gate_grad, sent_inputs)
+    grad_hidden, grad_scores = kernel_call(
         sums_body,
-        [shape((tokens, cols)), shape((extra // 2, cols), f32)],
-        ids, *swap(inputs, "pair", pairs), after=[done],
+        [shape((tokens, cols)), shape((picks, tokens), f32)],
+        ids, *swap(inputs, "pair", pairs), weights_t, after=[done],
     )
     perm = [
         ((d * pairs + z) * 2 + h, (z * pairs + d) * 2 + h)
@@ -653,12 +673,6 @@
     first = [first, along_x, hop(first, "dp", dp, 2), hop(along_x, "dp", dp, 2)]
     second = [second, hop(second, "dp", dp, 1), along_y, hop(along_y, "dp", dp, 1)]
     grad_values, token = widen(ids, first + second)
-    grad_scores, scored = kernel_call(
-        scores_body,
-        [shape((picks, tokens), f32), TOKEN],
-        ids, affinity, hop(affinity, "core", 2, 1), weights_t, after=[token],
-    )
-    grad_hidden = grad_hidden + (token[0, 0] + scored[0, 0]).astype(grad_hidden.dtype)
     return (branch_out, grad_hidden, grad_gate, grad_values, grad_scores.T)
 
 

time: 96.2 us -> 95.3 us (level); the launches traced: 94.8 us -> 95 us
  waiting for transfers between devices: 11.9 us -> 16.9 us
  local copies, waits for them, and re-layouts: 4.61 us -> 1.9 us
  between operations: 2.21 us -> 0.94 us
    ppermute x1, waiting for transfers between devices: 1.8 us -> 6.03 us  [local_square(): grad_hidden = lax.ppermute(grad_hidden, ('dp',) + TABLE, perm)]
    pallas_call x15 -> x13, Pallas kernels: 22 us -> 18.6 us  [kernel_call(): pl.pallas_call(whole_body, in_specs=[pl.BlockSpec(memory_space=pltpu.SMEM...]
    pallas_call x0 -> x1, Pallas kernels: none -> 3.02 us  [gate_grads(): pl.pallas_call(whole_body, grid_spec=pltpu.PrefetchScalarGridSpec(num_sca...]
    ppermute x4, waiting for transfers between devices: 4.41 us -> 7.31 us  [local_square(): mine.append(lax.ppermute(hidden_in, ('dp',) + TABLE, perm))]
    ppermute x24 -> x23, waiting for transfers between devices: 5.73 us -> 3.59 us  [hop(): return lax.ppermute(x, axis, [(i, i ^ mask) for i in range(size)])]
    unnamed x12 -> x11, local copies, waits for them, and re-layouts: 3.57 us -> 1.9 us
    ppermute x1, starting transfers between devices: 2.63 us -> 4.26 us  [local_square(): grad_hidden = lax.ppermute(grad_hidden, ('dp',) + TABLE, perm)]
    slice x2 -> x0, local copies, waits for them, and re-layouts: 1.05 us -> none  [the longest x1 0.53 us: local_square(): scored[0, 0]]
  transfers between devices with their start and end apart: 29 -> 28, of which waited for: 5 -> 5; matrix products, arithmetic and copies ran while one was open for 1% -> 0% of each run, Pallas kernels for 23% -> 22%
where the time goes in v5:
time: 95.3 us; the launch traced here: 95 us
  starting transfers between devices  36.8 us (39%)
  Pallas kernels  24.1 us (25%)
  waiting for transfers between devices  16.9 us (18%)
  blocking collectives  14.2 us (15%)
  local copies, waits for them, and re-layouts  1.9 us (2%)
    ppermute x23, starting transfers between devices, hop(): return lax.ppermute(x, axis, [(i, i ^ mask) for i in range(size)])  22.3 us
    pallas_call x13, Pallas kernels, kernel_call(): pl.pallas_call(whole_body, in_specs=[pl.BlockSpec(memory_space=pltpu.SMEM...  18.6 us
    all_gather x1, blocking collectives, local_square(): sent = lax.all_gather(sent_own, 'dp', axis=0)  14.2 us
    ppermute x4, starting transfers between devices, local_square(): mine.append(lax.ppermute(hidden_in, ('dp',) + TABLE, perm))  10.2 us
    ppermute x4, waiting for transfers between devices, local_square(): mine.append(lax.ppermute(hidden_in, ('dp',) + TABLE, perm))  7.31 us
    ppermute x1, waiting for transfers between devices, local_square(): grad_hidden = lax.ppermute(grad_hidden, ('dp',) + TABLE, perm)  6.03 us
    ppermute x1, starting transfers between devices, local_square(): grad_hidden = lax.ppermute(grad_hidden, ('dp',) + TABLE, perm)  4.26 us
    ppermute x23, waiting for transfers between devices, hop(): return lax.ppermute(x, axis, [(i, i ^ mask) for i in range(size)])  3.59 us
  transfers between devices with their start and end apart: 28, of which 5 were waited for; matrix products, arithmetic and copies ran while one was open for 0% of the time, Pallas kernels for 22%

profile of v5, /device:TPU:2, one launch (start us, length us, event | category | flops | bytes accessed | tf_op | source)
XLA Modules:
  0.0 95.0 jit_solution(18073235717420688742)
XLA Ops:
  0.7 4.9 %collective-permute-start = (bf16[128,512]{1,0:T(8,128)(2,1)}, bf16[128,512]{1,0:T(8,128)(2,1)S(1)}, u32[]{:S(2)}, u32[]{:S(2)}) collective-permute-start(bf16[128,512]{1,0:T(8,128)(2,1)} %param.6), channel_id=1, source_target_pairs={{0,0},{1,1},{2,8},{3,9},{4,16},{5,17},{6,24},{7,25},{8,2},{9,3},{1... | collective-permute-start | bytes 393224 | tf_op jit(solution)/shard_map/ppermute | solution.py:587
  5.6 4.4 %collective-permute-start.3 = (bf16[128,512]{1,0:T(8,128)(2,1)}, bf16[128,512]{1,0:T(8,128)(2,1)S(1)}, u32[]{:S(2)}, u32[]{:S(2)}) collective-permute-start(bf16[128,512]{1,0:T(8,128)(2,1)} %param.6), channel_id=1, source_target_pairs={{0,6},{1,7},{2,14},{3,15},{4,22},{5,23},{6,30},{7,31},{8,4},{9,5},... | collective-permute-start | bytes 393224 | tf_op jit(solution)/shard_map/ppermute | solution.py:587
  10.0 0.9 collective-permute-start.2
  11.0 1.2 %copy-done.1 = bf16[128,4096]{1,0:T(8,128)(2,1)S(1)} copy-done((bf16[128,4096]{1,0:T(8,128)(2,1)S(1)}, bf16[128,4096]{1,0:T(8,128)(2,1)}, u32[]{:S(2)}) %copy-start.1) | copy-done | bytes 1048600
  13.0 2.9 %collective-permute-done.3.refs_4_.refs_3_ = bf16[128,512]{1,0:T(8,128)(2,1)S(1)} collective-permute-done((bf16[128,512]{1,0:T(8,128)(2,1)}, bf16[128,512]{1,0:T(8,128)(2,1)S(1)}, u32[]{:S(2)}, u32[]{:S(2)}) %collective-permute-start.3) | collective-permute-done | bytes 131104 | tf_op jit(solution)/shard_map/ppermute | solution.py:587
  15.9 4.4 %collective-permute-done.2.refs_3_.refs_2_ = bf16[128,512]{1,0:T(8,128)(2,1)S(1)} collective-permute-done((bf16[128,512]{1,0:T(8,128)(2,1)}, bf16[128,512]{1,0:T(8,128)(2,1)S(1)}, u32[]{:S(2)}, u32[]{:S(2)}) %collective-permute-start.2) | collective-permute-done | bytes 131104 | tf_op jit(solution)/shard_map/ppermute | solution.py:587
  21.6 1.4 %collective-permute-start.8 = (bf16[256,512]{1,0:T(8,128)(2,1)S(1)}, bf16[256,512]{1,0:T(8,128)(2,1)S(1)}, u32[]{:S(2)}, u32[]{:S(2)}) collective-permute-start(bf16[256,512]{1,0:T(8,128)(2,1)S(1)} %get-tuple-element.52), channel_id=1, source_target_pairs={{0,2},{2,0},{4,6},{6,4},{1,3},{3,1},{5,7},{7,5},{8,10},{10,8},{12,... | collective-permute-start | bytes 786440 | tf_op jit(solution)/shard_map/ppermute | solution.py:27
  22.9 3.3 %collective-permute-start.9 = (bf16[256,512]{1,0:T(8,128)(2,1)S(1)}, bf16[256,512]{1,0:T(8,128)(2,1)S(1)}, u32[]{:S(2)}, u32[]{:S(2)}) collective-permute-start(bf16[256,512]{1,0:T(8,128)(2,1)S(1)} %get-tuple-element.53), channel_id=1, source_target_pairs={{0,4},{2,6},{4,0},{6,2},{1,5},{3,7},{5,1},{7,3},{8,12},{10,14},{12... | collective-permute-start | bytes 786440 | tf_op jit(solution)/shard_map/ppermute | solution.py:27
  26.2 1.3 %shard_map.102 = (bf16[256,512]{1,0:T(8,128)(2,1)S(1)}, bf16[256,512]{1,0:T(8,128)(2,1)S(1)}) custom-call(s32[3]{0:T(128)S(1)} %pad_add_fusion.refs_0_.ids, bf16[128,512]{1,0:T(8,128)(2,1)S(1)} %collective-permute-done.refs_1_.refs_0_, bf16[128,512]{1,0:T(8,128)(2,1)S(1)} %collective-permute-done.1.refs_2_.refs_1_, ...), custom_call_target="tpu_custom_call" | custom-call | tf_op jit(solution)/shard_map/pallas_call | solution.py:239
  28.3 14.2 %all-gather = bf16[640,512]{1,0:T(8,128)(2,1)S(1)} all-gather(bf16[160,512]{1,0:T(8,128)(2,1)S(1)} %get-tuple-element.49), channel_id=2, replica_groups=mesh['dp'=4,'pair'=4,'core'=2] {'dp'}, dimensions={0}, use_global_device_ids=true | all-gather | bytes 819200 | tf_op jit(solution)/shard_map/all_gather | solution.py:597
  42.6 0.8 shard_map.106
  43.9 1.5 %collective-permute-start.11 = (bf16[256,512]{1,0:T(8,128)(2,1)S(1)}, bf16[256,512]{1,0:T(8,128)(2,1)S(1)}, u32[]{:S(2)}, u32[]{:S(2)}) collective-permute-start(bf16[256,512]{1,0:T(8,128)(2,1)S(1)} %get-tuple-element.57), channel_id=1, source_target_pairs={{0,8},{8,0},{16,24},{24,16},{1,9},{9,1},{17,25},{25,17},{2,10},{10... | collective-permute-start | bytes 786440 | tf_op jit(solution)/shard_map/ppermute | solution.py:27
  45.5 0.9 collective-permute-start.12
  46.3 5.9 %shard_map.107 = (bf16[1024,512]{1,0:T(8,128)(2,1)S(1)}, bf16[256,512]{1,0:T(8,128)(2,1)S(1)}) custom-call(s32[3]{0:T(128)S(1)} %pad_add_fusion.refs_0_.ids, bf16[4,160,512]{2,1,0:T(8,128)(2,1)S(1)} %bitcast.8, f32[8,128]{1,0:T(8,128)S(1)} %get-tuple-element.58.refs_2_), custom_call_target="tpu_custom_call" | custom-call | tf_op jit(solution)/shard_map/pallas_call | solution.py:239
  52.3 1.9 %shard_map.108 = (bf16[512,512]{1,0:T(8,128)(2,1)S(1)}, f32[512,512]{1,0:T(8,128)S(1)}, f32[128,512]{1,0:T(8,128)S(1)}, bf16[128,512]{1,0:T(8,128)(2,1)S(1)}, bf...) custom-call(s32[3]{0:T(128)S(1)} %pad_add_fusion.refs_0_.ids, bf16[256,512]{1,0:T(8,128)(2,1)S(1)} %get-tuple-element.54.refs_1_, ...), custom_call_target="tpu_custom_call" | custom-call | tf_op jit(solution)/shard_map/pallas_call | solution.py:239
  54.2 1.3 %collective-permute-done.13.refs_2_ = bf16[128,512]{1,0:T(8,128)(2,1)S(1)} collective-permute-done((bf16[128,512]{1,0:T(8,128)(2,1)S(1)}, bf16[128,512]{1,0:T(8,128)(2,1)S(1)}, u32[]{:S(2)}, u32[]{:S(2)}) %collective-permute-start.13) | collective-permute-done | bytes 131104 | tf_op jit(solution)/shard_map/ppermute | solution.py:27
  56.2 2.6 %shard_map.110 = (bf16[512,512]{1,0:T(8,128)(2,1)S(1)}, bf16[128,512]{1,0:T(8,128)(2,1)}, bf16[528,512]{1,0:T(8,128)(2,1)S(1)}) custom-call(s32[3]{0:T(128)S(1)} %pad_add_fusion.refs_0_.ids, f32[512,512]{1,0:T(8,128)S(1)} %get-tuple-element.60.refs_1_, f32[128,512]{1,0:T(8,128)S(1)} %get-tuple-element.61.refs_2_, ...), custom_call_target="tpu_custom_call" | custom-call | tf_op jit(solution)/shard_map/pallas_call | solution.py:239
  58.9 1.1 %collective-permute-start.15 = (bf16[64,512]{1,0:T(8,128)(2,1)S(1)}, bf16[64,512]{1,0:T(8,128)(2,1)S(1)}, u32[]{:S(2)}, u32[]{:S(2)}) collective-permute-start(bf16[64,512]{1,0:T(8,128)(2,1)S(1)} %get-tuple-element.72), channel_id=1, source_target_pairs={{0,2},{2,0},{4,6},{6,4},{1,3},{3,1},{5,7},{7,5},{8,10},{10,8},{12,... | collective-permute-start | bytes 196616 | tf_op jit(solution)/shard_map/ppermute | solution.py:27
  60.0 2.4 %collective-permute-start.20 = (bf16[64,512]{1,0:T(8,128)(2,1)S(1)}, bf16[64,512]{1,0:T(8,128)(2,1)S(1)}, u32[]{:S(2)}, u32[]{:S(2)}) collective-permute-start(bf16[64,512]{1,0:T(8,128)(2,1)S(1)} %get-tuple-element.83), channel_id=1, source_target_pairs={{0,4},{2,6},{4,0},{6,2},{1,5},{3,7},{5,1},{7,3},{8,12},{10,14},{12... | collective-permute-start | bytes 196616 | tf_op jit(solution)/shard_map/ppermute | solution.py:27
  62.4 0.9 collective-permute-start.21
  63.3 1.4 %shard_map.111 = (bf16[144,512]{1,0:T(8,128)(2,1)S(1)}, bf16[144,512]{1,0:T(8,128)(2,1)S(1)}, bf16[144,512]{1,0:T(8,128)(2,1)S(1)}, bf16[144,512]{1,0:T(8,128)(2,1)S(1)}, f32[8,128]{1,0:T(8,128)S(1)}) custom-call(s32[3]{0:T(128)S(1)} %pad_add_fusion.refs_0_.ids, bf16[512,512]{1,0:T(8,128)(2,1)S(1)} %get-tuple-element.70.refs_1_.refs_5_, ...), custom_call_target="tpu_custom_call" | custom-call | tf_op jit(solution)/shard_map/pallas_call | solution.py:239
  64.7 1.2 %collective-permute-start.16 = (bf16[144,512]{1,0:T(8,128)(2,1)S(1)}, bf16[144,512]{1,0:T(8,128)(2,1)S(1)}, u32[]{:S(2)}, u32[]{:S(2)}) collective-permute-start(bf16[144,512]{1,0:T(8,128)(2,1)S(1)} %get-tuple-element.74), channel_id=1, source_target_pairs={{0,2},{2,0},{4,6},{6,4},{1,3},{3,1},{5,7},{7,5},{8,10},{10,8},{12,... | collective-permute-start | bytes 442376 | tf_op jit(solution)/shard_map/ppermute | solution.py:27
  65.9 3.3 %collective-permute-start.17 = (bf16[144,512]{1,0:T(8,128)(2,1)S(1)}, bf16[144,512]{1,0:T(8,128)(2,1)S(1)}, u32[]{:S(2)}, u32[]{:S(2)}) collective-permute-start(bf16[144,512]{1,0:T(8,128)(2,1)S(1)} %get-tuple-element.75), channel_id=1, source_target_pairs={{0,4},{2,6},{4,0},{6,2},{1,5},{3,7},{5,1},{7,3},{8,12},{10,14},{12... | collective-permute-start | bytes 442376 | tf_op jit(solution)/shard_map/ppermute | solution.py:27
  70.4 1.4 %collective-permute-start.26 = (bf16[16,4096]{1,0:T(8,128)(2,1)S(1)}, bf16[16,4096]{1,0:T(8,128)(2,1)S(1)}, u32[]{:S(2)}, u32[]{:S(2)}) collective-permute-start(bf16[16,4096]{1,0:T(8,128)(2,1)S(1)} %get-tuple-element.86.refs_4_), channel_id=1, source_target_pairs={{0,16},{8,24},{16,0},{24,8},{1,17},{9,25},{17,1},{25,9},{2,18},{10... | collective-permute-start | bytes 393224 | tf_op jit(solution)/shard_map/ppermute | solution.py:27
  71.9 3.0 %shard_map.112 = (f32[1024,512]{1,0:T(8,128)}, f32[8,128]{1,0:T(8,128)S(1)}) custom-call(s32[3]{0:T(128)S(1)} %pad_add_fusion.refs_0_.ids, bf16[128,512]{1,0:T(8,128)(2,1)S(1)} %collective-permute-done.refs_1_.refs_0_, bf16[128,512]{1,0:T(8,128)(2,1)S(1)} %collective-permute-done.1.refs_2_.refs_1_, ...), custom_call_target="tpu_custom_call" | custom-call | tf_op jit(solution)/shard_map/pallas_call | solution.py:552
  75.5 2.1 %collective-permute-start.25 = (bf16[16,4096]{1,0:T(8,128)(2,1)S(1)}, bf16[16,4096]{1,0:T(8,128)(2,1)S(1)}, u32[]{:S(2)}, u32[]{:S(2)}) collective-permute-start(bf16[16,4096]{1,0:T(8,128)(2,1)S(1)} %get-tuple-element.86.refs_4_), channel_id=1, source_target_pairs={{0,8},{8,0},{16,24},{24,16},{1,9},{9,1},{17,25},{25,17},{2,10},{10... | collective-permute-start | bytes 393224 | tf_op jit(solution)/shard_map/ppermute | solution.py:27
  77.6 2.2 %collective-permute-done.17.refs_3_ = bf16[144,512]{1,0:T(8,128)(2,1)S(1)} collective-permute-done((bf16[144,512]{1,0:T(8,128)(2,1)S(1)}, bf16[144,512]{1,0:T(8,128)(2,1)S(1)}, u32[]{:S(2)}, u32[]{:S(2)}) %collective-permute-start.17) | collective-permute-done | bytes 147488 | tf_op jit(solution)/shard_map/ppermute | solution.py:27
  80.3 1.2 %shard_map.113 = (bf16[128,512]{1,0:T(8,128)(2,1)S(1)}, f32[32,128]{1,0:T(8,128)}) custom-call(s32[3]{0:T(128)S(1)} %pad_add_fusion.refs_0_.ids, bf16[144,512]{1,0:T(8,128)(2,1)S(1)} %get-tuple-element.73.refs_1_, bf16[144,512]{1,0:T(8,128)(2,1)S(1)} %collective-permute-done.16.refs_2_, bf16[144,512]{1,0:T(8,128)(2,1)S(1)} %collective-permute-done.17.refs_3_, ...), custom_call_target="tpu_custom_call" | custom-call | tf_op jit(solution)/shard_map/pallas_call | solution.py:239
  81.5 4.3 %collective-permute-start.19 = (bf16[128,512]{1,0:T(8,128)(2,1)S(1)}, bf16[128,512]{1,0:T(8,128)(2,1)S(1)}, u32[]{:S(2)}, u32[]{:S(2)}) collective-permute-start(bf16[128,512]{1,0:T(8,128)(2,1)S(1)} %get-tuple-element.80), channel_id=1, source_target_pairs={{0,0},{1,1},{2,8},{3,9},{4,16},{5,17},{6,24},{7,25},{8,2},{9,3},{1... | collective-permute-start | bytes 393224 | tf_op jit(solution)/shard_map/ppermute | solution.py:668
  85.8 2.5 %shard_map.115 = (f32[128,4096]{1,0:T(8,128)}, f32[8,128]{1,0:T(8,128)}) custom-call(s32[3]{0:T(128)S(1)} %pad_add_fusion.refs_0_.ids, bf16[16,4096]{1,0:T(8,128)(2,1)S(1)} %get-tuple-element.85.refs_0_, bf16[16,4096]{1,0:T(8,128)(2,1)S(1)} %collective-permute-done.22.refs_1_, bf16[16,4096]{1,0:T(8,128)(2,1)S(1)} %collective-permute-done.23.refs_2_, ...), custom_call_target="tpu_custom_call" | custom-call | tf_op jit(solution)/shard_map/pallas_call | solution.py:513
  88.3 6.0 %collective-permute-done.19 = bf16[128,512]{1,0:T(8,128)(2,1)S(1)} collective-permute-done((bf16[128,512]{1,0:T(8,128)(2,1)S(1)}, bf16[128,512]{1,0:T(8,128)(2,1)S(1)}, u32[]{:S(2)}, u32[]{:S(2)}) %collective-permute-start.19) | collective-permute-done | bytes 131104 | tf_op jit(solution)/shard_map/ppermute | solution.py:668
  94.3 0.7 copy.12
  (52 shorter events, 6.4 us)
Async XLA Ops:
  0.6 25.6 %copy-start = (bf16[1024,512]{1,0:T(8,128)(2,1)S(1)}, bf16[1024,512]{1,0:T(8,128)(2,1)}, u32[]{:S(2)}) copy-start(bf16[1024,512]{1,0:T(8,128)(2,1)} %refs_2_.1) | copy-start | bytes 3145732
  0.6 12.3 %collective-permute-start.1 = (bf16[128,512]{1,0:T(8,128)(2,1)}, bf16[128,512]{1,0:T(8,128)(2,1)S(1)}, u32[]{:S(2)}, u32[]{:S(2)}) collective-permute-start(bf16[128,512]{1,0:T(8,128)(2,1)} %param.6), channel_id=1, source_target_pairs={{0,2},{1,3},{2,10},{3,11},{4,18},{5,19},{6,26},{7,27},{8,0},{9,1},... | collective-permute-start | bytes 393224 | tf_op jit(solution)/shard_map/ppermute | solution.py:587
  0.7 12.2 %collective-permute-start = (bf16[128,512]{1,0:T(8,128)(2,1)}, bf16[128,512]{1,0:T(8,128)(2,1)S(1)}, u32[]{:S(2)}, u32[]{:S(2)}) collective-permute-start(bf16[128,512]{1,0:T(8,128)(2,1)} %param.6), channel_id=1, source_target_pairs={{0,0},{1,1},{2,8},{3,9},{4,16},{5,17},{6,24},{7,25},{8,2},{9,3},{1... | collective-permute-start | bytes 393224 | tf_op jit(solution)/shard_map/ppermute | solution.py:587
  5.6 10.2 %collective-permute-start.3 = (bf16[128,512]{1,0:T(8,128)(2,1)}, bf16[128,512]{1,0:T(8,128)(2,1)S(1)}, u32[]{:S(2)}, u32[]{:S(2)}) collective-permute-start(bf16[128,512]{1,0:T(8,128)(2,1)} %param.6), channel_id=1, source_target_pairs={{0,6},{1,7},{2,14},{3,15},{4,22},{5,23},{6,30},{7,31},{8,4},{9,5},... | collective-permute-start | bytes 393224 | tf_op jit(solution)/shard_map/ppermute | solution.py:587
  10.0 10.2 %collective-permute-start.2 = (bf16[128,512]{1,0:T(8,128)(2,1)}, bf16[128,512]{1,0:T(8,128)(2,1)S(1)}, u32[]{:S(2)}, u32[]{:S(2)}) collective-permute-start(bf16[128,512]{1,0:T(8,128)(2,1)} %param.6), channel_id=1, source_target_pairs={{0,4},{1,5},{2,12},{3,13},{4,20},{5,21},{6,28},{7,29},{8,6},{9,7},... | collective-permute-start | bytes 393224 | tf_op jit(solution)/shard_map/ppermute | solution.py:587
  12.8 14.9 %copy-start.2 = (bf16[128,512]{1,0:T(8,128)(2,1)S(1)}, bf16[128,512]{1,0:T(8,128)(2,1)}, u32[]{:S(2)}) copy-start(bf16[128,512]{1,0:T(8,128)(2,1)} %refs_3_.1) | copy-start | bytes 393220
  12.8 14.9 %copy-start.3 = (s32[128,32]{0,1:T(8,128)S(1)}, s32[128,32]{0,1:T(8,128)}, u32[]{:S(2)}) copy-start(s32[128,32]{0,1:T(8,128)} %param.9) | copy-start | bytes 49156
  12.8 14.8 %copy-start.4 = (f32[128,32]{0,1:T(8,128)S(1)}, f32[128,32]{0,1:T(8,128)}, u32[]{:S(2)}) copy-start(f32[128,32]{0,1:T(8,128)} %param.10) | copy-start | bytes 49156
  12.9 8.1 %collective-permute-start.7 = (bf16[512,512]{1,0:T(8,128)(2,1)S(1)}, bf16[512,512]{1,0:T(8,128)(2,1)S(1)}, u32[]{:S(2)}, u32[]{:S(2)}) collective-permute-start(bf16[512,512]{1,0:T(8,128)(2,1)S(1)} %get-tuple-element.51), channel_id=1, source_target_pairs={{0,1},{1,0},{2,3},{3,2},{4,5},{5,4},{6,7},{7,6},{8,9},{9,8},{10,11... | collective-permute-start | bytes 1572872 | tf_op jit(solution)/shard_map/ppermute | solution.py:27
  20.8 5.4 %collective-permute-start.4 = (bf16[512,512]{1,0:T(8,128)(2,1)S(1)}, bf16[512,512]{1,0:T(8,128)(2,1)S(1)}, u32[]{:S(2)}, u32[]{:S(2)}) collective-permute-start(bf16[512,512]{1,0:T(8,128)(2,1)S(1)} %shard_map.101), channel_id=1, source_target_pairs={{0,1},{1,0},{2,3},{3,2},{4,5},{5,4},{6,7},{7,6},{8,9},{9,8},{10,11... | collective-permute-start | bytes 1572872 | tf_op jit(solution)/shard_map/ppermute | solution.py:27
  21.6 21.0 %collective-permute-start.8 = (bf16[256,512]{1,0:T(8,128)(2,1)S(1)}, bf16[256,512]{1,0:T(8,128)(2,1)S(1)}, u32[]{:S(2)}, u32[]{:S(2)}) collective-permute-start(bf16[256,512]{1,0:T(8,128)(2,1)S(1)} %get-tuple-element.52), channel_id=1, source_target_pairs={{0,2},{2,0},{4,6},{6,4},{1,3},{3,1},{5,7},{7,5},{8,10},{10,8},{12,... | collective-permute-start | bytes 786440 | tf_op jit(solution)/shard_map/ppermute | solution.py:27
  22.9 19.6 %collective-permute-start.9 = (bf16[256,512]{1,0:T(8,128)(2,1)S(1)}, bf16[256,512]{1,0:T(8,128)(2,1)S(1)}, u32[]{:S(2)}, u32[]{:S(2)}) collective-permute-start(bf16[256,512]{1,0:T(8,128)(2,1)S(1)} %get-tuple-element.53), channel_id=1, source_target_pairs={{0,4},{2,6},{4,0},{6,2},{1,5},{3,7},{5,1},{7,3},{8,12},{10,14},{12... | collective-permute-start | bytes 786440 | tf_op jit(solution)/shard_map/ppermute | solution.py:27
  27.5 15.0 %collective-permute-start.5 = (bf16[256,512]{1,0:T(8,128)(2,1)S(1)}, bf16[256,512]{1,0:T(8,128)(2,1)S(1)}, u32[]{:S(2)}, u32[]{:S(2)}) collective-permute-start(bf16[256,512]{1,0:T(8,128)(2,1)S(1)} %get-tuple-element.47.refs_1_), channel_id=1, source_target_pairs={{0,8},{8,0},{16,24},{24,16},{1,9},{9,1},{17,25},{25,17},{2,10},{10... | collective-permute-start | bytes 786440 | tf_op jit(solution)/shard_map/ppermute | solution.py:27
  27.6 14.9 %collective-permute-start.6 = (bf16[256,512]{1,0:T(8,128)(2,1)S(1)}, bf16[256,512]{1,0:T(8,128)(2,1)S(1)}, u32[]{:S(2)}, u32[]{:S(2)}) collective-permute-start(bf16[256,512]{1,0:T(8,128)(2,1)S(1)} %get-tuple-element.48.refs_3_), channel_id=1, source_target_pairs={{0,16},{8,24},{16,0},{24,8},{1,17},{9,25},{17,1},{25,9},{2,18},{10... | collective-permute-start | bytes 786440 | tf_op jit(solution)/shard_map/ppermute | solution.py:27
  43.4 8.9 %collective-permute-start.10 = (bf16[256,512]{1,0:T(8,128)(2,1)S(1)}, bf16[256,512]{1,0:T(8,128)(2,1)S(1)}, u32[]{:S(2)}, u32[]{:S(2)}) collective-permute-start(bf16[256,512]{1,0:T(8,128)(2,1)S(1)} %get-tuple-element.55), channel_id=1, source_target_pairs={{0,16},{8,24},{16,0},{24,8},{1,17},{9,25},{17,1},{25,9},{2,18},{10... | collective-permute-start | bytes 786440 | tf_op jit(solution)/shard_map/ppermute | solution.py:27
  43.9 8.4 %collective-permute-start.11 = (bf16[256,512]{1,0:T(8,128)(2,1)S(1)}, bf16[256,512]{1,0:T(8,128)(2,1)S(1)}, u32[]{:S(2)}, u32[]{:S(2)}) collective-permute-start(bf16[256,512]{1,0:T(8,128)(2,1)S(1)} %get-tuple-element.57), channel_id=1, source_target_pairs={{0,8},{8,0},{16,24},{24,16},{1,9},{9,1},{17,25},{25,17},{2,10},{10... | collective-permute-start | bytes 786440 | tf_op jit(solution)/shard_map/ppermute | solution.py:27
  45.5 10.7 %collective-permute-start.12 = (bf16[256,512]{1,0:T(8,128)(2,1)S(1)}, bf16[256,512]{1,0:T(8,128)(2,1)S(1)}, u32[]{:S(2)}, u32[]{:S(2)}) collective-permute-start(bf16[256,512]{1,0:T(8,128)(2,1)S(1)} %get-tuple-element.65), channel_id=1, source_target_pairs={{0,6},{2,4},{4,2},{6,0},{1,7},{3,5},{5,3},{7,1},{8,14},{10,12},{12... | collective-permute-start | bytes 786440 | tf_op jit(solution)/shard_map/ppermute | solution.py:27
  54.2 1.3 %collective-permute-start.13 = (bf16[128,512]{1,0:T(8,128)(2,1)S(1)}, bf16[128,512]{1,0:T(8,128)(2,1)S(1)}, u32[]{:S(2)}, u32[]{:S(2)}) collective-permute-start(bf16[128,512]{1,0:T(8,128)(2,1)S(1)} %get-tuple-element.67), channel_id=1, source_target_pairs={{0,1},{1,0},{2,3},{3,2},{4,5},{5,4},{6,7},{7,6},{8,9},{9,8},{10,11... | collective-permute-start | bytes 393224 | tf_op jit(solution)/shard_map/ppermute | solution.py:27
  58.7 4.6 %collective-permute-start.14 = (bf16[528,512]{1,0:T(8,128)(2,1)S(1)}, bf16[528,512]{1,0:T(8,128)(2,1)S(1)}, u32[]{:S(2)}, u32[]{:S(2)}) collective-permute-start(bf16[528,512]{1,0:T(8,128)(2,1)S(1)} %get-tuple-element.71.refs_3_), channel_id=1, source_target_pairs={{0,1},{1,0},{2,3},{3,2},{4,5},{5,4},{6,7},{7,6},{8,9},{9,8},{10,11... | collective-permute-start | bytes 1622024 | tf_op jit(solution)/shard_map/ppermute | solution.py:27
  58.9 4.4 %collective-permute-start.15 = (bf16[64,512]{1,0:T(8,128)(2,1)S(1)}, bf16[64,512]{1,0:T(8,128)(2,1)S(1)}, u32[]{:S(2)}, u32[]{:S(2)}) collective-permute-start(bf16[64,512]{1,0:T(8,128)(2,1)S(1)} %get-tuple-element.72), channel_id=1, source_target_pairs={{0,2},{2,0},{4,6},{6,4},{1,3},{3,1},{5,7},{7,5},{8,10},{10,8},{12,... | collective-permute-start | bytes 196616 | tf_op jit(solution)/shard_map/ppermute | solution.py:27
  60.0 9.3 %collective-permute-start.20 = (bf16[64,512]{1,0:T(8,128)(2,1)S(1)}, bf16[64,512]{1,0:T(8,128)(2,1)S(1)}, u32[]{:S(2)}, u32[]{:S(2)}) collective-permute-start(bf16[64,512]{1,0:T(8,128)(2,1)S(1)} %get-tuple-element.83), channel_id=1, source_target_pairs={{0,4},{2,6},{4,0},{6,2},{1,5},{3,7},{5,1},{7,3},{8,12},{10,14},{12... | collective-permute-start | bytes 196616 | tf_op jit(solution)/shard_map/ppermute | solution.py:27
  62.4 6.8 %collective-permute-start.21 = (bf16[64,512]{1,0:T(8,128)(2,1)S(1)}, bf16[64,512]{1,0:T(8,128)(2,1)S(1)}, u32[]{:S(2)}, u32[]{:S(2)}) collective-permute-start(bf16[64,512]{1,0:T(8,128)(2,1)S(1)} %get-tuple-element.84), channel_id=1, source_target_pairs={{0,6},{2,4},{4,2},{6,0},{1,7},{3,5},{5,3},{7,1},{8,14},{10,12},{12... | collective-permute-start | bytes 196616 | tf_op jit(solution)/shard_map/ppermute | solution.py:27
  64.7 13.0 %collective-permute-start.16 = (bf16[144,512]{1,0:T(8,128)(2,1)S(1)}, bf16[144,512]{1,0:T(8,128)(2,1)S(1)}, u32[]{:S(2)}, u32[]{:S(2)}) collective-permute-start(bf16[144,512]{1,0:T(8,128)(2,1)S(1)} %get-tuple-element.74), channel_id=1, source_target_pairs={{0,2},{2,0},{4,6},{6,4},{1,3},{3,1},{5,7},{7,5},{8,10},{10,8},{12,... | collective-permute-start | bytes 442376 | tf_op jit(solution)/shard_map/ppermute | solution.py:27
  65.9 13.9 %collective-permute-start.17 = (bf16[144,512]{1,0:T(8,128)(2,1)S(1)}, bf16[144,512]{1,0:T(8,128)(2,1)S(1)}, u32[]{:S(2)}, u32[]{:S(2)}) collective-permute-start(bf16[144,512]{1,0:T(8,128)(2,1)S(1)} %get-tuple-element.75), channel_id=1, source_target_pairs={{0,4},{2,6},{4,0},{6,2},{1,5},{3,7},{5,1},{7,3},{8,12},{10,14},{12... | collective-permute-start | bytes 442376 | tf_op jit(solution)/shard_map/ppermute | solution.py:27
  69.2 11.1 %collective-permute-start.18 = (bf16[144,512]{1,0:T(8,128)(2,1)S(1)}, bf16[144,512]{1,0:T(8,128)(2,1)S(1)}, u32[]{:S(2)}, u32[]{:S(2)}) collective-permute-start(bf16[144,512]{1,0:T(8,128)(2,1)S(1)} %get-tuple-element.76), channel_id=1, source_target_pairs={{0,6},{2,4},{4,2},{6,0},{1,7},{3,5},{5,3},{7,1},{8,14},{10,12},{12... | collective-permute-start | bytes 442376 | tf_op jit(solution)/shard_map/ppermute | solution.py:27
  69.8 5.1 %collective-permute-start.22 = (bf16[16,4096]{1,0:T(8,128)(2,1)S(1)}, bf16[16,4096]{1,0:T(8,128)(2,1)S(1)}, u32[]{:S(2)}, u32[]{:S(2)}) collective-permute-start(bf16[16,4096]{1,0:T(8,128)(2,1)S(1)} %get-tuple-element.85.refs_0_), channel_id=1, source_target_pairs={{0,8},{8,0},{16,24},{24,16},{1,9},{9,1},{17,25},{25,17},{2,10},{10... | collective-permute-start | bytes 393224 | tf_op jit(solution)/shard_map/ppermute | solution.py:27
  70.4 5.0 %collective-permute-start.26 = (bf16[16,4096]{1,0:T(8,128)(2,1)S(1)}, bf16[16,4096]{1,0:T(8,128)(2,1)S(1)}, u32[]{:S(2)}, u32[]{:S(2)}) collective-permute-start(bf16[16,4096]{1,0:T(8,128)(2,1)S(1)} %get-tuple-element.86.refs_4_), channel_id=1, source_target_pairs={{0,16},{8,24},{16,0},{24,8},{1,17},{9,25},{17,1},{25,9},{2,18},{10... | collective-permute-start | bytes 393224 | tf_op jit(solution)/shard_map/ppermute | solution.py:27
  74.9 10.9 %collective-permute-start.23 = (bf16[16,4096]{1,0:T(8,128)(2,1)S(1)}, bf16[16,4096]{1,0:T(8,128)(2,1)S(1)}, u32[]{:S(2)}, u32[]{:S(2)}) collective-permute-start(bf16[16,4096]{1,0:T(8,128)(2,1)S(1)} %get-tuple-element.85.refs_0_), channel_id=1, source_target_pairs={{0,16},{8,24},{16,0},{24,8},{1,17},{9,25},{17,1},{25,9},{2,18},{10... | collective-permute-start | bytes 393224 | tf_op jit(solution)/shard_map/ppermute | solution.py:27
  75.5 10.3 %collective-permute-start.25 = (bf16[16,4096]{1,0:T(8,128)(2,1)S(1)}, bf16[16,4096]{1,0:T(8,128)(2,1)S(1)}, u32[]{:S(2)}, u32[]{:S(2)}) collective-permute-start(bf16[16,4096]{1,0:T(8,128)(2,1)S(1)} %get-tuple-element.86.refs_4_), channel_id=1, source_target_pairs={{0,8},{8,0},{16,24},{24,16},{1,9},{9,1},{17,25},{25,17},{2,10},{10... | collective-permute-start | bytes 393224 | tf_op jit(solution)/shard_map/ppermute | solution.py:27
  77.6 8.2 %collective-permute-start.24 = (bf16[16,4096]{1,0:T(8,128)(2,1)S(1)}, bf16[16,4096]{1,0:T(8,128)(2,1)S(1)}, u32[]{:S(2)}, u32[]{:S(2)}) collective-permute-start(bf16[16,4096]{1,0:T(8,128)(2,1)S(1)} %collective-permute-done.22.refs_1_), channel_id=1, source_target_pairs={{0,16},{8,24},{16,0},{24,8},{1,17},{9,25},{17,1},{25,9},{2,18},{10... | collective-permute-start | bytes 393224 | tf_op jit(solution)/shard_map/ppermute | solution.py:27
  79.8 6.0 %collective-permute-start.27 = (bf16[16,4096]{1,0:T(8,128)(2,1)S(1)}, bf16[16,4096]{1,0:T(8,128)(2,1)S(1)}, u32[]{:S(2)}, u32[]{:S(2)}) collective-permute-start(bf16[16,4096]{1,0:T(8,128)(2,1)S(1)} %collective-permute-done.26.refs_6_), channel_id=1, source_target_pairs={{0,8},{8,0},{16,24},{24,16},{1,9},{9,1},{17,25},{25,17},{2,10},{10... | collective-permute-start | bytes 393224 | tf_op jit(solution)/shard_map/ppermute | solution.py:27
  81.5 12.8 %collective-permute-start.19 = (bf16[128,512]{1,0:T(8,128)(2,1)S(1)}, bf16[128,512]{1,0:T(8,128)(2,1)S(1)}, u32[]{:S(2)}, u32[]{:S(2)}) collective-permute-start(bf16[128,512]{1,0:T(8,128)(2,1)S(1)} %get-tuple-element.80), channel_id=1, source_target_pairs={{0,0},{1,1},{2,8},{3,9},{4,16},{5,17},{6,24},{7,25},{8,2},{9,3},{1... | collective-permute-start | bytes 393224 | tf_op jit(solution)/shard_map/ppermute | solution.py:668
  (1 other events, 1.2 us)

commit v6 on v5

--- a/solution.py
+++ b/solution.py
@@ -472,15 +472,18 @@
 
 
 def sums_body(ids, *refs):
-    pieces, (weights, out, grads) = refs[:-3], refs[-3:]
+    pieces, (out, affinity) = refs[:-2], refs[-2:]
     whole = 0.0
     for piece in pieces:
         whole = whole + piece[...].astype(jnp.float32)
     tokens = out.shape[0]
     out[...] = whole[:tokens].astype(out.dtype)
     half = (whole.shape[0] - tokens) // 2
-    whole = whole[tokens : tokens + half] + whole[tokens + half :]
-    w = weights[...]
+    affinity[...] = whole[tokens : tokens + half] + whole[tokens + half :]
+
+
+def scores_body(ids, whole_ref, weights, grads):
+    whole, w = whole_ref[...], weights[...]
     count, lanes = w.shape
     affinity = jnp.concatenate([row_of(whole, k, lanes) for k in range(count)], axis=0)
     grads[...] = w * (affinity - jnp.sum(w * affinity, axis=0, keepdims=True))
@@ -654,11 +657,14 @@
         after=back[1:2],
     )
     grad_gate, done = gate_grads(ids, mine, others, gate_grad, sent_inputs)
-    grad_hidden, grad_scores = kernel_call(
+    grad_hidden, affinity = kernel_call(
         sums_body,
-        [shape((tokens, cols)), shape((picks, tokens), f32)],
-        ids, *swap(inputs, "pair", pairs), weights_t, after=[done],
-    )
+        [shape((tokens, cols)), shape((extra // 2, cols), f32)],
+        ids, *swap(inputs, "pair", pairs), after=[done],
+    )
+    grad_scores = kernel_call(
+        scores_body, [shape((picks, tokens), f32)], ids, affinity, weights_t
+    )[0]
     perm = [
         ((d * pairs + z) * 2 + h, (z * pairs + d) * 2 + h)
         for d in range(dp)

time: 95.3 us -> 94.8 us (level)
  waiting for transfers between devices: 16.9 us -> 15.8 us
    ppermute x1, waiting for transfers between devices: 6.03 us -> 4.88 us  [local_square(): grad_hidden = lax.ppermute(grad_hidden, ('dp',) + TABLE, perm)]
    pallas_call x13 -> x14, Pallas kernels: 18.6 us -> 19.2 us  [kernel_call(): pl.pallas_call(whole_body, in_specs=[pl.BlockSpec(memory_space=pltpu.SMEM...]
  transfers between devices with their start and end apart: 28 -> 28, of which waited for: 5 -> 5; matrix products, arithmetic and copies ran while one was open for 0% -> 0% of each run, Pallas kernels for 22% -> 23%
where the time goes in v6:
time: 94.8 us; the launch traced here: 94.5 us
  starting transfers between devices  36.8 us (39%)
  Pallas kernels  24.7 us (26%)
  waiting for transfers between devices  15.8 us (17%)
  blocking collectives  14.2 us (15%)
  local copies, waits for them, and re-layouts  1.9 us (2%)
    ppermute x23, starting transfers between devices, hop(): return lax.ppermute(x, axis, [(i, i ^ mask) for i in range(size)])  22.3 us
    pallas_call x14, Pallas kernels, kernel_call(): pl.pallas_call(whole_body, in_specs=[pl.BlockSpec(memory_space=pltpu.SMEM...  19.2 us
    all_gather x1, blocking collectives, local_square(): sent = lax.all_gather(sent_own, 'dp', axis=0)  14.2 us
    ppermute x4, starting transfers between devices, local_square(): mine.append(lax.ppermute(hidden_in, ('dp',) + TABLE, perm))  10.2 us
    ppermute x4, waiting for transfers between devices, local_square(): mine.append(lax.ppermute(hidden_in, ('dp',) + TABLE, perm))  7.31 us
    ppermute x1, waiting for transfers between devices, local_square(): grad_hidden = lax.ppermute(grad_hidden, ('dp',) + TABLE, perm)  4.88 us
    ppermute x1, starting transfers between devices, local_square(): grad_hidden = lax.ppermute(grad_hidden, ('dp',) + TABLE, perm)  4.27 us
    ppermute x23, waiting for transfers between devices, hop(): return lax.ppermute(x, axis, [(i, i ^ mask) for i in range(size)])  3.59 us
  transfers between devices with their start and end apart: 28, of which 5 were waited for; matrix products, arithmetic and copies ran while one was open for 0% of the time, Pallas kernels for 23%

profile of v6, /device:TPU:2, one launch (start us, length us, event | category | flops | bytes accessed | tf_op | source)
XLA Modules:
  0.0 94.5 jit_solution(8095608720140957171)
XLA Ops:
  0.7 4.9 %collective-permute-start = (bf16[128,512]{1,0:T(8,128)(2,1)}, bf16[128,512]{1,0:T(8,128)(2,1)S(1)}, u32[]{:S(2)}, u32[]{:S(2)}) collective-permute-start(bf16[128,512]{1,0:T(8,128)(2,1)} %param.6), channel_id=1, source_target_pairs={{0,0},{1,1},{2,8},{3,9},{4,16},{5,17},{6,24},{7,25},{8,2},{9,3},{1... | collective-permute-start | bytes 393224 | tf_op jit(solution)/shard_map/ppermute | solution.py:590
  5.6 4.4 %collective-permute-start.3 = (bf16[128,512]{1,0:T(8,128)(2,1)}, bf16[128,512]{1,0:T(8,128)(2,1)S(1)}, u32[]{:S(2)}, u32[]{:S(2)}) collective-permute-start(bf16[128,512]{1,0:T(8,128)(2,1)} %param.6), channel_id=1, source_target_pairs={{0,6},{1,7},{2,14},{3,15},{4,22},{5,23},{6,30},{7,31},{8,4},{9,5},... | collective-permute-start | bytes 393224 | tf_op jit(solution)/shard_map/ppermute | solution.py:590
  10.0 0.9 collective-permute-start.2
  11.0 1.2 %copy-done.1 = bf16[128,4096]{1,0:T(8,128)(2,1)S(1)} copy-done((bf16[128,4096]{1,0:T(8,128)(2,1)S(1)}, bf16[128,4096]{1,0:T(8,128)(2,1)}, u32[]{:S(2)}) %copy-start.1) | copy-done | bytes 1048600
  13.0 2.9 %collective-permute-done.3.refs_4_.refs_3_ = bf16[128,512]{1,0:T(8,128)(2,1)S(1)} collective-permute-done((bf16[128,512]{1,0:T(8,128)(2,1)}, bf16[128,512]{1,0:T(8,128)(2,1)S(1)}, u32[]{:S(2)}, u32[]{:S(2)}) %collective-permute-start.3) | collective-permute-done | bytes 131104 | tf_op jit(solution)/shard_map/ppermute | solution.py:590
  15.9 4.4 %collective-permute-done.2.refs_3_.refs_2_ = bf16[128,512]{1,0:T(8,128)(2,1)S(1)} collective-permute-done((bf16[128,512]{1,0:T(8,128)(2,1)}, bf16[128,512]{1,0:T(8,128)(2,1)S(1)}, u32[]{:S(2)}, u32[]{:S(2)}) %collective-permute-start.2) | collective-permute-done | bytes 131104 | tf_op jit(solution)/shard_map/ppermute | solution.py:590
  21.6 1.4 %collective-permute-start.8 = (bf16[256,512]{1,0:T(8,128)(2,1)S(1)}, bf16[256,512]{1,0:T(8,128)(2,1)S(1)}, u32[]{:S(2)}, u32[]{:S(2)}) collective-permute-start(bf16[256,512]{1,0:T(8,128)(2,1)S(1)} %get-tuple-element.52), channel_id=1, source_target_pairs={{0,2},{2,0},{4,6},{6,4},{1,3},{3,1},{5,7},{7,5},{8,10},{10,8},{12,... | collective-permute-start | bytes 786440 | tf_op jit(solution)/shard_map/ppermute | solution.py:27
  22.9 3.3 %collective-permute-start.9 = (bf16[256,512]{1,0:T(8,128)(2,1)S(1)}, bf16[256,512]{1,0:T(8,128)(2,1)S(1)}, u32[]{:S(2)}, u32[]{:S(2)}) collective-permute-start(bf16[256,512]{1,0:T(8,128)(2,1)S(1)} %get-tuple-element.53), channel_id=1, source_target_pairs={{0,4},{2,6},{4,0},{6,2},{1,5},{3,7},{5,1},{7,3},{8,12},{10,14},{12... | collective-permute-start | bytes 786440 | tf_op jit(solution)/shard_map/ppermute | solution.py:27
  26.2 1.3 %shard_map.102 = (bf16[256,512]{1,0:T(8,128)(2,1)S(1)}, bf16[256,512]{1,0:T(8,128)(2,1)S(1)}) custom-call(s32[3]{0:T(128)S(1)} %pad_add_fusion.refs_0_.ids, bf16[128,512]{1,0:T(8,128)(2,1)S(1)} %collective-permute-done.refs_1_.refs_0_, bf16[128,512]{1,0:T(8,128)(2,1)S(1)} %collective-permute-done.1.refs_2_.refs_1_, ...), custom_call_target="tpu_custom_call" | custom-call | tf_op jit(solution)/shard_map/pallas_call | solution.py:239
  28.3 14.2 %all-gather = bf16[640,512]{1,0:T(8,128)(2,1)S(1)} all-gather(bf16[160,512]{1,0:T(8,128)(2,1)S(1)} %get-tuple-element.49), channel_id=2, replica_groups=mesh['dp'=4,'pair'=4,'core'=2] {'dp'}, dimensions={0}, use_global_device_ids=true | all-gather | bytes 819200 | tf_op jit(solution)/shard_map/all_gather | solution.py:600
  42.6 0.8 shard_map.106
  43.9 1.5 %collective-permute-start.11 = (bf16[256,512]{1,0:T(8,128)(2,1)S(1)}, bf16[256,512]{1,0:T(8,128)(2,1)S(1)}, u32[]{:S(2)}, u32[]{:S(2)}) collective-permute-start(bf16[256,512]{1,0:T(8,128)(2,1)S(1)} %get-tuple-element.57), channel_id=1, source_target_pairs={{0,8},{8,0},{16,24},{24,16},{1,9},{9,1},{17,25},{25,17},{2,10},{10... | collective-permute-start | bytes 786440 | tf_op jit(solution)/shard_map/ppermute | solution.py:27
  45.5 0.9 collective-permute-start.12
  46.3 5.9 %shard_map.107 = (bf16[1024,512]{1,0:T(8,128)(2,1)S(1)}, bf16[256,512]{1,0:T(8,128)(2,1)S(1)}) custom-call(s32[3]{0:T(128)S(1)} %pad_add_fusion.refs_0_.ids, bf16[4,160,512]{2,1,0:T(8,128)(2,1)S(1)} %bitcast.8, f32[8,128]{1,0:T(8,128)S(1)} %get-tuple-element.58.refs_2_), custom_call_target="tpu_custom_call" | custom-call | tf_op jit(solution)/shard_map/pallas_call | solution.py:239
  52.3 1.9 %shard_map.108 = (bf16[512,512]{1,0:T(8,128)(2,1)S(1)}, f32[512,512]{1,0:T(8,128)S(1)}, f32[128,512]{1,0:T(8,128)S(1)}, bf16[128,512]{1,0:T(8,128)(2,1)S(1)}, bf...) custom-call(s32[3]{0:T(128)S(1)} %pad_add_fusion.refs_0_.ids, bf16[256,512]{1,0:T(8,128)(2,1)S(1)} %get-tuple-element.54.refs_1_, ...), custom_call_target="tpu_custom_call" | custom-call | tf_op jit(solution)/shard_map/pallas_call | solution.py:239
  54.2 1.3 %collective-permute-done.13.refs_2_ = bf16[128,512]{1,0:T(8,128)(2,1)S(1)} collective-permute-done((bf16[128,512]{1,0:T(8,128)(2,1)S(1)}, bf16[128,512]{1,0:T(8,128)(2,1)S(1)}, u32[]{:S(2)}, u32[]{:S(2)}) %collective-permute-start.13) | collective-permute-done | bytes 131104 | tf_op jit(solution)/shard_map/ppermute | solution.py:27
  56.2 2.6 %shard_map.110 = (bf16[512,512]{1,0:T(8,128)(2,1)S(1)}, bf16[128,512]{1,0:T(8,128)(2,1)}, bf16[528,512]{1,0:T(8,128)(2,1)S(1)}) custom-call(s32[3]{0:T(128)S(1)} %pad_add_fusion.refs_0_.ids, f32[512,512]{1,0:T(8,128)S(1)} %get-tuple-element.60.refs_1_, f32[128,512]{1,0:T(8,128)S(1)} %get-tuple-element.61.refs_2_, ...), custom_call_target="tpu_custom_call" | custom-call | tf_op jit(solution)/shard_map/pallas_call | solution.py:239
  58.9 1.1 %collective-permute-start.15 = (bf16[64,512]{1,0:T(8,128)(2,1)S(1)}, bf16[64,512]{1,0:T(8,128)(2,1)S(1)}, u32[]{:S(2)}, u32[]{:S(2)}) collective-permute-start(bf16[64,512]{1,0:T(8,128)(2,1)S(1)} %get-tuple-element.72), channel_id=1, source_target_pairs={{0,2},{2,0},{4,6},{6,4},{1,3},{3,1},{5,7},{7,5},{8,10},{10,8},{12,... | collective-permute-start | bytes 196616 | tf_op jit(solution)/shard_map/ppermute | solution.py:27
  60.0 2.4 %collective-permute-start.20 = (bf16[64,512]{1,0:T(8,128)(2,1)S(1)}, bf16[64,512]{1,0:T(8,128)(2,1)S(1)}, u32[]{:S(2)}, u32[]{:S(2)}) collective-permute-start(bf16[64,512]{1,0:T(8,128)(2,1)S(1)} %get-tuple-element.82), channel_id=1, source_target_pairs={{0,4},{2,6},{4,0},{6,2},{1,5},{3,7},{5,1},{7,3},{8,12},{10,14},{12... | collective-permute-start | bytes 196616 | tf_op jit(solution)/shard_map/ppermute | solution.py:27
  62.4 0.9 collective-permute-start.21
  63.3 1.4 %shard_map.111 = (bf16[144,512]{1,0:T(8,128)(2,1)S(1)}, bf16[144,512]{1,0:T(8,128)(2,1)S(1)}, bf16[144,512]{1,0:T(8,128)(2,1)S(1)}, bf16[144,512]{1,0:T(8,128)(2,1)S(1)}, f32[8,128]{1,0:T(8,128)S(1)}) custom-call(s32[3]{0:T(128)S(1)} %pad_add_fusion.refs_0_.ids, bf16[512,512]{1,0:T(8,128)(2,1)S(1)} %get-tuple-element.70.refs_1_.refs_5_, ...), custom_call_target="tpu_custom_call" | custom-call | tf_op jit(solution)/shard_map/pallas_call | solution.py:239
  64.7 1.2 %collective-permute-start.16 = (bf16[144,512]{1,0:T(8,128)(2,1)S(1)}, bf16[144,512]{1,0:T(8,128)(2,1)S(1)}, u32[]{:S(2)}, u32[]{:S(2)}) collective-permute-start(bf16[144,512]{1,0:T(8,128)(2,1)S(1)} %get-tuple-element.74), channel_id=1, source_target_pairs={{0,2},{2,0},{4,6},{6,4},{1,3},{3,1},{5,7},{7,5},{8,10},{10,8},{12,... | collective-permute-start | bytes 442376 | tf_op jit(solution)/shard_map/ppermute | solution.py:27
  65.9 3.3 %collective-permute-start.17 = (bf16[144,512]{1,0:T(8,128)(2,1)S(1)}, bf16[144,512]{1,0:T(8,128)(2,1)S(1)}, u32[]{:S(2)}, u32[]{:S(2)}) collective-permute-start(bf16[144,512]{1,0:T(8,128)(2,1)S(1)} %get-tuple-element.75), channel_id=1, source_target_pairs={{0,4},{2,6},{4,0},{6,2},{1,5},{3,7},{5,1},{7,3},{8,12},{10,14},{12... | collective-permute-start | bytes 442376 | tf_op jit(solution)/shard_map/ppermute | solution.py:27
  70.4 1.4 %collective-permute-start.26 = (bf16[16,4096]{1,0:T(8,128)(2,1)S(1)}, bf16[16,4096]{1,0:T(8,128)(2,1)S(1)}, u32[]{:S(2)}, u32[]{:S(2)}) collective-permute-start(bf16[16,4096]{1,0:T(8,128)(2,1)S(1)} %get-tuple-element.85.refs_4_), channel_id=1, source_target_pairs={{0,16},{8,24},{16,0},{24,8},{1,17},{9,25},{17,1},{25,9},{2,18},{10... | collective-permute-start | bytes 393224 | tf_op jit(solution)/shard_map/ppermute | solution.py:27
  71.9 3.0 %shard_map.112 = (f32[1024,512]{1,0:T(8,128)}, f32[8,128]{1,0:T(8,128)S(1)}) custom-call(s32[3]{0:T(128)S(1)} %pad_add_fusion.refs_0_.ids, bf16[128,512]{1,0:T(8,128)(2,1)S(1)} %collective-permute-done.refs_1_.refs_0_, bf16[128,512]{1,0:T(8,128)(2,1)S(1)} %collective-permute-done.1.refs_2_.refs_1_, ...), custom_call_target="tpu_custom_call" | custom-call | tf_op jit(solution)/shard_map/pallas_call | solution.py:555
  75.5 2.1 %collective-permute-start.25 = (bf16[16,4096]{1,0:T(8,128)(2,1)S(1)}, bf16[16,4096]{1,0:T(8,128)(2,1)S(1)}, u32[]{:S(2)}, u32[]{:S(2)}) collective-permute-start(bf16[16,4096]{1,0:T(8,128)(2,1)S(1)} %get-tuple-element.85.refs_4_), channel_id=1, source_target_pairs={{0,8},{8,0},{16,24},{24,16},{1,9},{9,1},{17,25},{25,17},{2,10},{10... | collective-permute-start | bytes 393224 | tf_op jit(solution)/shard_map/ppermute | solution.py:27
  77.6 2.2 %collective-permute-done.17.refs_3_ = bf16[144,512]{1,0:T(8,128)(2,1)S(1)} collective-permute-done((bf16[144,512]{1,0:T(8,128)(2,1)S(1)}, bf16[144,512]{1,0:T(8,128)(2,1)S(1)}, u32[]{:S(2)}, u32[]{:S(2)}) %collective-permute-start.17) | collective-permute-done | bytes 147488 | tf_op jit(solution)/shard_map/ppermute | solution.py:27
  81.0 4.3 %collective-permute-start.19 = (bf16[128,512]{1,0:T(8,128)(2,1)S(1)}, bf16[128,512]{1,0:T(8,128)(2,1)S(1)}, u32[]{:S(2)}, u32[]{:S(2)}) collective-permute-start(bf16[128,512]{1,0:T(8,128)(2,1)S(1)} %get-tuple-element.79), channel_id=1, source_target_pairs={{0,0},{1,1},{2,8},{3,9},{4,16},{5,17},{6,24},{7,25},{8,2},{9,3},{1... | collective-permute-start | bytes 393224 | tf_op jit(solution)/shard_map/ppermute | solution.py:674
  85.2 1.2 %shard_map.116 = f32[32,128]{1,0:T(8,128)} custom-call(s32[3]{0:T(128)S(1)} %pad_add_fusion.refs_0_.ids, f32[8,512]{1,0:T(8,128)S(1)} %get-tuple-element.87.refs_1_, f32[32,128]{1,0:T(8,128)S(1)} %get-tuple-element.88.refs_2_), custom_call_target="tpu_custom_call" | custom-call | tf_op jit(solution)/shard_map/pallas_call | solution.py:239
  86.4 2.5 %shard_map.115 = (f32[128,4096]{1,0:T(8,128)}, f32[8,128]{1,0:T(8,128)}) custom-call(s32[3]{0:T(128)S(1)} %pad_add_fusion.refs_0_.ids, bf16[16,4096]{1,0:T(8,128)(2,1)S(1)} %get-tuple-element.84.refs_0_, bf16[16,4096]{1,0:T(8,128)(2,1)S(1)} %collective-permute-done.22.refs_1_, bf16[16,4096]{1,0:T(8,128)(2,1)S(1)} %collective-permute-done.23.refs_2_, ...), custom_call_target="tpu_custom_call" | custom-call | tf_op jit(solution)/shard_map/pallas_call | solution.py:516
  88.9 4.9 %collective-permute-done.19 = bf16[128,512]{1,0:T(8,128)(2,1)S(1)} collective-permute-done((bf16[128,512]{1,0:T(8,128)(2,1)S(1)}, bf16[128,512]{1,0:T(8,128)(2,1)S(1)}, u32[]{:S(2)}, u32[]{:S(2)}) %collective-permute-start.19) | collective-permute-done | bytes 131104 | tf_op jit(solution)/shard_map/ppermute | solution.py:674
  93.8 0.7 copy.12
  (53 shorter events, 7.0 us)
Async XLA Ops:
  0.6 25.6 %copy-start = (bf16[1024,512]{1,0:T(8,128)(2,1)S(1)}, bf16[1024,512]{1,0:T(8,128)(2,1)}, u32[]{:S(2)}) copy-start(bf16[1024,512]{1,0:T(8,128)(2,1)} %refs_2_.1) | copy-start | bytes 3145732
  0.6 12.3 %collective-permute-start.1 = (bf16[128,512]{1,0:T(8,128)(2,1)}, bf16[128,512]{1,0:T(8,128)(2,1)S(1)}, u32[]{:S(2)}, u32[]{:S(2)}) collective-permute-start(bf16[128,512]{1,0:T(8,128)(2,1)} %param.6), channel_id=1, source_target_pairs={{0,2},{1,3},{2,10},{3,11},{4,18},{5,19},{6,26},{7,27},{8,0},{9,1},... | collective-permute-start | bytes 393224 | tf_op jit(solution)/shard_map/ppermute | solution.py:590
  0.7 12.2 %collective-permute-start = (bf16[128,512]{1,0:T(8,128)(2,1)}, bf16[128,512]{1,0:T(8,128)(2,1)S(1)}, u32[]{:S(2)}, u32[]{:S(2)}) collective-permute-start(bf16[128,512]{1,0:T(8,128)(2,1)} %param.6), channel_id=1, source_target_pairs={{0,0},{1,1},{2,8},{3,9},{4,16},{5,17},{6,24},{7,25},{8,2},{9,3},{1... | collective-permute-start | bytes 393224 | tf_op jit(solution)/shard_map/ppermute | solution.py:590
  5.6 10.2 %collective-permute-start.3 = (bf16[128,512]{1,0:T(8,128)(2,1)}, bf16[128,512]{1,0:T(8,128)(2,1)S(1)}, u32[]{:S(2)}, u32[]{:S(2)}) collective-permute-start(bf16[128,512]{1,0:T(8,128)(2,1)} %param.6), channel_id=1, source_target_pairs={{0,6},{1,7},{2,14},{3,15},{4,22},{5,23},{6,30},{7,31},{8,4},{9,5},... | collective-permute-start | bytes 393224 | tf_op jit(solution)/shard_map/ppermute | solution.py:590
  10.0 10.2 %collective-permute-start.2 = (bf16[128,512]{1,0:T(8,128)(2,1)}, bf16[128,512]{1,0:T(8,128)(2,1)S(1)}, u32[]{:S(2)}, u32[]{:S(2)}) collective-permute-start(bf16[128,512]{1,0:T(8,128)(2,1)} %param.6), channel_id=1, source_target_pairs={{0,4},{1,5},{2,12},{3,13},{4,20},{5,21},{6,28},{7,29},{8,6},{9,7},... | collective-permute-start | bytes 393224 | tf_op jit(solution)/shard_map/ppermute | solution.py:590
  12.8 14.9 %copy-start.2 = (bf16[128,512]{1,0:T(8,128)(2,1)S(1)}, bf16[128,512]{1,0:T(8,128)(2,1)}, u32[]{:S(2)}) copy-start(bf16[128,512]{1,0:T(8,128)(2,1)} %refs_3_.1) | copy-start | bytes 393220
  12.8 14.9 %copy-start.3 = (s32[128,32]{0,1:T(8,128)S(1)}, s32[128,32]{0,1:T(8,128)}, u32[]{:S(2)}) copy-start(s32[128,32]{0,1:T(8,128)} %param.9) | copy-start | bytes 49156
  12.8 14.8 %copy-start.4 = (f32[128,32]{0,1:T(8,128)S(1)}, f32[128,32]{0,1:T(8,128)}, u32[]{:S(2)}) copy-start(f32[128,32]{0,1:T(8,128)} %param.10) | copy-start | bytes 49156
  12.9 8.1 %collective-permute-start.7 = (bf16[512,512]{1,0:T(8,128)(2,1)S(1)}, bf16[512,512]{1,0:T(8,128)(2,1)S(1)}, u32[]{:S(2)}, u32[]{:S(2)}) collective-permute-start(bf16[512,512]{1,0:T(8,128)(2,1)S(1)} %get-tuple-element.51), channel_id=1, source_target_pairs={{0,1},{1,0},{2,3},{3,2},{4,5},{5,4},{6,7},{7,6},{8,9},{9,8},{10,11... | collective-permute-start | bytes 1572872 | tf_op jit(solution)/shard_map/ppermute | solution.py:27
  20.8 5.4 %collective-permute-start.4 = (bf16[512,512]{1,0:T(8,128)(2,1)S(1)}, bf16[512,512]{1,0:T(8,128)(2,1)S(1)}, u32[]{:S(2)}, u32[]{:S(2)}) collective-permute-start(bf16[512,512]{1,0:T(8,128)(2,1)S(1)} %shard_map.101), channel_id=1, source_target_pairs={{0,1},{1,0},{2,3},{3,2},{4,5},{5,4},{6,7},{7,6},{8,9},{9,8},{10,11... | collective-permute-start | bytes 1572872 | tf_op jit(solution)/shard_map/ppermute | solution.py:27
  21.6 21.0 %collective-permute-start.8 = (bf16[256,512]{1,0:T(8,128)(2,1)S(1)}, bf16[256,512]{1,0:T(8,128)(2,1)S(1)}, u32[]{:S(2)}, u32[]{:S(2)}) collective-permute-start(bf16[256,512]{1,0:T(8,128)(2,1)S(1)} %get-tuple-element.52), channel_id=1, source_target_pairs={{0,2},{2,0},{4,6},{6,4},{1,3},{3,1},{5,7},{7,5},{8,10},{10,8},{12,... | collective-permute-start | bytes 786440 | tf_op jit(solution)/shard_map/ppermute | solution.py:27
  22.9 19.6 %collective-permute-start.9 = (bf16[256,512]{1,0:T(8,128)(2,1)S(1)}, bf16[256,512]{1,0:T(8,128)(2,1)S(1)}, u32[]{:S(2)}, u32[]{:S(2)}) collective-permute-start(bf16[256,512]{1,0:T(8,128)(2,1)S(1)} %get-tuple-element.53), channel_id=1, source_target_pairs={{0,4},{2,6},{4,0},{6,2},{1,5},{3,7},{5,1},{7,3},{8,12},{10,14},{12... | collective-permute-start | bytes 786440 | tf_op jit(solution)/shard_map/ppermute | solution.py:27
  27.5 15.0 %collective-permute-start.5 = (bf16[256,512]{1,0:T(8,128)(2,1)S(1)}, bf16[256,512]{1,0:T(8,128)(2,1)S(1)}, u32[]{:S(2)}, u32[]{:S(2)}) collective-permute-start(bf16[256,512]{1,0:T(8,128)(2,1)S(1)} %get-tuple-element.47.refs_1_), channel_id=1, source_target_pairs={{0,8},{8,0},{16,24},{24,16},{1,9},{9,1},{17,25},{25,17},{2,10},{10... | collective-permute-start | bytes 786440 | tf_op jit(solution)/shard_map/ppermute | solution.py:27
  27.6 14.9 %collective-permute-start.6 = (bf16[256,512]{1,0:T(8,128)(2,1)S(1)}, bf16[256,512]{1,0:T(8,128)(2,1)S(1)}, u32[]{:S(2)}, u32[]{:S(2)}) collective-permute-start(bf16[256,512]{1,0:T(8,128)(2,1)S(1)} %get-tuple-element.48.refs_3_), channel_id=1, source_target_pairs={{0,16},{8,24},{16,0},{24,8},{1,17},{9,25},{17,1},{25,9},{2,18},{10... | collective-permute-start | bytes 786440 | tf_op jit(solution)/shard_map/ppermute | solution.py:27
  43.4 8.9 %collective-permute-start.10 = (bf16[256,512]{1,0:T(8,128)(2,1)S(1)}, bf16[256,512]{1,0:T(8,128)(2,1)S(1)}, u32[]{:S(2)}, u32[]{:S(2)}) collective-permute-start(bf16[256,512]{1,0:T(8,128)(2,1)S(1)} %get-tuple-element.55), channel_id=1, source_target_pairs={{0,16},{8,24},{16,0},{24,8},{1,17},{9,25},{17,1},{25,9},{2,18},{10... | collective-permute-start | bytes 786440 | tf_op jit(solution)/shard_map/ppermute | solution.py:27
  43.9 8.4 %collective-permute-start.11 = (bf16[256,512]{1,0:T(8,128)(2,1)S(1)}, bf16[256,512]{1,0:T(8,128)(2,1)S(1)}, u32[]{:S(2)}, u32[]{:S(2)}) collective-permute-start(bf16[256,512]{1,0:T(8,128)(2,1)S(1)} %get-tuple-element.57), channel_id=1, source_target_pairs={{0,8},{8,0},{16,24},{24,16},{1,9},{9,1},{17,25},{25,17},{2,10},{10... | collective-permute-start | bytes 786440 | tf_op jit(solution)/shard_map/ppermute | solution.py:27
  45.5 10.7 %collective-permute-start.12 = (bf16[256,512]{1,0:T(8,128)(2,1)S(1)}, bf16[256,512]{1,0:T(8,128)(2,1)S(1)}, u32[]{:S(2)}, u32[]{:S(2)}) collective-permute-start(bf16[256,512]{1,0:T(8,128)(2,1)S(1)} %get-tuple-element.65), channel_id=1, source_target_pairs={{0,6},{2,4},{4,2},{6,0},{1,7},{3,5},{5,3},{7,1},{8,14},{10,12},{12... | collective-permute-start | bytes 786440 | tf_op jit(solution)/shard_map/ppermute | solution.py:27
  54.2 1.3 %collective-permute-start.13 = (bf16[128,512]{1,0:T(8,128)(2,1)S(1)}, bf16[128,512]{1,0:T(8,128)(2,1)S(1)}, u32[]{:S(2)}, u32[]{:S(2)}) collective-permute-start(bf16[128,512]{1,0:T(8,128)(2,1)S(1)} %get-tuple-element.67), channel_id=1, source_target_pairs={{0,1},{1,0},{2,3},{3,2},{4,5},{5,4},{6,7},{7,6},{8,9},{9,8},{10,11... | collective-permute-start | bytes 393224 | tf_op jit(solution)/shard_map/ppermute | solution.py:27
  58.7 4.6 %collective-permute-start.14 = (bf16[528,512]{1,0:T(8,128)(2,1)S(1)}, bf16[528,512]{1,0:T(8,128)(2,1)S(1)}, u32[]{:S(2)}, u32[]{:S(2)}) collective-permute-start(bf16[528,512]{1,0:T(8,128)(2,1)S(1)} %get-tuple-element.71.refs_3_), channel_id=1, source_target_pairs={{0,1},{1,0},{2,3},{3,2},{4,5},{5,4},{6,7},{7,6},{8,9},{9,8},{10,11... | collective-permute-start | bytes 1622024 | tf_op jit(solution)/shard_map/ppermute | solution.py:27
  58.9 4.4 %collective-permute-start.15 = (bf16[64,512]{1,0:T(8,128)(2,1)S(1)}, bf16[64,512]{1,0:T(8,128)(2,1)S(1)}, u32[]{:S(2)}, u32[]{:S(2)}) collective-permute-start(bf16[64,512]{1,0:T(8,128)(2,1)S(1)} %get-tuple-element.72), channel_id=1, source_target_pairs={{0,2},{2,0},{4,6},{6,4},{1,3},{3,1},{5,7},{7,5},{8,10},{10,8},{12,... | collective-permute-start | bytes 196616 | tf_op jit(solution)/shard_map/ppermute | solution.py:27
  60.0 9.3 %collective-permute-start.20 = (bf16[64,512]{1,0:T(8,128)(2,1)S(1)}, bf16[64,512]{1,0:T(8,128)(2,1)S(1)}, u32[]{:S(2)}, u32[]{:S(2)}) collective-permute-start(bf16[64,512]{1,0:T(8,128)(2,1)S(1)} %get-tuple-element.82), channel_id=1, source_target_pairs={{0,4},{2,6},{4,0},{6,2},{1,5},{3,7},{5,1},{7,3},{8,12},{10,14},{12... | collective-permute-start | bytes 196616 | tf_op jit(solution)/shard_map/ppermute | solution.py:27
  62.4 6.8 %collective-permute-start.21 = (bf16[64,512]{1,0:T(8,128)(2,1)S(1)}, bf16[64,512]{1,0:T(8,128)(2,1)S(1)}, u32[]{:S(2)}, u32[]{:S(2)}) collective-permute-start(bf16[64,512]{1,0:T(8,128)(2,1)S(1)} %get-tuple-element.83), channel_id=1, source_target_pairs={{0,6},{2,4},{4,2},{6,0},{1,7},{3,5},{5,3},{7,1},{8,14},{10,12},{12... | collective-permute-start | bytes 196616 | tf_op jit(solution)/shard_map/ppermute | solution.py:27
  64.7 13.0 %collective-permute-start.16 = (bf16[144,512]{1,0:T(8,128)(2,1)S(1)}, bf16[144,512]{1,0:T(8,128)(2,1)S(1)}, u32[]{:S(2)}, u32[]{:S(2)}) collective-permute-start(bf16[144,512]{1,0:T(8,128)(2,1)S(1)} %get-tuple-element.74), channel_id=1, source_target_pairs={{0,2},{2,0},{4,6},{6,4},{1,3},{3,1},{5,7},{7,5},{8,10},{10,8},{12,... | collective-permute-start | bytes 442376 | tf_op jit(solution)/shard_map/ppermute | solution.py:27
  65.9 13.9 %collective-permute-start.17 = (bf16[144,512]{1,0:T(8,128)(2,1)S(1)}, bf16[144,512]{1,0:T(8,128)(2,1)S(1)}, u32[]{:S(2)}, u32[]{:S(2)}) collective-permute-start(bf16[144,512]{1,0:T(8,128)(2,1)S(1)} %get-tuple-element.75), channel_id=1, source_target_pairs={{0,4},{2,6},{4,0},{6,2},{1,5},{3,7},{5,1},{7,3},{8,12},{10,14},{12... | collective-permute-start | bytes 442376 | tf_op jit(solution)/shard_map/ppermute | solution.py:27
  69.2 11.1 %collective-permute-start.18 = (bf16[144,512]{1,0:T(8,128)(2,1)S(1)}, bf16[144,512]{1,0:T(8,128)(2,1)S(1)}, u32[]{:S(2)}, u32[]{:S(2)}) collective-permute-start(bf16[144,512]{1,0:T(8,128)(2,1)S(1)} %get-tuple-element.76), channel_id=1, source_target_pairs={{0,6},{2,4},{4,2},{6,0},{1,7},{3,5},{5,3},{7,1},{8,14},{10,12},{12... | collective-permute-start | bytes 442376 | tf_op jit(solution)/shard_map/ppermute | solution.py:27
  69.8 5.1 %collective-permute-start.22 = (bf16[16,4096]{1,0:T(8,128)(2,1)S(1)}, bf16[16,4096]{1,0:T(8,128)(2,1)S(1)}, u32[]{:S(2)}, u32[]{:S(2)}) collective-permute-start(bf16[16,4096]{1,0:T(8,128)(2,1)S(1)} %get-tuple-element.84.refs_0_), channel_id=1, source_target_pairs={{0,8},{8,0},{16,24},{24,16},{1,9},{9,1},{17,25},{25,17},{2,10},{10... | collective-permute-start | bytes 393224 | tf_op jit(solution)/shard_map/ppermute | solution.py:27
  70.4 5.0 %collective-permute-start.26 = (bf16[16,4096]{1,0:T(8,128)(2,1)S(1)}, bf16[16,4096]{1,0:T(8,128)(2,1)S(1)}, u32[]{:S(2)}, u32[]{:S(2)}) collective-permute-start(bf16[16,4096]{1,0:T(8,128)(2,1)S(1)} %get-tuple-element.85.refs_4_), channel_id=1, source_target_pairs={{0,16},{8,24},{16,0},{24,8},{1,17},{9,25},{17,1},{25,9},{2,18},{10... | collective-permute-start | bytes 393224 | tf_op jit(solution)/shard_map/ppermute | solution.py:27
  74.9 11.5 %collective-permute-start.23 = (bf16[16,4096]{1,0:T(8,128)(2,1)S(1)}, bf16[16,4096]{1,0:T(8,128)(2,1)S(1)}, u32[]{:S(2)}, u32[]{:S(2)}) collective-permute-start(bf16[16,4096]{1,0:T(8,128)(2,1)S(1)} %get-tuple-element.84.refs_0_), channel_id=1, source_target_pairs={{0,16},{8,24},{16,0},{24,8},{1,17},{9,25},{17,1},{25,9},{2,18},{10... | collective-permute-start | bytes 393224 | tf_op jit(solution)/shard_map/ppermute | solution.py:27
  75.5 10.9 %collective-permute-start.25 = (bf16[16,4096]{1,0:T(8,128)(2,1)S(1)}, bf16[16,4096]{1,0:T(8,128)(2,1)S(1)}, u32[]{:S(2)}, u32[]{:S(2)}) collective-permute-start(bf16[16,4096]{1,0:T(8,128)(2,1)S(1)} %get-tuple-element.85.refs_4_), channel_id=1, source_target_pairs={{0,8},{8,0},{16,24},{24,16},{1,9},{9,1},{17,25},{25,17},{2,10},{10... | collective-permute-start | bytes 393224 | tf_op jit(solution)/shard_map/ppermute | solution.py:27
  77.6 8.8 %collective-permute-start.24 = (bf16[16,4096]{1,0:T(8,128)(2,1)S(1)}, bf16[16,4096]{1,0:T(8,128)(2,1)S(1)}, u32[]{:S(2)}, u32[]{:S(2)}) collective-permute-start(bf16[16,4096]{1,0:T(8,128)(2,1)S(1)} %collective-permute-done.22.refs_1_), channel_id=1, source_target_pairs={{0,16},{8,24},{16,0},{24,8},{1,17},{9,25},{17,1},{25,9},{2,18},{10... | collective-permute-start | bytes 393224 | tf_op jit(solution)/shard_map/ppermute | solution.py:27
  79.8 6.6 %collective-permute-start.27 = (bf16[16,4096]{1,0:T(8,128)(2,1)S(1)}, bf16[16,4096]{1,0:T(8,128)(2,1)S(1)}, u32[]{:S(2)}, u32[]{:S(2)}) collective-permute-start(bf16[16,4096]{1,0:T(8,128)(2,1)S(1)} %collective-permute-done.26.refs_6_), channel_id=1, source_target_pairs={{0,8},{8,0},{16,24},{24,16},{1,9},{9,1},{17,25},{25,17},{2,10},{10... | collective-permute-start | bytes 393224 | tf_op jit(solution)/shard_map/ppermute | solution.py:27
  81.0 12.9 %collective-permute-start.19 = (bf16[128,512]{1,0:T(8,128)(2,1)S(1)}, bf16[128,512]{1,0:T(8,128)(2,1)S(1)}, u32[]{:S(2)}, u32[]{:S(2)}) collective-permute-start(bf16[128,512]{1,0:T(8,128)(2,1)S(1)} %get-tuple-element.79), channel_id=1, source_target_pairs={{0,0},{1,1},{2,8},{3,9},{4,16},{5,17},{6,24},{7,25},{8,2},{9,3},{1... | collective-permute-start | bytes 393224 | tf_op jit(solution)/shard_map/ppermute | solution.py:674
  (1 other events, 1.2 us)

commit v7 on v6

--- a/solution.py
+++ b/solution.py
@@ -308,7 +308,7 @@
             high, low = row_of(packed, picks + k, tokens), row_of(packed, 2 * picks + k, tokens)
             rows[k : k + 1, span] = (high * 32.0 + low).astype(jnp.int32)
     rows[...] = moved(rows[...], rows_here, pair, core)
-    tile = 32
+    tile = 64
 
     def step(i, carry):
         base = pl.multiple_of(i * tile, tile)

time: 94.8 us -> 93.9 us (level)
    ppermute x1, waiting for transfers between devices: 4.88 us -> 3.84 us  [local_square(): grad_hidden = lax.ppermute(grad_hidden, ('dp',) + TABLE, perm)]
  transfers between devices with their start and end apart: 28 -> 28, of which waited for: 5 -> 6; matrix products, arithmetic and copies ran while one was open for 0% -> 0% of each run, Pallas kernels for 23% -> 23%
where the time goes in v7:
time: 93.9 us; the launch traced here: 93.7 us
  starting transfers between devices  36.4 us (39%)
  Pallas kernels  25.1 us (27%)
  waiting for transfers between devices  15.1 us (16%)
  blocking collectives  14.2 us (15%)
  local copies, waits for them, and re-layouts  1.9 us (2%)
    ppermute x23, starting transfers between devices, hop(): return lax.ppermute(x, axis, [(i, i ^ mask) for i in range(size)])  22.3 us
    pallas_call x14, Pallas kernels, kernel_call(): pl.pallas_call(whole_body, in_specs=[pl.BlockSpec(memory_space=pltpu.SMEM...  19.6 us
    all_gather x1, blocking collectives, local_square(): sent = lax.all_gather(sent_own, 'dp', axis=0)  14.2 us
    ppermute x4, starting transfers between devices, local_square(): mine.append(lax.ppermute(hidden_in, ('dp',) + TABLE, perm))  10.2 us
    ppermute x4, waiting for transfers between devices, local_square(): mine.append(lax.ppermute(hidden_in, ('dp',) + TABLE, perm))  7.31 us
    ppermute x23, waiting for transfers between devices, hop(): return lax.ppermute(x, axis, [(i, i ^ mask) for i in range(size)])  3.9 us
    ppermute x1, starting transfers between devices, local_square(): grad_hidden = lax.ppermute(grad_hidden, ('dp',) + TABLE, perm)  3.86 us
    ppermute x1, waiting for transfers between devices, local_square(): grad_hidden = lax.ppermute(grad_hidden, ('dp',) + TABLE, perm)  3.84 us
  transfers between devices with their start and end apart: 28, of which 6 were waited for; matrix products, arithmetic and copies ran while one was open for 0% of the time, Pallas kernels for 23%

profile of v7, /device:TPU:2, one launch (start us, length us, event | category | flops | bytes accessed | tf_op | source)
XLA Modules:
  0.0 93.7 jit_solution(18128901897886046897)
XLA Ops:
  0.7 4.9 %collective-permute-start = (bf16[128,512]{1,0:T(8,128)(2,1)}, bf16[128,512]{1,0:T(8,128)(2,1)S(1)}, u32[]{:S(2)}, u32[]{:S(2)}) collective-permute-start(bf16[128,512]{1,0:T(8,128)(2,1)} %param.6), channel_id=1, source_target_pairs={{0,0},{1,1},{2,8},{3,9},{4,16},{5,17},{6,24},{7,25},{8,2},{9,3},{1... | collective-permute-start | bytes 393224 | tf_op jit(solution)/shard_map/ppermute | solution.py:590
  5.6 4.4 %collective-permute-start.3 = (bf16[128,512]{1,0:T(8,128)(2,1)}, bf16[128,512]{1,0:T(8,128)(2,1)S(1)}, u32[]{:S(2)}, u32[]{:S(2)}) collective-permute-start(bf16[128,512]{1,0:T(8,128)(2,1)} %param.6), channel_id=1, source_target_pairs={{0,6},{1,7},{2,14},{3,15},{4,22},{5,23},{6,30},{7,31},{8,4},{9,5},... | collective-permute-start | bytes 393224 | tf_op jit(solution)/shard_map/ppermute | solution.py:590
  10.0 0.9 collective-permute-start.2
  11.0 1.2 %copy-done.1 = bf16[128,4096]{1,0:T(8,128)(2,1)S(1)} copy-done((bf16[128,4096]{1,0:T(8,128)(2,1)S(1)}, bf16[128,4096]{1,0:T(8,128)(2,1)}, u32[]{:S(2)}) %copy-start.1) | copy-done | bytes 1048600
  13.0 2.9 %collective-permute-done.3.refs_4_.refs_3_ = bf16[128,512]{1,0:T(8,128)(2,1)S(1)} collective-permute-done((bf16[128,512]{1,0:T(8,128)(2,1)}, bf16[128,512]{1,0:T(8,128)(2,1)S(1)}, u32[]{:S(2)}, u32[]{:S(2)}) %collective-permute-start.3) | collective-permute-done | bytes 131104 | tf_op jit(solution)/shard_map/ppermute | solution.py:590
  15.9 4.4 %collective-permute-done.2.refs_3_.refs_2_ = bf16[128,512]{1,0:T(8,128)(2,1)S(1)} collective-permute-done((bf16[128,512]{1,0:T(8,128)(2,1)}, bf16[128,512]{1,0:T(8,128)(2,1)S(1)}, u32[]{:S(2)}, u32[]{:S(2)}) %collective-permute-start.2) | collective-permute-done | bytes 131104 | tf_op jit(solution)/shard_map/ppermute | solution.py:590
  21.6 1.4 %collective-permute-start.8 = (bf16[256,512]{1,0:T(8,128)(2,1)S(1)}, bf16[256,512]{1,0:T(8,128)(2,1)S(1)}, u32[]{:S(2)}, u32[]{:S(2)}) collective-permute-start(bf16[256,512]{1,0:T(8,128)(2,1)S(1)} %get-tuple-element.52), channel_id=1, source_target_pairs={{0,2},{2,0},{4,6},{6,4},{1,3},{3,1},{5,7},{7,5},{8,10},{10,8},{12,... | collective-permute-start | bytes 786440 | tf_op jit(solution)/shard_map/ppermute | solution.py:27
  22.9 3.3 %collective-permute-start.9 = (bf16[256,512]{1,0:T(8,128)(2,1)S(1)}, bf16[256,512]{1,0:T(8,128)(2,1)S(1)}, u32[]{:S(2)}, u32[]{:S(2)}) collective-permute-start(bf16[256,512]{1,0:T(8,128)(2,1)S(1)} %get-tuple-element.53), channel_id=1, source_target_pairs={{0,4},{2,6},{4,0},{6,2},{1,5},{3,7},{5,1},{7,3},{8,12},{10,14},{12... | collective-permute-start | bytes 786440 | tf_op jit(solution)/shard_map/ppermute | solution.py:27
  26.2 1.3 %shard_map.102 = (bf16[256,512]{1,0:T(8,128)(2,1)S(1)}, bf16[256,512]{1,0:T(8,128)(2,1)S(1)}) custom-call(s32[3]{0:T(128)S(1)} %pad_add_fusion.refs_0_.ids, bf16[128,512]{1,0:T(8,128)(2,1)S(1)} %collective-permute-done.refs_1_.refs_0_, bf16[128,512]{1,0:T(8,128)(2,1)S(1)} %collective-permute-done.1.refs_2_.refs_1_, ...), custom_call_target="tpu_custom_call" | custom-call | tf_op jit(solution)/shard_map/pallas_call | solution.py:239
  28.3 14.2 %all-gather = bf16[640,512]{1,0:T(8,128)(2,1)S(1)} all-gather(bf16[160,512]{1,0:T(8,128)(2,1)S(1)} %get-tuple-element.49), channel_id=2, replica_groups=mesh['dp'=4,'pair'=4,'core'=2] {'dp'}, dimensions={0}, use_global_device_ids=true | all-gather | bytes 819200 | tf_op jit(solution)/shard_map/all_gather | solution.py:600
  42.6 0.8 shard_map.106
  43.9 1.5 %collective-permute-start.11 = (bf16[256,512]{1,0:T(8,128)(2,1)S(1)}, bf16[256,512]{1,0:T(8,128)(2,1)S(1)}, u32[]{:S(2)}, u32[]{:S(2)}) collective-permute-start(bf16[256,512]{1,0:T(8,128)(2,1)S(1)} %get-tuple-element.57), channel_id=1, source_target_pairs={{0,8},{8,0},{16,24},{24,16},{1,9},{9,1},{17,25},{25,17},{2,10},{10... | collective-permute-start | bytes 786440 | tf_op jit(solution)/shard_map/ppermute | solution.py:27
  45.5 0.9 collective-permute-start.12
  46.3 6.3 %shard_map.107 = (bf16[1024,512]{1,0:T(8,128)(2,1)S(1)}, bf16[256,512]{1,0:T(8,128)(2,1)S(1)}) custom-call(s32[3]{0:T(128)S(1)} %pad_add_fusion.refs_0_.ids, bf16[4,160,512]{2,1,0:T(8,128)(2,1)S(1)} %bitcast.8, f32[8,128]{1,0:T(8,128)S(1)} %get-tuple-element.58.refs_2_), custom_call_target="tpu_custom_call" | custom-call | tf_op jit(solution)/shard_map/pallas_call | solution.py:239
  52.7 1.9 %shard_map.108 = (bf16[512,512]{1,0:T(8,128)(2,1)S(1)}, f32[512,512]{1,0:T(8,128)S(1)}, f32[128,512]{1,0:T(8,128)S(1)}, bf16[128,512]{1,0:T(8,128)(2,1)S(1)}, bf...) custom-call(s32[3]{0:T(128)S(1)} %pad_add_fusion.refs_0_.ids, bf16[256,512]{1,0:T(8,128)(2,1)S(1)} %get-tuple-element.54.refs_1_, ...), custom_call_target="tpu_custom_call" | custom-call | tf_op jit(solution)/shard_map/pallas_call | solution.py:239
  54.6 1.3 %collective-permute-done.13.refs_2_ = bf16[128,512]{1,0:T(8,128)(2,1)S(1)} collective-permute-done((bf16[128,512]{1,0:T(8,128)(2,1)S(1)}, bf16[128,512]{1,0:T(8,128)(2,1)S(1)}, u32[]{:S(2)}, u32[]{:S(2)}) %collective-permute-start.13) | collective-permute-done | bytes 131104 | tf_op jit(solution)/shard_map/ppermute | solution.py:27
  56.6 2.6 %shard_map.110 = (bf16[512,512]{1,0:T(8,128)(2,1)S(1)}, bf16[128,512]{1,0:T(8,128)(2,1)}, bf16[528,512]{1,0:T(8,128)(2,1)S(1)}) custom-call(s32[3]{0:T(128)S(1)} %pad_add_fusion.refs_0_.ids, f32[512,512]{1,0:T(8,128)S(1)} %get-tuple-element.60.refs_1_, f32[128,512]{1,0:T(8,128)S(1)} %get-tuple-element.61.refs_2_, ...), custom_call_target="tpu_custom_call" | custom-call | tf_op jit(solution)/shard_map/pallas_call | solution.py:239
  59.3 0.7 collective-permute-start.15
  60.0 2.8 %collective-permute-start.20 = (bf16[64,512]{1,0:T(8,128)(2,1)S(1)}, bf16[64,512]{1,0:T(8,128)(2,1)S(1)}, u32[]{:S(2)}, u32[]{:S(2)}) collective-permute-start(bf16[64,512]{1,0:T(8,128)(2,1)S(1)} %get-tuple-element.82), channel_id=1, source_target_pairs={{0,4},{2,6},{4,0},{6,2},{1,5},{3,7},{5,1},{7,3},{8,12},{10,14},{12... | collective-permute-start | bytes 196616 | tf_op jit(solution)/shard_map/ppermute | solution.py:27
  62.8 0.9 collective-permute-start.21
  63.7 1.4 %shard_map.111 = (bf16[144,512]{1,0:T(8,128)(2,1)S(1)}, bf16[144,512]{1,0:T(8,128)(2,1)S(1)}, bf16[144,512]{1,0:T(8,128)(2,1)S(1)}, bf16[144,512]{1,0:T(8,128)(2,1)S(1)}, f32[8,128]{1,0:T(8,128)S(1)}) custom-call(s32[3]{0:T(128)S(1)} %pad_add_fusion.refs_0_.ids, bf16[512,512]{1,0:T(8,128)(2,1)S(1)} %get-tuple-element.70.refs_1_.refs_5_, ...), custom_call_target="tpu_custom_call" | custom-call | tf_op jit(solution)/shard_map/pallas_call | solution.py:239
  65.1 0.8 collective-permute-start.16
  65.9 3.7 %collective-permute-start.17 = (bf16[144,512]{1,0:T(8,128)(2,1)S(1)}, bf16[144,512]{1,0:T(8,128)(2,1)S(1)}, u32[]{:S(2)}, u32[]{:S(2)}) collective-permute-start(bf16[144,512]{1,0:T(8,128)(2,1)S(1)} %get-tuple-element.75), channel_id=1, source_target_pairs={{0,4},{2,6},{4,0},{6,2},{1,5},{3,7},{5,1},{7,3},{8,12},{10,14},{12... | collective-permute-start | bytes 442376 | tf_op jit(solution)/shard_map/ppermute | solution.py:27
  70.9 1.4 %collective-permute-start.26 = (bf16[16,4096]{1,0:T(8,128)(2,1)S(1)}, bf16[16,4096]{1,0:T(8,128)(2,1)S(1)}, u32[]{:S(2)}, u32[]{:S(2)}) collective-permute-start(bf16[16,4096]{1,0:T(8,128)(2,1)S(1)} %get-tuple-element.85.refs_4_), channel_id=1, source_target_pairs={{0,16},{8,24},{16,0},{24,8},{1,17},{9,25},{17,1},{25,9},{2,18},{10... | collective-permute-start | bytes 393224 | tf_op jit(solution)/shard_map/ppermute | solution.py:27
  72.3 3.0 %shard_map.112 = (f32[1024,512]{1,0:T(8,128)}, f32[8,128]{1,0:T(8,128)S(1)}) custom-call(s32[3]{0:T(128)S(1)} %pad_add_fusion.refs_0_.ids, bf16[128,512]{1,0:T(8,128)(2,1)S(1)} %collective-permute-done.refs_1_.refs_0_, bf16[128,512]{1,0:T(8,128)(2,1)S(1)} %collective-permute-done.1.refs_2_.refs_1_, ...), custom_call_target="tpu_custom_call" | custom-call | tf_op jit(solution)/shard_map/pallas_call | solution.py:555
  75.9 2.1 %collective-permute-start.25 = (bf16[16,4096]{1,0:T(8,128)(2,1)S(1)}, bf16[16,4096]{1,0:T(8,128)(2,1)S(1)}, u32[]{:S(2)}, u32[]{:S(2)}) collective-permute-start(bf16[16,4096]{1,0:T(8,128)(2,1)S(1)} %get-tuple-element.85.refs_4_), channel_id=1, source_target_pairs={{0,8},{8,0},{16,24},{24,16},{1,9},{9,1},{17,25},{25,17},{2,10},{10... | collective-permute-start | bytes 393224 | tf_op jit(solution)/shard_map/ppermute | solution.py:27
  78.1 2.2 %collective-permute-done.17.refs_3_ = bf16[144,512]{1,0:T(8,128)(2,1)S(1)} collective-permute-done((bf16[144,512]{1,0:T(8,128)(2,1)S(1)}, bf16[144,512]{1,0:T(8,128)(2,1)S(1)}, u32[]{:S(2)}, u32[]{:S(2)}) %collective-permute-start.17) | collective-permute-done | bytes 147488 | tf_op jit(solution)/shard_map/ppermute | solution.py:27
  81.4 3.9 %collective-permute-start.19 = (bf16[128,512]{1,0:T(8,128)(2,1)S(1)}, bf16[128,512]{1,0:T(8,128)(2,1)S(1)}, u32[]{:S(2)}, u32[]{:S(2)}) collective-permute-start(bf16[128,512]{1,0:T(8,128)(2,1)S(1)} %get-tuple-element.79), channel_id=1, source_target_pairs={{0,0},{1,1},{2,8},{3,9},{4,16},{5,17},{6,24},{7,25},{8,2},{9,3},{1... | collective-permute-start | bytes 393224 | tf_op jit(solution)/shard_map/ppermute | solution.py:674
  85.2 1.2 %shard_map.116 = f32[32,128]{1,0:T(8,128)} custom-call(s32[3]{0:T(128)S(1)} %pad_add_fusion.refs_0_.ids, f32[8,512]{1,0:T(8,128)S(1)} %get-tuple-element.87.refs_1_, f32[32,128]{1,0:T(8,128)S(1)} %get-tuple-element.88.refs_2_), custom_call_target="tpu_custom_call" | custom-call | tf_op jit(solution)/shard_map/pallas_call | solution.py:239
  86.7 2.5 %shard_map.115 = (f32[128,4096]{1,0:T(8,128)}, f32[8,128]{1,0:T(8,128)}) custom-call(s32[3]{0:T(128)S(1)} %pad_add_fusion.refs_0_.ids, bf16[16,4096]{1,0:T(8,128)(2,1)S(1)} %get-tuple-element.84.refs_0_, bf16[16,4096]{1,0:T(8,128)(2,1)S(1)} %collective-permute-done.22.refs_1_, bf16[16,4096]{1,0:T(8,128)(2,1)S(1)} %collective-permute-done.23.refs_2_, ...), custom_call_target="tpu_custom_call" | custom-call | tf_op jit(solution)/shard_map/pallas_call | solution.py:516
  89.2 3.8 %collective-permute-done.19 = bf16[128,512]{1,0:T(8,128)(2,1)S(1)} collective-permute-done((bf16[128,512]{1,0:T(8,128)(2,1)S(1)}, bf16[128,512]{1,0:T(8,128)(2,1)S(1)}, u32[]{:S(2)}, u32[]{:S(2)}) %collective-permute-start.19) | collective-permute-done | bytes 131104 | tf_op jit(solution)/shard_map/ppermute | solution.py:674
  93.0 0.7 copy.12
  (53 shorter events, 7.3 us)
Async XLA Ops:
  0.6 25.6 %copy-start = (bf16[1024,512]{1,0:T(8,128)(2,1)S(1)}, bf16[1024,512]{1,0:T(8,128)(2,1)}, u32[]{:S(2)}) copy-start(bf16[1024,512]{1,0:T(8,128)(2,1)} %refs_2_.1) | copy-start | bytes 3145732
  0.6 12.3 %collective-permute-start.1 = (bf16[128,512]{1,0:T(8,128)(2,1)}, bf16[128,512]{1,0:T(8,128)(2,1)S(1)}, u32[]{:S(2)}, u32[]{:S(2)}) collective-permute-start(bf16[128,512]{1,0:T(8,128)(2,1)} %param.6), channel_id=1, source_target_pairs={{0,2},{1,3},{2,10},{3,11},{4,18},{5,19},{6,26},{7,27},{8,0},{9,1},... | collective-permute-start | bytes 393224 | tf_op jit(solution)/shard_map/ppermute | solution.py:590
  0.7 12.2 %collective-permute-start = (bf16[128,512]{1,0:T(8,128)(2,1)}, bf16[128,512]{1,0:T(8,128)(2,1)S(1)}, u32[]{:S(2)}, u32[]{:S(2)}) collective-permute-start(bf16[128,512]{1,0:T(8,128)(2,1)} %param.6), channel_id=1, source_target_pairs={{0,0},{1,1},{2,8},{3,9},{4,16},{5,17},{6,24},{7,25},{8,2},{9,3},{1... | collective-permute-start | bytes 393224 | tf_op jit(solution)/shard_map/ppermute | solution.py:590
  5.6 10.2 %collective-permute-start.3 = (bf16[128,512]{1,0:T(8,128)(2,1)}, bf16[128,512]{1,0:T(8,128)(2,1)S(1)}, u32[]{:S(2)}, u32[]{:S(2)}) collective-permute-start(bf16[128,512]{1,0:T(8,128)(2,1)} %param.6), channel_id=1, source_target_pairs={{0,6},{1,7},{2,14},{3,15},{4,22},{5,23},{6,30},{7,31},{8,4},{9,5},... | collective-permute-start | bytes 393224 | tf_op jit(solution)/shard_map/ppermute | solution.py:590
  10.0 10.2 %collective-permute-start.2 = (bf16[128,512]{1,0:T(8,128)(2,1)}, bf16[128,512]{1,0:T(8,128)(2,1)S(1)}, u32[]{:S(2)}, u32[]{:S(2)}) collective-permute-start(bf16[128,512]{1,0:T(8,128)(2,1)} %param.6), channel_id=1, source_target_pairs={{0,4},{1,5},{2,12},{3,13},{4,20},{5,21},{6,28},{7,29},{8,6},{9,7},... | collective-permute-start | bytes 393224 | tf_op jit(solution)/shard_map/ppermute | solution.py:590
  12.8 14.9 %copy-start.2 = (bf16[128,512]{1,0:T(8,128)(2,1)S(1)}, bf16[128,512]{1,0:T(8,128)(2,1)}, u32[]{:S(2)}) copy-start(bf16[128,512]{1,0:T(8,128)(2,1)} %refs_3_.1) | copy-start | bytes 393220
  12.8 14.9 %copy-start.3 = (s32[128,32]{0,1:T(8,128)S(1)}, s32[128,32]{0,1:T(8,128)}, u32[]{:S(2)}) copy-start(s32[128,32]{0,1:T(8,128)} %param.9) | copy-start | bytes 49156
  12.8 14.8 %copy-start.4 = (f32[128,32]{0,1:T(8,128)S(1)}, f32[128,32]{0,1:T(8,128)}, u32[]{:S(2)}) copy-start(f32[128,32]{0,1:T(8,128)} %param.10) | copy-start | bytes 49156
  12.9 8.1 %collective-permute-start.7 = (bf16[512,512]{1,0:T(8,128)(2,1)S(1)}, bf16[512,512]{1,0:T(8,128)(2,1)S(1)}, u32[]{:S(2)}, u32[]{:S(2)}) collective-permute-start(bf16[512,512]{1,0:T(8,128)(2,1)S(1)} %get-tuple-element.51), channel_id=1, source_target_pairs={{0,1},{1,0},{2,3},{3,2},{4,5},{5,4},{6,7},{7,6},{8,9},{9,8},{10,11... | collective-permute-start | bytes 1572872 | tf_op jit(solution)/shard_map/ppermute | solution.py:27
  20.8 5.4 %collective-permute-start.4 = (bf16[512,512]{1,0:T(8,128)(2,1)S(1)}, bf16[512,512]{1,0:T(8,128)(2,1)S(1)}, u32[]{:S(2)}, u32[]{:S(2)}) collective-permute-start(bf16[512,512]{1,0:T(8,128)(2,1)S(1)} %shard_map.101), channel_id=1, source_target_pairs={{0,1},{1,0},{2,3},{3,2},{4,5},{5,4},{6,7},{7,6},{8,9},{9,8},{10,11... | collective-permute-start | bytes 1572872 | tf_op jit(solution)/shard_map/ppermute | solution.py:27
  21.6 21.0 %collective-permute-start.8 = (bf16[256,512]{1,0:T(8,128)(2,1)S(1)}, bf16[256,512]{1,0:T(8,128)(2,1)S(1)}, u32[]{:S(2)}, u32[]{:S(2)}) collective-permute-start(bf16[256,512]{1,0:T(8,128)(2,1)S(1)} %get-tuple-element.52), channel_id=1, source_target_pairs={{0,2},{2,0},{4,6},{6,4},{1,3},{3,1},{5,7},{7,5},{8,10},{10,8},{12,... | collective-permute-start | bytes 786440 | tf_op jit(solution)/shard_map/ppermute | solution.py:27
  22.9 19.6 %collective-permute-start.9 = (bf16[256,512]{1,0:T(8,128)(2,1)S(1)}, bf16[256,512]{1,0:T(8,128)(2,1)S(1)}, u32[]{:S(2)}, u32[]{:S(2)}) collective-permute-start(bf16[256,512]{1,0:T(8,128)(2,1)S(1)} %get-tuple-element.53), channel_id=1, source_target_pairs={{0,4},{2,6},{4,0},{6,2},{1,5},{3,7},{5,1},{7,3},{8,12},{10,14},{12... | collective-permute-start | bytes 786440 | tf_op jit(solution)/shard_map/ppermute | solution.py:27
  27.5 15.0 %collective-permute-start.5 = (bf16[256,512]{1,0:T(8,128)(2,1)S(1)}, bf16[256,512]{1,0:T(8,128)(2,1)S(1)}, u32[]{:S(2)}, u32[]{:S(2)}) collective-permute-start(bf16[256,512]{1,0:T(8,128)(2,1)S(1)} %get-tuple-element.47.refs_1_), channel_id=1, source_target_pairs={{0,8},{8,0},{16,24},{24,16},{1,9},{9,1},{17,25},{25,17},{2,10},{10... | collective-permute-start | bytes 786440 | tf_op jit(solution)/shard_map/ppermute | solution.py:27
  27.6 14.9 %collective-permute-start.6 = (bf16[256,512]{1,0:T(8,128)(2,1)S(1)}, bf16[256,512]{1,0:T(8,128)(2,1)S(1)}, u32[]{:S(2)}, u32[]{:S(2)}) collective-permute-start(bf16[256,512]{1,0:T(8,128)(2,1)S(1)} %get-tuple-element.48.refs_3_), channel_id=1, source_target_pairs={{0,16},{8,24},{16,0},{24,8},{1,17},{9,25},{17,1},{25,9},{2,18},{10... | collective-permute-start | bytes 786440 | tf_op jit(solution)/shard_map/ppermute | solution.py:27
  43.4 9.3 %collective-permute-start.10 = (bf16[256,512]{1,0:T(8,128)(2,1)S(1)}, bf16[256,512]{1,0:T(8,128)(2,1)S(1)}, u32[]{:S(2)}, u32[]{:S(2)}) collective-permute-start(bf16[256,512]{1,0:T(8,128)(2,1)S(1)} %get-tuple-element.55), channel_id=1, source_target_pairs={{0,16},{8,24},{16,0},{24,8},{1,17},{9,25},{17,1},{25,9},{2,18},{10... | collective-permute-start | bytes 786440 | tf_op jit(solution)/shard_map/ppermute | solution.py:27
  43.9 8.8 %collective-permute-start.11 = (bf16[256,512]{1,0:T(8,128)(2,1)S(1)}, bf16[256,512]{1,0:T(8,128)(2,1)S(1)}, u32[]{:S(2)}, u32[]{:S(2)}) collective-permute-start(bf16[256,512]{1,0:T(8,128)(2,1)S(1)} %get-tuple-element.57), channel_id=1, source_target_pairs={{0,8},{8,0},{16,24},{24,16},{1,9},{9,1},{17,25},{25,17},{2,10},{10... | collective-permute-start | bytes 786440 | tf_op jit(solution)/shard_map/ppermute | solution.py:27
  45.5 11.1 %collective-permute-start.12 = (bf16[256,512]{1,0:T(8,128)(2,1)S(1)}, bf16[256,512]{1,0:T(8,128)(2,1)S(1)}, u32[]{:S(2)}, u32[]{:S(2)}) collective-permute-start(bf16[256,512]{1,0:T(8,128)(2,1)S(1)} %get-tuple-element.65), channel_id=1, source_target_pairs={{0,6},{2,4},{4,2},{6,0},{1,7},{3,5},{5,3},{7,1},{8,14},{10,12},{12... | collective-permute-start | bytes 786440 | tf_op jit(solution)/shard_map/ppermute | solution.py:27
  54.6 1.3 %collective-permute-start.13 = (bf16[128,512]{1,0:T(8,128)(2,1)S(1)}, bf16[128,512]{1,0:T(8,128)(2,1)S(1)}, u32[]{:S(2)}, u32[]{:S(2)}) collective-permute-start(bf16[128,512]{1,0:T(8,128)(2,1)S(1)} %get-tuple-element.67), channel_id=1, source_target_pairs={{0,1},{1,0},{2,3},{3,2},{4,5},{5,4},{6,7},{7,6},{8,9},{9,8},{10,11... | collective-permute-start | bytes 393224 | tf_op jit(solution)/shard_map/ppermute | solution.py:27
  59.1 4.6 %collective-permute-start.14 = (bf16[528,512]{1,0:T(8,128)(2,1)S(1)}, bf16[528,512]{1,0:T(8,128)(2,1)S(1)}, u32[]{:S(2)}, u32[]{:S(2)}) collective-permute-start(bf16[528,512]{1,0:T(8,128)(2,1)S(1)} %get-tuple-element.71.refs_3_), channel_id=1, source_target_pairs={{0,1},{1,0},{2,3},{3,2},{4,5},{5,4},{6,7},{7,6},{8,9},{9,8},{10,11... | collective-permute-start | bytes 1622024 | tf_op jit(solution)/shard_map/ppermute | solution.py:27
  59.3 4.4 %collective-permute-start.15 = (bf16[64,512]{1,0:T(8,128)(2,1)S(1)}, bf16[64,512]{1,0:T(8,128)(2,1)S(1)}, u32[]{:S(2)}, u32[]{:S(2)}) collective-permute-start(bf16[64,512]{1,0:T(8,128)(2,1)S(1)} %get-tuple-element.72), channel_id=1, source_target_pairs={{0,2},{2,0},{4,6},{6,4},{1,3},{3,1},{5,7},{7,5},{8,10},{10,8},{12,... | collective-permute-start | bytes 196616 | tf_op jit(solution)/shard_map/ppermute | solution.py:27
  60.0 9.7 %collective-permute-start.20 = (bf16[64,512]{1,0:T(8,128)(2,1)S(1)}, bf16[64,512]{1,0:T(8,128)(2,1)S(1)}, u32[]{:S(2)}, u32[]{:S(2)}) collective-permute-start(bf16[64,512]{1,0:T(8,128)(2,1)S(1)} %get-tuple-element.82), channel_id=1, source_target_pairs={{0,4},{2,6},{4,0},{6,2},{1,5},{3,7},{5,1},{7,3},{8,12},{10,14},{12... | collective-permute-start | bytes 196616 | tf_op jit(solution)/shard_map/ppermute | solution.py:27
  62.8 6.8 %collective-permute-start.21 = (bf16[64,512]{1,0:T(8,128)(2,1)S(1)}, bf16[64,512]{1,0:T(8,128)(2,1)S(1)}, u32[]{:S(2)}, u32[]{:S(2)}) collective-permute-start(bf16[64,512]{1,0:T(8,128)(2,1)S(1)} %get-tuple-element.83), channel_id=1, source_target_pairs={{0,6},{2,4},{4,2},{6,0},{1,7},{3,5},{5,3},{7,1},{8,14},{10,12},{12... | collective-permute-start | bytes 196616 | tf_op jit(solution)/shard_map/ppermute | solution.py:27
  65.1 13.0 %collective-permute-start.16 = (bf16[144,512]{1,0:T(8,128)(2,1)S(1)}, bf16[144,512]{1,0:T(8,128)(2,1)S(1)}, u32[]{:S(2)}, u32[]{:S(2)}) collective-permute-start(bf16[144,512]{1,0:T(8,128)(2,1)S(1)} %get-tuple-element.74), channel_id=1, source_target_pairs={{0,2},{2,0},{4,6},{6,4},{1,3},{3,1},{5,7},{7,5},{8,10},{10,8},{12,... | collective-permute-start | bytes 442376 | tf_op jit(solution)/shard_map/ppermute | solution.py:27
  65.9 14.3 %collective-permute-start.17 = (bf16[144,512]{1,0:T(8,128)(2,1)S(1)}, bf16[144,512]{1,0:T(8,128)(2,1)S(1)}, u32[]{:S(2)}, u32[]{:S(2)}) collective-permute-start(bf16[144,512]{1,0:T(8,128)(2,1)S(1)} %get-tuple-element.75), channel_id=1, source_target_pairs={{0,4},{2,6},{4,0},{6,2},{1,5},{3,7},{5,1},{7,3},{8,12},{10,14},{12... | collective-permute-start | bytes 442376 | tf_op jit(solution)/shard_map/ppermute | solution.py:27
  69.6 11.1 %collective-permute-start.18 = (bf16[144,512]{1,0:T(8,128)(2,1)S(1)}, bf16[144,512]{1,0:T(8,128)(2,1)S(1)}, u32[]{:S(2)}, u32[]{:S(2)}) collective-permute-start(bf16[144,512]{1,0:T(8,128)(2,1)S(1)} %get-tuple-element.76), channel_id=1, source_target_pairs={{0,6},{2,4},{4,2},{6,0},{1,7},{3,5},{5,3},{7,1},{8,14},{10,12},{12... | collective-permute-start | bytes 442376 | tf_op jit(solution)/shard_map/ppermute | solution.py:27
  70.2 5.1 %collective-permute-start.22 = (bf16[16,4096]{1,0:T(8,128)(2,1)S(1)}, bf16[16,4096]{1,0:T(8,128)(2,1)S(1)}, u32[]{:S(2)}, u32[]{:S(2)}) collective-permute-start(bf16[16,4096]{1,0:T(8,128)(2,1)S(1)} %get-tuple-element.84.refs_0_), channel_id=1, source_target_pairs={{0,8},{8,0},{16,24},{24,16},{1,9},{9,1},{17,25},{25,17},{2,10},{10... | collective-permute-start | bytes 393224 | tf_op jit(solution)/shard_map/ppermute | solution.py:27
  70.9 5.0 %collective-permute-start.26 = (bf16[16,4096]{1,0:T(8,128)(2,1)S(1)}, bf16[16,4096]{1,0:T(8,128)(2,1)S(1)}, u32[]{:S(2)}, u32[]{:S(2)}) collective-permute-start(bf16[16,4096]{1,0:T(8,128)(2,1)S(1)} %get-tuple-element.85.refs_4_), channel_id=1, source_target_pairs={{0,16},{8,24},{16,0},{24,8},{1,17},{9,25},{17,1},{25,9},{2,18},{10... | collective-permute-start | bytes 393224 | tf_op jit(solution)/shard_map/ppermute | solution.py:27
  75.3 11.1 %collective-permute-start.23 = (bf16[16,4096]{1,0:T(8,128)(2,1)S(1)}, bf16[16,4096]{1,0:T(8,128)(2,1)S(1)}, u32[]{:S(2)}, u32[]{:S(2)}) collective-permute-start(bf16[16,4096]{1,0:T(8,128)(2,1)S(1)} %get-tuple-element.84.refs_0_), channel_id=1, source_target_pairs={{0,16},{8,24},{16,0},{24,8},{1,17},{9,25},{17,1},{25,9},{2,18},{10... | collective-permute-start | bytes 393224 | tf_op jit(solution)/shard_map/ppermute | solution.py:27
  75.9 10.5 %collective-permute-start.25 = (bf16[16,4096]{1,0:T(8,128)(2,1)S(1)}, bf16[16,4096]{1,0:T(8,128)(2,1)S(1)}, u32[]{:S(2)}, u32[]{:S(2)}) collective-permute-start(bf16[16,4096]{1,0:T(8,128)(2,1)S(1)} %get-tuple-element.85.refs_4_), channel_id=1, source_target_pairs={{0,8},{8,0},{16,24},{24,16},{1,9},{9,1},{17,25},{25,17},{2,10},{10... | collective-permute-start | bytes 393224 | tf_op jit(solution)/shard_map/ppermute | solution.py:27
  78.0 8.4 %collective-permute-start.24 = (bf16[16,4096]{1,0:T(8,128)(2,1)S(1)}, bf16[16,4096]{1,0:T(8,128)(2,1)S(1)}, u32[]{:S(2)}, u32[]{:S(2)}) collective-permute-start(bf16[16,4096]{1,0:T(8,128)(2,1)S(1)} %collective-permute-done.22.refs_1_), channel_id=1, source_target_pairs={{0,16},{8,24},{16,0},{24,8},{1,17},{9,25},{17,1},{25,9},{2,18},{10... | collective-permute-start | bytes 393224 | tf_op jit(solution)/shard_map/ppermute | solution.py:27
  80.2 6.5 %collective-permute-start.27 = (bf16[16,4096]{1,0:T(8,128)(2,1)S(1)}, bf16[16,4096]{1,0:T(8,128)(2,1)S(1)}, u32[]{:S(2)}, u32[]{:S(2)}) collective-permute-start(bf16[16,4096]{1,0:T(8,128)(2,1)S(1)} %collective-permute-done.26.refs_6_), channel_id=1, source_target_pairs={{0,8},{8,0},{16,24},{24,16},{1,9},{9,1},{17,25},{25,17},{2,10},{10... | collective-permute-start | bytes 393224 | tf_op jit(solution)/shard_map/ppermute | solution.py:27
  81.4 11.7 %collective-permute-start.19 = (bf16[128,512]{1,0:T(8,128)(2,1)S(1)}, bf16[128,512]{1,0:T(8,128)(2,1)S(1)}, u32[]{:S(2)}, u32[]{:S(2)}) collective-permute-start(bf16[128,512]{1,0:T(8,128)(2,1)S(1)} %get-tuple-element.79), channel_id=1, source_target_pairs={{0,0},{1,1},{2,8},{3,9},{4,16},{5,17},{6,24},{7,25},{8,2},{9,3},{1... | collective-permute-start | bytes 393224 | tf_op jit(solution)/shard_map/ppermute | solution.py:674
  (1 other events, 1.2 us)

commit v8 on v7

--- a/solution.py
+++ b/solution.py
@@ -319,7 +319,7 @@
         out[pl.ds(base, tile), :] = acc.astype(out.dtype)
         return carry
 
-    lax.fori_loop(0, out.shape[0] // tile, step, 0)
+    lax.fori_loop(0, out.shape[0] // tile, step, 0, unroll=2)
     sub = rows_here // dp
     for g in range(2):
         for z in range(pairs):

time: 93.9 us -> 94.2 us (level)
  transfers between devices with their start and end apart: 28 -> 28, of which waited for: 6 -> 7; matrix products, arithmetic and copies ran while one was open for 0% -> 0% of each run, Pallas kernels for 23% -> 24%
where the time goes in v8:
time: 94.2 us; the launch traced here: 94 us
  starting transfers between devices  36.8 us (39%)
  Pallas kernels  25.5 us (27%)
  waiting for transfers between devices  14.5 us (15%)
  blocking collectives  14.2 us (15%)
  local copies, waits for them, and re-layouts  1.9 us (2%)
    ppermute x23, starting transfers between devices, hop(): return lax.ppermute(x, axis, [(i, i ^ mask) for i in range(size)])  22.9 us
    pallas_call x14, Pallas kernels, kernel_call(): pl.pallas_call(whole_body, in_specs=[pl.BlockSpec(memory_space=pltpu.SMEM...  20 us
    all_gather x1, blocking collectives, local_square(): sent = lax.all_gather(sent_own, 'dp', axis=0)  14.2 us
    ppermute x4, starting transfers between devices, local_square(): mine.append(lax.ppermute(hidden_in, ('dp',) + TABLE, perm))  10.2 us
    ppermute x4, waiting for transfers between devices, local_square(): mine.append(lax.ppermute(hidden_in, ('dp',) + TABLE, perm))  7.31 us
    ppermute x1, waiting for transfers between devices, local_square(): grad_hidden = lax.ppermute(grad_hidden, ('dp',) + TABLE, perm)  3.71 us
    ppermute x1, starting transfers between devices, local_square(): grad_hidden = lax.ppermute(grad_hidden, ('dp',) + TABLE, perm)  3.64 us
    ppermute x23, waiting for transfers between devices, hop(): return lax.ppermute(x, axis, [(i, i ^ mask) for i in range(size)])  3.51 us
  transfers between devices with their start and end apart: 28, of which 7 were waited for; matrix products, arithmetic and copies ran while one was open for 0% of the time, Pallas kernels for 24%

profile of v8, /device:TPU:2, one launch (start us, length us, event | category | flops | bytes accessed | tf_op | source)
XLA Modules:
  0.0 94.0 jit_solution(7419763558749072940)
XLA Ops:
  0.7 4.9 %collective-permute-start = (bf16[128,512]{1,0:T(8,128)(2,1)}, bf16[128,512]{1,0:T(8,128)(2,1)S(1)}, u32[]{:S(2)}, u32[]{:S(2)}) collective-permute-start(bf16[128,512]{1,0:T(8,128)(2,1)} %param.6), channel_id=1, source_target_pairs={{0,0},{1,1},{2,8},{3,9},{4,16},{5,17},{6,24},{7,25},{8,2},{9,3},{1... | collective-permute-start | bytes 393224 | tf_op jit(solution)/shard_map/ppermute | solution.py:590
  5.6 4.4 %collective-permute-start.3 = (bf16[128,512]{1,0:T(8,128)(2,1)}, bf16[128,512]{1,0:T(8,128)(2,1)S(1)}, u32[]{:S(2)}, u32[]{:S(2)}) collective-permute-start(bf16[128,512]{1,0:T(8,128)(2,1)} %param.6), channel_id=1, source_target_pairs={{0,6},{1,7},{2,14},{3,15},{4,22},{5,23},{6,30},{7,31},{8,4},{9,5},... | collective-permute-start | bytes 393224 | tf_op jit(solution)/shard_map/ppermute | solution.py:590
  10.0 0.9 collective-permute-start.2
  11.0 1.2 %copy-done.1 = bf16[128,4096]{1,0:T(8,128)(2,1)S(1)} copy-done((bf16[128,4096]{1,0:T(8,128)(2,1)S(1)}, bf16[128,4096]{1,0:T(8,128)(2,1)}, u32[]{:S(2)}) %copy-start.1) | copy-done | bytes 1048600
  13.0 2.9 %collective-permute-done.3.refs_4_.refs_3_ = bf16[128,512]{1,0:T(8,128)(2,1)S(1)} collective-permute-done((bf16[128,512]{1,0:T(8,128)(2,1)}, bf16[128,512]{1,0:T(8,128)(2,1)S(1)}, u32[]{:S(2)}, u32[]{:S(2)}) %collective-permute-start.3) | collective-permute-done | bytes 131104 | tf_op jit(solution)/shard_map/ppermute | solution.py:590
  15.9 4.4 %collective-permute-done.2.refs_3_.refs_2_ = bf16[128,512]{1,0:T(8,128)(2,1)S(1)} collective-permute-done((bf16[128,512]{1,0:T(8,128)(2,1)}, bf16[128,512]{1,0:T(8,128)(2,1)S(1)}, u32[]{:S(2)}, u32[]{:S(2)}) %collective-permute-start.2) | collective-permute-done | bytes 131104 | tf_op jit(solution)/shard_map/ppermute | solution.py:590
  21.6 1.4 %collective-permute-start.8 = (bf16[256,512]{1,0:T(8,128)(2,1)S(1)}, bf16[256,512]{1,0:T(8,128)(2,1)S(1)}, u32[]{:S(2)}, u32[]{:S(2)}) collective-permute-start(bf16[256,512]{1,0:T(8,128)(2,1)S(1)} %get-tuple-element.52), channel_id=1, source_target_pairs={{0,2},{2,0},{4,6},{6,4},{1,3},{3,1},{5,7},{7,5},{8,10},{10,8},{12,... | collective-permute-start | bytes 786440 | tf_op jit(solution)/shard_map/ppermute | solution.py:27
  22.9 3.3 %collective-permute-start.9 = (bf16[256,512]{1,0:T(8,128)(2,1)S(1)}, bf16[256,512]{1,0:T(8,128)(2,1)S(1)}, u32[]{:S(2)}, u32[]{:S(2)}) collective-permute-start(bf16[256,512]{1,0:T(8,128)(2,1)S(1)} %get-tuple-element.53), channel_id=1, source_target_pairs={{0,4},{2,6},{4,0},{6,2},{1,5},{3,7},{5,1},{7,3},{8,12},{10,14},{12... | collective-permute-start | bytes 786440 | tf_op jit(solution)/shard_map/ppermute | solution.py:27
  26.2 1.3 %shard_map.102 = (bf16[256,512]{1,0:T(8,128)(2,1)S(1)}, bf16[256,512]{1,0:T(8,128)(2,1)S(1)}) custom-call(s32[3]{0:T(128)S(1)} %pad_add_fusion.refs_0_.ids, bf16[128,512]{1,0:T(8,128)(2,1)S(1)} %collective-permute-done.refs_1_.refs_0_, bf16[128,512]{1,0:T(8,128)(2,1)S(1)} %collective-permute-done.1.refs_2_.refs_1_, ...), custom_call_target="tpu_custom_call" | custom-call | tf_op jit(solution)/shard_map/pallas_call | solution.py:239
  28.3 14.2 %all-gather = bf16[640,512]{1,0:T(8,128)(2,1)S(1)} all-gather(bf16[160,512]{1,0:T(8,128)(2,1)S(1)} %get-tuple-element.49), channel_id=2, replica_groups=mesh['dp'=4,'pair'=4,'core'=2] {'dp'}, dimensions={0}, use_global_device_ids=true | all-gather | bytes 819200 | tf_op jit(solution)/shard_map/all_gather | solution.py:600
  42.6 0.8 shard_map.106
  43.9 1.5 %collective-permute-start.11 = (bf16[256,512]{1,0:T(8,128)(2,1)S(1)}, bf16[256,512]{1,0:T(8,128)(2,1)S(1)}, u32[]{:S(2)}, u32[]{:S(2)}) collective-permute-start(bf16[256,512]{1,0:T(8,128)(2,1)S(1)} %get-tuple-element.57), channel_id=1, source_target_pairs={{0,8},{8,0},{16,24},{24,16},{1,9},{9,1},{17,25},{25,17},{2,10},{10... | collective-permute-start | bytes 786440 | tf_op jit(solution)/shard_map/ppermute | solution.py:27
  45.5 0.9 collective-permute-start.12
  46.3 6.7 %shard_map.107 = (bf16[1024,512]{1,0:T(8,128)(2,1)S(1)}, bf16[256,512]{1,0:T(8,128)(2,1)S(1)}) custom-call(s32[3]{0:T(128)S(1)} %pad_add_fusion.refs_0_.ids, bf16[4,160,512]{2,1,0:T(8,128)(2,1)S(1)} %bitcast.8, f32[8,128]{1,0:T(8,128)S(1)} %get-tuple-element.58.refs_2_), custom_call_target="tpu_custom_call" | custom-call | tf_op jit(solution)/shard_map/pallas_call | solution.py:239
  53.1 1.9 %shard_map.108 = (bf16[512,512]{1,0:T(8,128)(2,1)S(1)}, f32[512,512]{1,0:T(8,128)S(1)}, f32[128,512]{1,0:T(8,128)S(1)}, bf16[128,512]{1,0:T(8,128)(2,1)S(1)}, bf...) custom-call(s32[3]{0:T(128)S(1)} %pad_add_fusion.refs_0_.ids, bf16[256,512]{1,0:T(8,128)(2,1)S(1)} %get-tuple-element.54.refs_1_, ...), custom_call_target="tpu_custom_call" | custom-call | tf_op jit(solution)/shard_map/pallas_call | solution.py:239
  55.0 1.3 %collective-permute-done.13.refs_2_ = bf16[128,512]{1,0:T(8,128)(2,1)S(1)} collective-permute-done((bf16[128,512]{1,0:T(8,128)(2,1)S(1)}, bf16[128,512]{1,0:T(8,128)(2,1)S(1)}, u32[]{:S(2)}, u32[]{:S(2)}) %collective-permute-start.13) | collective-permute-done | bytes 131104 | tf_op jit(solution)/shard_map/ppermute | solution.py:27
  57.0 2.6 %shard_map.110 = (bf16[512,512]{1,0:T(8,128)(2,1)S(1)}, bf16[128,512]{1,0:T(8,128)(2,1)}, bf16[528,512]{1,0:T(8,128)(2,1)S(1)}) custom-call(s32[3]{0:T(128)S(1)} %pad_add_fusion.refs_0_.ids, f32[512,512]{1,0:T(8,128)S(1)} %get-tuple-element.60.refs_1_, f32[128,512]{1,0:T(8,128)S(1)} %get-tuple-element.61.refs_2_, ...), custom_call_target="tpu_custom_call" | custom-call | tf_op jit(solution)/shard_map/pallas_call | solution.py:239
  60.0 3.2 %collective-permute-start.20 = (bf16[64,512]{1,0:T(8,128)(2,1)S(1)}, bf16[64,512]{1,0:T(8,128)(2,1)S(1)}, u32[]{:S(2)}, u32[]{:S(2)}) collective-permute-start(bf16[64,512]{1,0:T(8,128)(2,1)S(1)} %get-tuple-element.82), channel_id=1, source_target_pairs={{0,4},{2,6},{4,0},{6,2},{1,5},{3,7},{5,1},{7,3},{8,12},{10,14},{12... | collective-permute-start | bytes 196616 | tf_op jit(solution)/shard_map/ppermute | solution.py:27
  63.2 0.9 collective-permute-start.21
  64.1 1.4 %shard_map.111 = (bf16[144,512]{1,0:T(8,128)(2,1)S(1)}, bf16[144,512]{1,0:T(8,128)(2,1)S(1)}, bf16[144,512]{1,0:T(8,128)(2,1)S(1)}, bf16[144,512]{1,0:T(8,128)(2,1)S(1)}, f32[8,128]{1,0:T(8,128)S(1)}) custom-call(s32[3]{0:T(128)S(1)} %pad_add_fusion.refs_0_.ids, bf16[512,512]{1,0:T(8,128)(2,1)S(1)} %get-tuple-element.70.refs_1_.refs_5_, ...), custom_call_target="tpu_custom_call" | custom-call | tf_op jit(solution)/shard_map/pallas_call | solution.py:239
  65.9 4.1 %collective-permute-start.17 = (bf16[144,512]{1,0:T(8,128)(2,1)S(1)}, bf16[144,512]{1,0:T(8,128)(2,1)S(1)}, u32[]{:S(2)}, u32[]{:S(2)}) collective-permute-start(bf16[144,512]{1,0:T(8,128)(2,1)S(1)} %get-tuple-element.75), channel_id=1, source_target_pairs={{0,4},{2,6},{4,0},{6,2},{1,5},{3,7},{5,1},{7,3},{8,12},{10,14},{12... | collective-permute-start | bytes 442376 | tf_op jit(solution)/shard_map/ppermute | solution.py:27
  70.6 1.5 %collective-permute-start.22 = (bf16[16,4096]{1,0:T(8,128)(2,1)S(1)}, bf16[16,4096]{1,0:T(8,128)(2,1)S(1)}, u32[]{:S(2)}, u32[]{:S(2)}) collective-permute-start(bf16[16,4096]{1,0:T(8,128)(2,1)S(1)} %get-tuple-element.84.refs_0_), channel_id=1, source_target_pairs={{0,8},{8,0},{16,24},{24,16},{1,9},{9,1},{17,25},{25,17},{2,10},{10... | collective-permute-start | bytes 393224 | tf_op jit(solution)/shard_map/ppermute | solution.py:27
  72.7 3.0 %shard_map.112 = (f32[1024,512]{1,0:T(8,128)}, f32[8,128]{1,0:T(8,128)S(1)}) custom-call(s32[3]{0:T(128)S(1)} %pad_add_fusion.refs_0_.ids, bf16[128,512]{1,0:T(8,128)(2,1)S(1)} %collective-permute-done.refs_1_.refs_0_, bf16[128,512]{1,0:T(8,128)(2,1)S(1)} %collective-permute-done.1.refs_2_.refs_1_, ...), custom_call_target="tpu_custom_call" | custom-call | tf_op jit(solution)/shard_map/pallas_call | solution.py:555
  75.7 1.4 %collective-permute-start.23 = (bf16[16,4096]{1,0:T(8,128)(2,1)S(1)}, bf16[16,4096]{1,0:T(8,128)(2,1)S(1)}, u32[]{:S(2)}, u32[]{:S(2)}) collective-permute-start(bf16[16,4096]{1,0:T(8,128)(2,1)S(1)} %get-tuple-element.84.refs_0_), channel_id=1, source_target_pairs={{0,16},{8,24},{16,0},{24,8},{1,17},{9,25},{17,1},{25,9},{2,18},{10... | collective-permute-start | bytes 393224 | tf_op jit(solution)/shard_map/ppermute | solution.py:27
  77.2 0.8 collective-permute-done.26.refs_6_
  78.5 1.4 %collective-permute-start.24 = (bf16[16,4096]{1,0:T(8,128)(2,1)S(1)}, bf16[16,4096]{1,0:T(8,128)(2,1)S(1)}, u32[]{:S(2)}, u32[]{:S(2)}) collective-permute-start(bf16[16,4096]{1,0:T(8,128)(2,1)S(1)} %collective-permute-done.22.refs_1_), channel_id=1, source_target_pairs={{0,16},{8,24},{16,0},{24,8},{1,17},{9,25},{17,1},{25,9},{2,18},{10... | collective-permute-start | bytes 393224 | tf_op jit(solution)/shard_map/ppermute | solution.py:27
  79.8 0.8 collective-permute-done.17.refs_3_
  81.8 3.6 %collective-permute-start.19 = (bf16[128,512]{1,0:T(8,128)(2,1)S(1)}, bf16[128,512]{1,0:T(8,128)(2,1)S(1)}, u32[]{:S(2)}, u32[]{:S(2)}) collective-permute-start(bf16[128,512]{1,0:T(8,128)(2,1)S(1)} %get-tuple-element.79), channel_id=1, source_target_pairs={{0,0},{1,1},{2,8},{3,9},{4,16},{5,17},{6,24},{7,25},{8,2},{9,3},{1... | collective-permute-start | bytes 393224 | tf_op jit(solution)/shard_map/ppermute | solution.py:674
  85.4 1.2 %shard_map.116 = f32[32,128]{1,0:T(8,128)} custom-call(s32[3]{0:T(128)S(1)} %pad_add_fusion.refs_0_.ids, f32[8,512]{1,0:T(8,128)S(1)} %get-tuple-element.87.refs_1_, f32[32,128]{1,0:T(8,128)S(1)} %get-tuple-element.88.refs_2_), custom_call_target="tpu_custom_call" | custom-call | tf_op jit(solution)/shard_map/pallas_call | solution.py:239
  87.1 2.5 %shard_map.115 = (f32[128,4096]{1,0:T(8,128)}, f32[8,128]{1,0:T(8,128)}) custom-call(s32[3]{0:T(128)S(1)} %pad_add_fusion.refs_0_.ids, bf16[16,4096]{1,0:T(8,128)(2,1)S(1)} %get-tuple-element.84.refs_0_, bf16[16,4096]{1,0:T(8,128)(2,1)S(1)} %collective-permute-done.22.refs_1_, bf16[16,4096]{1,0:T(8,128)(2,1)S(1)} %collective-permute-done.23.refs_2_, ...), custom_call_target="tpu_custom_call" | custom-call | tf_op jit(solution)/shard_map/pallas_call | solution.py:516
  89.6 3.7 %collective-permute-done.19 = bf16[128,512]{1,0:T(8,128)(2,1)S(1)} collective-permute-done((bf16[128,512]{1,0:T(8,128)(2,1)S(1)}, bf16[128,512]{1,0:T(8,128)(2,1)S(1)}, u32[]{:S(2)}, u32[]{:S(2)}) %collective-permute-start.19) | collective-permute-done | bytes 131104 | tf_op jit(solution)/shard_map/ppermute | solution.py:674
  93.3 0.7 copy.12
  (53 shorter events, 8.2 us)
Async XLA Ops:
  0.6 25.6 %copy-start = (bf16[1024,512]{1,0:T(8,128)(2,1)S(1)}, bf16[1024,512]{1,0:T(8,128)(2,1)}, u32[]{:S(2)}) copy-start(bf16[1024,512]{1,0:T(8,128)(2,1)} %refs_2_.1) | copy-start | bytes 3145732
  0.6 12.3 %collective-permute-start.1 = (bf16[128,512]{1,0:T(8,128)(2,1)}, bf16[128,512]{1,0:T(8,128)(2,1)S(1)}, u32[]{:S(2)}, u32[]{:S(2)}) collective-permute-start(bf16[128,512]{1,0:T(8,128)(2,1)} %param.6), channel_id=1, source_target_pairs={{0,2},{1,3},{2,10},{3,11},{4,18},{5,19},{6,26},{7,27},{8,0},{9,1},... | collective-permute-start | bytes 393224 | tf_op jit(solution)/shard_map/ppermute | solution.py:590
  0.7 12.2 %collective-permute-start = (bf16[128,512]{1,0:T(8,128)(2,1)}, bf16[128,512]{1,0:T(8,128)(2,1)S(1)}, u32[]{:S(2)}, u32[]{:S(2)}) collective-permute-start(bf16[128,512]{1,0:T(8,128)(2,1)} %param.6), channel_id=1, source_target_pairs={{0,0},{1,1},{2,8},{3,9},{4,16},{5,17},{6,24},{7,25},{8,2},{9,3},{1... | collective-permute-start | bytes 393224 | tf_op jit(solution)/shard_map/ppermute | solution.py:590
  5.6 10.2 %collective-permute-start.3 = (bf16[128,512]{1,0:T(8,128)(2,1)}, bf16[128,512]{1,0:T(8,128)(2,1)S(1)}, u32[]{:S(2)}, u32[]{:S(2)}) collective-permute-start(bf16[128,512]{1,0:T(8,128)(2,1)} %param.6), channel_id=1, source_target_pairs={{0,6},{1,7},{2,14},{3,15},{4,22},{5,23},{6,30},{7,31},{8,4},{9,5},... | collective-permute-start | bytes 393224 | tf_op jit(solution)/shard_map/ppermute | solution.py:590
  10.0 10.2 %collective-permute-start.2 = (bf16[128,512]{1,0:T(8,128)(2,1)}, bf16[128,512]{1,0:T(8,128)(2,1)S(1)}, u32[]{:S(2)}, u32[]{:S(2)}) collective-permute-start(bf16[128,512]{1,0:T(8,128)(2,1)} %param.6), channel_id=1, source_target_pairs={{0,4},{1,5},{2,12},{3,13},{4,20},{5,21},{6,28},{7,29},{8,6},{9,7},... | collective-permute-start | bytes 393224 | tf_op jit(solution)/shard_map/ppermute | solution.py:590
  12.8 14.9 %copy-start.2 = (bf16[128,512]{1,0:T(8,128)(2,1)S(1)}, bf16[128,512]{1,0:T(8,128)(2,1)}, u32[]{:S(2)}) copy-start(bf16[128,512]{1,0:T(8,128)(2,1)} %refs_3_.1) | copy-start | bytes 393220
  12.8 14.9 %copy-start.3 = (s32[128,32]{0,1:T(8,128)S(1)}, s32[128,32]{0,1:T(8,128)}, u32[]{:S(2)}) copy-start(s32[128,32]{0,1:T(8,128)} %param.9) | copy-start | bytes 49156
  12.8 14.8 %copy-start.4 = (f32[128,32]{0,1:T(8,128)S(1)}, f32[128,32]{0,1:T(8,128)}, u32[]{:S(2)}) copy-start(f32[128,32]{0,1:T(8,128)} %param.10) | copy-start | bytes 49156
  12.9 8.1 %collective-permute-start.7 = (bf16[512,512]{1,0:T(8,128)(2,1)S(1)}, bf16[512,512]{1,0:T(8,128)(2,1)S(1)}, u32[]{:S(2)}, u32[]{:S(2)}) collective-permute-start(bf16[512,512]{1,0:T(8,128)(2,1)S(1)} %get-tuple-element.51), channel_id=1, source_target_pairs={{0,1},{1,0},{2,3},{3,2},{4,5},{5,4},{6,7},{7,6},{8,9},{9,8},{10,11... | collective-permute-start | bytes 1572872 | tf_op jit(solution)/shard_map/ppermute | solution.py:27
  20.8 5.4 %collective-permute-start.4 = (bf16[512,512]{1,0:T(8,128)(2,1)S(1)}, bf16[512,512]{1,0:T(8,128)(2,1)S(1)}, u32[]{:S(2)}, u32[]{:S(2)}) collective-permute-start(bf16[512,512]{1,0:T(8,128)(2,1)S(1)} %shard_map.101), channel_id=1, source_target_pairs={{0,1},{1,0},{2,3},{3,2},{4,5},{5,4},{6,7},{7,6},{8,9},{9,8},{10,11... | collective-permute-start | bytes 1572872 | tf_op jit(solution)/shard_map/ppermute | solution.py:27
  21.6 21.0 %collective-permute-start.8 = (bf16[256,512]{1,0:T(8,128)(2,1)S(1)}, bf16[256,512]{1,0:T(8,128)(2,1)S(1)}, u32[]{:S(2)}, u32[]{:S(2)}) collective-permute-start(bf16[256,512]{1,0:T(8,128)(2,1)S(1)} %get-tuple-element.52), channel_id=1, source_target_pairs={{0,2},{2,0},{4,6},{6,4},{1,3},{3,1},{5,7},{7,5},{8,10},{10,8},{12,... | collective-permute-start | bytes 786440 | tf_op jit(solution)/shard_map/ppermute | solution.py:27
  22.9 19.6 %collective-permute-start.9 = (bf16[256,512]{1,0:T(8,128)(2,1)S(1)}, bf16[256,512]{1,0:T(8,128)(2,1)S(1)}, u32[]{:S(2)}, u32[]{:S(2)}) collective-permute-start(bf16[256,512]{1,0:T(8,128)(2,1)S(1)} %get-tuple-element.53), channel_id=1, source_target_pairs={{0,4},{2,6},{4,0},{6,2},{1,5},{3,7},{5,1},{7,3},{8,12},{10,14},{12... | collective-permute-start | bytes 786440 | tf_op jit(solution)/shard_map/ppermute | solution.py:27
  27.5 15.0 %collective-permute-start.5 = (bf16[256,512]{1,0:T(8,128)(2,1)S(1)}, bf16[256,512]{1,0:T(8,128)(2,1)S(1)}, u32[]{:S(2)}, u32[]{:S(2)}) collective-permute-start(bf16[256,512]{1,0:T(8,128)(2,1)S(1)} %get-tuple-element.47.refs_1_), channel_id=1, source_target_pairs={{0,8},{8,0},{16,24},{24,16},{1,9},{9,1},{17,25},{25,17},{2,10},{10... | collective-permute-start | bytes 786440 | tf_op jit(solution)/shard_map/ppermute | solution.py:27
  27.6 14.9 %collective-permute-start.6 = (bf16[256,512]{1,0:T(8,128)(2,1)S(1)}, bf16[256,512]{1,0:T(8,128)(2,1)S(1)}, u32[]{:S(2)}, u32[]{:S(2)}) collective-permute-start(bf16[256,512]{1,0:T(8,128)(2,1)S(1)} %get-tuple-element.48.refs_3_), channel_id=1, source_target_pairs={{0,16},{8,24},{16,0},{24,8},{1,17},{9,25},{17,1},{25,9},{2,18},{10... | collective-permute-start | bytes 786440 | tf_op jit(solution)/shard_map/ppermute | solution.py:27
  43.4 9.7 %collective-permute-start.10 = (bf16[256,512]{1,0:T(8,128)(2,1)S(1)}, bf16[256,512]{1,0:T(8,128)(2,1)S(1)}, u32[]{:S(2)}, u32[]{:S(2)}) collective-permute-start(bf16[256,512]{1,0:T(8,128)(2,1)S(1)} %get-tuple-element.55), channel_id=1, source_target_pairs={{0,16},{8,24},{16,0},{24,8},{1,17},{9,25},{17,1},{25,9},{2,18},{10... | collective-permute-start | bytes 786440 | tf_op jit(solution)/shard_map/ppermute | solution.py:27
  43.9 9.2 %collective-permute-start.11 = (bf16[256,512]{1,0:T(8,128)(2,1)S(1)}, bf16[256,512]{1,0:T(8,128)(2,1)S(1)}, u32[]{:S(2)}, u32[]{:S(2)}) collective-permute-start(bf16[256,512]{1,0:T(8,128)(2,1)S(1)} %get-tuple-element.57), channel_id=1, source_target_pairs={{0,8},{8,0},{16,24},{24,16},{1,9},{9,1},{17,25},{25,17},{2,10},{10... | collective-permute-start | bytes 786440 | tf_op jit(solution)/shard_map/ppermute | solution.py:27
  45.5 11.5 %collective-permute-start.12 = (bf16[256,512]{1,0:T(8,128)(2,1)S(1)}, bf16[256,512]{1,0:T(8,128)(2,1)S(1)}, u32[]{:S(2)}, u32[]{:S(2)}) collective-permute-start(bf16[256,512]{1,0:T(8,128)(2,1)S(1)} %get-tuple-element.65), channel_id=1, source_target_pairs={{0,6},{2,4},{4,2},{6,0},{1,7},{3,5},{5,3},{7,1},{8,14},{10,12},{12... | collective-permute-start | bytes 786440 | tf_op jit(solution)/shard_map/ppermute | solution.py:27
  55.0 1.3 %collective-permute-start.13 = (bf16[128,512]{1,0:T(8,128)(2,1)S(1)}, bf16[128,512]{1,0:T(8,128)(2,1)S(1)}, u32[]{:S(2)}, u32[]{:S(2)}) collective-permute-start(bf16[128,512]{1,0:T(8,128)(2,1)S(1)} %get-tuple-element.67), channel_id=1, source_target_pairs={{0,1},{1,0},{2,3},{3,2},{4,5},{5,4},{6,7},{7,6},{8,9},{9,8},{10,11... | collective-permute-start | bytes 393224 | tf_op jit(solution)/shard_map/ppermute | solution.py:27
  59.5 4.6 %collective-permute-start.14 = (bf16[528,512]{1,0:T(8,128)(2,1)S(1)}, bf16[528,512]{1,0:T(8,128)(2,1)S(1)}, u32[]{:S(2)}, u32[]{:S(2)}) collective-permute-start(bf16[528,512]{1,0:T(8,128)(2,1)S(1)} %get-tuple-element.71.refs_3_), channel_id=1, source_target_pairs={{0,1},{1,0},{2,3},{3,2},{4,5},{5,4},{6,7},{7,6},{8,9},{9,8},{10,11... | collective-permute-start | bytes 1622024 | tf_op jit(solution)/shard_map/ppermute | solution.py:27
  59.7 4.4 %collective-permute-start.15 = (bf16[64,512]{1,0:T(8,128)(2,1)S(1)}, bf16[64,512]{1,0:T(8,128)(2,1)S(1)}, u32[]{:S(2)}, u32[]{:S(2)}) collective-permute-start(bf16[64,512]{1,0:T(8,128)(2,1)S(1)} %get-tuple-element.72), channel_id=1, source_target_pairs={{0,2},{2,0},{4,6},{6,4},{1,3},{3,1},{5,7},{7,5},{8,10},{10,8},{12,... | collective-permute-start | bytes 196616 | tf_op jit(solution)/shard_map/ppermute | solution.py:27
  60.0 10.1 %collective-permute-start.20 = (bf16[64,512]{1,0:T(8,128)(2,1)S(1)}, bf16[64,512]{1,0:T(8,128)(2,1)S(1)}, u32[]{:S(2)}, u32[]{:S(2)}) collective-permute-start(bf16[64,512]{1,0:T(8,128)(2,1)S(1)} %get-tuple-element.82), channel_id=1, source_target_pairs={{0,4},{2,6},{4,0},{6,2},{1,5},{3,7},{5,1},{7,3},{8,12},{10,14},{12... | collective-permute-start | bytes 196616 | tf_op jit(solution)/shard_map/ppermute | solution.py:27
  63.2 6.8 %collective-permute-start.21 = (bf16[64,512]{1,0:T(8,128)(2,1)S(1)}, bf16[64,512]{1,0:T(8,128)(2,1)S(1)}, u32[]{:S(2)}, u32[]{:S(2)}) collective-permute-start(bf16[64,512]{1,0:T(8,128)(2,1)S(1)} %get-tuple-element.83), channel_id=1, source_target_pairs={{0,6},{2,4},{4,2},{6,0},{1,7},{3,5},{5,3},{7,1},{8,14},{10,12},{12... | collective-permute-start | bytes 196616 | tf_op jit(solution)/shard_map/ppermute | solution.py:27
  65.5 13.0 %collective-permute-start.16 = (bf16[144,512]{1,0:T(8,128)(2,1)S(1)}, bf16[144,512]{1,0:T(8,128)(2,1)S(1)}, u32[]{:S(2)}, u32[]{:S(2)}) collective-permute-start(bf16[144,512]{1,0:T(8,128)(2,1)S(1)} %get-tuple-element.74), channel_id=1, source_target_pairs={{0,2},{2,0},{4,6},{6,4},{1,3},{3,1},{5,7},{7,5},{8,10},{10,8},{12,... | collective-permute-start | bytes 442376 | tf_op jit(solution)/shard_map/ppermute | solution.py:27
  65.9 14.7 %collective-permute-start.17 = (bf16[144,512]{1,0:T(8,128)(2,1)S(1)}, bf16[144,512]{1,0:T(8,128)(2,1)S(1)}, u32[]{:S(2)}, u32[]{:S(2)}) collective-permute-start(bf16[144,512]{1,0:T(8,128)(2,1)S(1)} %get-tuple-element.75), channel_id=1, source_target_pairs={{0,4},{2,6},{4,0},{6,2},{1,5},{3,7},{5,1},{7,3},{8,12},{10,14},{12... | collective-permute-start | bytes 442376 | tf_op jit(solution)/shard_map/ppermute | solution.py:27
  70.0 11.1 %collective-permute-start.18 = (bf16[144,512]{1,0:T(8,128)(2,1)S(1)}, bf16[144,512]{1,0:T(8,128)(2,1)S(1)}, u32[]{:S(2)}, u32[]{:S(2)}) collective-permute-start(bf16[144,512]{1,0:T(8,128)(2,1)S(1)} %get-tuple-element.76), channel_id=1, source_target_pairs={{0,6},{2,4},{4,2},{6,0},{1,7},{3,5},{5,3},{7,1},{8,14},{10,12},{12... | collective-permute-start | bytes 442376 | tf_op jit(solution)/shard_map/ppermute | solution.py:27
  70.6 5.1 %collective-permute-start.22 = (bf16[16,4096]{1,0:T(8,128)(2,1)S(1)}, bf16[16,4096]{1,0:T(8,128)(2,1)S(1)}, u32[]{:S(2)}, u32[]{:S(2)}) collective-permute-start(bf16[16,4096]{1,0:T(8,128)(2,1)S(1)} %get-tuple-element.84.refs_0_), channel_id=1, source_target_pairs={{0,8},{8,0},{16,24},{24,16},{1,9},{9,1},{17,25},{25,17},{2,10},{10... | collective-permute-start | bytes 393224 | tf_op jit(solution)/shard_map/ppermute | solution.py:27
  72.1 5.8 %collective-permute-start.26 = (bf16[16,4096]{1,0:T(8,128)(2,1)S(1)}, bf16[16,4096]{1,0:T(8,128)(2,1)S(1)}, u32[]{:S(2)}, u32[]{:S(2)}) collective-permute-start(bf16[16,4096]{1,0:T(8,128)(2,1)S(1)} %get-tuple-element.85.refs_4_), channel_id=1, source_target_pairs={{0,16},{8,24},{16,0},{24,8},{1,17},{9,25},{17,1},{25,9},{2,18},{10... | collective-permute-start | bytes 393224 | tf_op jit(solution)/shard_map/ppermute | solution.py:27
  75.7 10.9 %collective-permute-start.23 = (bf16[16,4096]{1,0:T(8,128)(2,1)S(1)}, bf16[16,4096]{1,0:T(8,128)(2,1)S(1)}, u32[]{:S(2)}, u32[]{:S(2)}) collective-permute-start(bf16[16,4096]{1,0:T(8,128)(2,1)S(1)} %get-tuple-element.84.refs_0_), channel_id=1, source_target_pairs={{0,16},{8,24},{16,0},{24,8},{1,17},{9,25},{17,1},{25,9},{2,18},{10... | collective-permute-start | bytes 393224 | tf_op jit(solution)/shard_map/ppermute | solution.py:27
  77.9 8.6 %collective-permute-start.25 = (bf16[16,4096]{1,0:T(8,128)(2,1)S(1)}, bf16[16,4096]{1,0:T(8,128)(2,1)S(1)}, u32[]{:S(2)}, u32[]{:S(2)}) collective-permute-start(bf16[16,4096]{1,0:T(8,128)(2,1)S(1)} %get-tuple-element.85.refs_4_), channel_id=1, source_target_pairs={{0,8},{8,0},{16,24},{24,16},{1,9},{9,1},{17,25},{25,17},{2,10},{10... | collective-permute-start | bytes 393224 | tf_op jit(solution)/shard_map/ppermute | solution.py:27
  78.5 8.1 %collective-permute-start.24 = (bf16[16,4096]{1,0:T(8,128)(2,1)S(1)}, bf16[16,4096]{1,0:T(8,128)(2,1)S(1)}, u32[]{:S(2)}, u32[]{:S(2)}) collective-permute-start(bf16[16,4096]{1,0:T(8,128)(2,1)S(1)} %collective-permute-done.22.refs_1_), channel_id=1, source_target_pairs={{0,16},{8,24},{16,0},{24,8},{1,17},{9,25},{17,1},{25,9},{2,18},{10... | collective-permute-start | bytes 393224 | tf_op jit(solution)/shard_map/ppermute | solution.py:27
  80.6 6.5 %collective-permute-start.27 = (bf16[16,4096]{1,0:T(8,128)(2,1)S(1)}, bf16[16,4096]{1,0:T(8,128)(2,1)S(1)}, u32[]{:S(2)}, u32[]{:S(2)}) collective-permute-start(bf16[16,4096]{1,0:T(8,128)(2,1)S(1)} %collective-permute-done.26.refs_6_), channel_id=1, source_target_pairs={{0,8},{8,0},{16,24},{24,16},{1,9},{9,1},{17,25},{25,17},{2,10},{10... | collective-permute-start | bytes 393224 | tf_op jit(solution)/shard_map/ppermute | solution.py:27
  81.8 11.5 %collective-permute-start.19 = (bf16[128,512]{1,0:T(8,128)(2,1)S(1)}, bf16[128,512]{1,0:T(8,128)(2,1)S(1)}, u32[]{:S(2)}, u32[]{:S(2)}) collective-permute-start(bf16[128,512]{1,0:T(8,128)(2,1)S(1)} %get-tuple-element.79), channel_id=1, source_target_pairs={{0,0},{1,1},{2,8},{3,9},{4,16},{5,17},{6,24},{7,25},{8,2},{9,3},{1... | collective-permute-start | bytes 393224 | tf_op jit(solution)/shard_map/ppermute | solution.py:674
  (1 other events, 1.2 us)
